TPU v7x, 32 devices: a whole 2x2x4 slice. The times are simulated.
32 devices in a mesh: groups: 2 (over y), tensor: 4 (over z), store: 4 (over x, core).
Axes of the slice: x: 2, y: 2, z: 4, core: 2. Of those that a mesh axis runs over, the one named last changes fastest.
Arguments:
- attention_input: bfloat16 [128, 16, 8192], P(('groups', 'store'), None, 'tensor'), parts along dimension 0, may hold values from -6 to 6
- base_projection_weight: bfloat16 [8192, 8192], P('tensor', 'store'), may hold values from -0.0625 to 0.0625
- stored_down_maps: bfloat16 [64, 8192, 64], P('store', 'tensor'), may hold values from -0.0625 to 0.0625
- stored_up_maps: bfloat16 [64, 64, 8192], P('store', None, 'tensor'), may hold values from -0.75 to 0.75
- request_adapter_index: int32 [128], P('groups'), parts along dimension 0, may hold values from 0 to 63, as said below
- adapter_store_slot: int32 [128], P('groups'), parts along dimension 0, may hold values from 0 to 63, as said below
- lengths: int32 [128], P(('groups', 'store')), parts along dimension 0, may hold values from 1 to 16, 768 in all
Outputs:
- projected: bfloat16 [128, 16, 8192], P(('groups', 'store'), None, 'tensor'), parts along dimension 0
There are 2 independent parts, one for each index of `groups`. A program takes and returns all parts, laid end to end along the dimension named above; an argument that names none is the same for every part. Nothing has to cross between parts.
Inputs may be any that keep to these rules, and one draw needn't show every extreme that they name: adapter_store_slot is a permutation of the 64 slots. `request_adapter_index`: among the 16 requests of one store index, at most 8 have adapters of one owner, and some owner has exactly 8 of them.
All inputs are finite; a program needn't handle non-finite values. No bound on the sum of `lengths` on one device may be relied on, other than what follows from the above.
Results may differ from a plain program's by a relative error of at most 0.015.
Values may be sent and summed in bfloat16 or wider, within the bound.
No kernel may reach another device: no remote copies, remote signals or barrier semaphores. Data moves between devices by JAX's collectives and lax.ppermute only.
A program may use at most 192 MiB of HBM per device.

v0:
```python
import jax
import jax.numpy as jnp
from jax import lax
from jax.sharding import PartitionSpec as P


def shards(
    attention_input,
    base_projection_weight,
    stored_down_maps,
    stored_up_maps,
    request_adapter_index,
    adapter_store_slot,
    lengths,
):
    requests, seq_len, width_in = attention_input.shape
    owner_grouping = stored_down_maps.shape[0]
    stores = lax.axis_size("store")
    my_index = lax.axis_index("store")
    capacity = (2 * requests + stores - 1) // stores
    partial_value = jnp.einsum(
        "qtk,kd->qtd",
        attention_input,
        lax.all_gather(base_projection_weight, "store", axis=1, tiled=True),
        preferred_element_type=jnp.float32,
    )
    base_out = lax.psum_scatter(
        partial_value.astype(jnp.bfloat16), "tensor", scatter_dimension=2, tiled=True
    ).astype(jnp.float32)
    slot_all = adapter_store_slot[request_adapter_index]
    owner_all = (slot_all // owner_grouping).reshape(stores, requests)
    local_all = (slot_all % owner_grouping).reshape(stores, requests)
    positions = jnp.arange(requests, dtype=jnp.int32)
    earlier = positions[None, :] < positions[:, None]
    same_owner = owner_all[:, :, None] == owner_all[:, None, :]
    rank_all = jnp.sum(same_owner & earlier[None], axis=2)
    owner_mine = lax.dynamic_index_in_dim(owner_all, my_index, 0, keepdims=False)
    rank_mine = lax.dynamic_index_in_dim(rank_all, my_index, 0, keepdims=False)
    owner_range = jnp.arange(stores, dtype=jnp.int32)
    slot_range = jnp.arange(capacity, dtype=jnp.int32)
    local_range = jnp.arange(owner_grouping, dtype=jnp.int32)
    pick_table = (
        (owner_mine[:, None, None] == owner_range[None, :, None])
        & (rank_mine[:, None, None] == slot_range[None, None, :])
    ).astype(jnp.bfloat16)
    selection_matrix = jnp.sum(
        (
            (owner_all == my_index)[:, :, None, None]
            & (rank_all[:, :, None, None] == slot_range[None, None, :, None])
            & (local_all[:, :, None, None] == local_range[None, None, None, :])
        ).astype(jnp.float32),
        axis=1,
    ).astype(jnp.bfloat16)
    outgoing = jnp.einsum(
        "qoc,qtk->octk", pick_table, attention_input, preferred_element_type=jnp.float32
    ).astype(jnp.bfloat16)
    arrived = lax.all_to_all(outgoing, "store", split_axis=0, concat_axis=0, tiled=True)
    down_sel = jnp.einsum(
        "pmb,bwf->pmwf", selection_matrix, stored_down_maps, preferred_element_type=jnp.float32
    ).astype(jnp.bfloat16)
    up_sel = jnp.einsum(
        "ehw,wkx->ehkx", selection_matrix, stored_up_maps, preferred_element_type=jnp.float32
    ).astype(jnp.bfloat16)
    low_part = jnp.einsum("octk,ockr->octr", arrived, down_sel, preferred_element_type=jnp.float32)
    low_full = lax.psum(low_part.astype(jnp.bfloat16), "tensor")
    delta_rows = jnp.einsum(
        "octr,ocrd->octd", low_full, up_sel, preferred_element_type=jnp.float32
    ).astype(jnp.bfloat16)
    returned = lax.all_to_all(delta_rows, "store", split_axis=0, concat_axis=0, tiled=True)
    my_delta = jnp.einsum("qoc,octd->qtd", pick_table, returned, preferred_element_type=jnp.float32)
    token_slots = jnp.arange(seq_len, dtype=jnp.int32)
    valid_mask = (token_slots[None, :] < lengths[:, None]).astype(jnp.float32)
    total = base_out + 2.0 * my_delta
    return (total * valid_mask[:, :, None]).astype(jnp.bfloat16)


def solution(mesh):
    in_specs = (
        P(("groups", "store"), None, "tensor"),
        P("tensor", "store"),
        P("store", "tensor", None),
        P("store", None, "tensor"),
        P("groups"),
        P("groups"),
        P(("groups", "store")),
    )
    out_specs = P(("groups", "store"), None, "tensor")
    return jax.shard_map(shards, mesh=mesh, in_specs=in_specs, out_specs=out_specs, check_vma=False)
```

profile of v0, /device:TPU:21, one launch (start us, length us, event | category | flops | bytes accessed | tf_op | source)
XLA Modules:
  0.0 329.3 jit_solution(10407843402027774883)
XLA Ops:
  7.4 0.0 copy-start
  7.4 0.0 copy-start.4
  7.4 0.0 copy-start.2
  7.4 0.0 all-gather.2.cloned.1.call-start
  7.4 0.7 all-gather.2.cloned.1.call-update
  8.1 0.0 copy-done.4
  8.1 0.0 copy-done
  8.1 0.8 gather_fusion
  8.9 0.1 gather.6
  9.0 0.2 convert_reduce_fusion.1
  9.3 0.0 copy-done.2
  9.3 2.7 convolution_convert_fusion.2
  12.0 4.2 %all-to-all-start = ((bf16[4,8,16,2048]{3,1,2,0:T(8,128)(2,1)}), bf16[4,8,16,2048]{3,1,2,0:T(8,128)(2,1)S(1)}, u32[]{:S(2)}, u32[]{:S(2)}) async-start(bf16[4,8,16,2048]{3,1,2,0:T(8,128)(2,1)} %convolution_convert_fusion.2), calls=%async_computation.1 | async-start | bytes 4194304 | tf_op jit(solution)/shard_map/all_to_all | solution.py:57
  16.3 0.0 all-reduce.2.cloned.1.call-start
  16.3 0.1 iota_compare_fusion
  16.3 0.1 fusion.27
  16.4 0.1 convert_reduce_fusion
  16.6 12.9 %convolution_convert_fusion.1 = bf16[4,8,2048,64]{2,1,3,0:T(8,128)(2,1)} fusion(bf16[16,2048,64]{1,2,0:T(8,128)(2,1)} %param.9, bf16[4,8,16]{2,1,0:T(8,128)(2,1)S(1)} %convert_reduce_fusion), kind=kOutput, calls=%fused_computation.9 | convolution fusion | flops 138412032 | bytes 12583936 | tf_op jit(solution)/shard_map/pmb,bwf->pmwf/dot_general | solution.py:58
  29.5 22.6 %all-to-all-done = bf16[4,8,16,2048]{3,1,2,0:T(8,128)(2,1)S(1)} async-done(((bf16[4,8,16,2048]{3,1,2,0:T(8,128)(2,1)}), bf16[4,8,16,2048]{3,1,2,0:T(8,128)(2,1)S(1)}, u32[]{:S(2)}, u32[]{:S(2)}) %all-to-all-start) | async-done | bytes 2097184 | tf_op jit(solution)/shard_map/all_to_all | solution.py:57
  52.1 9.6 %fusion.20 = bf16[4,8,16,64]{3,2,1,0:T(8,128)(2,1)} fusion(bf16[4,8,2048,64]{2,1,3,0:T(8,128)(2,1)} %convolution_convert_fusion.1, bf16[4,8,16,2048]{3,1,2,0:T(8,128)(2,1)S(1)} %all-to-all-done), kind=kOutput, calls=%fused_computation.22 | convolution fusion | flops 134250496 | bytes 10551296 | tf_op jit(solution)/shard_map/octk,ockr->octr/dot_general | solution.py:64
  61.7 0.0 all-reduce.2.cloned.1.call-update
  61.7 0.2 reduce-scatter.2.cloned.1.call-start
  62.0 162.4 %all-gather.2.cloned.1.call-done = bf16[2048,8192]{1,0:T(8,128)(2,1)} async-done(((bf16[2048,2048]{1,0:T(8,128)(2,1)}), bf16[2048,8192]{1,0:T(8,128)(2,1)}) %all-gather.2.cloned.1.call-update) | async-done | bytes 33554448 | tf_op jit(solution)/shard_map/all_gather | solution.py:24
  224.4 16.4 %fusion.2 = bf16[16,16,8192]{2,1,0:T(8,128)(2,1)} fusion(bf16[16,16,2048]{2,1,0:T(8,128)(2,1)S(1)} %copy-done.2, bf16[2048,8192]{1,0:T(8,128)(2,1)} %all-gather.2.cloned.1.call-done), kind=kOutput, calls=%fused_computation.3 | convolution fusion | flops 8592031744 | bytes 38797312 | tf_op jit(solution)/shard_map/qtk,kd->qtd/dot_general | solution.py:21
  240.8 0.0 reduce-scatter.2.cloned.1.call-update
  240.8 10.5 %convolution_convert_fusion = bf16[4,8,64,2048]{3,1,2,0:T(8,128)(2,1)} fusion(bf16[16,64,2048]{2,1,0:T(8,128)(2,1)} %param.10, bf16[4,8,16]{2,1,0:T(8,128)(2,1)S(1)} %convert_reduce_fusion), kind=kOutput, calls=%fused_computation.8 | convolution fusion | flops 138412032 | bytes 12583936 | tf_op jit(solution)/shard_map/ehw,wkx->ehkx/dot_general | solution.py:61
  251.3 0.0 all-reduce.2.cloned.1.call-done
  251.3 12.6 %fusion.13 = bf16[4,8,16,2048]{3,2,1,0:T(8,128)(2,1)S(1)} fusion(bf16[4,8,16,64]{3,2,1,0:T(8,128)(2,1)} %all-reduce.2.cloned.1.call-done, bf16[4,8,64,2048]{3,1,2,0:T(8,128)(2,1)} %convolution_convert_fusion), kind=kOutput, calls=%fused_computation.14 | convolution fusion | flops 135266304 | bytes 10551296 | tf_op jit(solution)/shard_map/octr,ocrd->octd/dot_general | solution.py:66
  263.9 0.0 copy-start.3
  263.9 2.5 copy.25
  266.4 3.8 %all-to-all-start.1 = ((bf16[4,8,16,2048]{3,1,2,0:T(8,128)(2,1)}), bf16[4,8,16,2048]{3,1,2,0:T(8,128)(2,1)S(1)}, u32[]{:S(2)}, u32[]{:S(2)}) async-start(bf16[4,8,16,2048]{3,1,2,0:T(8,128)(2,1)} %copy.25), calls=%async_computation.2 | async-start | bytes 4194304 | tf_op jit(solution)/shard_map/all_to_all | solution.py:69
  270.3 0.0 copy-done.3
  270.3 0.0 copy-start.1
  270.3 0.1 fusion.34
  270.3 24.9 %all-to-all-done.1 = bf16[4,8,16,2048]{3,1,2,0:T(8,128)(2,1)S(1)} async-done(((bf16[4,8,16,2048]{3,1,2,0:T(8,128)(2,1)}), bf16[4,8,16,2048]{3,1,2,0:T(8,128)(2,1)S(1)}, u32[]{:S(2)}, u32[]{:S(2)}) %all-to-all-start.1) | async-done | bytes 2097184 | tf_op jit(solution)/shard_map/all_to_all | solution.py:69
  295.2 1.8 convolution_bitcast_fusion
  297.0 20.7 %reduce-scatter.2.cloned.1.call-done = bf16[16,16,2048]{2,1,0:T(8,128)(2,1)} async-done(((bf16[16,16,8192]{2,1,0:T(8,128)(2,1)}), bf16[16,16,2048]{2,1,0:T(8,128)(2,1)}) %reduce-scatter.2.cloned.1.call-update) | async-done | bytes 1048592 | tf_op jit(solution)/shard_map/reduce_scatter | solution.py:27
  317.7 4.2 %fusion.18 = bf16[16,16,2048]{2,1,0:T(8,128)(2,1)} fusion(f32[16,16,2048]{2,0,1:T(8,128)} %convolution_bitcast_fusion, bf16[16,16,2048]{2,1,0:T(8,128)(2,1)} %reduce-scatter.2.cloned.1.call-done, f32[16,16]{1,0:T(8,128)S(1)} %fusion.34), kind=kLoop, calls=%fused_computation.20 | loop fusion | flops 2621440 | bytes 4195328 | tf_op jit(solution)/shard_map/convert_element_type | solution.py:74
  321.9 0.0 copy-done.1
  (8 shorter events, 0.1 us)
Async XLA Ops:
  7.4 0.8 copy-start
  7.4 0.7 copy-start.4
  7.4 1.9 copy-start.2
  7.4 217.0 %all-gather.2.cloned.1.call-start = ((), (), s32[]{:S(2)}) async-start(), calls=%async_computation.3 | async-start | bytes 41943040 | tf_op jit(solution)/shard_map/all_gather | solution.py:24
  12.0 40.1 %all-to-all-start = ((bf16[4,8,16,2048]{3,1,2,0:T(8,128)(2,1)}), bf16[4,8,16,2048]{3,1,2,0:T(8,128)(2,1)S(1)}, u32[]{:S(2)}, u32[]{:S(2)}) async-start(bf16[4,8,16,2048]{3,1,2,0:T(8,128)(2,1)} %convolution_convert_fusion.2), calls=%async_computation.1 | async-start | bytes 4194304 | tf_op jit(solution)/shard_map/all_to_all | solution.py:57
  16.3 235.1 %all-reduce.2.cloned.1.call-start = ((), (), s32[]{:S(2)}) async-start(), calls=%async_computation.5 | async-start | bytes 262144 | tf_op jit(solution)/shard_map/psum | solution.py:65
  61.7 256.0 %reduce-scatter.2.cloned.1.call-start = ((), (), s32[]{:S(2)}) async-start(), calls=%async_computation.4 | async-start | bytes 5242880 | tf_op jit(solution)/shard_map/reduce_scatter | solution.py:27
  263.9 6.3 %copy-start.3 = (s32[16]{0:T(128)S(1)}, s32[16]{0:T(128)}, u32[]{:S(2)}) copy-start(s32[16]{0:T(128)} %param.13) | copy-start | bytes 196
  266.4 28.8 %all-to-all-start.1 = ((bf16[4,8,16,2048]{3,1,2,0:T(8,128)(2,1)}), bf16[4,8,16,2048]{3,1,2,0:T(8,128)(2,1)S(1)}, u32[]{:S(2)}, u32[]{:S(2)}) async-start(bf16[4,8,16,2048]{3,1,2,0:T(8,128)(2,1)} %copy.25), calls=%async_computation.2 | async-start | bytes 4194304 | tf_op jit(solution)/shard_map/all_to_all | solution.py:69
  270.3 51.6 %copy-start.1 = (s32[64]{0:T(128)S(1)}, s32[64]{0:T(128)}, u32[]{:S(2)}) copy-start(s32[64]{0:T(128)} %param.12) | copy-start | bytes 772
Sparse Core Ops, SparseCore 0:
  9.8 214.4 all-gather.1
Sparse Core Ops, SparseCore 1:
  61.8 33.5 all-reduce.1
  240.9 76.8 reduce-scatter.1
where the time goes:
time: 331 us; the launch traced here: 329 us
  waiting for transfers between devices  231 us (70%)
  matrix products  66.5 us (20%)
  between operations  14.9 us (5%)
  starting transfers between devices  8.3 us (3%)
  other arithmetic  4.79 us (1%)
  local copies, waits for them, and re-layouts  3.39 us (1%)
    all_gather x1, waiting for transfers between devices, shards(): lax.all_gather(base_projection_weight, 'store', axis=1, tiled=True)  162 us
    all_to_all x1, waiting for transfers between devices, shards(): lax.all_to_all(delta_rows, 'store', split_axis=0, concat_axis=0, tiled=True)  24.9 us
    all_to_all x1, waiting for transfers between devices, shards(): lax.all_to_all(outgoing, 'store', split_axis=0, concat_axis=0, tiled=True)  22.6 us
    reduce_scatter x1, waiting for transfers between devices, shards(): lax.psum_scatter(partial_value.astype(jnp.bfloat16), 'tensor', scatter_di...  20.7 us
    dot_general x1, matrix products, shards(): jnp.einsum('qtk,kd->qtd', attention_input, lax.all_gather(base_projection...  16.4 us
    dot_general x1, matrix products, shards(): jnp.einsum('pmb,bwf->pmwf', selection_matrix, stored_down_maps, preferred...  12.9 us
    dot_general x1, matrix products, shards(): jnp.einsum('octr,ocrd->octd', low_full, up_sel, preferred_element_type=jn...  12.6 us
    dot_general x1, matrix products, shards(): jnp.einsum('ehw,wkx->ehkx', selection_matrix, stored_up_maps, preferred_e...  10.5 us
  transfers between devices with their start and end apart: 5, of which 4 were waited for; matrix products, arithmetic and copies ran while one was open for 21% of the time, Pallas kernels for 0%

commit v1 on v0

--- a/solution.py
+++ b/solution.py
@@ -1,10 +1,19 @@
+import functools
 import jax
 import jax.numpy as jnp
 from jax import lax
+from jax.experimental import pallas as pl
+from jax.experimental.pallas import tpu as pltpu
 from jax.sharding import PartitionSpec as P
 
-
-def shards(
+VMEM_LIMIT = 48 * 1024 * 1024
+STREAMS = 2
+CHUNK = 64
+BF16 = jnp.bfloat16
+F32 = jnp.float32
+
+
+def general(
     attention_input,
     base_projection_weight,
     stored_down_maps,
@@ -74,6 +83,273 @@
     return (total * valid_mask[:, :, None]).astype(jnp.bfloat16)
 
 
+def project_kernel(first, blocks, pos_ref, *refs):
+    x_refs, w_ref, out_ref, packed = refs[:blocks], refs[blocks], refs[blocks + 1], refs[blocks + 2]
+    rows = packed.shape[0]
+
+    @pl.when(pl.program_id(0) == 0)
+    def _():
+        width = x_refs[0].shape[0]
+        wanted = lax.broadcasted_iota(jnp.int32, (rows, width), 0) + first
+        acc = None
+        for b in range(blocks):
+            pick = (pos_ref[:, b * width : (b + 1) * width] == wanted).astype(F32).astype(BF16)
+            part = jnp.dot(pick, x_refs[b][...], preferred_element_type=F32)
+            acc = part if acc is None else acc + part
+        packed[...] = acc.astype(BF16)
+
+    out_ref[...] = jnp.dot(packed[...], w_ref[...], preferred_element_type=F32).astype(BF16)
+
+
+def project(pos, xs, w, first, rows, tile=512):
+    depth, cols = w.shape
+    blocks = len(xs)
+    block_rows = xs[0].shape[0]
+    return pl.pallas_call(
+        functools.partial(project_kernel, first, blocks),
+        grid=(cols // tile,),
+        in_specs=[pl.BlockSpec(pos.shape, lambda j: (0, 0))]
+        + [pl.BlockSpec((block_rows, depth), lambda j: (0, 0))] * blocks
+        + [pl.BlockSpec((depth, tile), lambda j: (0, j))],
+        out_specs=pl.BlockSpec((rows, tile), lambda j: (0, j)),
+        out_shape=jax.ShapeDtypeStruct((rows, cols), BF16),
+        scratch_shapes=[pltpu.VMEM((rows, depth), BF16)],
+        compiler_params=pltpu.CompilerParams(vmem_limit_bytes=VMEM_LIMIT),
+        cost_estimate=pl.CostEstimate(
+            flops=2 * rows * depth * (cols + blocks * block_rows),
+            bytes_accessed=2 * (depth * cols + rows * cols + blocks * block_rows * depth),
+            transcendentals=0,
+        ),
+    )(pos, *xs, w)
+
+
+def finish_kernel(pieces, deltas, base_pos_ref, delta_pos_ref, *refs):
+    piece_refs, delta_refs, out_ref = refs[:pieces], refs[pieces : pieces + deltas], refs[-1]
+    rows = base_pos_ref.shape[0]
+
+    def add(acc, pos_ref, group, start, value):
+        stack = jnp.concatenate([g[...] for g in group], axis=0) if len(group) > 1 else group[0][...]
+        columns = lax.broadcasted_iota(jnp.int32, (rows, stack.shape[0]), 1) + start
+        pick = jnp.where(pos_ref[...] == columns, F32(value), F32(0)).astype(BF16)
+        part = jnp.dot(pick, stack, preferred_element_type=F32)
+        return part if acc is None else acc + part
+
+    acc = None
+    for refs_, pos_ref, value in (
+        (piece_refs, base_pos_ref, 1.0),
+        (delta_refs, delta_pos_ref, 2.0),
+    ):
+        size = refs_[0].shape[0]
+        step = max(1, 256 // size)
+        for i in range(0, len(refs_), step):
+            acc = add(acc, pos_ref, refs_[i : i + step], i * size, value)
+    out_ref[...] = acc.astype(BF16)
+
+
+def finish(base_pos, delta_pos, pieces, deltas, tile=512):
+    rows = base_pos.shape[0]
+    cols = pieces[0].shape[1]
+    depth = sum(p.shape[0] for p in pieces) + sum(d.shape[0] for d in deltas)
+    return pl.pallas_call(
+        functools.partial(finish_kernel, len(pieces), len(deltas)),
+        grid=(cols // tile,),
+        in_specs=[pl.BlockSpec((rows, 1), lambda j: (0, 0))] * 2
+        + [pl.BlockSpec((a.shape[0], tile), lambda j: (0, j)) for a in list(pieces) + list(deltas)],
+        out_specs=pl.BlockSpec((rows, tile), lambda j: (0, j)),
+        out_shape=jax.ShapeDtypeStruct((rows, cols), BF16),
+        compiler_params=pltpu.CompilerParams(vmem_limit_bytes=VMEM_LIMIT),
+        cost_estimate=pl.CostEstimate(
+            flops=2 * rows * depth * cols, bytes_accessed=2 * (depth + rows) * cols, transcendentals=0
+        ),
+    )(base_pos, delta_pos, *pieces, *deltas)
+
+
+def on_store(value, flip):
+    return lax.ppermute(value, "store", [(i, i ^ flip) for i in range(4)])
+
+
+def forward(s):
+    return 1 if s >= 2 else -1
+
+
+def plane(s, u):
+    return u if s >= 2 else 3 - u
+
+
+def last_step(s):
+    return 3 if s in (0, 3) else 2
+
+
+def on_mesh(value, pairs):
+    return lax.ppermute(value, ("tensor", "store"), [(a * 4 + b, c * 4 + d) for (a, b), (c, d) in pairs])
+
+
+def placed(lens, tokens):
+    n = lens.shape[0]
+    before = jnp.arange(n)[None, :] < jnp.arange(n)[:, None]
+    return jnp.sum(jnp.where(before, lens[None, :], 0), axis=1), jnp.sum(lens)
+
+
+def square(x, w, down, up, request_adapter_index, adapter_store_slot, lengths):
+    requests, tokens, depth = x.shape
+    rows = requests * tokens
+    live = 3 * rows
+    held, _, rank = down.shape
+    capacity = requests // 2
+    span = STREAMS * CHUNK
+    steps = live // span
+    early = rows // span * span
+
+    s = lax.axis_index("store")
+    t = lax.axis_index("tensor")
+    chip = s // 2
+    u = jnp.where(chip == 1, t, 3 - t)
+
+    x_me = x.reshape(rows, depth)
+    len_me = lengths
+    len_sib = on_store(len_me, 1)
+    x_sib = on_store(x_me, 1)
+    x_far = on_store(x_me, 2)
+    len_far = on_store(len_me, 2)
+    len_fsib = on_store(len_me, 3)
+    x_fsib = on_store(x_far, 1)
+    xs = [x_me, x_sib, x_far, x_fsib]
+
+    token = jnp.arange(tokens, dtype=jnp.int32)
+    first_core = (s % 2) == 0
+    starts = [placed(l, tokens) for l in (len_me, len_sib, len_far, len_fsib)]
+    own = starts[0][1] + starts[1][1]
+    offs = [
+        jnp.where(first_core, 0, starts[1][1]),
+        jnp.where(first_core, starts[0][1], 0),
+        own + jnp.where(first_core, 0, starts[3][1]),
+        own + jnp.where(first_core, starts[2][1], 0),
+    ]
+
+    def where_rows(block, length, offset):
+        spot = block[:, None] + offset + token[None, :]
+        return jnp.where(token[None, :] < length[:, None], spot, -(1 << 20))
+
+    lens = [len_me, len_sib, len_far, len_fsib]
+    pos = [where_rows(starts[i][0], lens[i], offs[i] + u * span).reshape(1, rows) for i in range(4)]
+    pos_own = jnp.concatenate(pos[:2], axis=1)
+    pos_all = jnp.concatenate(pos, axis=1)
+
+    total_rows = live + 3 * span
+    parts = [(0, project(pos_own, xs[:2], w, 0, early))]
+    at = early
+    while at < total_rows:
+        size = min(early, total_rows - at)
+        parts.append((at, project(pos_all, xs, w, at, size)))
+        at += size
+
+    def shifted(start, size):
+        for base, value in parts:
+            if base <= start and start + size <= base + value.shape[0]:
+                return value[start - base : start - base + size]
+        raise ValueError
+
+    back_pairs = [((plane(b, 3), b), (plane(b, 2), b)) for b in (1, 2)]
+    final = []
+    carry = [None] * STREAMS
+    for k in range(steps + 3):
+        pairs = [
+            ((plane(b, v), b), (plane(b, v + 1), b))
+            for b in range(4)
+            for v in range(last_step(b))
+            if 0 <= k - v < steps
+        ]
+        for j in range(STREAMS):
+            value = None
+            if k < steps + 3:
+                value = shifted(k * span + j * CHUNK, CHUNK)
+            if carry[j] is not None or k >= 2:
+                total = value.astype(F32)
+                if carry[j] is not None:
+                    total = total + carry[j].astype(F32)
+                if 2 <= k < steps + 2:
+                    back = on_mesh(shifted((k + 1) * span + j * CHUNK, CHUNK), back_pairs)
+                    total = total + back.astype(F32)
+                value = total.astype(BF16)
+            if k >= 2:
+                final.append((k, j, value))
+            carry[j] = on_mesh(value, pairs) if pairs else None
+
+    is_root = s == t
+    across = [((v, v), (v, v ^ 2)) for v in range(4)]
+    beside = [((v, v), (v, v ^ 1)) for v in range(4)] + [((v, v ^ 2), (v, v ^ 3)) for v in range(4)]
+    pieces = []
+    for k, j, value in final:
+        if k >= 2 + rows // span:
+            value = jnp.where(is_root, value, on_mesh(value, across))
+        elif k == 2 + rows // span - 1 or k == 2:
+            value = value
+        got = on_mesh(value, beside)
+        keep = is_root | (s == (t ^ 2))
+        pieces.append(jnp.where(keep, value, got))
+
+    slot_all = adapter_store_slot[request_adapter_index]
+    owner_all = (slot_all // held).reshape(4, requests)
+    local_all = (slot_all % held).reshape(4, requests)
+    order = jnp.arange(requests, dtype=jnp.int32)
+    earlier = order[None, :] < order[:, None]
+    same_owner = owner_all[:, :, None] == owner_all[:, None, :]
+    rank_all = jnp.sum(same_owner & earlier[None], axis=2)
+    lanes = jnp.arange(held * rank, dtype=jnp.int32)
+    fold = (lanes[:, None] % rank == jnp.arange(rank)[None, :]).astype(BF16)
+    down_t = jnp.transpose(down, (0, 2, 1)).reshape(held * rank, depth)
+    up_2d = up.reshape(held * rank, up.shape[2])
+    slots = jnp.arange(capacity, dtype=jnp.int32)
+    low, slot_adapter = [], []
+    for i in range(4):
+        home = s ^ i
+        owner = lax.dynamic_index_in_dim(owner_all, home, 0, keepdims=False)
+        local = lax.dynamic_index_in_dim(local_all, home, 0, keepdims=False)
+        turn = lax.dynamic_index_in_dim(rank_all, home, 0, keepdims=False)
+        every = lax.dot_general(xs[i], down_t, (((1,), (1,)), ((), ())), preferred_element_type=F32)
+        row_local = jnp.repeat(local, tokens)
+        mask = (lanes[None, :] // rank) == row_local[:, None]
+        picked = jnp.where(mask, every.astype(BF16), jnp.zeros((), BF16))
+        mine = (owner == s)[None, :] & (turn[None, :] == slots[:, None])
+        slot_adapter.append(jnp.sum(jnp.where(mine, local[None, :], 0), axis=1))
+        choose = mine[:, None, :, None] & (token[None, :, None, None] == token[None, None, None, :])
+        choose = choose.reshape(capacity * tokens, rows).astype(BF16)
+        folded = jnp.dot(picked, fold, preferred_element_type=F32).astype(BF16)
+        low.append(jnp.dot(choose, folded, preferred_element_type=F32).astype(BF16))
+    low = jnp.concatenate(
+        [jnp.concatenate(low[:2], axis=0), jnp.concatenate(low[2:], axis=0)], axis=1
+    )
+    total = low.astype(F32)
+    for shift in (1, 2, 3):
+        total = total + lax.ppermute(low, "tensor", [(i, i ^ shift) for i in range(4)]).astype(F32)
+    total = total.astype(BF16)
+    total = jnp.concatenate([total[:, :rank], total[:, rank:]], axis=0)
+    adapter = jnp.repeat(jnp.concatenate(slot_adapter), tokens)
+    spread = jnp.where(
+        (lanes[None, :] // rank) == adapter[:, None],
+        jnp.tile(total, (1, held)),
+        jnp.zeros((), BF16),
+    )
+    delta = jnp.dot(spread, up_2d, preferred_element_type=F32).astype(BF16)
+    size = capacity * tokens
+    deltas = [delta[:size]] + [on_store(delta[i * size : (i + 1) * size], i) for i in (1, 2, 3)]
+
+    sums = [starts[i][1] for i in range(4)]
+    root_chip = t // 2
+    my_key = s ^ (2 * root_chip)
+    ahead = sum(jnp.where(((s ^ i) ^ (2 * root_chip)) < my_key, sums[i], 0) for i in range(1, 4))
+    delay = jnp.where((t == 0) | (t == 3), 1, 0)
+    base_pos = where_rows(starts[0][0], len_me, ahead + delay * span).reshape(rows, 1)
+    owner_me = lax.dynamic_index_in_dim(owner_all, s, 0, keepdims=False)
+    turn_me = lax.dynamic_index_in_dim(rank_all, s, 0, keepdims=False)
+    slot_row = ((owner_me ^ s) * capacity + turn_me) * tokens
+    delta_pos = jnp.where(
+        token[None, :] < len_me[:, None], slot_row[:, None] + token[None, :], -(1 << 20)
+    ).reshape(rows, 1)
+    out = finish(base_pos, delta_pos, pieces, deltas)
+    return out.reshape(requests, tokens, out.shape[1])
+
+
 def solution(mesh):
     in_specs = (
         P(("groups", "store"), None, "tensor"),
@@ -85,4 +361,6 @@
         P(("groups", "store")),
     )
     out_specs = P(("groups", "store"), None, "tensor")
-    return jax.shard_map(shards, mesh=mesh, in_specs=in_specs, out_specs=out_specs, check_vma=False)
+    four = mesh.shape["store"] == 4 and mesh.shape["tensor"] == 4
+    body = square if four else general
+    return jax.shard_map(body, mesh=mesh, in_specs=in_specs, out_specs=out_specs, check_vma=False)

time: 331 us -> 298 us (0.900)
  waiting for transfers between devices: 231 us -> 96.9 us
  starting transfers between devices: 8.3 us -> 101 us
  matrix products: 66.5 us -> 22 us
  Pallas kernels: 0 us -> 37.5 us
  other arithmetic: 4.79 us -> 20.4 us
  between operations: 14.9 us -> 6.93 us
  local copies, waits for them, and re-layouts: 3.39 us -> 9.67 us
    all_gather x1 -> x0, waiting for transfers between devices: 162 us -> none  [shards(): lax.all_gather(base_projection_weight, 'store', axis=1, tiled=True)]
    ppermute x0 -> x64, starting transfers between devices: none -> 101 us  [the longest x52 91.1 us: on_mesh(): lax.ppermute(value, ('tensor', 'store'), [(a * 4 + b, c * 4 + d) for (a,...]
    ppermute x0 -> x64, waiting for transfers between devices: none -> 96.9 us  [the longest x52 96.9 us: on_mesh(): lax.ppermute(value, ('tensor', 'store'), [(a * 4 + b, c * 4 + d) for (a,...]
    all_to_all x2 -> x0, waiting for transfers between devices: 47.5 us -> none  [the longest x1 24.9 us: shards(): lax.all_to_all(delta_rows, 'store', split_axis=0, concat_axis=0, tiled=True)]
    dot_general x7 -> x9, matrix products: 66.5 us -> 22 us  [the longest x4 16.5 us: square(): folded = jnp.dot(picked, fold, preferred_element_type=F32).astype(BF16)]
    pallas_call x0 -> x6, Pallas kernels: none -> 37.5 us  [the longest x5 33.5 us: project(): pl.pallas_call(functools.partial(project_kernel, first, blocks), grid=(co...]
    reduce_scatter x1 -> x0, waiting for transfers between devices: 20.7 us -> none  [shards(): lax.psum_scatter(partial_value.astype(jnp.bfloat16), 'tensor', scatter_di...]
    reduce_sum x2 -> x11, other arithmetic: 0.35 us -> 9.35 us  [the longest x8 8.84 us: placed(): return (jnp.sum(jnp.where(before, lens[None, :], 0), axis=1), jnp.sum(lens))]
  transfers between devices with their start and end apart: 5 -> 64, of which waited for: 4 -> 21; matrix products, arithmetic and copies ran while one was open for 21% -> 18% of each run, Pallas kernels for 0% -> 11%
where the time goes in v1:
time: 298 us; the launch traced here: 294 us
  starting transfers between devices  101 us (34%)
  waiting for transfers between devices  96.9 us (33%)
  Pallas kernels  37.5 us (13%)
  matrix products  22 us (7%)
  other arithmetic  20.4 us (7%)
  local copies, waits for them, and re-layouts  9.67 us (3%)
  between operations  6.93 us (2%)
    ppermute x52, waiting for transfers between devices, on_mesh(): lax.ppermute(value, ('tensor', 'store'), [(a * 4 + b, c * 4 + d) for (a,...  96.9 us
    ppermute x52, starting transfers between devices, on_mesh(): lax.ppermute(value, ('tensor', 'store'), [(a * 4 + b, c * 4 + d) for (a,...  91.1 us
    pallas_call x5, Pallas kernels, project(): pl.pallas_call(functools.partial(project_kernel, first, blocks), grid=(co...  33.5 us
    dot_general x4, matrix products, square(): folded = jnp.dot(picked, fold, preferred_element_type=F32).astype(BF16)  16.5 us
    reduce_sum x8, other arithmetic, placed(): return (jnp.sum(jnp.where(before, lens[None, :], 0), axis=1), jnp.sum(lens))  8.84 us
    ppermute x9, starting transfers between devices, on_store(): return lax.ppermute(value, 'store', [(i, i ^ flip) for i in range(4)])  6.57 us
  transfers between devices with their start and end apart: 64, of which 21 were waited for; matrix products, arithmetic and copies ran while one was open for 18% of the time, Pallas kernels for 11%

profile of v1, /device:TPU:21, one launch (start us, length us, event | category | flops | bytes accessed | tf_op | source)
XLA Modules:
  0.0 294.5 jit_solution(6442406863213135404)
XLA Ops:
  5.6 1.4 select_reduce_fusion.3
  16.5 4.0 %fusion.8 = bf16[256,64]{0,1:T(8,128)(2,1)S(1)} fusion(bf16[256,2048]{1,0:T(8,128)(2,1)} %bitcast.64, bf16[1024,2048]{1,0:T(8,128)(2,1)} %bitcast.70, s32[1024]{0:T(1024)} %get-tuple-element.61, s32[256]{0:T(256)S(1)} %eq.348, s32[1024]{0:T(1024)} %get-tuple-element.60), kind=kOutput, calls=%fused_computation.15 | convolution fusion | flops 1108164608 | bytes 5284864 | tf_op jit(solution)/shard_map/dot_general | solution.py:317
  21.4 1.4 reduce_sum.119
  38.1 6.2 %shard_map.74 = bf16[256,2048]{1,0:T(8,128)(2,1)S(1)} custom-call(s32[1,512]{1,0:T(1,128)S(1)} %pad_add_fusion.pos_ref, bf16[256,2048]{1,0:T(8,128)(2,1)S(1)} %bitcast.65, bf16[256,2048]{1,0:T(8,128)(2,1)S(1)} %collective-permute-done.3.refs_1_, bf16[2048,2048]{1,0:T(8,128)(2,1)} %refs_4_.7), custom_call_target="tpu_custom_call" | custom-call | flops 2684354560 | bytes 11534336 | tf_op jit(solution)/shard_map/pallas_call | solution.py:108
  48.0 4.3 %fusion.10 = bf16[256,64]{0,1:T(8,128)(2,1)} fusion(bf16[256,2048]{1,0:T(8,128)(2,1)S(1)} %collective-permute-done.4.refs_2_, bf16[1024,2048]{1,0:T(8,128)(2,1)} %bitcast.71, s32[1024]{0:T(1024)S(1)} %copy-done.4, s32[256]{0:T(256)S(1)} %copy-done.6, s32[1024]{0:T(1024)S(1)} %copy-done.3), kind=kOutput, calls=%fused_computation.17 | convolution fusion | flops 1108164608 | bytes 5284864 | tf_op jit(solution)/shard_map/dot_general | solution.py:317
  52.3 4.3 %fusion.9 = bf16[256,64]{0,1:T(8,128)(2,1)} fusion(bf16[256,2048]{1,0:T(8,128)(2,1)S(1)} %collective-permute-done.3.refs_1_, bf16[1024,2048]{1,0:T(8,128)(2,1)} %bitcast.72, s32[1024]{0:T(1024)S(1)} %copy-done.4, s32[256]{0:T(256)S(1)} %copy-done.7, s32[1024]{0:T(1024)S(1)} %copy-done.3), kind=kOutput, calls=%fused_computation.16 | convolution fusion | flops 1108164608 | bytes 5284864 | tf_op jit(solution)/shard_map/dot_general | solution.py:317
  58.4 2.6 collective-permute-done.6
  61.0 2.1 add_convert_fusion.13
  63.1 1.9 collective-permute-start.11
  65.0 2.1 collective-permute-start.7
  67.2 4.0 %fusion.11 = bf16[256,64]{0,1:T(8,128)(2,1)S(1)} fusion(bf16[256,2048]{1,0:T(8,128)(2,1)} %collective-permute-done.5.refs_3_, bf16[1024,2048]{1,0:T(8,128)(2,1)} %bitcast.73, s32[1024]{0:T(1024)} %get-tuple-element.61, s32[256]{0:T(256)} %eq.360, s32[1024]{0:T(1024)} %get-tuple-element.60), kind=kOutput, calls=%fused_computation.18 | convolution fusion | flops 1108164608 | bytes 5284864 | tf_op jit(solution)/shard_map/dot_general | solution.py:317
  71.4 2.1 collective-permute-start.58
  74.6 5.9 %shard_map.77 = bf16[128,2048]{1,0:T(8,128)(2,1)S(1)} custom-call(s32[1,1024]{1,0:T(1,128)S(1)} %constant_dynamic-update-slice_fusion.pos_ref, bf16[256,2048]{1,0:T(8,128)(2,1)S(1)} %bitcast.66, bf16[256,2048]{1,0:T(8,128)(2,1)S(1)} %collective-permute-done.3.refs_1_, bf16[256,2048]{1,0:T(8,128)(2,1)S(1)} %collective-permute-done.4.refs_2_, ...), custom_call_target="tpu_custom_call" | custom-call | flops 1610612736 | bytes 13107200 | tf_op jit(solution)/shard_map/pallas_call | solution.py:108
  80.6 7.1 %shard_map.75 = bf16[256,2048]{1,0:T(8,128)(2,1)S(1)} custom-call(s32[1,1024]{1,0:T(1,128)S(1)} %constant_dynamic-update-slice_fusion.pos_ref, bf16[256,2048]{1,0:T(8,128)(2,1)S(1)} %bitcast.67, bf16[256,2048]{1,0:T(8,128)(2,1)S(1)} %collective-permute-done.3.refs_1_, bf16[256,2048]{1,0:T(8,128)(2,1)S(1)} %collective-permute-done.4.refs_2_, ...), custom_call_target="tpu_custom_call" | custom-call | flops 3221225472 | bytes 13631488 | tf_op jit(solution)/shard_map/pallas_call | solution.py:108
  87.7 7.1 %shard_map.76 = bf16[256,2048]{1,0:T(8,128)(2,1)S(1)} custom-call(s32[1,1024]{1,0:T(1,128)S(1)} %constant_dynamic-update-slice_fusion.pos_ref, bf16[256,2048]{1,0:T(8,128)(2,1)S(1)} %bitcast.68, bf16[256,2048]{1,0:T(8,128)(2,1)S(1)} %collective-permute-done.3.refs_1_, bf16[256,2048]{1,0:T(8,128)(2,1)S(1)} %collective-permute-done.4.refs_2_, ...), custom_call_target="tpu_custom_call" | custom-call | flops 3221225472 | bytes 13631488 | tf_op jit(solution)/shard_map/pallas_call | solution.py:108
  95.0 7.2 %shard_map.73 = bf16[256,2048]{1,0:T(8,128)(2,1)S(1)} custom-call(s32[1,1024]{1,0:T(1,128)S(1)} %constant_dynamic-update-slice_fusion.pos_ref, bf16[256,2048]{1,0:T(8,128)(2,1)S(1)} %bitcast.69, bf16[256,2048]{1,0:T(8,128)(2,1)S(1)} %collective-permute-done.3.refs_1_, bf16[256,2048]{1,0:T(8,128)(2,1)S(1)} %collective-permute-done.4.refs_2_, ...), custom_call_target="tpu_custom_call" | custom-call | flops 3221225472 | bytes 13631488 | tf_op jit(solution)/shard_map/pallas_call | solution.py:108
  104.4 2.6 bitcast_convert_fusion
  109.8 8.8 %collective-permute-start.17 = (bf16[64,2048]{1,0:T(8,128)(2,1)S(1)}, bf16[64,2048]{1,0:T(8,128)(2,1)S(1)}, u32[]{:S(2)}, u32[]{:S(2)}) collective-permute-start(bf16[64,2048]{1,0:T(8,128)(2,1)S(1)} %get-tuple-element.23), channel_id=1, source_target_pairs={{12,8},{8,4},{4,0},{13,9},{9,5},{2,6},{6,10},{3,7},{7,11},{11,15},... | collective-permute-start | bytes 786440 | tf_op jit(solution)/shard_map/ppermute | solution.py:184
  118.6 1.9 collective-permute-start.14
  122.1 1.4 collective-permute-done.17
  124.2 2.1 collective-permute-done.14
  127.9 1.9 collective-permute-done.13
  131.1 2.1 collective-permute-done.9
  133.2 2.8 collective-permute-start.24
  137.3 5.5 %collective-permute-done.24 = bf16[64,2048]{1,0:T(8,128)(2,1)S(1)} collective-permute-done((bf16[64,2048]{1,0:T(8,128)(2,1)S(1)}, bf16[64,2048]{1,0:T(8,128)(2,1)S(1)}, u32[]{:S(2)}, u32[]{:S(2)}) %collective-permute-start.24) | collective-permute-done | bytes 262176 | tf_op jit(solution)/shard_map/ppermute | solution.py:184
  142.8 2.6 collective-permute-start.20
  146.8 2.4 collective-permute-done.16
  149.3 2.4 collective-permute-start.32
  153.8 5.1 %collective-permute-done.32 = bf16[64,2048]{1,0:T(8,128)(2,1)S(1)} collective-permute-done((bf16[64,2048]{1,0:T(8,128)(2,1)S(1)}, bf16[64,2048]{1,0:T(8,128)(2,1)S(1)}, u32[]{:S(2)}, u32[]{:S(2)}) %collective-permute-start.32) | collective-permute-done | bytes 262176 | tf_op jit(solution)/shard_map/ppermute | solution.py:184
  160.1 9.1 %collective-permute-start.40 = (bf16[64,2048]{1,0:T(8,128)(2,1)S(1)}, bf16[64,2048]{1,0:T(8,128)(2,1)S(1)}, u32[]{:S(2)}, u32[]{:S(2)}) collective-permute-start(bf16[64,2048]{1,0:T(8,128)(2,1)S(1)} %get-tuple-element.15), channel_id=1, source_target_pairs={{12,8},{8,4},{4,0},{13,9},{9,5},{2,6},{6,10},{3,7},{7,11},{11,15},... | collective-permute-start | bytes 786440 | tf_op jit(solution)/shard_map/ppermute | solution.py:184
  170.0 4.4 %collective-permute-done.40 = bf16[64,2048]{1,0:T(8,128)(2,1)S(1)} collective-permute-done((bf16[64,2048]{1,0:T(8,128)(2,1)S(1)}, bf16[64,2048]{1,0:T(8,128)(2,1)S(1)}, u32[]{:S(2)}, u32[]{:S(2)}) %collective-permute-start.40) | collective-permute-done | bytes 262176 | tf_op jit(solution)/shard_map/ppermute | solution.py:184
  174.4 4.1 %collective-permute-start.28 = (bf16[64,2048]{1,0:T(8,128)(2,1)S(1)}, bf16[64,2048]{1,0:T(8,128)(2,1)S(1)}, u32[]{:S(2)}, u32[]{:S(2)}) collective-permute-start(bf16[64,2048]{1,0:T(8,128)(2,1)S(1)} %get-tuple-element.16), channel_id=1, source_target_pairs={{12,8},{8,4},{4,0},{13,9},{9,5},{2,6},{6,10},{3,7},{7,11},{11,15},... | collective-permute-start | bytes 786440 | tf_op jit(solution)/shard_map/ppermute | solution.py:184
  179.3 3.4 %collective-permute-done.28 = bf16[64,2048]{1,0:T(8,128)(2,1)S(1)} collective-permute-done((bf16[64,2048]{1,0:T(8,128)(2,1)S(1)}, bf16[64,2048]{1,0:T(8,128)(2,1)S(1)}, u32[]{:S(2)}, u32[]{:S(2)}) %collective-permute-start.28) | collective-permute-done | bytes 262176 | tf_op jit(solution)/shard_map/ppermute | solution.py:184
  184.0 3.2 %collective-permute-done.27 = bf16[64,2048]{1,0:T(8,128)(2,1)S(1)} collective-permute-done((bf16[64,2048]{1,0:T(8,128)(2,1)S(1)}, bf16[64,2048]{1,0:T(8,128)(2,1)S(1)}, u32[]{:S(2)}, u32[]{:S(2)}) %collective-permute-start.27) | collective-permute-done | bytes 262176 | tf_op jit(solution)/shard_map/ppermute | solution.py:184
  188.0 8.4 %collective-permute-start.48 = (bf16[64,2048]{1,0:T(8,128)(2,1)S(1)}, bf16[64,2048]{1,0:T(8,128)(2,1)S(1)}, u32[]{:S(2)}, u32[]{:S(2)}) collective-permute-start(bf16[64,2048]{1,0:T(8,128)(2,1)S(1)} %add_convert_fusion.4), channel_id=1, source_target_pairs={{8,4},{4,0},{9,5},{6,10},{7,11},{11,15},{24,20},{20,16},{25,21},{2... | collective-permute-start | bytes 786440 | tf_op jit(solution)/shard_map/ppermute | solution.py:184
  196.5 3.1 %collective-permute-start.36 = (bf16[64,2048]{1,0:T(8,128)(2,1)S(1)}, bf16[64,2048]{1,0:T(8,128)(2,1)S(1)}, u32[]{:S(2)}, u32[]{:S(2)}) collective-permute-start(bf16[64,2048]{1,0:T(8,128)(2,1)S(1)} %add_convert_fusion.7), channel_id=1, source_target_pairs={{12,8},{8,4},{4,0},{13,9},{9,5},{2,6},{6,10},{3,7},{7,11},{11,15},... | collective-permute-start | bytes 786440 | tf_op jit(solution)/shard_map/ppermute | solution.py:184
  200.2 1.7 collective-permute-start.61
  201.9 4.0 %collective-permute-done.36 = bf16[64,2048]{1,0:T(8,128)(2,1)S(1)} collective-permute-done((bf16[64,2048]{1,0:T(8,128)(2,1)S(1)}, bf16[64,2048]{1,0:T(8,128)(2,1)S(1)}, u32[]{:S(2)}, u32[]{:S(2)}) %collective-permute-start.36) | collective-permute-done | bytes 262176 | tf_op jit(solution)/shard_map/ppermute | solution.py:184
  208.2 21.3 %collective-permute-done.35 = bf16[64,2048]{1,0:T(8,128)(2,1)S(1)} collective-permute-done((bf16[64,2048]{1,0:T(8,128)(2,1)S(1)}, bf16[64,2048]{1,0:T(8,128)(2,1)S(1)}, u32[]{:S(2)}, u32[]{:S(2)}) %collective-permute-start.35) | collective-permute-done | bytes 262176 | tf_op jit(solution)/shard_map/ppermute | solution.py:184
  230.8 2.1 collective-permute-done.23
  233.6 6.9 %collective-permute-start.44 = (bf16[64,2048]{1,0:T(8,128)(2,1)S(1)}, bf16[64,2048]{1,0:T(8,128)(2,1)S(1)}, u32[]{:S(2)}, u32[]{:S(2)}) collective-permute-start(bf16[64,2048]{1,0:T(8,128)(2,1)S(1)} %get-tuple-element.10), channel_id=1, source_target_pairs={{8,4},{4,0},{9,5},{6,10},{7,11},{11,15},{24,20},{20,16},{25,21},{2... | collective-permute-start | bytes 786440 | tf_op jit(solution)/shard_map/ppermute | solution.py:184
  241.8 2.4 collective-permute-done.44
  247.8 18.7 %collective-permute-done.31 = bf16[64,2048]{1,0:T(8,128)(2,1)S(1)} collective-permute-done((bf16[64,2048]{1,0:T(8,128)(2,1)S(1)}, bf16[64,2048]{1,0:T(8,128)(2,1)S(1)}, u32[]{:S(2)}, u32[]{:S(2)}) %collective-permute-start.31) | collective-permute-done | bytes 262176 | tf_op jit(solution)/shard_map/ppermute | solution.py:184
  269.4 2.0 collective-permute-done.51
  273.5 1.4 collective-permute-done.39
  278.2 8.0 %collective-permute-done.47 = bf16[64,2048]{1,0:T(8,128)(2,1)S(1)} collective-permute-done((bf16[64,2048]{1,0:T(8,128)(2,1)S(1)}, bf16[64,2048]{1,0:T(8,128)(2,1)S(1)}, u32[]{:S(2)}, u32[]{:S(2)}) %collective-permute-start.47) | collective-permute-done | bytes 262176 | tf_op jit(solution)/shard_map/ppermute | solution.py:184
  287.5 1.5 collective-permute-done.57
  290.5 4.0 %shard_map.78 = bf16[256,2048]{1,0:T(8,128)(2,1)} custom-call(s32[256,1]{1,0:T(8,128)S(1)} %select_n.433.base_pos_ref, s32[256,1]{1,0:T(8,128)S(1)} %select_n.434.delta_pos_ref, bf16[64,2048]{1,0:T(8,128)(2,1)S(1)} %broadcast_select_fusion.23.refs_0_, bf16[64,2048]{1,0:T(8,128)(2,1)S(1)} %broadcast_select_fusion.22.refs_1_, ...), custom_call_target="tpu_custom_call" | custom-call | flops 1476395008 | bytes 6815744 | tf_op jit(solution)/shard_map/pallas_call | solution.py:153
  (217 shorter events, 72.6 us)
Async XLA Ops:
  0.0 21.4 %collective-permute-start.1 = (s32[16]{0:T(128)}, s32[16]{0:T(128)}, u32[]{:S(2)}, u32[]{:S(2)}) collective-permute-start(s32[16]{0:T(128)} %param.13), channel_id=1, source_target_pairs={{0,2},{1,3},{2,0},{3,1},{4,6},{5,7},{6,4},{7,5},{8,10},{9,11},{10,... | collective-permute-start | bytes 200 | tf_op jit(solution)/shard_map/ppermute | solution.py:168
  1.2 22.3 %collective-permute-start = (s32[16]{0:T(128)}, s32[16]{0:T(128)}, u32[]{:S(2)}, u32[]{:S(2)}) collective-permute-start(s32[16]{0:T(128)} %param.13), channel_id=1, source_target_pairs={{0,1},{1,0},{2,3},{3,2},{4,5},{5,4},{6,7},{7,6},{8,9},{9,8},{10,11... | collective-permute-start | bytes 200 | tf_op jit(solution)/shard_map/ppermute | solution.py:168
  2.2 23.8 %collective-permute-start.2 = (s32[16]{0:T(128)}, s32[16]{0:T(128)}, u32[]{:S(2)}, u32[]{:S(2)}) collective-permute-start(s32[16]{0:T(128)} %param.13), channel_id=1, source_target_pairs={{0,3},{1,2},{2,1},{3,0},{4,7},{5,6},{6,5},{7,4},{8,11},{9,10},{10,... | collective-permute-start | bytes 200 | tf_op jit(solution)/shard_map/ppermute | solution.py:168
  2.3 45.5 %collective-permute-start.4 = (bf16[256,2048]{1,0:T(8,128)(2,1)}, bf16[256,2048]{1,0:T(8,128)(2,1)S(1)}, u32[]{:S(2)}, u32[]{:S(2)}) collective-permute-start(bf16[256,2048]{1,0:T(8,128)(2,1)} %bitcast.62), channel_id=1, source_target_pairs={{0,2},{1,3},{2,0},{3,1},{4,6},{5,7},{6,4},{7,5},{8,10},{9,11},{10,... | collective-permute-start | bytes 3145736 | tf_op jit(solution)/shard_map/ppermute | solution.py:168
  3.5 34.5 %collective-permute-start.3 = (bf16[256,2048]{1,0:T(8,128)(2,1)}, bf16[256,2048]{1,0:T(8,128)(2,1)S(1)}, u32[]{:S(2)}, u32[]{:S(2)}) collective-permute-start(bf16[256,2048]{1,0:T(8,128)(2,1)} %bitcast.63), channel_id=1, source_target_pairs={{0,1},{1,0},{2,3},{3,2},{4,5},{5,4},{6,7},{7,6},{8,9},{9,8},{10,11... | collective-permute-start | bytes 3145736 | tf_op jit(solution)/shard_map/ppermute | solution.py:168
  45.2 13.1 %collective-permute-start.10 = (bf16[64,2048]{1,0:T(8,128)(2,1)}, bf16[64,2048]{1,0:T(8,128)(2,1)}, u32[]{:S(2)}, u32[]{:S(2)}) collective-permute-start(bf16[64,2048]{1,0:T(8,128)(2,1)} %get-tuple-element.27), channel_id=1, source_target_pairs={{12,8},{13,9},{2,6},{3,7},{28,24},{29,25},{18,22},{19,23}} | collective-permute-start | bytes 786440 | tf_op jit(solution)/shard_map/ppermute | solution.py:184
  46.5 14.5 %collective-permute-start.6 = (bf16[64,2048]{1,0:T(8,128)(2,1)}, bf16[64,2048]{1,0:T(8,128)(2,1)}, u32[]{:S(2)}, u32[]{:S(2)}) collective-permute-start(bf16[64,2048]{1,0:T(8,128)(2,1)} %get-tuple-element.28), channel_id=1, source_target_pairs={{12,8},{13,9},{2,6},{3,7},{28,24},{29,25},{18,22},{19,23}} | collective-permute-start | bytes 786440 | tf_op jit(solution)/shard_map/ppermute | solution.py:184
  47.8 19.3 %collective-permute-start.5 = (bf16[256,2048]{1,0:T(8,128)(2,1)S(1)}, bf16[256,2048]{1,0:T(8,128)(2,1)}, u32[]{:S(2)}, u32[]{:S(2)}) collective-permute-start(bf16[256,2048]{1,0:T(8,128)(2,1)S(1)} %collective-permute-done.4.refs_2_), channel_id=1, source_target_pairs={{0,1},{1,0},{2,3},{3,2},{4,5},{5,4},{6,7},{7,6},{8,9},{9,8},{10,11... | collective-permute-start | bytes 3145736 | tf_op jit(solution)/shard_map/ppermute | solution.py:168
  63.1 43.9 %collective-permute-start.11 = (bf16[64,2048]{1,0:T(8,128)(2,1)}, bf16[64,2048]{1,0:T(8,128)(2,1)}, u32[]{:S(2)}, u32[]{:S(2)}) collective-permute-start(bf16[64,2048]{1,0:T(8,128)(2,1)} %get-tuple-element.25), channel_id=1, source_target_pairs={{12,8},{8,4},{13,9},{9,5},{2,6},{6,10},{3,7},{7,11},{28,24},{24,20... | collective-permute-start | bytes 786440 | tf_op jit(solution)/shard_map/ppermute | solution.py:184
  65.0 42.7 %collective-permute-start.7 = (bf16[64,2048]{1,0:T(8,128)(2,1)}, bf16[64,2048]{1,0:T(8,128)(2,1)}, u32[]{:S(2)}, u32[]{:S(2)}) collective-permute-start(bf16[64,2048]{1,0:T(8,128)(2,1)} %get-tuple-element.26), channel_id=1, source_target_pairs={{12,8},{8,4},{13,9},{9,5},{2,6},{6,10},{3,7},{7,11},{28,24},{24,20... | collective-permute-start | bytes 786440 | tf_op jit(solution)/shard_map/ppermute | solution.py:184
  71.3 30.9 %collective-permute-start.59 = (bf16[256,128]{0,1:T(8,128)(2,1)S(1)}, bf16[256,128]{0,1:T(8,128)(2,1)S(1)}, u32[]{:S(2)}, u32[]{:S(2)}) collective-permute-start(bf16[256,128]{0,1:T(8,128)(2,1)S(1)} %maximum_maximum_fusion), channel_id=1, source_target_pairs={{0,8},{4,12},{8,0},{12,4},{1,9},{5,13},{9,1},{13,5},{2,10},{6,14},... | collective-permute-start | bytes 196616 | tf_op jit(solution)/shard_map/ppermute | solution.py:324
  71.4 31.5 %collective-permute-start.58 = (bf16[256,128]{0,1:T(8,128)(2,1)S(1)}, bf16[256,128]{0,1:T(8,128)(2,1)S(1)}, u32[]{:S(2)}, u32[]{:S(2)}) collective-permute-start(bf16[256,128]{0,1:T(8,128)(2,1)S(1)} %maximum_maximum_fusion), channel_id=1, source_target_pairs={{0,4},{4,0},{8,12},{12,8},{1,5},{5,1},{9,13},{13,9},{2,6},{6,2},{1... | collective-permute-start | bytes 196616 | tf_op jit(solution)/shard_map/ppermute | solution.py:324
  73.5 30.1 %collective-permute-start.60 = (bf16[256,128]{0,1:T(8,128)(2,1)S(1)}, bf16[256,128]{0,1:T(8,128)(2,1)S(1)}, u32[]{:S(2)}, u32[]{:S(2)}) collective-permute-start(bf16[256,128]{0,1:T(8,128)(2,1)S(1)} %maximum_maximum_fusion), channel_id=1, source_target_pairs={{0,12},{4,8},{8,4},{12,0},{1,13},{5,9},{9,5},{13,1},{2,14},{6,10},... | collective-permute-start | bytes 196616 | tf_op jit(solution)/shard_map/ppermute | solution.py:324
  102.3 97.4 %collective-permute-start.49 = (bf16[64,2048]{1,0:T(8,128)(2,1)S(1)}, bf16[64,2048]{1,0:T(8,128)(2,1)S(1)}, u32[]{:S(2)}, u32[]{:S(2)}) collective-permute-start(bf16[64,2048]{1,0:T(8,128)(2,1)S(1)} %get-tuple-element.33), channel_id=1, source_target_pairs={{1,5},{14,10},{17,21},{30,26}} | collective-permute-start | bytes 786440 | tf_op jit(solution)/shard_map/ppermute | solution.py:184
  102.9 5.5 %collective-permute-start.12 = (bf16[64,2048]{1,0:T(8,128)(2,1)S(1)}, bf16[64,2048]{1,0:T(8,128)(2,1)S(1)}, u32[]{:S(2)}, u32[]{:S(2)}) collective-permute-start(bf16[64,2048]{1,0:T(8,128)(2,1)S(1)} %get-tuple-element.29), channel_id=1, source_target_pairs={{1,5},{14,10},{17,21},{30,26}} | collective-permute-start | bytes 786440 | tf_op jit(solution)/shard_map/ppermute | solution.py:184
  103.6 4.8 %collective-permute-start.8 = (bf16[64,2048]{1,0:T(8,128)(2,1)S(1)}, bf16[64,2048]{1,0:T(8,128)(2,1)S(1)}, u32[]{:S(2)}, u32[]{:S(2)}) collective-permute-start(bf16[64,2048]{1,0:T(8,128)(2,1)S(1)} %get-tuple-element.30), channel_id=1, source_target_pairs={{1,5},{14,10},{17,21},{30,26}} | collective-permute-start | bytes 786440 | tf_op jit(solution)/shard_map/ppermute | solution.py:184
  107.1 13.7 %collective-permute-start.18 = (bf16[64,2048]{1,0:T(8,128)(2,1)S(1)}, bf16[64,2048]{1,0:T(8,128)(2,1)S(1)}, u32[]{:S(2)}, u32[]{:S(2)}) collective-permute-start(bf16[64,2048]{1,0:T(8,128)(2,1)S(1)} %get-tuple-element.19), channel_id=1, source_target_pairs={{1,5},{14,10},{17,21},{30,26}} | collective-permute-start | bytes 786440 | tf_op jit(solution)/shard_map/ppermute | solution.py:184
  107.8 13.7 %collective-permute-start.15 = (bf16[64,2048]{1,0:T(8,128)(2,1)S(1)}, bf16[64,2048]{1,0:T(8,128)(2,1)S(1)}, u32[]{:S(2)}, u32[]{:S(2)}) collective-permute-start(bf16[64,2048]{1,0:T(8,128)(2,1)S(1)} %get-tuple-element.20), channel_id=1, source_target_pairs={{1,5},{14,10},{17,21},{30,26}} | collective-permute-start | bytes 786440 | tf_op jit(solution)/shard_map/ppermute | solution.py:184
  109.8 13.8 %collective-permute-start.17 = (bf16[64,2048]{1,0:T(8,128)(2,1)S(1)}, bf16[64,2048]{1,0:T(8,128)(2,1)S(1)}, u32[]{:S(2)}, u32[]{:S(2)}) collective-permute-start(bf16[64,2048]{1,0:T(8,128)(2,1)S(1)} %get-tuple-element.23), channel_id=1, source_target_pairs={{12,8},{8,4},{4,0},{13,9},{9,5},{2,6},{6,10},{3,7},{7,11},{11,15},... | collective-permute-start | bytes 786440 | tf_op jit(solution)/shard_map/ppermute | solution.py:184
  118.6 7.8 %collective-permute-start.14 = (bf16[64,2048]{1,0:T(8,128)(2,1)S(1)}, bf16[64,2048]{1,0:T(8,128)(2,1)S(1)}, u32[]{:S(2)}, u32[]{:S(2)}) collective-permute-start(bf16[64,2048]{1,0:T(8,128)(2,1)S(1)} %get-tuple-element.24), channel_id=1, source_target_pairs={{12,8},{8,4},{4,0},{13,9},{9,5},{2,6},{6,10},{3,7},{7,11},{11,15},... | collective-permute-start | bytes 786440 | tf_op jit(solution)/shard_map/ppermute | solution.py:184
  120.7 15.3 %collective-permute-start.25 = (bf16[64,2048]{1,0:T(8,128)(2,1)S(1)}, bf16[64,2048]{1,0:T(8,128)(2,1)S(1)}, u32[]{:S(2)}, u32[]{:S(2)}) collective-permute-start(bf16[64,2048]{1,0:T(8,128)(2,1)S(1)} %get-tuple-element.17), channel_id=1, source_target_pairs={{1,5},{14,10},{17,21},{30,26}} | collective-permute-start | bytes 786440 | tf_op jit(solution)/shard_map/ppermute | solution.py:184
  121.4 30.3 %collective-permute-start.21 = (bf16[64,2048]{1,0:T(8,128)(2,1)S(1)}, bf16[64,2048]{1,0:T(8,128)(2,1)S(1)}, u32[]{:S(2)}, u32[]{:S(2)}) collective-permute-start(bf16[64,2048]{1,0:T(8,128)(2,1)S(1)} %get-tuple-element.18), channel_id=1, source_target_pairs={{1,5},{14,10},{17,21},{30,26}} | collective-permute-start | bytes 786440 | tf_op jit(solution)/shard_map/ppermute | solution.py:184
  123.5 28.9 %collective-permute-start.33 = (bf16[64,2048]{1,0:T(8,128)(2,1)S(1)}, bf16[64,2048]{1,0:T(8,128)(2,1)S(1)}, u32[]{:S(2)}, u32[]{:S(2)}) collective-permute-start(bf16[64,2048]{1,0:T(8,128)(2,1)S(1)} %get-tuple-element.13), channel_id=1, source_target_pairs={{1,5},{14,10},{17,21},{30,26}} | collective-permute-start | bytes 786440 | tf_op jit(solution)/shard_map/ppermute | solution.py:184
  133.2 9.6 %collective-permute-start.24 = (bf16[64,2048]{1,0:T(8,128)(2,1)S(1)}, bf16[64,2048]{1,0:T(8,128)(2,1)S(1)}, u32[]{:S(2)}, u32[]{:S(2)}) collective-permute-start(bf16[64,2048]{1,0:T(8,128)(2,1)S(1)} %get-tuple-element.21), channel_id=1, source_target_pairs={{12,8},{8,4},{4,0},{13,9},{9,5},{2,6},{6,10},{3,7},{7,11},{11,15},... | collective-permute-start | bytes 786440 | tf_op jit(solution)/shard_map/ppermute | solution.py:184
  136.0 9.5 %collective-permute-start.19 = (bf16[64,2048]{1,0:T(8,128)(2,1)S(1)}, bf16[64,2048]{1,0:T(8,128)(2,1)S(1)}, u32[]{:S(2)}, u32[]{:S(2)}) collective-permute-start(bf16[64,2048]{1,0:T(8,128)(2,1)S(1)} %get-tuple-element.21), channel_id=1, source_target_pairs={{0,1},{5,4},{10,11},{15,14},{2,3},{7,6},{8,9},{13,12},{16,17},{21,... | collective-permute-start | bytes 786440 | tf_op jit(solution)/shard_map/ppermute | solution.py:184
  142.8 10.3 %collective-permute-start.20 = (bf16[64,2048]{1,0:T(8,128)(2,1)S(1)}, bf16[64,2048]{1,0:T(8,128)(2,1)S(1)}, u32[]{:S(2)}, u32[]{:S(2)}) collective-permute-start(bf16[64,2048]{1,0:T(8,128)(2,1)S(1)} %get-tuple-element.22), channel_id=1, source_target_pairs={{12,8},{8,4},{4,0},{13,9},{9,5},{2,6},{6,10},{3,7},{7,11},{11,15},... | collective-permute-start | bytes 786440 | tf_op jit(solution)/shard_map/ppermute | solution.py:184
  149.3 9.6 %collective-permute-start.32 = (bf16[64,2048]{1,0:T(8,128)(2,1)S(1)}, bf16[64,2048]{1,0:T(8,128)(2,1)S(1)}, u32[]{:S(2)}, u32[]{:S(2)}) collective-permute-start(bf16[64,2048]{1,0:T(8,128)(2,1)S(1)} %add_convert_fusion.8), channel_id=1, source_target_pairs={{12,8},{8,4},{4,0},{13,9},{9,5},{2,6},{6,10},{3,7},{7,11},{11,15},... | collective-permute-start | bytes 786440 | tf_op jit(solution)/shard_map/ppermute | solution.py:184
  151.7 88.8 %collective-permute-start.45 = (bf16[64,2048]{1,0:T(8,128)(2,1)S(1)}, bf16[64,2048]{1,0:T(8,128)(2,1)S(1)}, u32[]{:S(2)}, u32[]{:S(2)}) collective-permute-start(bf16[64,2048]{1,0:T(8,128)(2,1)S(1)} %get-tuple-element.34), channel_id=1, source_target_pairs={{1,5},{14,10},{17,21},{30,26}} | collective-permute-start | bytes 786440 | tf_op jit(solution)/shard_map/ppermute | solution.py:184
  152.4 16.9 %collective-permute-start.41 = (bf16[64,2048]{1,0:T(8,128)(2,1)S(1)}, bf16[64,2048]{1,0:T(8,128)(2,1)S(1)}, u32[]{:S(2)}, u32[]{:S(2)}) collective-permute-start(bf16[64,2048]{1,0:T(8,128)(2,1)S(1)} %get-tuple-element.11), channel_id=1, source_target_pairs={{1,5},{14,10},{17,21},{30,26}} | collective-permute-start | bytes 786440 | tf_op jit(solution)/shard_map/ppermute | solution.py:184
  153.1 46.7 %collective-permute-start.37 = (bf16[64,2048]{1,0:T(8,128)(2,1)S(1)}, bf16[64,2048]{1,0:T(8,128)(2,1)S(1)}, u32[]{:S(2)}, u32[]{:S(2)}) collective-permute-start(bf16[64,2048]{1,0:T(8,128)(2,1)S(1)} %get-tuple-element.12), channel_id=1, source_target_pairs={{1,5},{14,10},{17,21},{30,26}} | collective-permute-start | bytes 786440 | tf_op jit(solution)/shard_map/ppermute | solution.py:184
  160.1 14.3 %collective-permute-start.40 = (bf16[64,2048]{1,0:T(8,128)(2,1)S(1)}, bf16[64,2048]{1,0:T(8,128)(2,1)S(1)}, u32[]{:S(2)}, u32[]{:S(2)}) collective-permute-start(bf16[64,2048]{1,0:T(8,128)(2,1)S(1)} %get-tuple-element.15), channel_id=1, source_target_pairs={{12,8},{8,4},{4,0},{13,9},{9,5},{2,6},{6,10},{3,7},{7,11},{11,15},... | collective-permute-start | bytes 786440 | tf_op jit(solution)/shard_map/ppermute | solution.py:184
  169.3 9.3 %collective-permute-start.29 = (bf16[64,2048]{1,0:T(8,128)(2,1)S(1)}, bf16[64,2048]{1,0:T(8,128)(2,1)S(1)}, u32[]{:S(2)}, u32[]{:S(2)}) collective-permute-start(bf16[64,2048]{1,0:T(8,128)(2,1)S(1)} %get-tuple-element.14), channel_id=1, source_target_pairs={{1,5},{14,10},{17,21},{30,26}} | collective-permute-start | bytes 786440 | tf_op jit(solution)/shard_map/ppermute | solution.py:184
  174.4 8.3 %collective-permute-start.28 = (bf16[64,2048]{1,0:T(8,128)(2,1)S(1)}, bf16[64,2048]{1,0:T(8,128)(2,1)S(1)}, u32[]{:S(2)}, u32[]{:S(2)}) collective-permute-start(bf16[64,2048]{1,0:T(8,128)(2,1)S(1)} %get-tuple-element.16), channel_id=1, source_target_pairs={{12,8},{8,4},{4,0},{13,9},{9,5},{2,6},{6,10},{3,7},{7,11},{11,15},... | collective-permute-start | bytes 786440 | tf_op jit(solution)/shard_map/ppermute | solution.py:184
  178.6 9.4 %collective-permute-start.34 = (bf16[64,2048]{1,0:T(8,128)(2,1)S(1)}, bf16[64,2048]{1,0:T(8,128)(2,1)S(1)}, u32[]{:S(2)}, u32[]{:S(2)}) collective-permute-start(bf16[64,2048]{1,0:T(8,128)(2,1)S(1)} %get-tuple-element.15), channel_id=1, source_target_pairs={{0,2},{5,7},{10,8},{15,13},{16,18},{21,23},{26,24},{31,29}} | collective-permute-start | bytes 786440 | tf_op jit(solution)/shard_map/ppermute | solution.py:184
  182.6 4.6 %collective-permute-start.27 = (bf16[64,2048]{1,0:T(8,128)(2,1)S(1)}, bf16[64,2048]{1,0:T(8,128)(2,1)S(1)}, u32[]{:S(2)}, u32[]{:S(2)}) collective-permute-start(bf16[64,2048]{1,0:T(8,128)(2,1)S(1)} %broadcast_select_fusion.8), channel_id=1, source_target_pairs={{0,1},{5,4},{10,11},{15,14},{2,3},{7,6},{8,9},{13,12},{16,17},{21,... | collective-permute-start | bytes 786440 | tf_op jit(solution)/shard_map/ppermute | solution.py:184
  187.3 9.2 %collective-permute-start.22 = (bf16[64,2048]{1,0:T(8,128)(2,1)S(1)}, bf16[64,2048]{1,0:T(8,128)(2,1)S(1)}, u32[]{:S(2)}, u32[]{:S(2)}) collective-permute-start(bf16[64,2048]{1,0:T(8,128)(2,1)S(1)} %get-tuple-element.16), channel_id=1, source_target_pairs={{0,2},{5,7},{10,8},{15,13},{16,18},{21,23},{26,24},{31,29}} | collective-permute-start | bytes 786440 | tf_op jit(solution)/shard_map/ppermute | solution.py:184
  188.0 12.3 %collective-permute-start.48 = (bf16[64,2048]{1,0:T(8,128)(2,1)S(1)}, bf16[64,2048]{1,0:T(8,128)(2,1)S(1)}, u32[]{:S(2)}, u32[]{:S(2)}) collective-permute-start(bf16[64,2048]{1,0:T(8,128)(2,1)S(1)} %add_convert_fusion.4), channel_id=1, source_target_pairs={{8,4},{4,0},{9,5},{6,10},{7,11},{11,15},{24,20},{20,16},{25,21},{2... | collective-permute-start | bytes 786440 | tf_op jit(solution)/shard_map/ppermute | solution.py:184
  196.5 9.4 %collective-permute-start.36 = (bf16[64,2048]{1,0:T(8,128)(2,1)S(1)}, bf16[64,2048]{1,0:T(8,128)(2,1)S(1)}, u32[]{:S(2)}, u32[]{:S(2)}) collective-permute-start(bf16[64,2048]{1,0:T(8,128)(2,1)S(1)} %add_convert_fusion.7), channel_id=1, source_target_pairs={{12,8},{8,4},{4,0},{13,9},{9,5},{2,6},{6,10},{3,7},{7,11},{11,15},... | collective-permute-start | bytes 786440 | tf_op jit(solution)/shard_map/ppermute | solution.py:184
  199.7 90.7 %collective-permute-start.63 = (bf16[128,2048]{1,0:T(8,128)(2,1)S(1)}, bf16[128,2048]{1,0:T(8,128)(2,1)S(1)}, u32[]{:S(2)}, u32[]{:S(2)}) collective-permute-start(bf16[128,2048]{1,0:T(8,128)(2,1)S(1)} %get-tuple-element.5), channel_id=1, source_target_pairs={{0,3},{1,2},{2,1},{3,0},{4,7},{5,6},{6,5},{7,4},{8,11},{9,10},{10,... | collective-permute-start | bytes 1572872 | tf_op jit(solution)/shard_map/ppermute | solution.py:168
  199.8 90.7 %collective-permute-start.62 = (bf16[128,2048]{1,0:T(8,128)(2,1)S(1)}, bf16[128,2048]{1,0:T(8,128)(2,1)S(1)}, u32[]{:S(2)}, u32[]{:S(2)}) collective-permute-start(bf16[128,2048]{1,0:T(8,128)(2,1)S(1)} %get-tuple-element.6), channel_id=1, source_target_pairs={{0,2},{1,3},{2,0},{3,1},{4,6},{5,7},{6,4},{7,5},{8,10},{9,11},{10,... | collective-permute-start | bytes 1572872 | tf_op jit(solution)/shard_map/ppermute | solution.py:168
  200.2 90.2 %collective-permute-start.61 = (bf16[128,2048]{1,0:T(8,128)(2,1)S(1)}, bf16[128,2048]{1,0:T(8,128)(2,1)S(1)}, u32[]{:S(2)}, u32[]{:S(2)}) collective-permute-start(bf16[128,2048]{1,0:T(8,128)(2,1)S(1)} %get-tuple-element.7), channel_id=1, source_target_pairs={{0,1},{1,0},{2,3},{3,2},{4,5},{5,4},{6,7},{7,6},{8,9},{9,8},{10,11... | collective-permute-start | bytes 1572872 | tf_op jit(solution)/shard_map/ppermute | solution.py:168
  206.8 22.6 %collective-permute-start.35 = (bf16[64,2048]{1,0:T(8,128)(2,1)S(1)}, bf16[64,2048]{1,0:T(8,128)(2,1)S(1)}, u32[]{:S(2)}, u32[]{:S(2)}) collective-permute-start(bf16[64,2048]{1,0:T(8,128)(2,1)S(1)} %broadcast_select_fusion.6), channel_id=1, source_target_pairs={{0,1},{5,4},{10,11},{15,14},{2,3},{7,6},{8,9},{13,12},{16,17},{21,... | collective-permute-start | bytes 786440 | tf_op jit(solution)/shard_map/ppermute | solution.py:184
  233.6 10.6 %collective-permute-start.44 = (bf16[64,2048]{1,0:T(8,128)(2,1)S(1)}, bf16[64,2048]{1,0:T(8,128)(2,1)S(1)}, u32[]{:S(2)}, u32[]{:S(2)}) collective-permute-start(bf16[64,2048]{1,0:T(8,128)(2,1)S(1)} %get-tuple-element.10), channel_id=1, source_target_pairs={{8,4},{4,0},{9,5},{6,10},{7,11},{11,15},{24,20},{20,16},{25,21},{2... | collective-permute-start | bytes 786440 | tf_op jit(solution)/shard_map/ppermute | solution.py:184
  244.2 23.1 %collective-permute-start.55 = (bf16[64,2048]{1,0:T(8,128)(2,1)S(1)}, bf16[64,2048]{1,0:T(8,128)(2,1)S(1)}, u32[]{:S(2)}, u32[]{:S(2)}) collective-permute-start(bf16[64,2048]{1,0:T(8,128)(2,1)S(1)} %get-tuple-element.9), channel_id=1, source_target_pairs={{4,0},{11,15},{20,16},{27,31}} | collective-permute-start | bytes 786440 | tf_op jit(solution)/shard_map/ppermute | solution.py:184
  246.5 20.1 %collective-permute-start.31 = (bf16[64,2048]{1,0:T(8,128)(2,1)S(1)}, bf16[64,2048]{1,0:T(8,128)(2,1)S(1)}, u32[]{:S(2)}, u32[]{:S(2)}) collective-permute-start(bf16[64,2048]{1,0:T(8,128)(2,1)S(1)} %broadcast_select_fusion.7), channel_id=1, source_target_pairs={{0,1},{5,4},{10,11},{15,14},{2,3},{7,6},{8,9},{13,12},{16,17},{21,... | collective-permute-start | bytes 786440 | tf_op jit(solution)/shard_map/ppermute | solution.py:184
  267.3 5.5 %collective-permute-start.46 = (bf16[64,2048]{1,0:T(8,128)(2,1)S(1)}, bf16[64,2048]{1,0:T(8,128)(2,1)S(1)}, u32[]{:S(2)}, u32[]{:S(2)}) collective-permute-start(bf16[64,2048]{1,0:T(8,128)(2,1)S(1)} %add_convert_fusion.3), channel_id=1, source_target_pairs={{0,2},{5,7},{10,8},{15,13},{16,18},{21,23},{26,24},{31,29}} | collective-permute-start | bytes 786440 | tf_op jit(solution)/shard_map/ppermute | solution.py:184
  275.5 10.7 %collective-permute-start.47 = (bf16[64,2048]{1,0:T(8,128)(2,1)S(1)}, bf16[64,2048]{1,0:T(8,128)(2,1)S(1)}, u32[]{:S(2)}, u32[]{:S(2)}) collective-permute-start(bf16[64,2048]{1,0:T(8,128)(2,1)S(1)} %broadcast_select_fusion.3), channel_id=1, source_target_pairs={{0,1},{5,4},{10,11},{15,14},{2,3},{7,6},{8,9},{13,12},{16,17},{21,... | collective-permute-start | bytes 786440 | tf_op jit(solution)/shard_map/ppermute | solution.py:184
  276.9 12.1 %collective-permute-start.57 = (bf16[64,2048]{1,0:T(8,128)(2,1)S(1)}, bf16[64,2048]{1,0:T(8,128)(2,1)S(1)}, u32[]{:S(2)}, u32[]{:S(2)}) collective-permute-start(bf16[64,2048]{1,0:T(8,128)(2,1)S(1)} %broadcast_select_fusion), channel_id=1, source_target_pairs={{0,1},{5,4},{10,11},{15,14},{2,3},{7,6},{8,9},{13,12},{16,17},{21,... | collective-permute-start | bytes 786440 | tf_op jit(solution)/shard_map/ppermute | solution.py:184
  (25 other events, 131.1 us)

commit v2 on v0

--- a/solution.py
+++ b/solution.py
@@ -1,10 +1,21 @@
+import functools
 import jax
 import jax.numpy as jnp
 from jax import lax
+from jax.experimental import pallas as pl
+from jax.experimental.pallas import tpu as pltpu
 from jax.sharding import PartitionSpec as P
 
-
-def shards(
+VMEM_LIMIT = 52 * 1024 * 1024
+SMALL_VMEM = 32 * 1024 * 1024
+STREAMS = 2
+SPAN = 128
+BF16 = jnp.bfloat16
+F32 = jnp.float32
+LIGHT = pl.CostEstimate(flops=0, bytes_accessed=0, transcendentals=0)
+
+
+def general(
     attention_input,
     base_projection_weight,
     stored_down_maps,
@@ -74,6 +85,451 @@
     return (total * valid_mask[:, :, None]).astype(jnp.bfloat16)
 
 
+def where_am_i(meta_ref):
+    s, t = meta_ref[0], meta_ref[1]
+    chip = s // 2
+    return s, t, chip, jnp.where(chip == 1, t, 3 - t)
+
+
+def total_of(ref):
+    total = ref[0]
+    for q in range(1, ref.shape[0]):
+        total = total + ref[q]
+    return total
+
+
+def tie_kernel(*refs):
+    pass
+
+
+def after(value, *deps):
+    anywhere = pl.BlockSpec(memory_space=pl.ANY)
+    return pl.pallas_call(
+        tie_kernel,
+        in_specs=[anywhere] * (1 + len(deps)),
+        out_specs=anywhere,
+        out_shape=jax.ShapeDtypeStruct(value.shape, value.dtype),
+        input_output_aliases={0: 0},
+        cost_estimate=LIGHT,
+    )(value, *deps)
+
+
+def project_kernel(first, blocks, tokens, span, ndeps, *refs):
+    meta_ref, len_refs = refs[0], refs[1 : 1 + blocks]
+    x_refs, w_ref = refs[1 + blocks : 1 + 2 * blocks], refs[1 + 2 * blocks]
+    out_ref, packed = refs[-2], refs[-1]
+    rows = packed.shape[0]
+
+    @pl.when(pl.program_id(0) == 0)
+    def _():
+        s, _, _, u = where_am_i(meta_ref)
+        width = x_refs[0].shape[0]
+        lead = (s % 2) == 0
+        sums = [total_of(r) for r in len_refs]
+        starts = [jnp.where(lead, 0, sums[1]), jnp.where(lead, sums[0], 0)]
+        if blocks == 4:
+            own = sums[0] + sums[1]
+            starts += [own + jnp.where(lead, 0, sums[3]), own + jnp.where(lead, sums[2], 0)]
+        lane = lax.broadcasted_iota(jnp.int32, (1, width), 1)
+        token = lane % tokens
+        wanted = lax.broadcasted_iota(jnp.int32, (rows, width), 0)
+        picks = []
+        for b in range(blocks):
+            start = starts[b] + u * span - first
+            spot = jnp.full((1, width), -1, jnp.int32)
+            for q in range(width // tokens):
+                length = len_refs[b][q]
+                here = (lane // tokens == q) & (token < length)
+                spot = jnp.where(here, start + token, spot)
+                start = start + length
+            picks.append(jnp.where(spot == wanted, F32(1), F32(0)).astype(BF16))
+        pick = jnp.concatenate(picks, axis=1)
+        held_rows = jnp.concatenate([r[...] for r in x_refs], axis=0)
+        packed[...] = jnp.dot(pick, held_rows, preferred_element_type=F32).astype(BF16)
+
+    out_ref[...] = jnp.dot(packed[...], w_ref[...], preferred_element_type=F32).astype(BF16)
+
+
+def project(meta, lens, xs, w, first, rows, span, deps=(), tile=512):
+    depth, cols = w.shape
+    blocks = len(xs)
+    block_rows = xs[0].shape[0]
+    tokens = block_rows // lens[0].shape[0]
+    smem = pl.BlockSpec(memory_space=pltpu.SMEM)
+    return pl.pallas_call(
+        functools.partial(project_kernel, first, blocks, tokens, span, len(deps)),
+        grid=(cols // tile,),
+        in_specs=[smem] * (1 + blocks)
+        + [pl.BlockSpec((block_rows, depth), lambda j: (0, 0))] * blocks
+        + [pl.BlockSpec((depth, tile), lambda j: (0, j))]
+        + [pl.BlockSpec(memory_space=pl.ANY)] * len(deps),
+        out_specs=pl.BlockSpec((rows, tile), lambda j: (0, j)),
+        out_shape=jax.ShapeDtypeStruct((rows, cols), BF16),
+        scratch_shapes=[pltpu.VMEM((rows, depth), BF16)],
+        compiler_params=pltpu.CompilerParams(vmem_limit_bytes=VMEM_LIMIT),
+        cost_estimate=LIGHT,
+    )(meta, *lens, *xs, w, *deps)
+
+
+def visit(meta_ref, req_ref, slot_ref, flip, held, requests, tokens, act):
+    s = meta_ref[0]
+    home = s ^ flip
+    count = jnp.int32(0)
+    for q in range(requests):
+        slot = slot_ref[req_ref[home * requests + q]]
+        local = lax.rem(slot, held)
+        mine = lax.div(slot, held) == s
+        row = pl.multiple_of(count * tokens, tokens)
+
+        @pl.when(mine)
+        def _():
+            act(q, row, local)
+
+        count = count + mine.astype(jnp.int32)
+
+
+def low_kernel(flips, has_before, held, rank, requests, tokens, *refs):
+    meta_ref, req_ref, slot_ref = refs[:3]
+    x_refs = refs[3 : 3 + len(flips)]
+    down_ref = refs[3 + len(flips)]
+    before_ref = refs[4 + len(flips)] if has_before else None
+    out_ref, gathered, every = refs[-3:]
+    size = out_ref.shape[0] // len(flips)
+    lanes = held * rank
+    gathered[...] = jnp.zeros(gathered.shape, BF16)
+    for i, flip in enumerate(flips):
+
+        def collect(q, row, local, i=i):
+            gathered[pl.ds(i * size + row, tokens), :] = x_refs[i][q * tokens : (q + 1) * tokens, :]
+
+        visit(meta_ref, req_ref, slot_ref, flip, held, requests, tokens, collect)
+    product = lax.dot_general(
+        gathered[...], down_ref[...], (((1,), (1,)), ((), ())), preferred_element_type=F32
+    )
+    gathered[:, :lanes] = product.astype(BF16)
+    every[...] = jnp.zeros(every.shape, BF16)
+    group = lax.broadcasted_iota(jnp.int32, (1, lanes), 1) // rank
+    for i, flip in enumerate(flips):
+
+        def mask(q, row, local, i=i):
+            here = pl.ds(i * size + row, tokens)
+            value = gathered[here, :lanes].astype(F32)
+            every[here, :] = jnp.where(group == local, value, F32(0)).astype(BF16)
+
+        visit(meta_ref, req_ref, slot_ref, flip, held, requests, tokens, mask)
+    source = lax.broadcasted_iota(jnp.int32, (lanes, 2 * rank), 0) % rank
+    target = lax.broadcasted_iota(jnp.int32, (lanes, 2 * rank), 1)
+    shift = rank if before_ref is not None else 0
+    fold = jnp.where(source + shift == target, F32(1), F32(0)).astype(BF16)
+    result = jnp.dot(every[...], fold, preferred_element_type=F32)
+    if before_ref is not None:
+        result = result + before_ref[...].astype(F32)
+    out_ref[...] = result.astype(BF16)
+
+
+def low_rank(meta, req, slot, xs, flips, down_t, before, held, rank, tokens, capacity, deps):
+    requests = xs[0].shape[0] // tokens
+    size = capacity * tokens * len(flips)
+    depth = xs[0].shape[1]
+    smem = pl.BlockSpec(memory_space=pltpu.SMEM)
+    vmem = pl.BlockSpec(memory_space=pltpu.VMEM)
+    extra = [] if before is None else [before]
+    return pl.pallas_call(
+        functools.partial(low_kernel, flips, before is not None, held, rank, requests, tokens),
+        in_specs=[smem] * 3 + [vmem] * (len(flips) + 1 + len(extra)) + [pl.BlockSpec(memory_space=pl.ANY)] * len(deps),
+        out_specs=vmem,
+        out_shape=jax.ShapeDtypeStruct((size, 2 * rank), BF16),
+        scratch_shapes=[pltpu.VMEM((size, depth), BF16), pltpu.VMEM((size, held * rank), BF16)],
+        compiler_params=pltpu.CompilerParams(vmem_limit_bytes=VMEM_LIMIT),
+        cost_estimate=LIGHT,
+    )(meta, req, slot, *xs, down_t, *extra, *deps)
+
+
+def up_kernel(ndeps, held, rank, requests, tokens, meta_ref, req_ref, slot_ref, *refs):
+    low_refs, up_ref, out_refs = refs[:4], refs[4], refs[5 + ndeps : 9 + ndeps]
+    wide, spread = refs[-2:]
+    lanes = held * rank
+    half = low_refs[0].shape[0]
+    size = half // 2
+
+    @pl.when(pl.program_id(0) == 0)
+    def _():
+        total = low_refs[0][...].astype(F32)
+        for r in low_refs[1:]:
+            total = total + r[...].astype(F32)
+        total = total.astype(BF16)
+        source = lax.broadcasted_iota(jnp.int32, (2 * rank, lanes), 0)
+        target = lax.broadcasted_iota(jnp.int32, (2 * rank, lanes), 1) % rank
+        for h in range(2):
+            tile = jnp.where(source == target + h * rank, F32(1), F32(0)).astype(BF16)
+            wide[h * half : (h + 1) * half, :] = jnp.dot(
+                total, tile, preferred_element_type=F32
+            ).astype(BF16)
+        spread[...] = jnp.zeros(spread.shape, BF16)
+        group = lax.broadcasted_iota(jnp.int32, (1, lanes), 1) // rank
+        for i in range(4):
+
+            def mask(q, row, local, i=i):
+                here = pl.ds(i * size + row, tokens)
+                value = wide[here, :].astype(F32)
+                spread[here, :] = jnp.where(group == local, value, F32(0)).astype(BF16)
+
+            visit(meta_ref, req_ref, slot_ref, i, held, requests, tokens, mask)
+
+    result = jnp.dot(spread[...], up_ref[...], preferred_element_type=F32).astype(BF16)
+    for i in range(4):
+        out_refs[i][...] = result[i * size : (i + 1) * size, :]
+
+
+def up_project(meta, req, slot, lows, up_2d, held, rank, tokens, capacity, requests, deps, tile=512):
+    cols = up_2d.shape[1]
+    size = capacity * tokens
+    smem = pl.BlockSpec(memory_space=pltpu.SMEM)
+    return pl.pallas_call(
+        functools.partial(up_kernel, len(deps), held, rank, requests, tokens),
+        grid=(cols // tile,),
+        in_specs=[smem] * 3
+        + [pl.BlockSpec(lows[0].shape, lambda j: (0, 0))] * 4
+        + [pl.BlockSpec((held * rank, tile), lambda j: (0, j))]
+        + [pl.BlockSpec(memory_space=pl.ANY)] * len(deps),
+        out_specs=[pl.BlockSpec((size, tile), lambda j: (0, j))] * 4,
+        out_shape=[jax.ShapeDtypeStruct((size, cols), BF16)] * 4,
+        scratch_shapes=[pltpu.VMEM((4 * size, held * rank), BF16)] * 2,
+        compiler_params=pltpu.CompilerParams(vmem_limit_bytes=VMEM_LIMIT),
+        cost_estimate=LIGHT,
+    )(meta, req, slot, *lows, up_2d, *deps)
+
+
+def finish_kernel(n, sizes, first, span, held, requests, tokens, capacity, with_delta, with_acc, *refs):
+    meta_ref, req_ref, slot_ref = refs[:3]
+    len_refs = refs[3:7]
+    at = 7
+    value_refs, got_refs = refs[at : at + n], refs[at + n : at + 2 * n]
+    at += 2 * n
+    delta_refs = refs[at : at + 4] if with_delta else ()
+    at += len(delta_refs)
+    acc_ref = refs[at] if with_acc else None
+    out_ref, picks, dpicks = refs[-3:]
+    s, t, _, _ = where_am_i(meta_ref)
+    size = capacity * tokens
+    keep = (s == t) | (s == (t ^ 2))
+
+    @pl.when(pl.program_id(0) == 0)
+    def _():
+        flip = 2 * (t // 2)
+        key = s ^ flip
+        start = jnp.where((t == 0) | (t == 3), 3, 2) * span - first
+        for i in range(1, 4):
+            start = start + jnp.where(((s ^ i) ^ flip) < key, total_of(len_refs[i]), 0)
+        depth = picks.shape[1]
+        token = lax.broadcasted_iota(jnp.int32, (tokens, depth), 0)
+        base = lax.broadcasted_iota(jnp.int32, (tokens, depth), 1) - token
+        wide = dpicks.shape[1]
+        dtoken = lax.broadcasted_iota(jnp.int32, (tokens, wide), 0)
+        dbase = lax.broadcasted_iota(jnp.int32, (tokens, wide), 1) - dtoken
+        counts = [jnp.int32(0)] * 4
+        for q in range(requests):
+            length = len_refs[0][q]
+            here = (base == start) & (token < length)
+            picks[q * tokens : (q + 1) * tokens, :] = jnp.where(here, F32(1), F32(0)).astype(BF16)
+            start = start + length
+            if with_delta:
+                owner = lax.div(slot_ref[req_ref[s * requests + q]], held) ^ s
+                turn = jnp.int32(0)
+                for i in range(4):
+                    turn = turn + jnp.where(owner == i, counts[i], 0)
+                    counts[i] = counts[i] + jnp.where(owner == i, 1, 0)
+                here = (dbase == owner * size + turn * tokens) & (dtoken < length)
+                dpicks[q * tokens : (q + 1) * tokens, :] = jnp.where(here, F32(2), F32(0)).astype(BF16)
+
+    def run(group):
+        total = None
+        for i, (ref, count) in enumerate(zip(group, sizes)):
+            offset = sum(sizes[:i])
+            part = jnp.dot(picks[:, offset : offset + count], ref[...], preferred_element_type=F32)
+            total = part if total is None else total + part
+        if with_delta:
+            stack = jnp.concatenate([r[...] for r in delta_refs], axis=0)
+            total = total + jnp.dot(dpicks[...], stack, preferred_element_type=F32)
+        if with_acc:
+            total = total + acc_ref[...]
+        out_ref[...] = total.astype(out_ref.dtype)
+
+    @pl.when(keep)
+    def _():
+        run(value_refs)
+
+    @pl.when(jnp.logical_not(keep))
+    def _():
+        run(got_refs)
+
+
+def finish(meta, req, slot, lens, values, gots, first, deltas, acc, out_dtype, span, held, tokens, capacity, tile=512):
+    requests = lens[0].shape[0]
+    rows = requests * tokens
+    cols = values[0].shape[1]
+    sizes = [v.shape[0] for v in values]
+    depth = sum(sizes)
+    wide = 4 * capacity * tokens
+    smem = pl.BlockSpec(memory_space=pltpu.SMEM)
+    big = list(values) + list(gots) + list(deltas) + ([] if acc is None else [acc])
+    return pl.pallas_call(
+        functools.partial(
+            finish_kernel,
+            len(sizes), sizes, first, span, held, requests, tokens, capacity, bool(deltas), acc is not None,
+        ),
+        grid=(cols // tile,),
+        in_specs=[smem] * 7 + [pl.BlockSpec((a.shape[0], tile), lambda j: (0, j)) for a in big],
+        out_specs=pl.BlockSpec((rows, tile), lambda j: (0, j)),
+        out_shape=jax.ShapeDtypeStruct((rows, cols), out_dtype),
+        scratch_shapes=[
+            pltpu.VMEM((rows, depth), BF16),
+            pltpu.VMEM((rows, wide if deltas else 128), BF16),
+        ],
+        compiler_params=pltpu.CompilerParams(vmem_limit_bytes=SMALL_VMEM),
+        cost_estimate=LIGHT,
+    )(meta, req, slot, *lens, *big)
+
+
+def on_store(value, flip):
+    return lax.ppermute(value, "store", [(i, i ^ flip) for i in range(4)])
+
+
+def plane(s, u):
+    return u if s >= 2 else 3 - u
+
+
+def last_step(s):
+    return 3 if s in (0, 3) else 2
+
+
+def on_mesh(value, pairs):
+    return lax.ppermute(value, ("tensor", "store"), [(a * 4 + b, c * 4 + d) for (a, b), (c, d) in pairs])
+
+
+def square(x, w, down, up, req, slot, lengths):
+    requests, tokens, depth = x.shape
+    cols = w.shape[1]
+    rows = requests * tokens
+    live = 3 * rows
+    held, _, rank = down.shape
+    capacity = requests // 2
+    span = SPAN
+    steps = live // span
+    edge = cols // 2 + 128
+    bounds = ((0, edge), (edge, cols))
+
+    s = lax.axis_index("store")
+    t = lax.axis_index("tensor")
+    meta = jnp.stack([s, t]).astype(jnp.int32)
+
+    x_me = x.reshape(rows, depth)
+    x_far = on_store(x_me, 2)
+    len_me = lengths
+    len_sib = on_store(len_me, 1)
+    x_sib = on_store(x_me, 1)
+    lens_far = on_store(jnp.concatenate([len_me, len_sib]), 2)
+    len_far, len_fsib = lens_far[:requests], lens_far[requests:]
+    x_fsib = on_store(x_far, 1)
+    lens = [len_me, len_sib, len_far, len_fsib]
+    xs = [x_me, x_sib, x_far, x_fsib]
+    down_t = jnp.transpose(down, (0, 2, 1)).reshape(held * rank, depth)
+    up_2d = up.reshape(held * rank, cols)
+
+    early = rows // span
+    back_pairs = [((plane(b, 3), b), (plane(b, 2), b)) for b in (1, 2)]
+    across = [((v, v), (v, v ^ 2)) for v in range(4)]
+    beside = [((v, v), (v, v ^ 1)) for v in range(4)] + [((v, v ^ 2), (v, v ^ 3)) for v in range(4)]
+    is_root = s == t
+    chip = s // 2
+    u = jnp.where(chip == 1, t, 3 - t)
+
+    final, carry, parts = {}, [None] * STREAMS, {}
+
+    def chunk_of(source, k, j):
+        at = jnp.clip(k - u, 0, steps - 1) * span
+        lo, hi = bounds[j]
+        return lax.dynamic_slice(source, (at, lo), (span, hi - lo))
+
+    def chain_step(k, *deps):
+        pairs = [
+            ((plane(b, v), b), (plane(b, v + 1), b))
+            for b in range(4)
+            for v in range(last_step(b))
+            if 0 <= k - v < steps
+        ]
+        for j in range(STREAMS):
+            if k < early:
+                value = parts[0][k * span : (k + 1) * span, bounds[j][0] : bounds[j][1]]
+            elif k == early:
+                value = parts[1][:, bounds[j][0] : bounds[j][1]]
+            else:
+                value = chunk_of(parts[2], k, j)
+            if carry[j] is not None:
+                came = carry[j]
+                if deps and not j:
+                    came = after(came, *deps)
+                value = (value.astype(F32) + came.astype(F32)).astype(BF16)
+            final[k, j] = value
+            carry[j] = on_mesh(value, pairs) if pairs else None
+
+    values, gots = [], []
+
+    def post(lo, hi):
+        columns = []
+        for j in range(STREAMS):
+            column = []
+            for k in range(lo, hi):
+                value = final[k, j]
+                if k < steps + 2:
+                    value = (value.astype(F32) + chunk_of(back, k, j).astype(F32)).astype(BF16)
+                column.append(value)
+            columns.append(jnp.concatenate(column, axis=0))
+        value = jnp.concatenate(columns, axis=1)
+        if (hi - 2) * span > rows:
+            value = jnp.where(is_root, value, on_mesh(value, across))
+        values.append(value)
+        gots.append(on_mesh(value, beside))
+
+    parts[0] = project(meta, lens[:2], xs[:2], w, 0, early * span, span)
+    chain_step(0)
+    low = low_rank(
+        meta, req, slot, xs[:2], (0, 1), down_t, None, held, rank, tokens, capacity, (parts[0],)
+    )
+    chain_step(1)
+    x_far = after(x_far, final[1, 0], final[1, 1], low)
+    x_fsib = on_store(x_far, 1)
+    xs = [x_me, x_sib, x_far, x_fsib]
+    parts[1] = project(meta, lens, xs, w, early * span, span, span)
+    chain_step(2)
+    parts[2] = project(meta, lens, xs, w, 0, live, 0, (final[2, 0], final[2, 1]))
+    chain_step(3)
+    back = on_mesh(parts[2], back_pairs)
+    low = low_rank(
+        meta, req, slot, xs[2:], (2, 3), down_t, low, held, rank, tokens, capacity, (final[3, 0], final[3, 1])
+    )
+    lows = [low] + [lax.ppermute(low, "tensor", [(i, i ^ f) for i in range(4)]) for f in (1, 2, 3)]
+    chain_step(4, low)
+    delta = up_project(meta, req, slot, lows, up_2d, held, rank, tokens, capacity, requests, (final[4, 0], final[4, 1]))
+    deltas = [delta[0]] + [on_store(delta[i], i) for i in (1, 2, 3)]
+    chain_step(5, delta[0])
+    back = after(back, final[5, 0], final[5, 1])
+    post(2, 4)
+    chain_step(6)
+    post(4, 6)
+    chain_step(7)
+    partial = finish(
+        meta, req, slot, lens, values[:1], gots[:1], 2 * span, deltas, None, F32, span, held, tokens, capacity
+    )
+    chain_step(8, partial)
+    post(6, 8)
+    post(8, 9)
+    out = finish(
+        meta, req, slot, lens, values[1:], gots[1:], 4 * span, (), partial, BF16, span, held, tokens, capacity
+    )
+    return out.reshape(requests, tokens, cols)
+
+
 def solution(mesh):
     in_specs = (
         P(("groups", "store"), None, "tensor"),
@@ -85,4 +541,6 @@
         P(("groups", "store")),
     )
     out_specs = P(("groups", "store"), None, "tensor")
-    return jax.shard_map(shards, mesh=mesh, in_specs=in_specs, out_specs=out_specs, check_vma=False)
+    four = mesh.shape["store"] == 4 and mesh.shape["tensor"] == 4
+    body = square if four else general
+    return jax.shard_map(body, mesh=mesh, in_specs=in_specs, out_specs=out_specs, check_vma=False)

time: 331 us -> 207 us (0.63)
  waiting for transfers between devices: 231 us -> 52.7 us
  matrix products: 66.5 us -> 0 us
  starting transfers between devices: 8.3 us -> 64.2 us
  Pallas kernels: 0 us -> 52.2 us
  other arithmetic: 4.79 us -> 29.6 us
  between operations: 14.9 us -> 0.75 us
    all_gather x1 -> x0, waiting for transfers between devices: 162 us -> none  [shards(): lax.all_gather(base_projection_weight, 'store', axis=1, tiled=True)]
    dot_general x7 -> x0, matrix products: 66.5 us -> none  [the longest x1 16.4 us: shards(): jnp.einsum('qtk,kd->qtd', attention_input, lax.all_gather(base_projection...]
    ppermute x0 -> x35, starting transfers between devices: none -> 64.2 us  [the longest x24 52 us: on_mesh(): lax.ppermute(value, ('tensor', 'store'), [(a * 4 + b, c * 4 + d) for (a,...]
    ppermute x0 -> x35, waiting for transfers between devices: none -> 52.7 us  [the longest x24 35.7 us: on_mesh(): lax.ppermute(value, ('tensor', 'store'), [(a * 4 + b, c * 4 + d) for (a,...]
    pallas_call x0 -> x13, Pallas kernels: none -> 52.2 us  [the longest x3 27.9 us: project(): pl.pallas_call(functools.partial(project_kernel, first, blocks, tokens, s...]
    all_to_all x2 -> x0, waiting for transfers between devices: 47.5 us -> none  [the longest x1 24.9 us: shards(): lax.all_to_all(delta_rows, 'store', split_axis=0, concat_axis=0, tiled=True)]
    reduce_scatter x1 -> x0, waiting for transfers between devices: 20.7 us -> none  [shards(): lax.psum_scatter(partial_value.astype(jnp.bfloat16), 'tensor', scatter_di...]
    convert_element_type x2 -> x16, other arithmetic: 4.23 us -> 22.5 us  [the longest x12 13.1 us: chain_step(): value = (value.astype(F32) + came.astype(F32)).astype(BF16)]
  transfers between devices with their start and end apart: 5 -> 35, of which waited for: 4 -> 16; matrix products, arithmetic and copies ran while one was open for 21% -> 13% of each run, Pallas kernels for 0% -> 17%
where the time goes in v2:
time: 207 us; the launch traced here: 205 us
  starting transfers between devices  64.2 us (31%)
  waiting for transfers between devices  52.7 us (25%)
  Pallas kernels  52.2 us (25%)
  other arithmetic  29.6 us (14%)
  local copies, waits for them, and re-layouts  5.74 us (3%)
    ppermute x24, starting transfers between devices, on_mesh(): lax.ppermute(value, ('tensor', 'store'), [(a * 4 + b, c * 4 + d) for (a,...  52 us
    ppermute x24, waiting for transfers between devices, on_mesh(): lax.ppermute(value, ('tensor', 'store'), [(a * 4 + b, c * 4 + d) for (a,...  35.7 us
    pallas_call x3, Pallas kernels, project(): pl.pallas_call(functools.partial(project_kernel, first, blocks, tokens, s...  27.9 us
    ppermute x8, waiting for transfers between devices, on_store(): return lax.ppermute(value, 'store', [(i, i ^ flip) for i in range(4)])  17 us
    convert_element_type x12, other arithmetic, chain_step(): value = (value.astype(F32) + came.astype(F32)).astype(BF16)  13.1 us
    pallas_call x2, Pallas kernels, low_rank(): pl.pallas_call(functools.partial(low_kernel, flips, before is not None, h...  10.5 us
    ppermute x8, starting transfers between devices, on_store(): return lax.ppermute(value, 'store', [(i, i ^ flip) for i in range(4)])  9.41 us
    convert_element_type x4, other arithmetic, post(): value = (value.astype(F32) + chunk_of(back, k, j).astype(F32)).astype(BF16)  9.34 us
  transfers between devices with their start and end apart: 35, of which 16 were waited for; matrix products, arithmetic and copies ran while one was open for 13% of the time, Pallas kernels for 17%

profile of v2, /device:TPU:21, one launch (start us, length us, event | category | flops | bytes accessed | tf_op | source)
XLA Modules:
  0.0 205.3 jit_solution(18114829696234104335)
XLA Ops:
  4.0 7.0 %shard_map.73.refs_6_ = bf16[256,2048]{1,0:T(8,128)(2,1)S(1)} custom-call(s32[2]{0:T(128)S(1)} %pad_add_fusion.refs_0_.meta_ref, s32[16]{0:T(128)S(1)} %copy-done.12, s32[16]{0:T(128)S(1)} %collective-permute-done.refs_2_.refs_4_, bf16[256,2048]{1,0:T(8,128)(2,1)} %bitcast.10, bf16[256,2048]{1,0:T(8,128)(2,1)} %collective-permute-done.2.refs_4_.refs_6_, ...), custom_call_target="tpu_custom_call" | custom-call | tf_op jit(solution)/shard_map/pallas_call | solution.py:159
  13.7 5.3 %shard_map.74.refs_3_.refs_6_ = bf16[256,128]{1,0:T(8,128)(2,1)S(1)} custom-call(s32[2]{0:T(128)S(1)} %pad_add_fusion.refs_0_.meta_ref, s32[64]{0:T(128)S(1)} %copy-done.14, s32[64]{0:T(128)S(1)} %copy-done.15, bf16[256,2048]{1,0:T(8,128)(2,1)S(1)} %bitcast.11, bf16[256,2048]{1,0:T(8,128)(2,1)} %collective-permute-done.2.refs_4_.refs_6_, ...), custom_call_target="tpu_custom_call" | custom-call | tf_op jit(solution)/shard_map/pallas_call | solution.py:237
  19.7 1.7 add_convert_fusion.27.refs_2_
  21.4 4.6 %collective-permute-done.4 = bf16[128,1152]{1,0:T(8,128)(2,1)S(1)} collective-permute-done((bf16[128,1152]{1,0:T(8,128)(2,1)S(1)}, bf16[128,1152]{1,0:T(8,128)(2,1)S(1)}, u32[]{:S(2)}, u32[]{:S(2)}) %collective-permute-start.4) | collective-permute-done | bytes 294944 | tf_op jit(solution)/shard_map/ppermute | solution.py:407
  26.0 1.8 add_convert_fusion.13.refs_1_
  30.0 1.9 collective-permute-start.7
  32.0 2.4 %collective-permute-done.1 = s32[32]{0:T(128)S(1)} collective-permute-done((s32[32]{0:T(128)S(1)}, s32[32]{0:T(128)S(1)}, u32[]{:S(2)}, u32[]{:S(2)}) %collective-permute-start.1) | collective-permute-done | bytes 160 | tf_op jit(solution)/shard_map/ppermute | solution.py:395
  34.5 1.9 collective-permute-start.8
  37.4 6.7 %shard_map.76 = bf16[128,2048]{1,0:T(8,128)(2,1)S(1)} custom-call(s32[2]{0:T(128)S(1)} %pad_add_fusion.refs_0_.meta_ref, s32[16]{0:T(128)S(1)} %copy-done.12, s32[16]{0:T(128)S(1)} %collective-permute-done.refs_2_.refs_4_, s32[16]{0:T(128)S(1)} %get-tuple-element.34.refs_3_.refs_5_, s32[16]{0:T(128)S(1)} %get-tuple-element.33.refs_4_.refs_6_, ...), custom_call_target="tpu_custom_call" | custom-call | tf_op jit(solution)/shard_map/pallas_call | solution.py:159
  45.3 14.3 %shard_map.77 = bf16[768,2048]{1,0:T(8,128)(2,1)} custom-call(s32[2]{0:T(128)S(1)} %pad_add_fusion.refs_0_.meta_ref, s32[16]{0:T(128)S(1)} %copy-done.12, s32[16]{0:T(128)S(1)} %collective-permute-done.refs_2_.refs_4_, s32[16]{0:T(128)S(1)} %get-tuple-element.34.refs_3_.refs_5_, s32[16]{0:T(128)S(1)} %get-tuple-element.33.refs_4_.refs_6_, ...), custom_call_target="tpu_custom_call" | custom-call | tf_op jit(solution)/shard_map/pallas_call | solution.py:159
  59.6 2.4 %collective-permute-start.12 = (bf16[768,2048]{1,0:T(8,128)(2,1)}, bf16[768,2048]{1,0:T(8,128)(2,1)}, u32[]{:S(2)}, u32[]{:S(2)}) collective-permute-start(bf16[768,2048]{1,0:T(8,128)(2,1)} %shard_map.77), channel_id=1, source_target_pairs={{1,5},{14,10},{17,21},{30,26}} | collective-permute-start | bytes 9437192 | tf_op jit(solution)/shard_map/ppermute | solution.py:407
  62.0 1.9 collective-permute-start.11
  63.9 1.9 collective-permute-start.9
  65.9 4.2 %collective-permute-done.11 = bf16[128,896]{1,0:T(8,128)(2,1)S(1)} collective-permute-done((bf16[128,896]{1,0:T(8,128)(2,1)S(1)}, bf16[128,896]{1,0:T(8,128)(2,1)S(1)}, u32[]{:S(2)}, u32[]{:S(2)}) %collective-permute-start.11) | collective-permute-done | bytes 229408 | tf_op jit(solution)/shard_map/ppermute | solution.py:407
  71.1 1.9 collective-permute-start.17
  73.0 3.4 %collective-permute-done.9 = bf16[128,1152]{1,0:T(8,128)(2,1)S(1)} collective-permute-done((bf16[128,1152]{1,0:T(8,128)(2,1)S(1)}, bf16[128,1152]{1,0:T(8,128)(2,1)S(1)}, u32[]{:S(2)}, u32[]{:S(2)}) %collective-permute-start.9) | collective-permute-done | bytes 294944 | tf_op jit(solution)/shard_map/ppermute | solution.py:407
  77.5 1.9 collective-permute-start.10
  79.4 5.3 %shard_map.78.refs_1_.refs_0_ = bf16[256,128]{1,0:T(8,128)(2,1)S(1)} custom-call(s32[2]{0:T(128)S(1)} %pad_add_fusion.refs_0_.meta_ref, s32[64]{0:T(128)S(1)} %copy-done.14, s32[64]{0:T(128)S(1)} %copy-done.15, bf16[256,2048]{1,0:T(8,128)(2,1)S(1)} %copy-done.4, bf16[256,2048]{1,0:T(8,128)(2,1)} %copy-done.16, bf16[1024,2048]{1,0:T(8,128)(2,1)} %bitcast.15, ...), custom_call_target="tpu_custom_call" | custom-call | tf_op jit(solution)/shard_map/pallas_call | solution.py:237
  84.7 1.5 collective-permute-start.14
  88.5 2.3 %collective-permute-start.18 = (bf16[128,896]{1,0:T(8,128)(2,1)S(1)}, bf16[128,896]{1,0:T(8,128)(2,1)S(1)}, u32[]{:S(2)}, u32[]{:S(2)}) collective-permute-start(bf16[128,896]{1,0:T(8,128)(2,1)S(1)} %add_convert_fusion.24.refs_6_), channel_id=1, source_target_pairs={{12,8},{8,4},{4,0},{13,9},{9,5},{2,6},{6,10},{3,7},{7,11},{11,15},... | collective-permute-start | bytes 688136 | tf_op jit(solution)/shard_map/ppermute | solution.py:407
  92.0 10.9 %collective-permute-start.13 = (bf16[128,1152]{1,0:T(8,128)(2,1)S(1)}, bf16[128,1152]{1,0:T(8,128)(2,1)S(1)}, u32[]{:S(2)}, u32[]{:S(2)}) collective-permute-start(bf16[128,1152]{1,0:T(8,128)(2,1)S(1)} %add_convert_fusion.10.refs_5_), channel_id=1, source_target_pairs={{12,8},{8,4},{4,0},{13,9},{9,5},{2,6},{6,10},{3,7},{7,11},{11,15},... | collective-permute-start | bytes 884744 | tf_op jit(solution)/shard_map/ppermute | solution.py:407
  103.8 7.2 %shard_map.80 = (bf16[128,2048]{1,0:T(8,128)(2,1)S(1)}, bf16[128,2048]{1,0:T(8,128)(2,1)S(1)}, bf16[128,2048]{1,0:T(8,128)(2,1)}, bf16[128,2048]{1,0:T(8,128)(2,1)}) custom-call(s32[2]{0:T(128)S(1)} %pad_add_fusion.refs_0_.meta_ref, s32[64]{0:T(128)S(1)} %copy-done.14, s32[64]{0:T(128)S(1)} %copy-done.15, bf16[256,128]{1,0:T(8,128)(2,1)S(1)} %copy-done.9, ...), custom_call_target="tpu_custom_call" | custom-call | tf_op jit(solution)/shard_map/pallas_call | solution.py:288
  111.0 1.9 add_convert_fusion.23.refs_2_
  112.9 1.9 collective-permute-start.22
  116.7 1.9 collective-permute-start.20
  118.7 3.3 %collective-permute-done.22 = bf16[128,896]{1,0:T(8,128)(2,1)S(1)} collective-permute-done((bf16[128,896]{1,0:T(8,128)(2,1)}, bf16[128,896]{1,0:T(8,128)(2,1)S(1)}, u32[]{:S(2)}, u32[]{:S(2)}) %collective-permute-start.22) | collective-permute-done | bytes 229408 | tf_op jit(solution)/shard_map/ppermute | solution.py:407
  122.0 1.9 add_convert_fusion.19
  123.8 2.1 %collective-permute-start.23 = (bf16[128,896]{1,0:T(8,128)(2,1)S(1)}, bf16[128,896]{1,0:T(8,128)(2,1)S(1)}, u32[]{:S(2)}, u32[]{:S(2)}) collective-permute-start(bf16[128,896]{1,0:T(8,128)(2,1)S(1)} %get-tuple-element.18), channel_id=1, source_target_pairs={{8,4},{4,0},{9,5},{6,10},{7,11},{11,15},{24,20},{20,16},{25,21},{2... | collective-permute-start | bytes 688136 | tf_op jit(solution)/shard_map/ppermute | solution.py:407
  126.2 1.9 add_convert_fusion.5
  128.2 4.9 %collective-permute-start.21 = (bf16[128,1152]{1,0:T(8,128)(2,1)S(1)}, bf16[128,1152]{1,0:T(8,128)(2,1)}, u32[]{:S(2)}, u32[]{:S(2)}) collective-permute-start(bf16[128,1152]{1,0:T(8,128)(2,1)S(1)} %get-tuple-element.14), channel_id=1, source_target_pairs={{8,4},{4,0},{9,5},{6,10},{7,11},{11,15},{24,20},{20,16},{25,21},{2... | collective-permute-start | bytes 884744 | tf_op jit(solution)/shard_map/ppermute | solution.py:407
  133.1 2.8 %add_convert_fusion.16 = (bf16[128,896]{1,0:T(8,128)(2,1)S(1)}, bf16[128,896]{1,0:T(8,128)(2,1)S(1)}, bf16[128,896]{1,0:T(8,128)(2,1)}, bf16[128,896]{1,0:T(8,12...) fusion(bf16[128,896]{1,0:T(8,128)(2,1)S(1)} %add_convert_fusion.26.refs_11_, ...), kind=kLoop, calls=%fused_computation.23 | loop fusion | flops 2752512 | bytes 3899412 | tf_op jit(solution)/shard_map/convert_element_type | solution.py:485
  136.2 2.8 %add_convert_fusion.2 = (bf16[128,1152]{1,0:T(8,128)(2,1)S(1)}, bf16[128,1152]{1,0:T(8,128)(2,1)S(1)}, bf16[128,1152]{1,0:T(8,128)(2,1)}, bf16[128,1152]{1,0:T(8...) fusion(bf16[128,1152]{1,0:T(8,128)(2,1)S(1)} %add_convert_fusion.12.refs_10_, ...), kind=kLoop, calls=%fused_computation.7 | loop fusion | flops 3538944 | bytes 5013524 | tf_op jit(solution)/shard_map/convert_element_type | solution.py:485
  141.7 4.7 %collective-permute-start.28 = (bf16[128,2048]{1,0:T(8,128)(2,1)}, bf16[128,2048]{1,0:T(8,128)(2,1)S(1)}, u32[]{:S(2)}, u32[]{:S(2)}) collective-permute-start(bf16[128,2048]{1,0:T(8,128)(2,1)} %get-tuple-element.11), channel_id=1, source_target_pairs={{0,2},{1,3},{2,0},{3,1},{4,6},{5,7},{6,4},{7,5},{8,10},{9,11},{10,... | collective-permute-start | bytes 1572872 | tf_op jit(solution)/shard_map/ppermute | solution.py:395
  147.1 2.5 %maximum_maximum_fusion.1 = bf16[256,2048]{1,0:T(8,128)(2,1)} fusion(bf16[128,896]{1,0:T(8,128)(2,1)} %get-tuple-element.29, bf16[128,896]{1,0:T(8,128)(2,1)} %get-tuple-element.17, bf16[128,1152]{1,0:T(8,128)(2,1)} %get-tuple-element.23, bf16[128,1152]{1,0:T(8,128)(2,1)} %get-tuple-element.13), kind=kLoop, calls=%fused_computation.1 | loop fusion | flops 4194304 | bytes 2097152 | tf_op jit(solution)/shard_map/concatenate | solution.py:488
  149.7 1.4 collective-permute-start.25
  151.1 1.7 collective-permute-start.24
  154.9 4.0 %collective-permute-done.28.refs_11_ = bf16[128,2048]{1,0:T(8,128)(2,1)S(1)} collective-permute-done((bf16[128,2048]{1,0:T(8,128)(2,1)}, bf16[128,2048]{1,0:T(8,128)(2,1)S(1)}, u32[]{:S(2)}, u32[]{:S(2)}) %collective-permute-start.28) | collective-permute-done | bytes 524320 | tf_op jit(solution)/shard_map/ppermute | solution.py:395
  158.9 1.7 collective-permute-start.19
  160.5 9.6 %collective-permute-done.29.refs_12_ = bf16[128,2048]{1,0:T(8,128)(2,1)S(1)} collective-permute-done((bf16[128,2048]{1,0:T(8,128)(2,1)}, bf16[128,2048]{1,0:T(8,128)(2,1)S(1)}, u32[]{:S(2)}, u32[]{:S(2)}) %collective-permute-start.29) | collective-permute-done | bytes 524320 | tf_op jit(solution)/shard_map/ppermute | solution.py:395
  170.1 3.0 %shard_map.83.refs_1_.refs_13_ = f32[256,2048]{1,0:T(8,128)S(1)} custom-call(s32[2]{0:T(128)S(1)} %pad_add_fusion.refs_0_.meta_ref, s32[64]{0:T(128)S(1)} %copy-done.14, s32[64]{0:T(128)S(1)} %copy-done.15, s32[16]{0:T(128)S(1)} %copy-done.13, s32[16]{0:T(128)S(1)} %collective-permute-done.refs_2_.refs_4_, s32[16]{0:T(128)S(1)} %get-tuple-element.34.refs_3_.refs_5_, ...), custom_call_target="tpu_custom_call" | custom-call | tf_op jit(solution)/shard_map/pallas_call | solution.py:376
  173.1 1.3 copy-done
  176.6 1.5 broadcast_select_fusion.refs_8_
  178.2 1.4 collective-permute-start.33
  179.7 1.5 broadcast_select_fusion.1.refs_7_
  184.0 3.3 %collective-permute-done.33.refs_11_ = bf16[256,2048]{1,0:T(8,128)(2,1)S(1)} collective-permute-done((bf16[256,2048]{1,0:T(8,128)(2,1)S(1)}, bf16[256,2048]{1,0:T(8,128)(2,1)S(1)}, u32[]{:S(2)}, u32[]{:S(2)}) %collective-permute-start.33) | collective-permute-done | bytes 1048608 | tf_op jit(solution)/shard_map/ppermute | solution.py:407
  187.2 11.1 %collective-permute-done.32.refs_10_ = bf16[256,2048]{1,0:T(8,128)(2,1)S(1)} collective-permute-done((bf16[256,2048]{1,0:T(8,128)(2,1)S(1)}, bf16[256,2048]{1,0:T(8,128)(2,1)S(1)}, u32[]{:S(2)}, u32[]{:S(2)}) %collective-permute-start.32) | collective-permute-done | bytes 1048608 | tf_op jit(solution)/shard_map/ppermute | solution.py:407
  198.3 3.3 %collective-permute-done.34.refs_12_ = bf16[128,2048]{1,0:T(8,128)(2,1)S(1)} collective-permute-done((bf16[128,2048]{1,0:T(8,128)(2,1)S(1)}, bf16[128,2048]{1,0:T(8,128)(2,1)S(1)}, u32[]{:S(2)}, u32[]{:S(2)}) %collective-permute-start.34) | collective-permute-done | bytes 524320 | tf_op jit(solution)/shard_map/ppermute | solution.py:407
  201.7 3.6 %shard_map.85 = bf16[256,2048]{1,0:T(8,128)(2,1)} custom-call(s32[2]{0:T(128)S(1)} %pad_add_fusion.refs_0_.meta_ref, s32[64]{0:T(128)S(1)} %copy-done.14, s32[64]{0:T(128)S(1)} %copy-done.15, s32[16]{0:T(128)S(1)} %copy-done.13, s32[16]{0:T(128)S(1)} %collective-permute-done.refs_2_.refs_4_, s32[16]{0:T(128)S(1)} %get-tuple-element.34.refs_3_.refs_5_, ...), custom_call_target="tpu_custom_call" | custom-call | tf_op jit(solution)/shard_map/pallas_call | solution.py:376
  (131 shorter events, 31.2 us)
Async XLA Ops:
  0.0 3.3 %collective-permute-start.2 = (bf16[256,2048]{1,0:T(8,128)(2,1)}, bf16[256,2048]{1,0:T(8,128)(2,1)}, u32[]{:S(2)}, u32[]{:S(2)}) collective-permute-start(bf16[256,2048]{1,0:T(8,128)(2,1)} %bitcast.8), channel_id=1, source_target_pairs={{0,1},{1,0},{2,3},{3,2},{4,5},{5,4},{6,7},{7,6},{8,9},{9,8},{10,11... | collective-permute-start | bytes 3145736 | tf_op jit(solution)/shard_map/ppermute | solution.py:395
  0.7 27.1 %collective-permute-start.3 = (bf16[256,2048]{1,0:T(8,128)(2,1)}, bf16[256,2048]{1,0:T(8,128)(2,1)S(1)}, u32[]{:S(2)}, u32[]{:S(2)}) collective-permute-start(bf16[256,2048]{1,0:T(8,128)(2,1)} %bitcast.9), channel_id=1, source_target_pairs={{0,2},{1,3},{2,0},{3,1},{4,6},{5,7},{6,4},{7,5},{8,10},{9,11},{10,... | collective-permute-start | bytes 3145736 | tf_op jit(solution)/shard_map/ppermute | solution.py:395
  1.9 1.3 collective-permute-start
  2.2 11.5 %copy-start.14 = (s32[64]{0:T(128)S(1)}, s32[64]{0:T(128)}, u32[]{:S(2)}) copy-start(s32[64]{0:T(128)} %refs_1_.13) | copy-start | bytes 772
  2.2 11.5 %copy-start.15 = (s32[64]{0:T(128)S(1)}, s32[64]{0:T(128)}, u32[]{:S(2)}) copy-start(s32[64]{0:T(128)} %refs_2_.7) | copy-start | bytes 772
  2.3 11.4 %copy-start.2 = (bf16[16,16,2048]{2,1,0:T(8,128)(2,1)S(1)}, bf16[16,16,2048]{2,1,0:T(8,128)(2,1)}, u32[]{:S(2)}) copy-start(bf16[16,16,2048]{2,1,0:T(8,128)(2,1)} %param.7) | copy-start | bytes 3145732
  11.0 8.7 %collective-permute-start.5 = (bf16[128,896]{1,0:T(8,128)(2,1)S(1)}, bf16[128,896]{1,0:T(8,128)(2,1)S(1)}, u32[]{:S(2)}, u32[]{:S(2)}) collective-permute-start(bf16[128,896]{1,0:T(8,128)(2,1)S(1)} %slice.35), channel_id=1, source_target_pairs={{12,8},{13,9},{2,6},{3,7},{28,24},{29,25},{18,22},{19,23}} | collective-permute-start | bytes 688136 | tf_op jit(solution)/shard_map/ppermute | solution.py:407
  12.3 13.7 %collective-permute-start.4 = (bf16[128,1152]{1,0:T(8,128)(2,1)S(1)}, bf16[128,1152]{1,0:T(8,128)(2,1)S(1)}, u32[]{:S(2)}, u32[]{:S(2)}) collective-permute-start(bf16[128,1152]{1,0:T(8,128)(2,1)S(1)} %slice.33), channel_id=1, source_target_pairs={{12,8},{13,9},{2,6},{3,7},{28,24},{29,25},{18,22},{19,23}} | collective-permute-start | bytes 884744 | tf_op jit(solution)/shard_map/ppermute | solution.py:407
  21.4 13.1 %copy-start.32 = (bf16[128,896]{1,0:T(8,128)(2,1)S(1)}, bf16[128,896]{1,0:T(8,128)(2,1)}, u32[]{:S(2)}) copy-start(bf16[128,896]{1,0:T(8,128)(2,1)} %add_convert_fusion.27.refs_2_) | copy-start | bytes 688132
  28.8 7.6 %collective-permute-start.6 = (bf16[256,2048]{1,0:T(8,128)(2,1)}, bf16[256,2048]{1,0:T(8,128)(2,1)S(1)}, u32[]{:S(2)}, u32[]{:S(2)}) collective-permute-start(bf16[256,2048]{1,0:T(8,128)(2,1)} %shard_map.75.refs_7_.refs_3_), channel_id=1, source_target_pairs={{0,1},{1,0},{2,3},{3,2},{4,5},{5,4},{6,7},{7,6},{8,9},{9,8},{10,11... | collective-permute-start | bytes 3145736 | tf_op jit(solution)/shard_map/ppermute | solution.py:395
  30.0 14.1 %collective-permute-start.7 = (bf16[128,1152]{1,0:T(8,128)(2,1)S(1)}, bf16[128,1152]{1,0:T(8,128)(2,1)S(1)}, u32[]{:S(2)}, u32[]{:S(2)}) collective-permute-start(bf16[128,1152]{1,0:T(8,128)(2,1)S(1)} %copy-done.31), channel_id=1, source_target_pairs={{12,8},{8,4},{13,9},{9,5},{2,6},{6,10},{3,7},{7,11},{28,24},{24,20... | collective-permute-start | bytes 884744 | tf_op jit(solution)/shard_map/ppermute | solution.py:407
  32.0 2.4 %collective-permute-start.1 = (s32[32]{0:T(128)S(1)}, s32[32]{0:T(128)S(1)}, u32[]{:S(2)}, u32[]{:S(2)}) collective-permute-start(s32[32]{0:T(128)S(1)} %pad_add_fusion.1), channel_id=1, source_target_pairs={{0,2},{1,3},{2,0},{3,1},{4,6},{5,7},{6,4},{7,5},{8,10},{9,11},{10,... | collective-permute-start | bytes 392 | tf_op jit(solution)/shard_map/ppermute | solution.py:395
  34.5 10.8 %collective-permute-start.8 = (bf16[128,896]{1,0:T(8,128)(2,1)S(1)}, bf16[128,896]{1,0:T(8,128)(2,1)S(1)}, u32[]{:S(2)}, u32[]{:S(2)}) collective-permute-start(bf16[128,896]{1,0:T(8,128)(2,1)S(1)} %copy-done.32), channel_id=1, source_target_pairs={{12,8},{8,4},{13,9},{9,5},{2,6},{6,10},{3,7},{7,11},{28,24},{24,20... | collective-permute-start | bytes 688136 | tf_op jit(solution)/shard_map/ppermute | solution.py:407
  45.3 34.1 %copy-start.11 = (bf16[256,128]{1,0:T(8,128)(2,1)S(1)}, bf16[256,128]{1,0:T(8,128)(2,1)}, u32[]{:S(2)}) copy-start(bf16[256,128]{1,0:T(8,128)(2,1)} %copy-done.10) | copy-start | bytes 196612
  59.6 19.8 %copy-start.4 = (bf16[256,2048]{1,0:T(8,128)(2,1)S(1)}, bf16[256,2048]{1,0:T(8,128)(2,1)}, u32[]{:S(2)}) copy-start(bf16[256,2048]{1,0:T(8,128)(2,1)} %shard_map.75.refs_7_.refs_3_) | copy-start | bytes 3145732
  59.6 59.1 %collective-permute-start.12 = (bf16[768,2048]{1,0:T(8,128)(2,1)}, bf16[768,2048]{1,0:T(8,128)(2,1)}, u32[]{:S(2)}, u32[]{:S(2)}) collective-permute-start(bf16[768,2048]{1,0:T(8,128)(2,1)} %shard_map.77), channel_id=1, source_target_pairs={{1,5},{14,10},{17,21},{30,26}} | collective-permute-start | bytes 9437192 | tf_op jit(solution)/shard_map/ppermute | solution.py:407
  62.0 8.0 %collective-permute-start.11 = (bf16[128,896]{1,0:T(8,128)(2,1)S(1)}, bf16[128,896]{1,0:T(8,128)(2,1)S(1)}, u32[]{:S(2)}, u32[]{:S(2)}) collective-permute-start(bf16[128,896]{1,0:T(8,128)(2,1)S(1)} %add_convert_fusion.26.refs_11_), channel_id=1, source_target_pairs={{12,8},{8,4},{4,0},{13,9},{9,5},{2,6},{6,10},{3,7},{7,11},{11,15},... | collective-permute-start | bytes 688136 | tf_op jit(solution)/shard_map/ppermute | solution.py:407
  63.9 12.4 %collective-permute-start.9 = (bf16[128,1152]{1,0:T(8,128)(2,1)S(1)}, bf16[128,1152]{1,0:T(8,128)(2,1)S(1)}, u32[]{:S(2)}, u32[]{:S(2)}) collective-permute-start(bf16[128,1152]{1,0:T(8,128)(2,1)S(1)} %add_convert_fusion.12.refs_10_), channel_id=1, source_target_pairs={{12,8},{8,4},{4,0},{13,9},{9,5},{2,6},{6,10},{3,7},{7,11},{11,15},... | collective-permute-start | bytes 884744 | tf_op jit(solution)/shard_map/ppermute | solution.py:407
  71.1 15.1 %collective-permute-start.17 = (bf16[128,896]{1,0:T(8,128)(2,1)S(1)}, bf16[128,896]{1,0:T(8,128)(2,1)S(1)}, u32[]{:S(2)}, u32[]{:S(2)}) collective-permute-start(bf16[128,896]{1,0:T(8,128)(2,1)S(1)} %add_convert_fusion.25.refs_8_), channel_id=1, source_target_pairs={{12,8},{8,4},{4,0},{13,9},{9,5},{2,6},{6,10},{3,7},{7,11},{11,15},... | collective-permute-start | bytes 688136 | tf_op jit(solution)/shard_map/ppermute | solution.py:407
  77.5 11.1 %collective-permute-start.10 = (bf16[128,1152]{1,0:T(8,128)(2,1)S(1)}, bf16[128,1152]{1,0:T(8,128)(2,1)S(1)}, u32[]{:S(2)}, u32[]{:S(2)}) collective-permute-start(bf16[128,1152]{1,0:T(8,128)(2,1)S(1)} %add_convert_fusion.11.refs_7_), channel_id=1, source_target_pairs={{12,8},{8,4},{4,0},{13,9},{9,5},{2,6},{6,10},{3,7},{7,11},{11,15},... | collective-permute-start | bytes 884744 | tf_op jit(solution)/shard_map/ppermute | solution.py:407
  84.7 7.3 %collective-permute-start.14 = (bf16[256,128]{1,0:T(8,128)(2,1)S(1)}, bf16[256,128]{1,0:T(8,128)(2,1)S(1)}, u32[]{:S(2)}, u32[]{:S(2)}) collective-permute-start(bf16[256,128]{1,0:T(8,128)(2,1)S(1)} %shard_map.78.refs_1_.refs_0_), channel_id=1, source_target_pairs={{0,4},{4,0},{8,12},{12,8},{1,5},{5,1},{9,13},{13,9},{2,6},{6,2},{1... | collective-permute-start | bytes 196616 | tf_op jit(solution)/shard_map/ppermute | solution.py:511
  86.2 16.7 %collective-permute-start.15 = (bf16[256,128]{1,0:T(8,128)(2,1)S(1)}, bf16[256,128]{1,0:T(8,128)(2,1)S(1)}, u32[]{:S(2)}, u32[]{:S(2)}) collective-permute-start(bf16[256,128]{1,0:T(8,128)(2,1)S(1)} %shard_map.78.refs_1_.refs_0_), channel_id=1, source_target_pairs={{0,8},{4,12},{8,0},{12,4},{1,9},{5,13},{9,1},{13,5},{2,10},{6,14},... | collective-permute-start | bytes 196616 | tf_op jit(solution)/shard_map/ppermute | solution.py:511
  86.2 16.7 %collective-permute-start.16 = (bf16[256,128]{1,0:T(8,128)(2,1)S(1)}, bf16[256,128]{1,0:T(8,128)(2,1)S(1)}, u32[]{:S(2)}, u32[]{:S(2)}) collective-permute-start(bf16[256,128]{1,0:T(8,128)(2,1)S(1)} %shard_map.78.refs_1_.refs_0_), channel_id=1, source_target_pairs={{0,12},{4,8},{8,4},{12,0},{1,13},{5,9},{9,5},{13,1},{2,14},{6,10},... | collective-permute-start | bytes 196616 | tf_op jit(solution)/shard_map/ppermute | solution.py:511
  88.5 22.5 %collective-permute-start.18 = (bf16[128,896]{1,0:T(8,128)(2,1)S(1)}, bf16[128,896]{1,0:T(8,128)(2,1)S(1)}, u32[]{:S(2)}, u32[]{:S(2)}) collective-permute-start(bf16[128,896]{1,0:T(8,128)(2,1)S(1)} %add_convert_fusion.24.refs_6_), channel_id=1, source_target_pairs={{12,8},{8,4},{4,0},{13,9},{9,5},{2,6},{6,10},{3,7},{7,11},{11,15},... | collective-permute-start | bytes 688136 | tf_op jit(solution)/shard_map/ppermute | solution.py:407
  92.0 22.8 %collective-permute-start.13 = (bf16[128,1152]{1,0:T(8,128)(2,1)S(1)}, bf16[128,1152]{1,0:T(8,128)(2,1)S(1)}, u32[]{:S(2)}, u32[]{:S(2)}) collective-permute-start(bf16[128,1152]{1,0:T(8,128)(2,1)S(1)} %add_convert_fusion.10.refs_5_), channel_id=1, source_target_pairs={{12,8},{8,4},{4,0},{13,9},{9,5},{2,6},{6,10},{3,7},{7,11},{11,15},... | collective-permute-start | bytes 884744 | tf_op jit(solution)/shard_map/ppermute | solution.py:407
  112.9 9.0 %collective-permute-start.22 = (bf16[128,896]{1,0:T(8,128)(2,1)}, bf16[128,896]{1,0:T(8,128)(2,1)S(1)}, u32[]{:S(2)}, u32[]{:S(2)}) collective-permute-start(bf16[128,896]{1,0:T(8,128)(2,1)} %add_convert_fusion.23.refs_2_), channel_id=1, source_target_pairs={{12,8},{8,4},{4,0},{13,9},{9,5},{2,6},{6,10},{3,7},{7,11},{11,15},... | collective-permute-start | bytes 688136 | tf_op jit(solution)/shard_map/ppermute | solution.py:407
  116.7 9.5 %collective-permute-start.20 = (bf16[128,1152]{1,0:T(8,128)(2,1)S(1)}, bf16[128,1152]{1,0:T(8,128)(2,1)S(1)}, u32[]{:S(2)}, u32[]{:S(2)}) collective-permute-start(bf16[128,1152]{1,0:T(8,128)(2,1)S(1)} %add_convert_fusion.9.refs_1_), channel_id=1, source_target_pairs={{12,8},{8,4},{4,0},{13,9},{9,5},{2,6},{6,10},{3,7},{7,11},{11,15},... | collective-permute-start | bytes 884744 | tf_op jit(solution)/shard_map/ppermute | solution.py:407
  123.8 9.3 %collective-permute-start.23 = (bf16[128,896]{1,0:T(8,128)(2,1)S(1)}, bf16[128,896]{1,0:T(8,128)(2,1)S(1)}, u32[]{:S(2)}, u32[]{:S(2)}) collective-permute-start(bf16[128,896]{1,0:T(8,128)(2,1)S(1)} %get-tuple-element.18), channel_id=1, source_target_pairs={{8,4},{4,0},{9,5},{6,10},{7,11},{11,15},{24,20},{20,16},{25,21},{2... | collective-permute-start | bytes 688136 | tf_op jit(solution)/shard_map/ppermute | solution.py:407
  128.2 8.0 %copy-start.21 = (bf16[128,1152]{1,0:T(8,128)(2,1)S(1)}, bf16[128,1152]{1,0:T(8,128)(2,1)}, u32[]{:S(2)}) copy-start(bf16[128,1152]{1,0:T(8,128)(2,1)} %copy-done.20) | copy-start | bytes 884740
  128.2 8.0 %collective-permute-start.21 = (bf16[128,1152]{1,0:T(8,128)(2,1)S(1)}, bf16[128,1152]{1,0:T(8,128)(2,1)}, u32[]{:S(2)}, u32[]{:S(2)}) collective-permute-start(bf16[128,1152]{1,0:T(8,128)(2,1)S(1)} %get-tuple-element.14), channel_id=1, source_target_pairs={{8,4},{4,0},{9,5},{6,10},{7,11},{11,15},{24,20},{20,16},{25,21},{2... | collective-permute-start | bytes 884744 | tf_op jit(solution)/shard_map/ppermute | solution.py:407
  139.1 31.0 %collective-permute-start.26 = (bf16[256,2048]{1,0:T(8,128)(2,1)S(1)}, bf16[256,2048]{1,0:T(8,128)(2,1)S(1)}, u32[]{:S(2)}, u32[]{:S(2)}) collective-permute-start(bf16[256,2048]{1,0:T(8,128)(2,1)S(1)} %maximum_maximum_fusion.2.refs_7_), channel_id=1, source_target_pairs={{0,1},{5,4},{10,11},{15,14},{2,3},{7,6},{8,9},{13,12},{16,17},{21,... | collective-permute-start | bytes 3145736 | tf_op jit(solution)/shard_map/ppermute | solution.py:407
  140.4 9.3 %collective-permute-start.27 = (bf16[128,2048]{1,0:T(8,128)(2,1)S(1)}, bf16[128,2048]{1,0:T(8,128)(2,1)S(1)}, u32[]{:S(2)}, u32[]{:S(2)}) collective-permute-start(bf16[128,2048]{1,0:T(8,128)(2,1)S(1)} %get-tuple-element.10), channel_id=1, source_target_pairs={{0,1},{1,0},{2,3},{3,2},{4,5},{5,4},{6,7},{7,6},{8,9},{9,8},{10,11... | collective-permute-start | bytes 1572872 | tf_op jit(solution)/shard_map/ppermute | solution.py:395
  141.7 11.1 %copy-start.17 = (bf16[128,1152]{1,0:T(8,128)(2,1)S(1)}, bf16[128,1152]{1,0:T(8,128)(2,1)}, u32[]{:S(2)}) copy-start(bf16[128,1152]{1,0:T(8,128)(2,1)} %get-tuple-element.26) | copy-start | bytes 884740
  141.7 11.1 %copy-start.24 = (bf16[128,896]{1,0:T(8,128)(2,1)S(1)}, bf16[128,896]{1,0:T(8,128)(2,1)}, u32[]{:S(2)}) copy-start(bf16[128,896]{1,0:T(8,128)(2,1)} %get-tuple-element.31) | copy-start | bytes 688132
  141.7 11.1 %copy-start.26 = (bf16[128,896]{1,0:T(8,128)(2,1)S(1)}, bf16[128,896]{1,0:T(8,128)(2,1)}, u32[]{:S(2)}) copy-start(bf16[128,896]{1,0:T(8,128)(2,1)} %get-tuple-element.32) | copy-start | bytes 688132
  141.7 17.2 %collective-permute-start.28 = (bf16[128,2048]{1,0:T(8,128)(2,1)}, bf16[128,2048]{1,0:T(8,128)(2,1)S(1)}, u32[]{:S(2)}, u32[]{:S(2)}) collective-permute-start(bf16[128,2048]{1,0:T(8,128)(2,1)} %get-tuple-element.11), channel_id=1, source_target_pairs={{0,2},{1,3},{2,0},{3,1},{4,6},{5,7},{6,4},{7,5},{8,10},{9,11},{10,... | collective-permute-start | bytes 1572872 | tf_op jit(solution)/shard_map/ppermute | solution.py:395
  146.4 23.7 %collective-permute-start.29 = (bf16[128,2048]{1,0:T(8,128)(2,1)}, bf16[128,2048]{1,0:T(8,128)(2,1)S(1)}, u32[]{:S(2)}, u32[]{:S(2)}) collective-permute-start(bf16[128,2048]{1,0:T(8,128)(2,1)} %get-tuple-element.12), channel_id=1, source_target_pairs={{0,3},{1,2},{2,1},{3,0},{4,7},{5,6},{6,5},{7,4},{8,11},{9,10},{10,... | collective-permute-start | bytes 1572872 | tf_op jit(solution)/shard_map/ppermute | solution.py:395
  146.5 4.6 %collective-permute-start.30 = (bf16[128,896]{1,0:T(8,128)(2,1)}, bf16[128,896]{1,0:T(8,128)(2,1)S(1)}, u32[]{:S(2)}, u32[]{:S(2)}) collective-permute-start(bf16[128,896]{1,0:T(8,128)(2,1)} %get-tuple-element.30), channel_id=1, source_target_pairs={{4,0},{11,15},{20,16},{27,31}} | collective-permute-start | bytes 688136 | tf_op jit(solution)/shard_map/ppermute | solution.py:407
  147.1 23.0 %copy-start.7 = (bf16[128,2048]{1,0:T(8,128)(2,1)S(1)}, bf16[128,2048]{1,0:T(8,128)(2,1)}, u32[]{:S(2)}) copy-start(bf16[128,2048]{1,0:T(8,128)(2,1)} %copy-done.6) | copy-start | bytes 1572868
  147.1 23.0 %copy-start.13 = (s32[16]{0:T(128)S(1)}, s32[16]{0:T(128)}, u32[]{:S(2)}) copy-start(s32[16]{0:T(128)} %refs_3_.3) | copy-start | bytes 196
  149.7 24.8 %collective-permute-start.25 = (bf16[128,1152]{1,0:T(8,128)(2,1)S(1)}, bf16[128,1152]{1,0:T(8,128)(2,1)}, u32[]{:S(2)}, u32[]{:S(2)}) collective-permute-start(bf16[128,1152]{1,0:T(8,128)(2,1)S(1)} %copy-done.33), channel_id=1, source_target_pairs={{4,0},{11,15},{20,16},{27,31}} | collective-permute-start | bytes 884744 | tf_op jit(solution)/shard_map/ppermute | solution.py:407
  151.1 25.5 %collective-permute-start.24 = (bf16[256,2048]{1,0:T(8,128)(2,1)}, bf16[256,2048]{1,0:T(8,128)(2,1)}, u32[]{:S(2)}, u32[]{:S(2)}) collective-permute-start(bf16[256,2048]{1,0:T(8,128)(2,1)} %maximum_maximum_fusion.1), channel_id=1, source_target_pairs={{0,2},{5,7},{10,8},{15,13},{16,18},{21,23},{26,24},{31,29}} | collective-permute-start | bytes 3145736 | tf_op jit(solution)/shard_map/ppermute | solution.py:407
  158.9 20.8 %collective-permute-start.19 = (bf16[256,2048]{1,0:T(8,128)(2,1)}, bf16[256,2048]{1,0:T(8,128)(2,1)}, u32[]{:S(2)}, u32[]{:S(2)}) collective-permute-start(bf16[256,2048]{1,0:T(8,128)(2,1)} %maximum_maximum_fusion), channel_id=1, source_target_pairs={{0,2},{5,7},{10,8},{15,13},{16,18},{21,23},{26,24},{31,29}} | collective-permute-start | bytes 3145736 | tf_op jit(solution)/shard_map/ppermute | solution.py:407
  175.8 6.8 %collective-permute-start.31 = (bf16[128,2048]{1,0:T(8,128)(2,1)S(1)}, bf16[128,2048]{1,0:T(8,128)(2,1)S(1)}, u32[]{:S(2)}, u32[]{:S(2)}) collective-permute-start(bf16[128,2048]{1,0:T(8,128)(2,1)S(1)} %pad_maximum_fusion), channel_id=1, source_target_pairs={{0,2},{5,7},{10,8},{15,13},{16,18},{21,23},{26,24},{31,29}} | collective-permute-start | bytes 1572872 | tf_op jit(solution)/shard_map/ppermute | solution.py:407
  178.2 23.5 %copy-start.1 = (f32[256,2048]{1,0:T(8,128)S(1)}, f32[256,2048]{1,0:T(8,128)}, u32[]{:S(2)}) copy-start(f32[256,2048]{1,0:T(8,128)} %copy-done) | copy-start | bytes 6291460
  178.2 9.0 %collective-permute-start.33 = (bf16[256,2048]{1,0:T(8,128)(2,1)S(1)}, bf16[256,2048]{1,0:T(8,128)(2,1)S(1)}, u32[]{:S(2)}, u32[]{:S(2)}) collective-permute-start(bf16[256,2048]{1,0:T(8,128)(2,1)S(1)} %broadcast_select_fusion.refs_8_), channel_id=1, source_target_pairs={{0,1},{5,4},{10,11},{15,14},{2,3},{7,6},{8,9},{13,12},{16,17},{21,... | collective-permute-start | bytes 3145736 | tf_op jit(solution)/shard_map/ppermute | solution.py:407
  181.2 17.1 %collective-permute-start.32 = (bf16[256,2048]{1,0:T(8,128)(2,1)S(1)}, bf16[256,2048]{1,0:T(8,128)(2,1)S(1)}, u32[]{:S(2)}, u32[]{:S(2)}) collective-permute-start(bf16[256,2048]{1,0:T(8,128)(2,1)S(1)} %broadcast_select_fusion.1.refs_7_), channel_id=1, source_target_pairs={{0,1},{5,4},{10,11},{15,14},{2,3},{7,6},{8,9},{13,12},{16,17},{21,... | collective-permute-start | bytes 3145736 | tf_op jit(solution)/shard_map/ppermute | solution.py:407
  182.7 19.0 %collective-permute-start.34 = (bf16[128,2048]{1,0:T(8,128)(2,1)S(1)}, bf16[128,2048]{1,0:T(8,128)(2,1)S(1)}, u32[]{:S(2)}, u32[]{:S(2)}) collective-permute-start(bf16[128,2048]{1,0:T(8,128)(2,1)S(1)} %broadcast_select_fusion.2.refs_9_), channel_id=1, source_target_pairs={{0,1},{5,4},{10,11},{15,14},{2,3},{7,6},{8,9},{13,12},{16,17},{21,... | collective-permute-start | bytes 1572872 | tf_op jit(solution)/shard_map/ppermute | solution.py:407
  (21 other events, 60.5 us)

commit v3 on v2

--- a/solution.py
+++ b/solution.py
@@ -10,6 +10,7 @@
 SMALL_VMEM = 32 * 1024 * 1024
 STREAMS = 2
 SPAN = 128
+SLOTS = 16
 BF16 = jnp.bfloat16
 F32 = jnp.float32
 LIGHT = pl.CostEstimate(flops=0, bytes_accessed=0, transcendentals=0)
@@ -114,7 +115,7 @@
     )(value, *deps)
 
 
-def project_kernel(first, blocks, tokens, span, ndeps, *refs):
+def project_kernel(first, blocks, block_rows, tokens, span, *refs):
     meta_ref, len_refs = refs[0], refs[1 : 1 + blocks]
     x_refs, w_ref = refs[1 + blocks : 1 + 2 * blocks], refs[1 + 2 * blocks]
     out_ref, packed = refs[-2], refs[-1]
@@ -123,7 +124,7 @@
     @pl.when(pl.program_id(0) == 0)
     def _():
         s, _, _, u = where_am_i(meta_ref)
-        width = x_refs[0].shape[0]
+        width = block_rows
         lead = (s % 2) == 0
         sums = [total_of(r) for r in len_refs]
         starts = [jnp.where(lead, 0, sums[1]), jnp.where(lead, sums[0], 0)]
@@ -153,11 +154,11 @@
 def project(meta, lens, xs, w, first, rows, span, deps=(), tile=512):
     depth, cols = w.shape
     blocks = len(xs)
-    block_rows = xs[0].shape[0]
-    tokens = block_rows // lens[0].shape[0]
+    block_rows = lens[0].shape[0] * SLOTS
+    tokens = SLOTS
     smem = pl.BlockSpec(memory_space=pltpu.SMEM)
     return pl.pallas_call(
-        functools.partial(project_kernel, first, blocks, tokens, span, len(deps)),
+        functools.partial(project_kernel, first, blocks, block_rows, tokens, span),
         grid=(cols // tile,),
         in_specs=[smem] * (1 + blocks)
         + [pl.BlockSpec((block_rows, depth), lambda j: (0, 0))] * blocks
@@ -228,7 +229,7 @@
 
 
 def low_rank(meta, req, slot, xs, flips, down_t, before, held, rank, tokens, capacity, deps):
-    requests = xs[0].shape[0] // tokens
+    requests = 2 * capacity
     size = capacity * tokens * len(flips)
     depth = xs[0].shape[1]
     smem = pl.BlockSpec(memory_space=pltpu.SMEM)
@@ -298,6 +299,69 @@
         compiler_params=pltpu.CompilerParams(vmem_limit_bytes=VMEM_LIMIT),
         cost_estimate=LIGHT,
     )(meta, req, slot, *lows, up_2d, *deps)
+
+
+def extend_kernel(len_ref, x_ref, out_ref):
+    rows, depth = x_ref.shape
+    extra = out_ref.shape[0] - rows
+    out_ref[:rows, :] = x_ref[...]
+    lane = lax.broadcasted_iota(jnp.int32, (extra, depth), 1)
+    below = jnp.zeros((extra, depth), F32)
+    for q in range(len_ref.shape[0]):
+        below = jnp.where(lane == q, len_ref[q].astype(F32), below)
+    out_ref[rows:, :] = below.astype(BF16)
+
+
+def extend(lengths, x, extra):
+    vmem = pl.BlockSpec(memory_space=pltpu.VMEM)
+    return pl.pallas_call(
+        extend_kernel,
+        in_specs=[pl.BlockSpec(memory_space=pltpu.SMEM), vmem],
+        out_specs=vmem,
+        out_shape=jax.ShapeDtypeStruct((x.shape[0] + extra, x.shape[1]), BF16),
+        compiler_params=pltpu.CompilerParams(vmem_limit_bytes=SMALL_VMEM),
+        cost_estimate=LIGHT,
+    )(lengths, x)
+
+
+def merge_kernel(count, streams, has_back, u_ref, *refs):
+    out_ref = refs[-1]
+    span = refs[0].shape[0]
+    for i in range(count):
+        at = 0
+        for j in range(streams):
+            piece = refs[i * streams + j]
+            value = piece[...]
+            width = piece.shape[1]
+            if has_back:
+                back = refs[count * streams + i][:, at : at + width]
+                value = (value.astype(F32) + back.astype(F32)).astype(BF16)
+            out_ref[i * span : (i + 1) * span, at : at + width] = value
+            at += width
+
+
+def merge(u, pieces, backs, steps_of):
+    count, streams = len(steps_of), len(pieces) // len(steps_of)
+    span = pieces[0].shape[0]
+    cols = sum(p.shape[1] for p in pieces[:streams])
+
+    def spec_of(low, high, k):
+        return pl.BlockSpec((span, cols), lambda i, r: (jnp.clip(k - r[0], low, high) - low, 0))
+
+    specs = [pl.BlockSpec(p.shape, lambda i, r: (0, 0)) for p in pieces]
+    specs += [spec_of(low, high, k) for k, (_, low, high) in zip(steps_of, backs)]
+    return pl.pallas_call(
+        functools.partial(merge_kernel, count, streams, bool(backs)),
+        grid_spec=pltpu.PrefetchScalarGridSpec(
+            num_scalar_prefetch=1,
+            grid=(1,),
+            in_specs=specs,
+            out_specs=pl.BlockSpec((count * span, cols), lambda i, r: (0, 0)),
+        ),
+        out_shape=jax.ShapeDtypeStruct((count * span, cols), BF16),
+        compiler_params=pltpu.CompilerParams(vmem_limit_bytes=SMALL_VMEM),
+        cost_estimate=LIGHT,
+    )(u, *pieces, *[b[0] for b in backs])
 
 
 def finish_kernel(n, sizes, first, span, held, requests, tokens, capacity, with_delta, with_acc, *refs):
@@ -364,7 +428,7 @@
         run(got_refs)
 
 
-def finish(meta, req, slot, lens, values, gots, first, deltas, acc, out_dtype, span, held, tokens, capacity, tile=512):
+def finish(meta, req, slot, lens, values, gots, first, deltas, acc, out_dtype, span, held, tokens, capacity, deps=(), tile=512):
     requests = lens[0].shape[0]
     rows = requests * tokens
     cols = values[0].shape[1]
@@ -379,7 +443,9 @@
             len(sizes), sizes, first, span, held, requests, tokens, capacity, bool(deltas), acc is not None,
         ),
         grid=(cols // tile,),
-        in_specs=[smem] * 7 + [pl.BlockSpec((a.shape[0], tile), lambda j: (0, j)) for a in big],
+        in_specs=[smem] * 7
+        + [pl.BlockSpec((a.shape[0], tile), lambda j: (0, j)) for a in big]
+        + [pl.BlockSpec(memory_space=pl.ANY)] * len(deps),
         out_specs=pl.BlockSpec((rows, tile), lambda j: (0, j)),
         out_shape=jax.ShapeDtypeStruct((rows, cols), out_dtype),
         scratch_shapes=[
@@ -388,7 +454,7 @@
         ],
         compiler_params=pltpu.CompilerParams(vmem_limit_bytes=SMALL_VMEM),
         cost_estimate=LIGHT,
-    )(meta, req, slot, *lens, *big)
+    )(meta, req, slot, *lens, *big, *deps)
 
 
 def on_store(value, flip):
@@ -424,15 +490,15 @@
     meta = jnp.stack([s, t]).astype(jnp.int32)
 
     x_me = x.reshape(rows, depth)
-    x_far = on_store(x_me, 2)
-    len_me = lengths
-    len_sib = on_store(len_me, 1)
-    x_sib = on_store(x_me, 1)
-    lens_far = on_store(jnp.concatenate([len_me, len_sib]), 2)
-    len_far, len_fsib = lens_far[:requests], lens_far[requests:]
-    x_fsib = on_store(x_far, 1)
-    lens = [len_me, len_sib, len_far, len_fsib]
-    xs = [x_me, x_sib, x_far, x_fsib]
+    x_out = extend(lengths, x_me, tokens)
+    x_far = on_store(x_out, 2)
+    x_sib = on_store(x_out, 1)
+
+    def lengths_of(array):
+        return array[rows, :requests].astype(jnp.int32)
+
+    lens = [lengths, lengths_of(x_sib)]
+    xs = [x_me, x_sib]
     down_t = jnp.transpose(down, (0, 2, 1)).reshape(held * rank, depth)
     up_2d = up.reshape(held * rank, cols)
 
@@ -461,36 +527,35 @@
         for j in range(STREAMS):
             if k < early:
                 value = parts[0][k * span : (k + 1) * span, bounds[j][0] : bounds[j][1]]
-            elif k == early:
-                value = parts[1][:, bounds[j][0] : bounds[j][1]]
             else:
-                value = chunk_of(parts[2], k, j)
+                value = chunk_of(parts[1], k, j)
             if carry[j] is not None:
                 came = carry[j]
                 if deps and not j:
                     came = after(came, *deps)
-                value = (value.astype(F32) + came.astype(F32)).astype(BF16)
+                total = value.astype(F32) + came.astype(F32)
+                value = total.astype(BF16)
             final[k, j] = value
             carry[j] = on_mesh(value, pairs) if pairs else None
 
     values, gots = [], []
 
-    def post(lo, hi):
-        columns = []
-        for j in range(STREAMS):
-            column = []
-            for k in range(lo, hi):
-                value = final[k, j]
-                if k < steps + 2:
-                    value = (value.astype(F32) + chunk_of(back, k, j).astype(F32)).astype(BF16)
-                column.append(value)
-            columns.append(jnp.concatenate(column, axis=0))
-        value = jnp.concatenate(columns, axis=1)
-        if (hi - 2) * span > rows:
-            value = jnp.where(is_root, value, on_mesh(value, across))
+    def merged(lo, hi):
+        ks = range(lo, hi)
+        backs = []
+        if hi <= steps + 2:
+            for k in ks:
+                backs.append(next(b for b in back if b[1] <= k - 2 <= b[2]))
+        return merge(u_vec, [final[k, j] for k in ks for j in range(STREAMS)], backs, ks)
+
+    def cross(value):
+        return jnp.where(is_root, value, on_mesh(value, across))
+
+    def hand_on(value):
         values.append(value)
         gots.append(on_mesh(value, beside))
 
+    u_vec = u.astype(jnp.int32).reshape(1)
     parts[0] = project(meta, lens[:2], xs[:2], w, 0, early * span, span)
     chain_step(0)
     low = low_rank(
@@ -500,30 +565,41 @@
     x_far = after(x_far, final[1, 0], final[1, 1], low)
     x_fsib = on_store(x_far, 1)
     xs = [x_me, x_sib, x_far, x_fsib]
-    parts[1] = project(meta, lens, xs, w, early * span, span, span)
+    lens = lens + [lengths_of(x_far), lengths_of(x_fsib)]
+    low = low_rank(meta, req, slot, xs[2:], (2, 3), down_t, low, held, rank, tokens, capacity, ())
+    lows = [low] + [lax.ppermute(low, "tensor", [(i, i ^ f) for i in range(4)]) for f in (1, 2, 3)]
+    parts[1] = project(meta, lens, xs, w, 0, live, 0, (low,))
     chain_step(2)
-    parts[2] = project(meta, lens, xs, w, 0, live, 0, (final[2, 0], final[2, 1]))
-    chain_step(3)
-    back = on_mesh(parts[2], back_pairs)
-    low = low_rank(
-        meta, req, slot, xs[2:], (2, 3), down_t, low, held, rank, tokens, capacity, (final[3, 0], final[3, 1])
+    delta = up_project(
+        meta, req, slot, lows, up_2d, held, rank, tokens, capacity, requests, (final[2, 0], final[2, 1])
     )
-    lows = [low] + [lax.ppermute(low, "tensor", [(i, i ^ f) for i in range(4)]) for f in (1, 2, 3)]
-    chain_step(4, low)
-    delta = up_project(meta, req, slot, lows, up_2d, held, rank, tokens, capacity, requests, (final[4, 0], final[4, 1]))
     deltas = [delta[0]] + [on_store(delta[i], i) for i in (1, 2, 3)]
-    chain_step(5, delta[0])
-    back = after(back, final[5, 0], final[5, 1])
-    post(2, 4)
-    chain_step(6)
-    post(4, 6)
-    chain_step(7)
+    chain_step(3, delta[0])
+    cut = steps // 2
+
+    def send_back(low, high, *deps):
+        rows_of = after(parts[1][low * span : (high + 1) * span], *deps)
+        return on_mesh(rows_of, back_pairs), low, high
+
+    back = [send_back(0, cut - 1, final[3, 0], final[3, 1])]
+    chain_step(4, deltas[1])
+    back.append(send_back(cut, steps - 1, final[4, 0], final[4, 1]))
+    chain_step(5, deltas[2])
+    chain_step(6, deltas[3])
+    one = merged(2, 4)
+    two = merged(4, 6)
+    chain_step(7, two)
+    hand_on(one)
+    two = cross(two)
+    three = merged(6, 8)
+    chain_step(8, two)
+    hand_on(two)
+    hand_on(cross(three))
     partial = finish(
-        meta, req, slot, lens, values[:1], gots[:1], 2 * span, deltas, None, F32, span, held, tokens, capacity
+        meta, req, slot, lens, values[:1], gots[:1], 2 * span, deltas, None, F32, span, held, tokens, capacity,
+        (final[8, 0], final[8, 1]),
     )
-    chain_step(8, partial)
-    post(6, 8)
-    post(8, 9)
+    hand_on(cross(merged(8, 9)))
     out = finish(
         meta, req, slot, lens, values[1:], gots[1:], 4 * span, (), partial, BF16, span, held, tokens, capacity
     )

time: 207 us -> 189 us (0.913)
  the two profiles are of different devices: /device:TPU:21 before, /device:TPU:0 now
where the time goes in v3:
time: 189 us; the launch traced here: 188 us
  starting transfers between devices  53.9 us (29%)
  Pallas kernels  52.9 us (28%)
  waiting for transfers between devices  36.1 us (19%)
  other arithmetic  28.9 us (15%)
  local copies, waits for them, and re-layouts  15 us (8%)
    ppermute x25, starting transfers between devices, on_mesh(): lax.ppermute(value, ('tensor', 'store'), [(a * 4 + b, c * 4 + d) for (a,...  36.7 us
    ppermute x25, waiting for transfers between devices, on_mesh(): lax.ppermute(value, ('tensor', 'store'), [(a * 4 + b, c * 4 + d) for (a,...  28.9 us
    convert_element_type x16, other arithmetic, chain_step(): value = total.astype(BF16)  24.1 us
    pallas_call x2, Pallas kernels, project(): pl.pallas_call(functools.partial(project_kernel, first, blocks, block_row...  21.4 us
    unnamed x60, local copies, waits for them, and re-layouts  10.9 us
    pallas_call x2, Pallas kernels, low_rank(): pl.pallas_call(functools.partial(low_kernel, flips, before is not None, h...  10.5 us
    ppermute x6, starting transfers between devices, on_store(): return lax.ppermute(value, 'store', [(i, i ^ flip) for i in range(4)])  8.61 us
    ppermute x3, starting transfers between devices, square(): lax.ppermute(low, 'tensor', [(i, i ^ f) for i in range(4)])  8.57 us
  transfers between devices with their start and end apart: 34, of which 9 were waited for; matrix products, arithmetic and copies ran while one was open for 18% of the time, Pallas kernels for 26%

profile of v3, /device:TPU:0, one launch (start us, length us, event | category | flops | bytes accessed | tf_op | source)
XLA Modules:
  0.0 187.5 jit_solution(16828758488427074084)
XLA Ops:
  3.0 2.6 %collective-permute-start.1 = (bf16[272,2048]{1,0:T(8,128)(2,1)S(1)}, bf16[272,2048]{1,0:T(8,128)(2,1)S(1)}, u32[]{:S(2)}, u32[]{:S(2)}) collective-permute-start(bf16[272,2048]{1,0:T(8,128)(2,1)S(1)} %shard_map.73), channel_id=1, source_target_pairs={{0,2},{1,3},{2,0},{3,1},{4,6},{5,7},{6,4},{7,5},{8,10},{9,11},{10,... | collective-permute-start | bytes 3342344 | tf_op jit(solution)/shard_map/ppermute | solution.py:461
  7.0 7.1 %shard_map.74.refs_6_ = bf16[256,2048]{1,0:T(8,128)(2,1)S(1)} custom-call(s32[2]{0:T(128)S(1)} %pad_add_fusion.refs_0_.meta_ref, s32[16]{0:T(128)S(1)} %copy-done.22, s32[16]{0:T(128)S(1)} %fusion.2.refs_2_.refs_4_, bf16[256,2048]{1,0:T(8,128)(2,1)} %bitcast.24, bf16[272,2048]{1,0:T(8,128)(2,1)} %collective-permute-done.refs_4_.refs_6_, ...), custom_call_target="tpu_custom_call" | custom-call | tf_op jit(solution)/shard_map/pallas_call | solution.py:160
  15.6 5.3 %shard_map.75.refs_3_.refs_6_ = bf16[256,128]{1,0:T(8,128)(2,1)S(1)} custom-call(s32[2]{0:T(128)S(1)} %pad_add_fusion.refs_0_.meta_ref, s32[64]{0:T(128)S(1)} %copy-done.24, s32[64]{0:T(128)S(1)} %copy-done.25, bf16[256,2048]{1,0:T(8,128)(2,1)S(1)} %bitcast.26, bf16[272,2048]{1,0:T(8,128)(2,1)} %collective-permute-done.refs_4_.refs_6_, ...), custom_call_target="tpu_custom_call" | custom-call | tf_op jit(solution)/shard_map/pallas_call | solution.py:238
  20.9 1.7 add_convert_fusion.15.refs_2_
  22.6 1.8 add_convert_fusion.7.refs_1_
  24.4 6.3 %collective-permute-done.1.refs_0_ = bf16[272,2048]{1,0:T(8,128)(2,1)S(1)} collective-permute-done((bf16[272,2048]{1,0:T(8,128)(2,1)S(1)}, bf16[272,2048]{1,0:T(8,128)(2,1)S(1)}, u32[]{:S(2)}, u32[]{:S(2)}) %collective-permute-start.1) | collective-permute-done | bytes 1114144 | tf_op jit(solution)/shard_map/ppermute | solution.py:461
  37.8 5.3 %shard_map.77.refs_10_.refs_0_ = bf16[256,128]{1,0:T(8,128)(2,1)S(1)} custom-call(s32[2]{0:T(128)S(1)} %pad_add_fusion.refs_0_.meta_ref, s32[64]{0:T(128)S(1)} %copy-done.24, s32[64]{0:T(128)S(1)} %copy-done.25, bf16[272,2048]{1,0:T(8,128)(2,1)S(1)} %copy-done.3, bf16[272,2048]{1,0:T(8,128)(2,1)} %copy-done.26, bf16[1024,2048]{1,0:T(8,128)(2,1)} %bitcast.29, ...), custom_call_target="tpu_custom_call" | custom-call | tf_op jit(solution)/shard_map/pallas_call | solution.py:238
  43.1 2.2 %collective-permute-start.7 = (bf16[256,128]{1,0:T(8,128)(2,1)S(1)}, bf16[256,128]{1,0:T(8,128)(2,1)S(1)}, u32[]{:S(2)}, u32[]{:S(2)}) collective-permute-start(bf16[256,128]{1,0:T(8,128)(2,1)S(1)} %shard_map.77.refs_10_.refs_0_), channel_id=1, source_target_pairs={{0,4},{4,0},{8,12},{12,8},{1,5},{5,1},{9,13},{13,9},{2,6},{6,2},{1... | collective-permute-start | bytes 196616 | tf_op jit(solution)/shard_map/ppermute | solution.py:570
  45.4 6.3 %collective-permute-start.8 = (bf16[256,128]{1,0:T(8,128)(2,1)S(1)}, bf16[256,128]{1,0:T(8,128)(2,1)S(1)}, u32[]{:S(2)}, u32[]{:S(2)}) collective-permute-start(bf16[256,128]{1,0:T(8,128)(2,1)S(1)} %shard_map.77.refs_10_.refs_0_), channel_id=1, source_target_pairs={{0,8},{4,12},{8,0},{12,4},{1,9},{5,13},{9,1},{13,5},{2,10},{6,14},... | collective-permute-start | bytes 196616 | tf_op jit(solution)/shard_map/ppermute | solution.py:570
  52.4 14.3 %shard_map.78 = bf16[768,2048]{1,0:T(8,128)(2,1)} custom-call(s32[2]{0:T(128)S(1)} %pad_add_fusion.refs_0_.meta_ref, s32[16]{0:T(128)S(1)} %copy-done.23, s32[16]{0:T(128)S(1)} %fusion.2.refs_2_.refs_4_, s32[16]{0:T(128)S(1)} %fusion.1.refs_3_.refs_5_, s32[16]{0:T(128)S(1)} %fusion.refs_4_.refs_6_, bf16[256,2048]{1,0:T(8,128)(2,1)S(1)} %bitcast.27, ...), custom_call_target="tpu_custom_call" | custom-call | tf_op jit(solution)/shard_map/pallas_call | solution.py:160
  67.7 1.3 collective-permute-start.13
  70.0 1.5 collective-permute-start.6
  71.6 7.2 %shard_map.79 = (bf16[128,2048]{1,0:T(8,128)(2,1)S(1)}, bf16[128,2048]{1,0:T(8,128)(2,1)S(1)}, bf16[128,2048]{1,0:T(8,128)(2,1)}, bf16[128,2048]{1,0:T(8,128)(2,1)}) custom-call(s32[2]{0:T(128)S(1)} %pad_add_fusion.refs_0_.meta_ref, s32[64]{0:T(128)S(1)} %copy-done.24, s32[64]{0:T(128)S(1)} %copy-done.25, bf16[256,128]{1,0:T(8,128)(2,1)S(1)} %shard_map.77.refs_10_.refs_0_, ...), custom_call_target="tpu_custom_call" | custom-call | tf_op jit(solution)/shard_map/pallas_call | solution.py:289
  80.0 1.3 collective-permute-start.14
  83.2 1.3 collective-permute-start.11
  84.5 4.0 %fusion.3 = (bf16[384,2048]{1,0:T(8,128)(2,1)}, bf16[384,2048]{1,0:T(8,128)(2,1)}) fusion(bf16[768,2048]{1,0:T(8,128)(2,1)} %shard_map.78), kind=kLoop, calls=%fused_computation.26 | loop fusion | bytes 6291456 | tf_op jit(solution)/shard_map/slice | solution.py:581
  89.3 1.8 add_convert_fusion.12.refs_2_.refs_1_
  91.1 2.7 %collective-permute-done.11.refs_0_ = bf16[128,1152]{1,0:T(8,128)(2,1)} collective-permute-done((bf16[128,1152]{1,0:T(8,128)(2,1)S(1)}, bf16[128,1152]{1,0:T(8,128)(2,1)}, u32[]{:S(2)}, u32[]{:S(2)}) %collective-permute-start.11) | collective-permute-done | bytes 294944 | tf_op jit(solution)/shard_map/ppermute | solution.py:473
  94.6 1.8 add_convert_fusion.4.refs_1_.refs_0_
  97.2 3.6 %collective-permute-start.16 = (bf16[128,2048]{1,0:T(8,128)(2,1)}, bf16[128,2048]{1,0:T(8,128)(2,1)}, u32[]{:S(2)}, u32[]{:S(2)}) collective-permute-start(bf16[128,2048]{1,0:T(8,128)(2,1)} %get-tuple-element.11), channel_id=1, source_target_pairs={{0,2},{1,3},{2,0},{3,1},{4,6},{5,7},{6,4},{7,5},{8,10},{9,11},{10,... | collective-permute-start | bytes 1572872 | tf_op jit(solution)/shard_map/ppermute | solution.py:461
  100.8 1.3 collective-permute-start.17
  102.1 1.3 collective-permute-start.15
  103.4 6.2 %collective-permute-done.17 = bf16[128,896]{1,0:T(8,128)(2,1)} collective-permute-done((bf16[128,896]{1,0:T(8,128)(2,1)}, bf16[128,896]{1,0:T(8,128)(2,1)}, u32[]{:S(2)}, u32[]{:S(2)}) %collective-permute-start.17) | collective-permute-done | bytes 229408 | tf_op jit(solution)/shard_map/ppermute | solution.py:473
  109.6 2.0 %collective-permute-start.22 = (bf16[128,2048]{1,0:T(8,128)(2,1)}, bf16[128,2048]{1,0:T(8,128)(2,1)}, u32[]{:S(2)}, u32[]{:S(2)}) collective-permute-start(bf16[128,2048]{1,0:T(8,128)(2,1)} %get-tuple-element.12), channel_id=1, source_target_pairs={{0,3},{1,2},{2,1},{3,0},{4,7},{5,6},{6,5},{7,4},{8,11},{9,10},{10,... | collective-permute-start | bytes 1572872 | tf_op jit(solution)/shard_map/ppermute | solution.py:461
  111.6 1.8 add_convert_fusion.11.refs_3_
  113.4 1.3 collective-permute-start.23
  114.7 1.8 add_convert_fusion.3.refs_2_
  117.8 6.4 %collective-permute-done.23 = bf16[128,896]{1,0:T(8,128)(2,1)} collective-permute-done((bf16[128,896]{1,0:T(8,128)(2,1)}, bf16[128,896]{1,0:T(8,128)(2,1)}, u32[]{:S(2)}, u32[]{:S(2)}) %collective-permute-start.23) | collective-permute-done | bytes 229408 | tf_op jit(solution)/shard_map/ppermute | solution.py:473
  124.2 1.8 add_convert_fusion.10.refs_1_
  127.3 1.4 collective-permute-done.21.refs_0_
  130.6 2.3 %shard_map.85.refs_1_ = bf16[256,2048]{1,0:T(8,128)(2,1)} custom-call(s32[1]{0:T(128)} %bitcast.9.u_ref, bf16[128,1152]{1,0:T(8,128)(2,1)S(1)} %copy-done.9, bf16[128,896]{1,0:T(8,128)(2,1)S(1)} %copy-done.16, bf16[128,1152]{1,0:T(8,128)(2,1)} %add_convert_fusion.3.refs_2_, bf16[128,896]{1,0:T(8,128)(2,1)} %add_convert_fusion.11.refs_3_, ...), custom_call_target="tpu_custom_call" | custom-call | tf_op jit(solution)/shard_map/pallas_call | solution.py:353
  132.8 6.0 %collective-permute-start.20 = (bf16[256,2048]{1,0:T(8,128)(2,1)}, bf16[256,2048]{1,0:T(8,128)(2,1)}, u32[]{:S(2)}, u32[]{:S(2)}) collective-permute-start(bf16[256,2048]{1,0:T(8,128)(2,1)} %shard_map.85.refs_1_), channel_id=1, source_target_pairs={{0,2},{5,7},{10,8},{15,13},{16,18},{21,23},{26,24},{31,29}} | collective-permute-start | bytes 3145736 | tf_op jit(solution)/shard_map/ppermute | solution.py:473
  138.8 1.8 add_convert_fusion.2.refs_0_
  142.0 1.8 add_convert_fusion.9.refs_3_
  145.0 4.5 %collective-permute-done.24.refs_0_ = bf16[128,1152]{1,0:T(8,128)(2,1)} collective-permute-done((bf16[128,1152]{1,0:T(8,128)(2,1)}, bf16[128,1152]{1,0:T(8,128)(2,1)}, u32[]{:S(2)}, u32[]{:S(2)}) %collective-permute-start.24) | collective-permute-done | bytes 294944 | tf_op jit(solution)/shard_map/ppermute | solution.py:473
  150.7 2.5 %shard_map.88 = bf16[256,2048]{1,0:T(8,128)(2,1)} custom-call(s32[1]{0:T(128)} %bitcast.9.u_ref, bf16[128,1152]{1,0:T(8,128)(2,1)} %add_convert_fusion.2.refs_0_, bf16[128,896]{1,0:T(8,128)(2,1)} %add_convert_fusion.10.refs_1_, bf16[128,1152]{1,0:T(8,128)(2,1)S(1)} %add_convert_fusion.1.refs_2_, bf16[128,896]{1,0:T(8,128)(2,1)} %add_convert_fusion.9.refs_3_, ...), custom_call_target="tpu_custom_call" | custom-call | tf_op jit(solution)/shard_map/pallas_call | solution.py:353
  153.2 2.3 %collective-permute-start.26 = (bf16[256,2048]{1,0:T(8,128)(2,1)}, bf16[256,2048]{1,0:T(8,128)(2,1)}, u32[]{:S(2)}, u32[]{:S(2)}) collective-permute-start(bf16[256,2048]{1,0:T(8,128)(2,1)} %shard_map.88), channel_id=1, source_target_pairs={{0,2},{5,7},{10,8},{15,13},{16,18},{21,23},{26,24},{31,29}} | collective-permute-start | bytes 3145736 | tf_op jit(solution)/shard_map/ppermute | solution.py:473
  156.9 2.3 %collective-permute-start.33 = (bf16[256,2048]{1,0:T(8,128)(2,1)S(1)}, bf16[256,2048]{1,0:T(8,128)(2,1)}, u32[]{:S(2)}, u32[]{:S(2)}) collective-permute-start(bf16[256,2048]{1,0:T(8,128)(2,1)S(1)} %shard_map.91.refs_7_), channel_id=1, source_target_pairs={{0,1},{5,4},{10,11},{15,14},{2,3},{7,6},{8,9},{13,12},{16,17},{21,... | collective-permute-start | bytes 3145736 | tf_op jit(solution)/shard_map/ppermute | solution.py:473
  160.5 1.3 broadcast_select_fusion.1.refs_1_.refs_7_
  161.8 2.3 %collective-permute-start.30 = (bf16[256,2048]{1,0:T(8,128)(2,1)S(1)}, bf16[256,2048]{1,0:T(8,128)(2,1)}, u32[]{:S(2)}, u32[]{:S(2)}) collective-permute-start(bf16[256,2048]{1,0:T(8,128)(2,1)S(1)} %broadcast_select_fusion.1.refs_1_.refs_7_), channel_id=1, source_target_pairs={{0,1},{5,4},{10,11},{15,14},{2,3},{7,6},{8,9},{13,12},{16,17},{21,... | collective-permute-start | bytes 3145736 | tf_op jit(solution)/shard_map/ppermute | solution.py:473
  164.1 3.7 %collective-permute-done.27.refs_0_ = bf16[128,1152]{1,0:T(8,128)(2,1)S(1)} collective-permute-done((bf16[128,1152]{1,0:T(8,128)(2,1)S(1)}, bf16[128,1152]{1,0:T(8,128)(2,1)S(1)}, u32[]{:S(2)}, u32[]{:S(2)}) %collective-permute-start.27) | collective-permute-done | bytes 294944 | tf_op jit(solution)/shard_map/ppermute | solution.py:473
  169.8 1.3 collective-permute-start.29
  171.1 1.3 broadcast_select_fusion.refs_8_
  172.5 1.4 collective-permute-start.31
  173.8 3.9 %collective-permute-done.29 = bf16[128,2048]{1,0:T(8,128)(2,1)S(1)} collective-permute-done((bf16[128,2048]{1,0:T(8,128)(2,1)S(1)}, bf16[128,2048]{1,0:T(8,128)(2,1)S(1)}, u32[]{:S(2)}, u32[]{:S(2)}) %collective-permute-start.29) | collective-permute-done | bytes 524320 | tf_op jit(solution)/shard_map/ppermute | solution.py:473
  177.8 1.5 collective-permute-start.32
  179.3 3.8 %shard_map.92.refs_13_ = f32[256,2048]{1,0:T(8,128)S(1)} custom-call(s32[2]{0:T(128)S(1)} %pad_add_fusion.refs_0_.meta_ref, s32[64]{0:T(128)S(1)} %copy-done.24, s32[64]{0:T(128)S(1)} %copy-done.25, s32[16]{0:T(128)S(1)} %copy-done.23, s32[16]{0:T(128)S(1)} %fusion.2.refs_2_.refs_4_, s32[16]{0:T(128)S(1)} %fusion.1.refs_3_.refs_5_, ...), custom_call_target="tpu_custom_call" | custom-call | tf_op jit(solution)/shard_map/pallas_call | solution.py:440
  183.2 4.4 %shard_map.93 = bf16[256,2048]{1,0:T(8,128)(2,1)} custom-call(s32[2]{0:T(128)S(1)} %pad_add_fusion.refs_0_.meta_ref, s32[64]{0:T(128)S(1)} %copy-done.24, s32[64]{0:T(128)S(1)} %copy-done.25, s32[16]{0:T(128)S(1)} %copy-done.23, s32[16]{0:T(128)S(1)} %fusion.2.refs_2_.refs_4_, s32[16]{0:T(128)S(1)} %fusion.1.refs_3_.refs_5_, s32[16]{0:T(128)S(1)} %fusion.refs_4_.refs_6_, ...), custom_call_target="tpu_custom_call" | custom-call | tf_op jit(solution)/shard_map/pallas_call | solution.py:440
  (127 shorter events, 34.0 us)
Async XLA Ops:
  2.5 3.2 %collective-permute-start = (bf16[272,2048]{1,0:T(8,128)(2,1)S(1)}, bf16[272,2048]{1,0:T(8,128)(2,1)}, u32[]{:S(2)}, u32[]{:S(2)}) collective-permute-start(bf16[272,2048]{1,0:T(8,128)(2,1)S(1)} %shard_map.73), channel_id=1, source_target_pairs={{0,1},{1,0},{2,3},{3,2},{4,5},{5,4},{6,7},{7,6},{8,9},{9,8},{10,11... | collective-permute-start | bytes 3342344 | tf_op jit(solution)/shard_map/ppermute | solution.py:461
  3.0 27.7 %collective-permute-start.1 = (bf16[272,2048]{1,0:T(8,128)(2,1)S(1)}, bf16[272,2048]{1,0:T(8,128)(2,1)S(1)}, u32[]{:S(2)}, u32[]{:S(2)}) collective-permute-start(bf16[272,2048]{1,0:T(8,128)(2,1)S(1)} %shard_map.73), channel_id=1, source_target_pairs={{0,2},{1,3},{2,0},{3,1},{4,6},{5,7},{6,4},{7,5},{8,10},{9,11},{10,... | collective-permute-start | bytes 3342344 | tf_op jit(solution)/shard_map/ppermute | solution.py:461
  7.0 8.6 %copy-start.1 = (bf16[16,16,2048]{2,1,0:T(8,128)(2,1)S(1)}, bf16[16,16,2048]{2,1,0:T(8,128)(2,1)}, u32[]{:S(2)}) copy-start(bf16[16,16,2048]{2,1,0:T(8,128)(2,1)} %param.7) | copy-start | bytes 3145732
  7.0 8.6 %copy-start.24 = (s32[64]{0:T(128)S(1)}, s32[64]{0:T(128)}, u32[]{:S(2)}) copy-start(s32[64]{0:T(128)} %refs_1_.11) | copy-start | bytes 772
  7.0 8.6 %copy-start.25 = (s32[64]{0:T(128)S(1)}, s32[64]{0:T(128)}, u32[]{:S(2)}) copy-start(s32[64]{0:T(128)} %refs_2_.7) | copy-start | bytes 772
  14.2 6.7 %collective-permute-start.3 = (bf16[128,896]{1,0:T(8,128)(2,1)S(1)}, bf16[128,896]{1,0:T(8,128)(2,1)S(1)}, u32[]{:S(2)}, u32[]{:S(2)}) collective-permute-start(bf16[128,896]{1,0:T(8,128)(2,1)S(1)} %slice.40), channel_id=1, source_target_pairs={{12,8},{13,9},{2,6},{3,7},{28,24},{29,25},{18,22},{19,23}} | collective-permute-start | bytes 688136 | tf_op jit(solution)/shard_map/ppermute | solution.py:473
  14.9 7.7 %collective-permute-start.2 = (bf16[128,1152]{1,0:T(8,128)(2,1)S(1)}, bf16[128,1152]{1,0:T(8,128)(2,1)S(1)}, u32[]{:S(2)}, u32[]{:S(2)}) collective-permute-start(bf16[128,1152]{1,0:T(8,128)(2,1)S(1)} %slice.38), channel_id=1, source_target_pairs={{12,8},{13,9},{2,6},{3,7},{28,24},{29,25},{18,22},{19,23}} | collective-permute-start | bytes 884744 | tf_op jit(solution)/shard_map/ppermute | solution.py:473
  22.6 9.1 %copy-start.29 = (bf16[128,896]{1,0:T(8,128)(2,1)S(1)}, bf16[128,896]{1,0:T(8,128)(2,1)}, u32[]{:S(2)}) copy-start(bf16[128,896]{1,0:T(8,128)(2,1)} %add_convert_fusion.15.refs_2_) | copy-start | bytes 688132
  31.8 3.0 %collective-permute-start.4 = (bf16[272,2048]{1,0:T(8,128)(2,1)}, bf16[272,2048]{1,0:T(8,128)(2,1)S(1)}, u32[]{:S(2)}, u32[]{:S(2)}) collective-permute-start(bf16[272,2048]{1,0:T(8,128)(2,1)} %shard_map.76.refs_3_.refs_7_), channel_id=1, source_target_pairs={{0,1},{1,0},{2,3},{3,2},{4,5},{5,4},{6,7},{7,6},{8,9},{9,8},{10,11... | collective-permute-start | bytes 3342344 | tf_op jit(solution)/shard_map/ppermute | solution.py:461
  31.8 34.9 %collective-permute-start.10 = (bf16[128,896]{1,0:T(8,128)(2,1)S(1)}, bf16[128,896]{1,0:T(8,128)(2,1)S(1)}, u32[]{:S(2)}, u32[]{:S(2)}) collective-permute-start(bf16[128,896]{1,0:T(8,128)(2,1)S(1)} %copy-done.29), channel_id=1, source_target_pairs={{12,8},{8,4},{13,9},{9,5},{2,6},{6,10},{3,7},{7,11},{28,24},{24,20... | collective-permute-start | bytes 688136 | tf_op jit(solution)/shard_map/ppermute | solution.py:473
  32.4 19.9 %copy-start.23 = (s32[16]{0:T(128)S(1)}, s32[16]{0:T(128)}, u32[]{:S(2)}) copy-start(s32[16]{0:T(128)} %refs_3_.3) | copy-start | bytes 196
  33.2 35.8 %collective-permute-start.5 = (bf16[128,1152]{1,0:T(8,128)(2,1)}, bf16[128,1152]{1,0:T(8,128)(2,1)S(1)}, u32[]{:S(2)}, u32[]{:S(2)}) collective-permute-start(bf16[128,1152]{1,0:T(8,128)(2,1)} %add_convert_fusion.7.refs_1_), channel_id=1, source_target_pairs={{12,8},{8,4},{13,9},{9,5},{2,6},{6,10},{3,7},{7,11},{28,24},{24,20... | collective-permute-start | bytes 884744 | tf_op jit(solution)/shard_map/ppermute | solution.py:473
  43.1 28.4 %collective-permute-start.7 = (bf16[256,128]{1,0:T(8,128)(2,1)S(1)}, bf16[256,128]{1,0:T(8,128)(2,1)S(1)}, u32[]{:S(2)}, u32[]{:S(2)}) collective-permute-start(bf16[256,128]{1,0:T(8,128)(2,1)S(1)} %shard_map.77.refs_10_.refs_0_), channel_id=1, source_target_pairs={{0,4},{4,0},{8,12},{12,8},{1,5},{5,1},{9,13},{13,9},{2,6},{6,2},{1... | collective-permute-start | bytes 196616 | tf_op jit(solution)/shard_map/ppermute | solution.py:570
  45.4 26.2 %collective-permute-start.8 = (bf16[256,128]{1,0:T(8,128)(2,1)S(1)}, bf16[256,128]{1,0:T(8,128)(2,1)S(1)}, u32[]{:S(2)}, u32[]{:S(2)}) collective-permute-start(bf16[256,128]{1,0:T(8,128)(2,1)S(1)} %shard_map.77.refs_10_.refs_0_), channel_id=1, source_target_pairs={{0,8},{4,12},{8,0},{12,4},{1,9},{5,13},{9,1},{13,5},{2,10},{6,14},... | collective-permute-start | bytes 196616 | tf_op jit(solution)/shard_map/ppermute | solution.py:570
  51.7 19.9 %collective-permute-start.9 = (bf16[256,128]{1,0:T(8,128)(2,1)S(1)}, bf16[256,128]{1,0:T(8,128)(2,1)S(1)}, u32[]{:S(2)}, u32[]{:S(2)}) collective-permute-start(bf16[256,128]{1,0:T(8,128)(2,1)S(1)} %shard_map.77.refs_10_.refs_0_), channel_id=1, source_target_pairs={{0,12},{4,8},{8,4},{12,0},{1,13},{5,9},{9,5},{13,1},{2,14},{6,10},... | collective-permute-start | bytes 196616 | tf_op jit(solution)/shard_map/ppermute | solution.py:570
  67.6 12.3 %copy-start.17 = (bf16[128,896]{1,0:T(8,128)(2,1)}, bf16[128,896]{1,0:T(8,128)(2,1)S(1)}, u32[]{:S(2)}) copy-start(bf16[128,896]{1,0:T(8,128)(2,1)S(1)} %add_convert_fusion.14.refs_6_.refs_1_) | copy-start | bytes 688132
  67.7 11.1 %collective-permute-start.13 = (bf16[128,896]{1,0:T(8,128)(2,1)S(1)}, bf16[128,896]{1,0:T(8,128)(2,1)S(1)}, u32[]{:S(2)}, u32[]{:S(2)}) collective-permute-start(bf16[128,896]{1,0:T(8,128)(2,1)S(1)} %add_convert_fusion.14.refs_6_.refs_1_), channel_id=1, source_target_pairs={{12,8},{8,4},{4,0},{13,9},{9,5},{2,6},{6,10},{3,7},{7,11},{11,15},... | collective-permute-start | bytes 688136 | tf_op jit(solution)/shard_map/ppermute | solution.py:473
  70.0 11.3 %collective-permute-start.6 = (bf16[128,1152]{1,0:T(8,128)(2,1)S(1)}, bf16[128,1152]{1,0:T(8,128)(2,1)S(1)}, u32[]{:S(2)}, u32[]{:S(2)}) collective-permute-start(bf16[128,1152]{1,0:T(8,128)(2,1)S(1)} %add_convert_fusion.6.refs_5_.refs_0_), channel_id=1, source_target_pairs={{12,8},{8,4},{4,0},{13,9},{9,5},{2,6},{6,10},{3,7},{7,11},{11,15},... | collective-permute-start | bytes 884744 | tf_op jit(solution)/shard_map/ppermute | solution.py:473
  78.8 15.0 %collective-permute-start.12 = (bf16[128,2048]{1,0:T(8,128)(2,1)S(1)}, bf16[128,2048]{1,0:T(8,128)(2,1)S(1)}, u32[]{:S(2)}, u32[]{:S(2)}) collective-permute-start(bf16[128,2048]{1,0:T(8,128)(2,1)S(1)} %get-tuple-element.10), channel_id=1, source_target_pairs={{0,1},{1,0},{2,3},{3,2},{4,5},{5,4},{6,7},{7,6},{8,9},{9,8},{10,11... | collective-permute-start | bytes 1572872 | tf_op jit(solution)/shard_map/ppermute | solution.py:461
  80.0 8.5 %copy-start.14 = (bf16[128,896]{1,0:T(8,128)(2,1)}, bf16[128,896]{1,0:T(8,128)(2,1)S(1)}, u32[]{:S(2)}) copy-start(bf16[128,896]{1,0:T(8,128)(2,1)S(1)} %add_convert_fusion.13.refs_2_.refs_3_) | copy-start | bytes 688132
  80.0 9.3 %collective-permute-start.14 = (bf16[128,896]{1,0:T(8,128)(2,1)S(1)}, bf16[128,896]{1,0:T(8,128)(2,1)}, u32[]{:S(2)}, u32[]{:S(2)}) collective-permute-start(bf16[128,896]{1,0:T(8,128)(2,1)S(1)} %add_convert_fusion.13.refs_2_.refs_3_), channel_id=1, source_target_pairs={{12,8},{8,4},{4,0},{13,9},{9,5},{2,6},{6,10},{3,7},{7,11},{11,15},... | collective-permute-start | bytes 688136 | tf_op jit(solution)/shard_map/ppermute | solution.py:473
  83.2 10.6 %collective-permute-start.11 = (bf16[128,1152]{1,0:T(8,128)(2,1)S(1)}, bf16[128,1152]{1,0:T(8,128)(2,1)}, u32[]{:S(2)}, u32[]{:S(2)}) collective-permute-start(bf16[128,1152]{1,0:T(8,128)(2,1)S(1)} %add_convert_fusion.5.refs_1_.refs_2_), channel_id=1, source_target_pairs={{12,8},{8,4},{4,0},{13,9},{9,5},{2,6},{6,10},{3,7},{7,11},{11,15},... | collective-permute-start | bytes 884744 | tf_op jit(solution)/shard_map/ppermute | solution.py:473
  88.5 40.2 %collective-permute-start.18 = (bf16[384,2048]{1,0:T(8,128)(2,1)}, bf16[384,2048]{1,0:T(8,128)(2,1)S(1)}, u32[]{:S(2)}, u32[]{:S(2)}) collective-permute-start(bf16[384,2048]{1,0:T(8,128)(2,1)} %shard_map.83), channel_id=1, source_target_pairs={{1,5},{14,10},{17,21},{30,26}} | collective-permute-start | bytes 4718600 | tf_op jit(solution)/shard_map/ppermute | solution.py:473
  96.5 32.2 %collective-permute-start.19 = (bf16[384,2048]{1,0:T(8,128)(2,1)}, bf16[384,2048]{1,0:T(8,128)(2,1)S(1)}, u32[]{:S(2)}, u32[]{:S(2)}) collective-permute-start(bf16[384,2048]{1,0:T(8,128)(2,1)} %shard_map.84), channel_id=1, source_target_pairs={{1,5},{14,10},{17,21},{30,26}} | collective-permute-start | bytes 4718600 | tf_op jit(solution)/shard_map/ppermute | solution.py:473
  97.2 16.1 %collective-permute-start.16 = (bf16[128,2048]{1,0:T(8,128)(2,1)}, bf16[128,2048]{1,0:T(8,128)(2,1)}, u32[]{:S(2)}, u32[]{:S(2)}) collective-permute-start(bf16[128,2048]{1,0:T(8,128)(2,1)} %get-tuple-element.11), channel_id=1, source_target_pairs={{0,2},{1,3},{2,0},{3,1},{4,6},{5,7},{6,4},{7,5},{8,10},{9,11},{10,... | collective-permute-start | bytes 1572872 | tf_op jit(solution)/shard_map/ppermute | solution.py:461
  100.8 8.8 %collective-permute-start.17 = (bf16[128,896]{1,0:T(8,128)(2,1)}, bf16[128,896]{1,0:T(8,128)(2,1)}, u32[]{:S(2)}, u32[]{:S(2)}) collective-permute-start(bf16[128,896]{1,0:T(8,128)(2,1)} %add_convert_fusion.12.refs_2_.refs_1_), channel_id=1, source_target_pairs={{12,8},{8,4},{4,0},{13,9},{9,5},{2,6},{6,10},{3,7},{7,11},{11,15},... | collective-permute-start | bytes 688136 | tf_op jit(solution)/shard_map/ppermute | solution.py:473
  102.1 12.5 %collective-permute-start.15 = (bf16[128,1152]{1,0:T(8,128)(2,1)}, bf16[128,1152]{1,0:T(8,128)(2,1)}, u32[]{:S(2)}, u32[]{:S(2)}) collective-permute-start(bf16[128,1152]{1,0:T(8,128)(2,1)} %add_convert_fusion.4.refs_1_.refs_0_), channel_id=1, source_target_pairs={{12,8},{8,4},{4,0},{13,9},{9,5},{2,6},{6,10},{3,7},{7,11},{11,15},... | collective-permute-start | bytes 884744 | tf_op jit(solution)/shard_map/ppermute | solution.py:473
  109.6 17.7 %collective-permute-start.22 = (bf16[128,2048]{1,0:T(8,128)(2,1)}, bf16[128,2048]{1,0:T(8,128)(2,1)}, u32[]{:S(2)}, u32[]{:S(2)}) collective-permute-start(bf16[128,2048]{1,0:T(8,128)(2,1)} %get-tuple-element.12), channel_id=1, source_target_pairs={{0,3},{1,2},{2,1},{3,0},{4,7},{5,6},{6,5},{7,4},{8,11},{9,10},{10,... | collective-permute-start | bytes 1572872 | tf_op jit(solution)/shard_map/ppermute | solution.py:461
  113.4 10.8 %collective-permute-start.23 = (bf16[128,896]{1,0:T(8,128)(2,1)}, bf16[128,896]{1,0:T(8,128)(2,1)}, u32[]{:S(2)}, u32[]{:S(2)}) collective-permute-start(bf16[128,896]{1,0:T(8,128)(2,1)} %add_convert_fusion.11.refs_3_), channel_id=1, source_target_pairs={{12,8},{8,4},{4,0},{13,9},{9,5},{2,6},{6,10},{3,7},{7,11},{11,15},... | collective-permute-start | bytes 688136 | tf_op jit(solution)/shard_map/ppermute | solution.py:473
  116.5 12.2 %collective-permute-start.21 = (bf16[128,1152]{1,0:T(8,128)(2,1)}, bf16[128,1152]{1,0:T(8,128)(2,1)}, u32[]{:S(2)}, u32[]{:S(2)}) collective-permute-start(bf16[128,1152]{1,0:T(8,128)(2,1)} %add_convert_fusion.3.refs_2_), channel_id=1, source_target_pairs={{12,8},{8,4},{4,0},{13,9},{9,5},{2,6},{6,10},{3,7},{7,11},{11,15},... | collective-permute-start | bytes 884744 | tf_op jit(solution)/shard_map/ppermute | solution.py:473
  126.0 16.0 %collective-permute-start.25 = (bf16[128,896]{1,0:T(8,128)(2,1)}, bf16[128,896]{1,0:T(8,128)(2,1)}, u32[]{:S(2)}, u32[]{:S(2)}) collective-permute-start(bf16[128,896]{1,0:T(8,128)(2,1)} %add_convert_fusion.10.refs_1_), channel_id=1, source_target_pairs={{8,4},{4,0},{9,5},{6,10},{7,11},{11,15},{24,20},{20,16},{25,21},{2... | collective-permute-start | bytes 688136 | tf_op jit(solution)/shard_map/ppermute | solution.py:473
  132.8 27.6 %collective-permute-start.20 = (bf16[256,2048]{1,0:T(8,128)(2,1)}, bf16[256,2048]{1,0:T(8,128)(2,1)}, u32[]{:S(2)}, u32[]{:S(2)}) collective-permute-start(bf16[256,2048]{1,0:T(8,128)(2,1)} %shard_map.85.refs_1_), channel_id=1, source_target_pairs={{0,2},{5,7},{10,8},{15,13},{16,18},{21,23},{26,24},{31,29}} | collective-permute-start | bytes 3145736 | tf_op jit(solution)/shard_map/ppermute | solution.py:473
  140.6 8.9 %collective-permute-start.24 = (bf16[128,1152]{1,0:T(8,128)(2,1)}, bf16[128,1152]{1,0:T(8,128)(2,1)}, u32[]{:S(2)}, u32[]{:S(2)}) collective-permute-start(bf16[128,1152]{1,0:T(8,128)(2,1)} %add_convert_fusion.2.refs_0_), channel_id=1, source_target_pairs={{8,4},{4,0},{9,5},{6,10},{7,11},{11,15},{24,20},{20,16},{25,21},{2... | collective-permute-start | bytes 884744 | tf_op jit(solution)/shard_map/ppermute | solution.py:473
  143.7 11.7 %collective-permute-start.28 = (bf16[128,896]{1,0:T(8,128)(2,1)}, bf16[128,896]{1,0:T(8,128)(2,1)}, u32[]{:S(2)}, u32[]{:S(2)}) collective-permute-start(bf16[128,896]{1,0:T(8,128)(2,1)} %add_convert_fusion.9.refs_3_), channel_id=1, source_target_pairs={{4,0},{11,15},{20,16},{27,31}} | collective-permute-start | bytes 688136 | tf_op jit(solution)/shard_map/ppermute | solution.py:473
  150.7 5.9 %copy-start.8 = (bf16[128,1152]{1,0:T(8,128)(2,1)S(1)}, bf16[128,1152]{1,0:T(8,128)(2,1)}, u32[]{:S(2)}) copy-start(bf16[128,1152]{1,0:T(8,128)(2,1)} %copy-done.7) | copy-start | bytes 884740
  150.7 5.9 %copy-start.15 = (bf16[128,896]{1,0:T(8,128)(2,1)S(1)}, bf16[128,896]{1,0:T(8,128)(2,1)}, u32[]{:S(2)}) copy-start(bf16[128,896]{1,0:T(8,128)(2,1)} %copy-done.14) | copy-start | bytes 688132
  150.7 5.9 %copy-start.18 = (bf16[128,896]{1,0:T(8,128)(2,1)S(1)}, bf16[128,896]{1,0:T(8,128)(2,1)}, u32[]{:S(2)}) copy-start(bf16[128,896]{1,0:T(8,128)(2,1)} %copy-done.17) | copy-start | bytes 688132
  153.2 17.9 %collective-permute-start.26 = (bf16[256,2048]{1,0:T(8,128)(2,1)}, bf16[256,2048]{1,0:T(8,128)(2,1)}, u32[]{:S(2)}, u32[]{:S(2)}) collective-permute-start(bf16[256,2048]{1,0:T(8,128)(2,1)} %shard_map.88), channel_id=1, source_target_pairs={{0,2},{5,7},{10,8},{15,13},{16,18},{21,23},{26,24},{31,29}} | collective-permute-start | bytes 3145736 | tf_op jit(solution)/shard_map/ppermute | solution.py:473
  156.9 22.4 %collective-permute-start.33 = (bf16[256,2048]{1,0:T(8,128)(2,1)S(1)}, bf16[256,2048]{1,0:T(8,128)(2,1)}, u32[]{:S(2)}, u32[]{:S(2)}) collective-permute-start(bf16[256,2048]{1,0:T(8,128)(2,1)S(1)} %shard_map.91.refs_7_), channel_id=1, source_target_pairs={{0,1},{5,4},{10,11},{15,14},{2,3},{7,6},{8,9},{13,12},{16,17},{21,... | collective-permute-start | bytes 3145736 | tf_op jit(solution)/shard_map/ppermute | solution.py:473
  159.2 8.6 %collective-permute-start.27 = (bf16[128,1152]{1,0:T(8,128)(2,1)S(1)}, bf16[128,1152]{1,0:T(8,128)(2,1)S(1)}, u32[]{:S(2)}, u32[]{:S(2)}) collective-permute-start(bf16[128,1152]{1,0:T(8,128)(2,1)S(1)} %add_convert_fusion.1.refs_2_), channel_id=1, source_target_pairs={{4,0},{11,15},{20,16},{27,31}} | collective-permute-start | bytes 884744 | tf_op jit(solution)/shard_map/ppermute | solution.py:473
  161.8 6.0 %copy-start.4 = (bf16[256,2048]{1,0:T(8,128)(2,1)}, bf16[256,2048]{1,0:T(8,128)(2,1)S(1)}, u32[]{:S(2)}) copy-start(bf16[256,2048]{1,0:T(8,128)(2,1)S(1)} %broadcast_select_fusion.1.refs_1_.refs_7_) | copy-start | bytes 3145732
  161.8 21.3 %collective-permute-start.30 = (bf16[256,2048]{1,0:T(8,128)(2,1)S(1)}, bf16[256,2048]{1,0:T(8,128)(2,1)}, u32[]{:S(2)}, u32[]{:S(2)}) collective-permute-start(bf16[256,2048]{1,0:T(8,128)(2,1)S(1)} %broadcast_select_fusion.1.refs_1_.refs_7_), channel_id=1, source_target_pairs={{0,1},{5,4},{10,11},{15,14},{2,3},{7,6},{8,9},{13,12},{16,17},{21,... | collective-permute-start | bytes 3145736 | tf_op jit(solution)/shard_map/ppermute | solution.py:473
  168.5 10.8 %copy-start.11 = (bf16[128,2048]{1,0:T(8,128)(2,1)S(1)}, bf16[128,2048]{1,0:T(8,128)(2,1)}, u32[]{:S(2)}) copy-start(bf16[128,2048]{1,0:T(8,128)(2,1)} %copy-done.10) | copy-start | bytes 1572868
  168.5 10.8 %copy-start.13 = (bf16[128,2048]{1,0:T(8,128)(2,1)S(1)}, bf16[128,2048]{1,0:T(8,128)(2,1)}, u32[]{:S(2)}) copy-start(bf16[128,2048]{1,0:T(8,128)(2,1)} %copy-done.12) | copy-start | bytes 1572868
  169.8 8.0 %collective-permute-start.29 = (bf16[128,2048]{1,0:T(8,128)(2,1)S(1)}, bf16[128,2048]{1,0:T(8,128)(2,1)S(1)}, u32[]{:S(2)}, u32[]{:S(2)}) collective-permute-start(bf16[128,2048]{1,0:T(8,128)(2,1)S(1)} %shard_map.90), channel_id=1, source_target_pairs={{0,2},{5,7},{10,8},{15,13},{16,18},{21,23},{26,24},{31,29}} | collective-permute-start | bytes 1572872 | tf_op jit(solution)/shard_map/ppermute | solution.py:473
  172.5 10.7 %collective-permute-start.31 = (bf16[256,2048]{1,0:T(8,128)(2,1)S(1)}, bf16[256,2048]{1,0:T(8,128)(2,1)S(1)}, u32[]{:S(2)}, u32[]{:S(2)}) collective-permute-start(bf16[256,2048]{1,0:T(8,128)(2,1)S(1)} %broadcast_select_fusion.refs_8_), channel_id=1, source_target_pairs={{0,1},{5,4},{10,11},{15,14},{2,3},{7,6},{8,9},{13,12},{16,17},{21,... | collective-permute-start | bytes 3145736 | tf_op jit(solution)/shard_map/ppermute | solution.py:473
  177.8 5.4 %copy-start.5 = (bf16[256,2048]{1,0:T(8,128)(2,1)S(1)}, bf16[256,2048]{1,0:T(8,128)(2,1)}, u32[]{:S(2)}) copy-start(bf16[256,2048]{1,0:T(8,128)(2,1)} %copy-done.4) | copy-start | bytes 3145732
  177.8 5.4 %collective-permute-start.32 = (bf16[128,2048]{1,0:T(8,128)(2,1)S(1)}, bf16[128,2048]{1,0:T(8,128)(2,1)S(1)}, u32[]{:S(2)}, u32[]{:S(2)}) collective-permute-start(bf16[128,2048]{1,0:T(8,128)(2,1)S(1)} %broadcast_select_fusion.2.refs_9_), channel_id=1, source_target_pairs={{0,1},{5,4},{10,11},{15,14},{2,3},{7,6},{8,9},{13,12},{16,17},{21,... | collective-permute-start | bytes 1572872 | tf_op jit(solution)/shard_map/ppermute | solution.py:473
  (16 other events, 21.9 us)

commit v4 on v3

--- a/solution.py
+++ b/solution.py
@@ -324,8 +324,33 @@
     )(lengths, x)
 
 
-def merge_kernel(count, streams, has_back, u_ref, *refs):
-    out_ref = refs[-1]
+def keep_kernel(meta_ref, came_ref, own_ref, *refs):
+    out_ref, held, sem = refs[-3:]
+
+    @pl.when(meta_ref[0] == meta_ref[1])
+    def _():
+        for source, target in ((own_ref, held), (held, out_ref)):
+            copy = pltpu.make_async_copy(source, target, sem)
+            copy.start()
+            copy.wait()
+
+
+def keep(meta, came, own, deps=()):
+    anywhere = pl.BlockSpec(memory_space=pl.ANY)
+    return pl.pallas_call(
+        keep_kernel,
+        in_specs=[pl.BlockSpec(memory_space=pltpu.SMEM)] + [anywhere] * (2 + len(deps)),
+        out_specs=anywhere,
+        out_shape=jax.ShapeDtypeStruct(came.shape, came.dtype),
+        scratch_shapes=[pltpu.VMEM(came.shape, came.dtype), pltpu.SemaphoreType.DMA],
+        input_output_aliases={1: 0},
+        compiler_params=pltpu.CompilerParams(vmem_limit_bytes=SMALL_VMEM),
+        cost_estimate=LIGHT,
+    )(meta, came, own, *deps)
+
+
+def merge_kernel(count, streams, has_back, tail, u_ref, *refs):
+    out_ref, tail_ref = (refs[-2], refs[-1]) if tail else (refs[-1], None)
     span = refs[0].shape[0]
     for i in range(count):
         at = 0
@@ -337,10 +362,12 @@
                 back = refs[count * streams + i][:, at : at + width]
                 value = (value.astype(F32) + back.astype(F32)).astype(BF16)
             out_ref[i * span : (i + 1) * span, at : at + width] = value
+            if tail and i == count - 1:
+                tail_ref[:, at : at + width] = value
             at += width
 
 
-def merge(u, pieces, backs, steps_of):
+def merge(u, pieces, backs, steps_of, tail=False, deps=()):
     count, streams = len(steps_of), len(pieces) // len(steps_of)
     span = pieces[0].shape[0]
     cols = sum(p.shape[1] for p in pieces[:streams])
@@ -350,18 +377,20 @@
 
     specs = [pl.BlockSpec(p.shape, lambda i, r: (0, 0)) for p in pieces]
     specs += [spec_of(low, high, k) for k, (_, low, high) in zip(steps_of, backs)]
-    return pl.pallas_call(
-        functools.partial(merge_kernel, count, streams, bool(backs)),
+    specs += [pl.BlockSpec(memory_space=pl.ANY)] * len(deps)
+    sizes = [count * span] + [span] * tail
+    return pl.pallas_call(
+        functools.partial(merge_kernel, count, streams, bool(backs), tail),
         grid_spec=pltpu.PrefetchScalarGridSpec(
             num_scalar_prefetch=1,
             grid=(1,),
             in_specs=specs,
-            out_specs=pl.BlockSpec((count * span, cols), lambda i, r: (0, 0)),
+            out_specs=[pl.BlockSpec((n, cols), lambda i, r: (0, 0)) for n in sizes],
         ),
-        out_shape=jax.ShapeDtypeStruct((count * span, cols), BF16),
+        out_shape=[jax.ShapeDtypeStruct((n, cols), BF16) for n in sizes],
         compiler_params=pltpu.CompilerParams(vmem_limit_bytes=SMALL_VMEM),
         cost_estimate=LIGHT,
-    )(u, *pieces, *[b[0] for b in backs])
+    )(u, *pieces, *[b[0] for b in backs], *deps)
 
 
 def finish_kernel(n, sizes, first, span, held, requests, tokens, capacity, with_delta, with_acc, *refs):
@@ -506,7 +535,6 @@
     back_pairs = [((plane(b, 3), b), (plane(b, 2), b)) for b in (1, 2)]
     across = [((v, v), (v, v ^ 2)) for v in range(4)]
     beside = [((v, v), (v, v ^ 1)) for v in range(4)] + [((v, v ^ 2), (v, v ^ 3)) for v in range(4)]
-    is_root = s == t
     chip = s // 2
     u = jnp.where(chip == 1, t, 3 - t)
 
@@ -517,13 +545,18 @@
         lo, hi = bounds[j]
         return lax.dynamic_slice(source, (at, lo), (span, hi - lo))
 
-    def chain_step(k, *deps):
-        pairs = [
+    def pairs_of(k):
+        return [
             ((plane(b, v), b), (plane(b, v + 1), b))
             for b in range(4)
             for v in range(last_step(b))
             if 0 <= k - v < steps
         ]
+
+    last_pairs = pairs_of(steps + 1)
+
+    def chain_step(k, *deps):
+        pairs = pairs_of(k)
         for j in range(STREAMS):
             if k < early:
                 value = parts[0][k * span : (k + 1) * span, bounds[j][0] : bounds[j][1]]
@@ -536,20 +569,20 @@
                 total = value.astype(F32) + came.astype(F32)
                 value = total.astype(BF16)
             final[k, j] = value
-            carry[j] = on_mesh(value, pairs) if pairs else None
+            carry[j] = on_mesh(value, pairs) if k < steps + 1 else None
 
     values, gots = [], []
 
-    def merged(lo, hi):
+    def merged(lo, hi, tail=False, deps=()):
         ks = range(lo, hi)
         backs = []
         if hi <= steps + 2:
             for k in ks:
                 backs.append(next(b for b in back if b[1] <= k - 2 <= b[2]))
-        return merge(u_vec, [final[k, j] for k in ks for j in range(STREAMS)], backs, ks)
+        return merge(u_vec, [final[k, j] for k in ks for j in range(STREAMS)], backs, ks, tail, deps)
 
     def cross(value):
-        return jnp.where(is_root, value, on_mesh(value, across))
+        return on_mesh(value, across), value
 
     def hand_on(value):
         values.append(value)
@@ -566,40 +599,44 @@
     x_fsib = on_store(x_far, 1)
     xs = [x_me, x_sib, x_far, x_fsib]
     lens = lens + [lengths_of(x_far), lengths_of(x_fsib)]
-    low = low_rank(meta, req, slot, xs[2:], (2, 3), down_t, low, held, rank, tokens, capacity, ())
+    parts[1] = project(meta, lens, xs, w, 0, live, 0)
+    chain_step(2)
+    low = low_rank(
+        meta, req, slot, xs[2:], (2, 3), down_t, low, held, rank, tokens, capacity, (final[2, 0], final[2, 1])
+    )
     lows = [low] + [lax.ppermute(low, "tensor", [(i, i ^ f) for i in range(4)]) for f in (1, 2, 3)]
-    parts[1] = project(meta, lens, xs, w, 0, live, 0, (low,))
-    chain_step(2)
+    chain_step(3, low)
     delta = up_project(
-        meta, req, slot, lows, up_2d, held, rank, tokens, capacity, requests, (final[2, 0], final[2, 1])
+        meta, req, slot, lows, up_2d, held, rank, tokens, capacity, requests, (final[3, 0], final[3, 1])
     )
     deltas = [delta[0]] + [on_store(delta[i], i) for i in (1, 2, 3)]
-    chain_step(3, delta[0])
-    cut = steps // 2
+    chain_step(4, delta[0])
+    cut = steps - 2
 
     def send_back(low, high, *deps):
         rows_of = after(parts[1][low * span : (high + 1) * span], *deps)
         return on_mesh(rows_of, back_pairs), low, high
 
-    back = [send_back(0, cut - 1, final[3, 0], final[3, 1])]
-    chain_step(4, deltas[1])
-    back.append(send_back(cut, steps - 1, final[4, 0], final[4, 1]))
-    chain_step(5, deltas[2])
-    chain_step(6, deltas[3])
-    one = merged(2, 4)
-    two = merged(4, 6)
-    chain_step(7, two)
+    back = [send_back(0, cut - 1, final[4, 0], final[4, 1])]
+    chain_step(5, deltas[1])
+    back.append(send_back(cut, steps - 1, final[5, 0], final[5, 1]))
+    chain_step(6, deltas[2])
+    (two,) = merged(4, 6)
+    chain_step(7, two, deltas[3])
+    two = keep(meta, *cross(two))
+    three, last = merged(6, 8, True)
+    came = on_mesh(last, last_pairs)
+    (one,) = merged(2, 4, deps=(last,))
+    three = cross(three)
     hand_on(one)
-    two = cross(two)
-    three = merged(6, 8)
-    chain_step(8, two)
+    (four,) = merge(u_vec, [came], [(parts[1], 0, steps - 1)], [steps + 2], deps=(two,))
     hand_on(two)
-    hand_on(cross(three))
     partial = finish(
         meta, req, slot, lens, values[:1], gots[:1], 2 * span, deltas, None, F32, span, held, tokens, capacity,
-        (final[8, 0], final[8, 1]),
-    )
-    hand_on(cross(merged(8, 9)))
+        (four,),
+    )
+    hand_on(keep(meta, *three, (partial,)))
+    hand_on(keep(meta, *cross(four)))
     out = finish(
         meta, req, slot, lens, values[1:], gots[1:], 4 * span, (), partial, BF16, span, held, tokens, capacity
     )

time: 189 us -> 178 us (0.942)
  the two profiles are of different devices: /device:TPU:0 before, /device:TPU:21 now
where the time goes in v4:
time: 178 us; the launch traced here: 176 us
  Pallas kernels  56.4 us (32%)
  starting transfers between devices  51.9 us (29%)
  waiting for transfers between devices  32.2 us (18%)
  other arithmetic  23.7 us (13%)
  local copies, waits for them, and re-layouts  11.1 us (6%)
    ppermute x24, starting transfers between devices, on_mesh(): lax.ppermute(value, ('tensor', 'store'), [(a * 4 + b, c * 4 + d) for (a,...  41.7 us
    ppermute x24, waiting for transfers between devices, on_mesh(): lax.ppermute(value, ('tensor', 'store'), [(a * 4 + b, c * 4 + d) for (a,...  31 us
    convert_element_type x14, other arithmetic, chain_step(): value = total.astype(BF16)  22.3 us
    pallas_call x2, Pallas kernels, project(): pl.pallas_call(functools.partial(project_kernel, first, blocks, block_row...  21.4 us
    pallas_call x2, Pallas kernels, low_rank(): pl.pallas_call(functools.partial(low_kernel, flips, before is not None, h...  11.3 us
    unnamed x50, local copies, waits for them, and re-layouts  8.52 us
    pallas_call x2, Pallas kernels, finish(): pl.pallas_call(functools.partial(finish_kernel, len(sizes), sizes, first,...  8.1 us
    pallas_call x1, Pallas kernels, up_project(): pl.pallas_call(functools.partial(up_kernel, len(deps), held, rank, reques...  7.21 us
  transfers between devices with their start and end apart: 33, of which 9 were waited for; matrix products, arithmetic and copies ran while one was open for 14% of the time, Pallas kernels for 29%

profile of v4, /device:TPU:21, one launch (start us, length us, event | category | flops | bytes accessed | tf_op | source)
XLA Modules:
  0.0 176.0 jit_solution(17332744711297375292)
XLA Ops:
  7.1 7.1 %shard_map.74.refs_6_ = bf16[256,2048]{1,0:T(8,128)(2,1)S(1)} custom-call(s32[2]{0:T(128)S(1)} %pad_add_fusion.refs_0_.meta_ref, s32[16]{0:T(128)S(1)} %copy-done.18, s32[16]{0:T(128)S(1)} %fusion.2.refs_2_.refs_4_, bf16[256,2048]{1,0:T(8,128)(2,1)} %bitcast.24, bf16[272,2048]{1,0:T(8,128)(2,1)} %collective-permute-done.refs_4_.refs_6_, ...), custom_call_target="tpu_custom_call" | custom-call | tf_op jit(solution)/shard_map/pallas_call | solution.py:160
  14.3 1.3 collective-permute-start.3
  15.6 1.3 collective-permute-start.2
  16.9 5.2 %shard_map.75.refs_3_.refs_6_ = bf16[256,128]{1,0:T(8,128)(2,1)S(1)} custom-call(s32[2]{0:T(128)S(1)} %pad_add_fusion.refs_0_.meta_ref, s32[64]{0:T(128)S(1)} %copy-done.20, s32[64]{0:T(128)S(1)} %copy-done.21, bf16[256,2048]{1,0:T(8,128)(2,1)S(1)} %bitcast.26, bf16[272,2048]{1,0:T(8,128)(2,1)} %collective-permute-done.refs_4_.refs_6_, ...), custom_call_target="tpu_custom_call" | custom-call | tf_op jit(solution)/shard_map/pallas_call | solution.py:238
  23.0 1.7 add_convert_fusion.13.refs_2_
  24.7 4.6 %collective-permute-done.2 = bf16[128,1152]{1,0:T(8,128)(2,1)S(1)} collective-permute-done((bf16[128,1152]{1,0:T(8,128)(2,1)S(1)}, bf16[128,1152]{1,0:T(8,128)(2,1)S(1)}, u32[]{:S(2)}, u32[]{:S(2)}) %collective-permute-start.2) | collective-permute-done | bytes 294944 | tf_op jit(solution)/shard_map/ppermute | solution.py:502
  29.3 1.8 %add_convert_fusion.6.refs_1_ = bf16[128,1152]{1,0:T(8,128)(2,1)} fusion(bf16[128,1152]{1,0:T(8,128)(2,1)S(1)} %collective-permute-done.2, bf16[256,2048]{1,0:T(8,128)(2,1)} %copy-done.5), kind=kLoop, calls=%fused_computation.6 | loop fusion | flops 589824 | bytes 884736 | tf_op jit(solution)/shard_map/convert_element_type | solution.py:570
  33.3 1.9 %collective-permute-start.7 = (bf16[128,896]{1,0:T(8,128)(2,1)S(1)}, bf16[128,896]{1,0:T(8,128)(2,1)S(1)}, u32[]{:S(2)}, u32[]{:S(2)}) collective-permute-start(bf16[128,896]{1,0:T(8,128)(2,1)S(1)} %copy-done.24), channel_id=1, source_target_pairs={{12,8},{8,4},{13,9},{9,5},{2,6},{6,10},{3,7},{7,11},{28,24},{24,20... | collective-permute-start | bytes 688136 | tf_op jit(solution)/shard_map/ppermute | solution.py:502
  35.9 1.9 %collective-permute-start.5 = (bf16[128,1152]{1,0:T(8,128)(2,1)}, bf16[128,1152]{1,0:T(8,128)(2,1)S(1)}, u32[]{:S(2)}, u32[]{:S(2)}) collective-permute-start(bf16[128,1152]{1,0:T(8,128)(2,1)} %add_convert_fusion.6.refs_1_), channel_id=1, source_target_pairs={{12,8},{8,4},{13,9},{9,5},{2,6},{6,10},{3,7},{7,11},{28,24},{24,20... | collective-permute-start | bytes 884744 | tf_op jit(solution)/shard_map/ppermute | solution.py:502
  38.8 14.3 %shard_map.77.refs_1_ = bf16[768,2048]{1,0:T(8,128)(2,1)} custom-call(s32[2]{0:T(128)S(1)} %pad_add_fusion.refs_0_.meta_ref, s32[16]{0:T(128)S(1)} %copy-done.19, s32[16]{0:T(128)S(1)} %fusion.2.refs_2_.refs_4_, s32[16]{0:T(128)S(1)} %fusion.1.refs_3_.refs_5_, s32[16]{0:T(128)S(1)} %fusion.refs_4_.refs_6_, bf16[256,2048]{1,0:T(8,128)(2,1)S(1)} %bitcast.27, ...), custom_call_target="tpu_custom_call" | custom-call | tf_op jit(solution)/shard_map/pallas_call | solution.py:160
  53.1 1.7 add_convert_fusion.12.refs_8_.refs_1_
  54.8 1.9 %collective-permute-start.12 = (bf16[128,896]{1,0:T(8,128)(2,1)}, bf16[128,896]{1,0:T(8,128)(2,1)}, u32[]{:S(2)}, u32[]{:S(2)}) collective-permute-start(bf16[128,896]{1,0:T(8,128)(2,1)} %add_convert_fusion.12.refs_8_.refs_1_), channel_id=1, source_target_pairs={{12,8},{8,4},{4,0},{13,9},{9,5},{2,6},{6,10},{3,7},{7,11},{11,15},... | collective-permute-start | bytes 688136 | tf_op jit(solution)/shard_map/ppermute | solution.py:502
  57.8 1.9 %collective-permute-start.6 = (bf16[128,1152]{1,0:T(8,128)(2,1)S(1)}, bf16[128,1152]{1,0:T(8,128)(2,1)}, u32[]{:S(2)}, u32[]{:S(2)}) collective-permute-start(bf16[128,1152]{1,0:T(8,128)(2,1)S(1)} %add_convert_fusion.5.refs_7_.refs_0_), channel_id=1, source_target_pairs={{12,8},{8,4},{4,0},{13,9},{9,5},{2,6},{6,10},{3,7},{7,11},{11,15},... | collective-permute-start | bytes 884744 | tf_op jit(solution)/shard_map/ppermute | solution.py:502
  61.0 6.0 %shard_map.78.refs_1_.refs_0_ = bf16[256,128]{1,0:T(8,128)(2,1)} custom-call(s32[2]{0:T(128)S(1)} %pad_add_fusion.refs_0_.meta_ref, s32[64]{0:T(128)S(1)} %copy-done.20, s32[64]{0:T(128)S(1)} %copy-done.21, bf16[272,2048]{1,0:T(8,128)(2,1)S(1)} %copy-done.4, bf16[272,2048]{1,0:T(8,128)(2,1)} %copy-done.23, bf16[1024,2048]{1,0:T(8,128)(2,1)} %bitcast.29, ...), custom_call_target="tpu_custom_call" | custom-call | tf_op jit(solution)/shard_map/pallas_call | solution.py:238
  67.1 2.2 %collective-permute-start.9 = (bf16[256,128]{1,0:T(8,128)(2,1)}, bf16[256,128]{1,0:T(8,128)(2,1)S(1)}, u32[]{:S(2)}, u32[]{:S(2)}) collective-permute-start(bf16[256,128]{1,0:T(8,128)(2,1)} %shard_map.78.refs_1_.refs_0_), channel_id=1, source_target_pairs={{0,4},{4,0},{8,12},{12,8},{1,5},{5,1},{9,13},{13,9},{2,6},{6,2},{1... | collective-permute-start | bytes 196616 | tf_op jit(solution)/shard_map/ppermute | solution.py:607
  70.5 1.7 add_convert_fusion.11.refs_6_.refs_3_
  72.2 2.1 %collective-permute-start.13 = (bf16[128,896]{1,0:T(8,128)(2,1)}, bf16[128,896]{1,0:T(8,128)(2,1)}, u32[]{:S(2)}, u32[]{:S(2)}) collective-permute-start(bf16[128,896]{1,0:T(8,128)(2,1)} %add_convert_fusion.11.refs_6_.refs_3_), channel_id=1, source_target_pairs={{12,8},{8,4},{4,0},{13,9},{9,5},{2,6},{6,10},{3,7},{7,11},{11,15},... | collective-permute-start | bytes 688136 | tf_op jit(solution)/shard_map/ppermute | solution.py:502
  75.4 2.1 %collective-permute-start.8 = (bf16[128,1152]{1,0:T(8,128)(2,1)S(1)}, bf16[128,1152]{1,0:T(8,128)(2,1)}, u32[]{:S(2)}, u32[]{:S(2)}) collective-permute-start(bf16[128,1152]{1,0:T(8,128)(2,1)S(1)} %add_convert_fusion.4.refs_5_.refs_2_), channel_id=1, source_target_pairs={{12,8},{8,4},{4,0},{13,9},{9,5},{2,6},{6,10},{3,7},{7,11},{11,15},... | collective-permute-start | bytes 884744 | tf_op jit(solution)/shard_map/ppermute | solution.py:502
  77.5 1.5 slice.43.refs_0_
  79.0 7.2 %shard_map.80 = (bf16[128,2048]{1,0:T(8,128)(2,1)S(1)}, bf16[128,2048]{1,0:T(8,128)(2,1)S(1)}, bf16[128,2048]{1,0:T(8,128)(2,1)}, bf16[128,2048]{1,0:T(8,128)(2,1)}) custom-call(s32[2]{0:T(128)S(1)} %pad_add_fusion.refs_0_.meta_ref, s32[64]{0:T(128)S(1)} %copy-done.20, s32[64]{0:T(128)S(1)} %copy-done.21, bf16[256,128]{1,0:T(8,128)(2,1)} %shard_map.78.refs_1_.refs_0_, ...), custom_call_target="tpu_custom_call" | custom-call | tf_op jit(solution)/shard_map/pallas_call | solution.py:289
  87.0 1.9 %add_convert_fusion.10.refs_2_.refs_1_ = bf16[128,896]{1,0:T(8,128)(2,1)} fusion(bf16[128,896]{1,0:T(8,128)(2,1)} %collective-permute-done.13, bf16[768,2048]{1,0:T(8,128)(2,1)S(1)} %copy-done, s32[]{:T(128)S(6)} %select_n.34), kind=kLoop, calls=%fused_computation.10 | loop fusion | flops 458752 | bytes 688132 | tf_op jit(solution)/shard_map/convert_element_type | solution.py:570
  88.9 1.8 %add_convert_fusion.3.refs_1_.refs_0_ = bf16[128,1152]{1,0:T(8,128)(2,1)} fusion(bf16[128,1152]{1,0:T(8,128)(2,1)} %shard_map.81, bf16[768,2048]{1,0:T(8,128)(2,1)S(1)} %copy-done, s32[]{:T(128)S(6)} %select_n.34), kind=kLoop, calls=%fused_computation.3 | loop fusion | flops 589824 | bytes 884740 | tf_op jit(solution)/shard_map/convert_element_type | solution.py:570
  90.7 2.1 %collective-permute-start.17 = (bf16[512,2048]{1,0:T(8,128)(2,1)}, bf16[512,2048]{1,0:T(8,128)(2,1)}, u32[]{:S(2)}, u32[]{:S(2)}) collective-permute-start(bf16[512,2048]{1,0:T(8,128)(2,1)} %shard_map.83), channel_id=1, source_target_pairs={{1,5},{14,10},{17,21},{30,26}} | collective-permute-start | bytes 6291464 | tf_op jit(solution)/shard_map/ppermute | solution.py:502
  92.9 2.5 %collective-permute-start.15 = (bf16[128,2048]{1,0:T(8,128)(2,1)}, bf16[128,2048]{1,0:T(8,128)(2,1)}, u32[]{:S(2)}, u32[]{:S(2)}) collective-permute-start(bf16[128,2048]{1,0:T(8,128)(2,1)} %copy-done.22), channel_id=1, source_target_pairs={{0,1},{1,0},{2,3},{3,2},{4,5},{5,4},{6,7},{7,6},{8,9},{9,8},{10,11... | collective-permute-start | bytes 1572872 | tf_op jit(solution)/shard_map/ppermute | solution.py:490
  95.3 1.9 %collective-permute-start.16 = (bf16[128,896]{1,0:T(8,128)(2,1)}, bf16[128,896]{1,0:T(8,128)(2,1)}, u32[]{:S(2)}, u32[]{:S(2)}) collective-permute-start(bf16[128,896]{1,0:T(8,128)(2,1)} %add_convert_fusion.10.refs_2_.refs_1_), channel_id=1, source_target_pairs={{12,8},{8,4},{4,0},{13,9},{9,5},{2,6},{6,10},{3,7},{7,11},{11,15},... | collective-permute-start | bytes 688136 | tf_op jit(solution)/shard_map/ppermute | solution.py:502
  97.3 1.9 %collective-permute-start.14 = (bf16[128,1152]{1,0:T(8,128)(2,1)S(1)}, bf16[128,1152]{1,0:T(8,128)(2,1)}, u32[]{:S(2)}, u32[]{:S(2)}) collective-permute-start(bf16[128,1152]{1,0:T(8,128)(2,1)S(1)} %copy-done.6), channel_id=1, source_target_pairs={{12,8},{8,4},{4,0},{13,9},{9,5},{2,6},{6,10},{3,7},{7,11},{11,15},... | collective-permute-start | bytes 884744 | tf_op jit(solution)/shard_map/ppermute | solution.py:502
  100.3 4.4 %collective-permute-done.16 = bf16[128,896]{1,0:T(8,128)(2,1)} collective-permute-done((bf16[128,896]{1,0:T(8,128)(2,1)}, bf16[128,896]{1,0:T(8,128)(2,1)}, u32[]{:S(2)}, u32[]{:S(2)}) %collective-permute-start.16) | collective-permute-done | bytes 229408 | tf_op jit(solution)/shard_map/ppermute | solution.py:502
  104.8 1.7 add_convert_fusion.9.refs_3_.refs_2_
  106.5 2.1 %collective-permute-start.21 = (bf16[128,896]{1,0:T(8,128)(2,1)}, bf16[128,896]{1,0:T(8,128)(2,1)}, u32[]{:S(2)}, u32[]{:S(2)}) collective-permute-start(bf16[128,896]{1,0:T(8,128)(2,1)} %add_convert_fusion.9.refs_3_.refs_2_), channel_id=1, source_target_pairs={{12,8},{8,4},{4,0},{13,9},{9,5},{2,6},{6,10},{3,7},{7,11},{11,15},... | collective-permute-start | bytes 688136 | tf_op jit(solution)/shard_map/ppermute | solution.py:502
  108.6 2.5 %collective-permute-done.14.refs_0_ = bf16[128,1152]{1,0:T(8,128)(2,1)} collective-permute-done((bf16[128,1152]{1,0:T(8,128)(2,1)S(1)}, bf16[128,1152]{1,0:T(8,128)(2,1)}, u32[]{:S(2)}, u32[]{:S(2)}) %collective-permute-start.14) | collective-permute-done | bytes 294944 | tf_op jit(solution)/shard_map/ppermute | solution.py:502
  111.1 1.8 %add_convert_fusion.2.refs_2_.refs_1_ = bf16[128,1152]{1,0:T(8,128)(2,1)} fusion(bf16[128,1152]{1,0:T(8,128)(2,1)} %shard_map.82, bf16[768,2048]{1,0:T(8,128)(2,1)S(1)} %copy-done, s32[]{:T(128)S(6)} %select_n.37), kind=kLoop, calls=%fused_computation.2 | loop fusion | flops 589824 | bytes 884740 | tf_op jit(solution)/shard_map/convert_element_type | solution.py:570
  112.9 2.1 %collective-permute-start.19 = (bf16[128,1152]{1,0:T(8,128)(2,1)}, bf16[128,1152]{1,0:T(8,128)(2,1)}, u32[]{:S(2)}, u32[]{:S(2)}) collective-permute-start(bf16[128,1152]{1,0:T(8,128)(2,1)} %add_convert_fusion.2.refs_2_.refs_1_), channel_id=1, source_target_pairs={{12,8},{8,4},{4,0},{13,9},{9,5},{2,6},{6,10},{3,7},{7,11},{11,15},... | collective-permute-start | bytes 884744 | tf_op jit(solution)/shard_map/ppermute | solution.py:502
  116.1 1.7 collective-permute-start.25
  117.7 1.7 add_convert_fusion.8.refs_1_
  119.4 3.1 %collective-permute-start.24 = (bf16[128,896]{1,0:T(8,128)(2,1)}, bf16[128,896]{1,0:T(8,128)(2,1)}, u32[]{:S(2)}, u32[]{:S(2)}) collective-permute-start(bf16[128,896]{1,0:T(8,128)(2,1)} %add_convert_fusion.8.refs_1_), channel_id=1, source_target_pairs={{8,4},{4,0},{9,5},{6,10},{7,11},{11,15},{24,20},{20,16},{25,21},{2... | collective-permute-start | bytes 688136 | tf_op jit(solution)/shard_map/ppermute | solution.py:502
  122.8 1.8 add_convert_fusion.1.refs_0_
  124.5 3.1 %collective-permute-start.22 = (bf16[128,1152]{1,0:T(8,128)(2,1)}, bf16[128,1152]{1,0:T(8,128)(2,1)}, u32[]{:S(2)}, u32[]{:S(2)}) collective-permute-start(bf16[128,1152]{1,0:T(8,128)(2,1)} %add_convert_fusion.1.refs_0_), channel_id=1, source_target_pairs={{8,4},{4,0},{9,5},{6,10},{7,11},{11,15},{24,20},{20,16},{25,21},{2... | collective-permute-start | bytes 884744 | tf_op jit(solution)/shard_map/ppermute | solution.py:502
  127.6 1.7 add_convert_fusion.7.refs_3_
  130.3 2.6 %shard_map.84.own_ref.refs_1_ = bf16[256,2048]{1,0:T(8,128)(2,1)} custom-call(s32[1]{0:T(128)} %bitcast.9.u_ref, bf16[128,1152]{1,0:T(8,128)(2,1)S(1)} %copy-done.6, bf16[128,896]{1,0:T(8,128)(2,1)S(1)} %copy-done.13, bf16[128,1152]{1,0:T(8,128)(2,1)} %add_convert_fusion.2.refs_2_.refs_1_, bf16[128,896]{1,0:T(8,128)(2,1)} %add_convert_fusion.9.refs_3_.refs_2_, ...), custom_call_target="tpu_custom_call" | custom-call | tf_op jit(solution)/shard_map/pallas_call | solution.py:382
  132.9 1.8 %collective-permute-start.18 = (bf16[256,2048]{1,0:T(8,128)(2,1)}, bf16[256,2048]{1,0:T(8,128)(2,1)}, u32[]{:S(2)}, u32[]{:S(2)}) collective-permute-start(bf16[256,2048]{1,0:T(8,128)(2,1)} %shard_map.84.own_ref.refs_1_), channel_id=1, source_target_pairs={{0,2},{5,7},{10,8},{15,13},{16,18},{21,23},{26,24},{31,29}} | collective-permute-start | bytes 3145736 | tf_op jit(solution)/shard_map/ppermute | solution.py:502
  136.7 1.7 shard_map.89
  138.4 1.7 shard_map.90.refs_7_
  143.5 1.4 collective-permute-start.30
  145.8 3.9 %shard_map.92.refs_0_.refs_13_ = f32[256,2048]{1,0:T(8,128)S(1)} custom-call(s32[2]{0:T(128)S(1)} %pad_add_fusion.refs_0_.meta_ref, s32[64]{0:T(128)S(1)} %copy-done.20, s32[64]{0:T(128)S(1)} %copy-done.21, s32[16]{0:T(128)S(1)} %copy-done.19, s32[16]{0:T(128)S(1)} %fusion.2.refs_2_.refs_4_, s32[16]{0:T(128)S(1)} %fusion.1.refs_3_.refs_5_, ...), custom_call_target="tpu_custom_call" | custom-call | tf_op jit(solution)/shard_map/pallas_call | solution.py:469
  153.4 2.7 %collective-permute-done.30.refs_10_ = bf16[256,2048]{1,0:T(8,128)(2,1)S(1)} collective-permute-done((bf16[256,2048]{1,0:T(8,128)(2,1)}, bf16[256,2048]{1,0:T(8,128)(2,1)S(1)}, u32[]{:S(2)}, u32[]{:S(2)}) %collective-permute-start.30) | collective-permute-done | bytes 1048608 | tf_op jit(solution)/shard_map/ppermute | solution.py:502
  156.1 10.8 %collective-permute-done.31.refs_11_ = bf16[256,2048]{1,0:T(8,128)(2,1)S(1)} collective-permute-done((bf16[256,2048]{1,0:T(8,128)(2,1)S(1)}, bf16[256,2048]{1,0:T(8,128)(2,1)S(1)}, u32[]{:S(2)}, u32[]{:S(2)}) %collective-permute-start.31) | collective-permute-done | bytes 1048608 | tf_op jit(solution)/shard_map/ppermute | solution.py:502
  166.9 4.9 %collective-permute-done.32.refs_12_ = bf16[128,2048]{1,0:T(8,128)(2,1)S(1)} collective-permute-done((bf16[128,2048]{1,0:T(8,128)(2,1)S(1)}, bf16[128,2048]{1,0:T(8,128)(2,1)S(1)}, u32[]{:S(2)}, u32[]{:S(2)}) %collective-permute-start.32) | collective-permute-done | bytes 524320 | tf_op jit(solution)/shard_map/ppermute | solution.py:502
  171.8 4.2 %shard_map.95 = bf16[256,2048]{1,0:T(8,128)(2,1)} custom-call(s32[2]{0:T(128)S(1)} %pad_add_fusion.refs_0_.meta_ref, s32[64]{0:T(128)S(1)} %copy-done.20, s32[64]{0:T(128)S(1)} %copy-done.21, s32[16]{0:T(128)S(1)} %copy-done.19, s32[16]{0:T(128)S(1)} %fusion.2.refs_2_.refs_4_, s32[16]{0:T(128)S(1)} %fusion.1.refs_3_.refs_5_, s32[16]{0:T(128)S(1)} %fusion.refs_4_.refs_6_, ...), custom_call_target="tpu_custom_call" | custom-call | tf_op jit(solution)/shard_map/pallas_call | solution.py:469
  (113 shorter events, 30.6 us)
Async XLA Ops:
  2.5 3.3 %collective-permute-start = (bf16[272,2048]{1,0:T(8,128)(2,1)S(1)}, bf16[272,2048]{1,0:T(8,128)(2,1)}, u32[]{:S(2)}, u32[]{:S(2)}) collective-permute-start(bf16[272,2048]{1,0:T(8,128)(2,1)S(1)} %shard_map.73), channel_id=1, source_target_pairs={{0,1},{1,0},{2,3},{3,2},{4,5},{5,4},{6,7},{7,6},{8,9},{9,8},{10,11... | collective-permute-start | bytes 3342344 | tf_op jit(solution)/shard_map/ppermute | solution.py:490
  3.2 27.8 %collective-permute-start.1 = (bf16[272,2048]{1,0:T(8,128)(2,1)S(1)}, bf16[272,2048]{1,0:T(8,128)(2,1)S(1)}, u32[]{:S(2)}, u32[]{:S(2)}) collective-permute-start(bf16[272,2048]{1,0:T(8,128)(2,1)S(1)} %shard_map.73), channel_id=1, source_target_pairs={{0,2},{1,3},{2,0},{3,1},{4,6},{5,7},{6,4},{7,5},{8,10},{9,11},{10,... | collective-permute-start | bytes 3342344 | tf_op jit(solution)/shard_map/ppermute | solution.py:490
  7.1 9.8 %copy-start.2 = (bf16[16,16,2048]{2,1,0:T(8,128)(2,1)S(1)}, bf16[16,16,2048]{2,1,0:T(8,128)(2,1)}, u32[]{:S(2)}) copy-start(bf16[16,16,2048]{2,1,0:T(8,128)(2,1)} %param.7) | copy-start | bytes 3145732
  7.1 9.8 %copy-start.20 = (s32[64]{0:T(128)S(1)}, s32[64]{0:T(128)}, u32[]{:S(2)}) copy-start(s32[64]{0:T(128)} %refs_1_.11) | copy-start | bytes 772
  7.1 9.8 %copy-start.21 = (s32[64]{0:T(128)S(1)}, s32[64]{0:T(128)}, u32[]{:S(2)}) copy-start(s32[64]{0:T(128)} %refs_2_.7) | copy-start | bytes 772
  14.2 2.7 %copy-start.5 = (bf16[256,2048]{1,0:T(8,128)(2,1)}, bf16[256,2048]{1,0:T(8,128)(2,1)S(1)}, u32[]{:S(2)}) copy-start(bf16[256,2048]{1,0:T(8,128)(2,1)S(1)} %shard_map.74.refs_6_) | copy-start | bytes 3145732
  14.3 8.7 %collective-permute-start.3 = (bf16[128,896]{1,0:T(8,128)(2,1)S(1)}, bf16[128,896]{1,0:T(8,128)(2,1)S(1)}, u32[]{:S(2)}, u32[]{:S(2)}) collective-permute-start(bf16[128,896]{1,0:T(8,128)(2,1)S(1)} %slice.40), channel_id=1, source_target_pairs={{12,8},{13,9},{2,6},{3,7},{28,24},{29,25},{18,22},{19,23}} | collective-permute-start | bytes 688136 | tf_op jit(solution)/shard_map/ppermute | solution.py:502
  15.6 13.7 %collective-permute-start.2 = (bf16[128,1152]{1,0:T(8,128)(2,1)S(1)}, bf16[128,1152]{1,0:T(8,128)(2,1)S(1)}, u32[]{:S(2)}, u32[]{:S(2)}) collective-permute-start(bf16[128,1152]{1,0:T(8,128)(2,1)S(1)} %slice.38), channel_id=1, source_target_pairs={{12,8},{13,9},{2,6},{3,7},{28,24},{29,25},{18,22},{19,23}} | collective-permute-start | bytes 884744 | tf_op jit(solution)/shard_map/ppermute | solution.py:502
  22.2 7.1 %copy-start.15 = (bf16[256,128]{1,0:T(8,128)(2,1)}, bf16[256,128]{1,0:T(8,128)(2,1)S(1)}, u32[]{:S(2)}) copy-start(bf16[256,128]{1,0:T(8,128)(2,1)S(1)} %shard_map.75.refs_3_.refs_6_) | copy-start | bytes 196612
  22.2 16.6 %copy-start.19 = (s32[16]{0:T(128)S(1)}, s32[16]{0:T(128)}, u32[]{:S(2)}) copy-start(s32[16]{0:T(128)} %refs_3_.3) | copy-start | bytes 196
  24.7 8.6 %copy-start.24 = (bf16[128,896]{1,0:T(8,128)(2,1)S(1)}, bf16[128,896]{1,0:T(8,128)(2,1)}, u32[]{:S(2)}) copy-start(bf16[128,896]{1,0:T(8,128)(2,1)} %add_convert_fusion.13.refs_2_) | copy-start | bytes 688132
  32.1 5.7 %collective-permute-start.4 = (bf16[272,2048]{1,0:T(8,128)(2,1)}, bf16[272,2048]{1,0:T(8,128)(2,1)S(1)}, u32[]{:S(2)}, u32[]{:S(2)}) collective-permute-start(bf16[272,2048]{1,0:T(8,128)(2,1)} %shard_map.76.refs_7_.refs_3_), channel_id=1, source_target_pairs={{0,1},{1,0},{2,3},{3,2},{4,5},{5,4},{6,7},{7,6},{8,9},{9,8},{10,11... | collective-permute-start | bytes 3342344 | tf_op jit(solution)/shard_map/ppermute | solution.py:490
  33.3 19.8 %collective-permute-start.7 = (bf16[128,896]{1,0:T(8,128)(2,1)S(1)}, bf16[128,896]{1,0:T(8,128)(2,1)S(1)}, u32[]{:S(2)}, u32[]{:S(2)}) collective-permute-start(bf16[128,896]{1,0:T(8,128)(2,1)S(1)} %copy-done.24), channel_id=1, source_target_pairs={{12,8},{8,4},{13,9},{9,5},{2,6},{6,10},{3,7},{7,11},{28,24},{24,20... | collective-permute-start | bytes 688136 | tf_op jit(solution)/shard_map/ppermute | solution.py:502
  35.9 20.9 %collective-permute-start.5 = (bf16[128,1152]{1,0:T(8,128)(2,1)}, bf16[128,1152]{1,0:T(8,128)(2,1)S(1)}, u32[]{:S(2)}, u32[]{:S(2)}) collective-permute-start(bf16[128,1152]{1,0:T(8,128)(2,1)} %add_convert_fusion.6.refs_1_), channel_id=1, source_target_pairs={{12,8},{8,4},{13,9},{9,5},{2,6},{6,10},{3,7},{7,11},{28,24},{24,20... | collective-permute-start | bytes 884744 | tf_op jit(solution)/shard_map/ppermute | solution.py:502
  38.8 21.0 %copy-start.16 = (bf16[256,128]{1,0:T(8,128)(2,1)S(1)}, bf16[256,128]{1,0:T(8,128)(2,1)}, u32[]{:S(2)}) copy-start(bf16[256,128]{1,0:T(8,128)(2,1)} %copy-done.15) | copy-start | bytes 196612
  54.8 15.7 %collective-permute-start.12 = (bf16[128,896]{1,0:T(8,128)(2,1)}, bf16[128,896]{1,0:T(8,128)(2,1)}, u32[]{:S(2)}, u32[]{:S(2)}) collective-permute-start(bf16[128,896]{1,0:T(8,128)(2,1)} %add_convert_fusion.12.refs_8_.refs_1_), channel_id=1, source_target_pairs={{12,8},{8,4},{4,0},{13,9},{9,5},{2,6},{6,10},{3,7},{7,11},{11,15},... | collective-permute-start | bytes 688136 | tf_op jit(solution)/shard_map/ppermute | solution.py:502
  57.8 9.2 %copy-start.9 = (bf16[128,1152]{1,0:T(8,128)(2,1)}, bf16[128,1152]{1,0:T(8,128)(2,1)S(1)}, u32[]{:S(2)}) copy-start(bf16[128,1152]{1,0:T(8,128)(2,1)S(1)} %add_convert_fusion.5.refs_7_.refs_0_) | copy-start | bytes 884740
  57.8 16.5 %collective-permute-start.6 = (bf16[128,1152]{1,0:T(8,128)(2,1)S(1)}, bf16[128,1152]{1,0:T(8,128)(2,1)}, u32[]{:S(2)}, u32[]{:S(2)}) collective-permute-start(bf16[128,1152]{1,0:T(8,128)(2,1)S(1)} %add_convert_fusion.5.refs_7_.refs_0_), channel_id=1, source_target_pairs={{12,8},{8,4},{4,0},{13,9},{9,5},{2,6},{6,10},{3,7},{7,11},{11,15},... | collective-permute-start | bytes 884744 | tf_op jit(solution)/shard_map/ppermute | solution.py:502
  61.0 9.5 %copy-start = (bf16[768,2048]{1,0:T(8,128)(2,1)S(1)}, bf16[768,2048]{1,0:T(8,128)(2,1)}, u32[]{:S(2)}) copy-start(bf16[768,2048]{1,0:T(8,128)(2,1)} %shard_map.77.refs_1_) | copy-start | bytes 9437188
  67.1 11.9 %collective-permute-start.9 = (bf16[256,128]{1,0:T(8,128)(2,1)}, bf16[256,128]{1,0:T(8,128)(2,1)S(1)}, u32[]{:S(2)}, u32[]{:S(2)}) collective-permute-start(bf16[256,128]{1,0:T(8,128)(2,1)} %shard_map.78.refs_1_.refs_0_), channel_id=1, source_target_pairs={{0,4},{4,0},{8,12},{12,8},{1,5},{5,1},{9,13},{13,9},{2,6},{6,2},{1... | collective-permute-start | bytes 196616 | tf_op jit(solution)/shard_map/ppermute | solution.py:607
  69.3 9.8 %collective-permute-start.10 = (bf16[256,128]{1,0:T(8,128)(2,1)}, bf16[256,128]{1,0:T(8,128)(2,1)}, u32[]{:S(2)}, u32[]{:S(2)}) collective-permute-start(bf16[256,128]{1,0:T(8,128)(2,1)} %shard_map.78.refs_1_.refs_0_), channel_id=1, source_target_pairs={{0,8},{4,12},{8,0},{12,4},{1,9},{5,13},{9,1},{13,5},{2,10},{6,14},... | collective-permute-start | bytes 196616 | tf_op jit(solution)/shard_map/ppermute | solution.py:607
  69.3 9.8 %collective-permute-start.11 = (bf16[256,128]{1,0:T(8,128)(2,1)}, bf16[256,128]{1,0:T(8,128)(2,1)}, u32[]{:S(2)}, u32[]{:S(2)}) collective-permute-start(bf16[256,128]{1,0:T(8,128)(2,1)} %shard_map.78.refs_1_.refs_0_), channel_id=1, source_target_pairs={{0,12},{4,8},{8,4},{12,0},{1,13},{5,9},{9,5},{13,1},{2,14},{6,10},... | collective-permute-start | bytes 196616 | tf_op jit(solution)/shard_map/ppermute | solution.py:607
  72.2 14.8 %collective-permute-start.13 = (bf16[128,896]{1,0:T(8,128)(2,1)}, bf16[128,896]{1,0:T(8,128)(2,1)}, u32[]{:S(2)}, u32[]{:S(2)}) collective-permute-start(bf16[128,896]{1,0:T(8,128)(2,1)} %add_convert_fusion.11.refs_6_.refs_3_), channel_id=1, source_target_pairs={{12,8},{8,4},{4,0},{13,9},{9,5},{2,6},{6,10},{3,7},{7,11},{11,15},... | collective-permute-start | bytes 688136 | tf_op jit(solution)/shard_map/ppermute | solution.py:502
  75.4 10.8 %copy-start.7 = (bf16[128,1152]{1,0:T(8,128)(2,1)}, bf16[128,1152]{1,0:T(8,128)(2,1)S(1)}, u32[]{:S(2)}) copy-start(bf16[128,1152]{1,0:T(8,128)(2,1)S(1)} %add_convert_fusion.4.refs_5_.refs_2_) | copy-start | bytes 884740
  75.4 13.5 %collective-permute-start.8 = (bf16[128,1152]{1,0:T(8,128)(2,1)S(1)}, bf16[128,1152]{1,0:T(8,128)(2,1)}, u32[]{:S(2)}, u32[]{:S(2)}) collective-permute-start(bf16[128,1152]{1,0:T(8,128)(2,1)S(1)} %add_convert_fusion.4.refs_5_.refs_2_), channel_id=1, source_target_pairs={{12,8},{8,4},{4,0},{13,9},{9,5},{2,6},{6,10},{3,7},{7,11},{11,15},... | collective-permute-start | bytes 884744 | tf_op jit(solution)/shard_map/ppermute | solution.py:502
  90.7 6.5 %copy-start.6 = (bf16[128,1152]{1,0:T(8,128)(2,1)S(1)}, bf16[128,1152]{1,0:T(8,128)(2,1)}, u32[]{:S(2)}) copy-start(bf16[128,1152]{1,0:T(8,128)(2,1)} %add_convert_fusion.3.refs_1_.refs_0_) | copy-start | bytes 884740
  90.7 38.6 %collective-permute-start.17 = (bf16[512,2048]{1,0:T(8,128)(2,1)}, bf16[512,2048]{1,0:T(8,128)(2,1)}, u32[]{:S(2)}, u32[]{:S(2)}) collective-permute-start(bf16[512,2048]{1,0:T(8,128)(2,1)} %shard_map.83), channel_id=1, source_target_pairs={{1,5},{14,10},{17,21},{30,26}} | collective-permute-start | bytes 6291464 | tf_op jit(solution)/shard_map/ppermute | solution.py:502
  92.9 15.7 %collective-permute-start.15 = (bf16[128,2048]{1,0:T(8,128)(2,1)}, bf16[128,2048]{1,0:T(8,128)(2,1)}, u32[]{:S(2)}, u32[]{:S(2)}) collective-permute-start(bf16[128,2048]{1,0:T(8,128)(2,1)} %copy-done.22), channel_id=1, source_target_pairs={{0,1},{1,0},{2,3},{3,2},{4,5},{5,4},{6,7},{7,6},{8,9},{9,8},{10,11... | collective-permute-start | bytes 1572872 | tf_op jit(solution)/shard_map/ppermute | solution.py:490
  95.3 9.4 %collective-permute-start.16 = (bf16[128,896]{1,0:T(8,128)(2,1)}, bf16[128,896]{1,0:T(8,128)(2,1)}, u32[]{:S(2)}, u32[]{:S(2)}) collective-permute-start(bf16[128,896]{1,0:T(8,128)(2,1)} %add_convert_fusion.10.refs_2_.refs_1_), channel_id=1, source_target_pairs={{12,8},{8,4},{4,0},{13,9},{9,5},{2,6},{6,10},{3,7},{7,11},{11,15},... | collective-permute-start | bytes 688136 | tf_op jit(solution)/shard_map/ppermute | solution.py:502
  97.3 13.8 %collective-permute-start.14 = (bf16[128,1152]{1,0:T(8,128)(2,1)S(1)}, bf16[128,1152]{1,0:T(8,128)(2,1)}, u32[]{:S(2)}, u32[]{:S(2)}) collective-permute-start(bf16[128,1152]{1,0:T(8,128)(2,1)S(1)} %copy-done.6), channel_id=1, source_target_pairs={{12,8},{8,4},{4,0},{13,9},{9,5},{2,6},{6,10},{3,7},{7,11},{11,15},... | collective-permute-start | bytes 884744 | tf_op jit(solution)/shard_map/ppermute | solution.py:502
  99.2 20.2 %collective-permute-start.20 = (bf16[128,2048]{1,0:T(8,128)(2,1)}, bf16[128,2048]{1,0:T(8,128)(2,1)}, u32[]{:S(2)}, u32[]{:S(2)}) collective-permute-start(bf16[128,2048]{1,0:T(8,128)(2,1)} %get-tuple-element.13), channel_id=1, source_target_pairs={{0,2},{1,3},{2,0},{3,1},{4,6},{5,7},{6,4},{7,5},{8,10},{9,11},{10,... | collective-permute-start | bytes 1572872 | tf_op jit(solution)/shard_map/ppermute | solution.py:490
  106.5 9.6 %collective-permute-start.21 = (bf16[128,896]{1,0:T(8,128)(2,1)}, bf16[128,896]{1,0:T(8,128)(2,1)}, u32[]{:S(2)}, u32[]{:S(2)}) collective-permute-start(bf16[128,896]{1,0:T(8,128)(2,1)} %add_convert_fusion.9.refs_3_.refs_2_), channel_id=1, source_target_pairs={{12,8},{8,4},{4,0},{13,9},{9,5},{2,6},{6,10},{3,7},{7,11},{11,15},... | collective-permute-start | bytes 688136 | tf_op jit(solution)/shard_map/ppermute | solution.py:502
  112.9 9.9 %collective-permute-start.19 = (bf16[128,1152]{1,0:T(8,128)(2,1)}, bf16[128,1152]{1,0:T(8,128)(2,1)}, u32[]{:S(2)}, u32[]{:S(2)}) collective-permute-start(bf16[128,1152]{1,0:T(8,128)(2,1)} %add_convert_fusion.2.refs_2_.refs_1_), channel_id=1, source_target_pairs={{12,8},{8,4},{4,0},{13,9},{9,5},{2,6},{6,10},{3,7},{7,11},{11,15},... | collective-permute-start | bytes 884744 | tf_op jit(solution)/shard_map/ppermute | solution.py:502
  116.0 18.6 %collective-permute-start.23 = (bf16[128,2048]{1,0:T(8,128)(2,1)}, bf16[128,2048]{1,0:T(8,128)(2,1)}, u32[]{:S(2)}, u32[]{:S(2)}) collective-permute-start(bf16[128,2048]{1,0:T(8,128)(2,1)} %get-tuple-element.14), channel_id=1, source_target_pairs={{0,3},{1,2},{2,1},{3,0},{4,7},{5,6},{6,5},{7,4},{8,11},{9,10},{10,... | collective-permute-start | bytes 1572872 | tf_op jit(solution)/shard_map/ppermute | solution.py:490
  116.1 19.7 %collective-permute-start.25 = (bf16[256,2048]{1,0:T(8,128)(2,1)}, bf16[256,2048]{1,0:T(8,128)(2,1)}, u32[]{:S(2)}, u32[]{:S(2)}) collective-permute-start(bf16[256,2048]{1,0:T(8,128)(2,1)} %shard_map.88), channel_id=1, source_target_pairs={{1,5},{14,10},{17,21},{30,26}} | collective-permute-start | bytes 3145736 | tf_op jit(solution)/shard_map/ppermute | solution.py:502
  119.4 8.2 %collective-permute-start.24 = (bf16[128,896]{1,0:T(8,128)(2,1)}, bf16[128,896]{1,0:T(8,128)(2,1)}, u32[]{:S(2)}, u32[]{:S(2)}) collective-permute-start(bf16[128,896]{1,0:T(8,128)(2,1)} %add_convert_fusion.8.refs_1_), channel_id=1, source_target_pairs={{8,4},{4,0},{9,5},{6,10},{7,11},{11,15},{24,20},{20,16},{25,21},{2... | collective-permute-start | bytes 688136 | tf_op jit(solution)/shard_map/ppermute | solution.py:502
  124.5 10.2 %collective-permute-start.22 = (bf16[128,1152]{1,0:T(8,128)(2,1)}, bf16[128,1152]{1,0:T(8,128)(2,1)}, u32[]{:S(2)}, u32[]{:S(2)}) collective-permute-start(bf16[128,1152]{1,0:T(8,128)(2,1)} %add_convert_fusion.1.refs_0_), channel_id=1, source_target_pairs={{8,4},{4,0},{9,5},{6,10},{7,11},{11,15},{24,20},{20,16},{25,21},{2... | collective-permute-start | bytes 884744 | tf_op jit(solution)/shard_map/ppermute | solution.py:502
  132.9 5.5 %copy-start.8 = (bf16[128,1152]{1,0:T(8,128)(2,1)S(1)}, bf16[128,1152]{1,0:T(8,128)(2,1)}, u32[]{:S(2)}) copy-start(bf16[128,1152]{1,0:T(8,128)(2,1)} %copy-done.7) | copy-start | bytes 884740
  132.9 10.0 %collective-permute-start.18 = (bf16[256,2048]{1,0:T(8,128)(2,1)}, bf16[256,2048]{1,0:T(8,128)(2,1)}, u32[]{:S(2)}, u32[]{:S(2)}) collective-permute-start(bf16[256,2048]{1,0:T(8,128)(2,1)} %shard_map.84.own_ref.refs_1_), channel_id=1, source_target_pairs={{0,2},{5,7},{10,8},{15,13},{16,18},{21,23},{26,24},{31,29}} | collective-permute-start | bytes 3145736 | tf_op jit(solution)/shard_map/ppermute | solution.py:502
  134.7 3.7 %copy-start.10 = (bf16[128,1152]{1,0:T(8,128)(2,1)S(1)}, bf16[128,1152]{1,0:T(8,128)(2,1)}, u32[]{:S(2)}) copy-start(bf16[128,1152]{1,0:T(8,128)(2,1)} %copy-done.9) | copy-start | bytes 884740
  140.1 5.6 %collective-permute-start.27 = (bf16[256,2048]{1,0:T(8,128)(2,1)S(1)}, bf16[256,2048]{1,0:T(8,128)(2,1)S(1)}, u32[]{:S(2)}, u32[]{:S(2)}) collective-permute-start(bf16[256,2048]{1,0:T(8,128)(2,1)S(1)} %shard_map.90.refs_7_), channel_id=1, source_target_pairs={{0,1},{5,4},{10,11},{15,14},{2,3},{7,6},{8,9},{13,12},{16,17},{21,... | collective-permute-start | bytes 3145736 | tf_op jit(solution)/shard_map/ppermute | solution.py:502
  141.4 8.2 %collective-permute-start.26 = (bf16[256,2048]{1,0:T(8,128)(2,1)S(1)}, bf16[256,2048]{1,0:T(8,128)(2,1)S(1)}, u32[]{:S(2)}, u32[]{:S(2)}) collective-permute-start(bf16[256,2048]{1,0:T(8,128)(2,1)S(1)} %get-tuple-element.15.own_ref), channel_id=1, source_target_pairs={{0,2},{5,7},{10,8},{15,13},{16,18},{21,23},{26,24},{31,29}} | collective-permute-start | bytes 3145736 | tf_op jit(solution)/shard_map/ppermute | solution.py:502
  142.2 2.7 %collective-permute-start.28 = (bf16[128,2048]{1,0:T(8,128)(2,1)S(1)}, bf16[128,2048]{1,0:T(8,128)(2,1)S(1)}, u32[]{:S(2)}, u32[]{:S(2)}) collective-permute-start(bf16[128,2048]{1,0:T(8,128)(2,1)S(1)} %get-tuple-element.16.refs_6_), channel_id=1, source_target_pairs={{4,0},{11,15},{20,16},{27,31}} | collective-permute-start | bytes 1572872 | tf_op jit(solution)/shard_map/ppermute | solution.py:502
  143.5 2.3 %copy-start.12 = (bf16[128,2048]{1,0:T(8,128)(2,1)S(1)}, bf16[128,2048]{1,0:T(8,128)(2,1)}, u32[]{:S(2)}) copy-start(bf16[128,2048]{1,0:T(8,128)(2,1)} %copy-done.11) | copy-start | bytes 1572868
  143.5 12.7 %collective-permute-start.30 = (bf16[256,2048]{1,0:T(8,128)(2,1)}, bf16[256,2048]{1,0:T(8,128)(2,1)S(1)}, u32[]{:S(2)}, u32[]{:S(2)}) collective-permute-start(bf16[256,2048]{1,0:T(8,128)(2,1)} %shard_map.85.refs_2_.refs_7_), channel_id=1, source_target_pairs={{0,1},{5,4},{10,11},{15,14},{2,3},{7,6},{8,9},{13,12},{16,17},{21,... | collective-permute-start | bytes 3145736 | tf_op jit(solution)/shard_map/ppermute | solution.py:502
  145.0 6.5 %collective-permute-start.29 = (bf16[128,2048]{1,0:T(8,128)(2,1)S(1)}, bf16[128,2048]{1,0:T(8,128)(2,1)S(1)}, u32[]{:S(2)}, u32[]{:S(2)}) collective-permute-start(bf16[128,2048]{1,0:T(8,128)(2,1)S(1)} %shard_map.91.refs_13_.own_ref), channel_id=1, source_target_pairs={{0,2},{5,7},{10,8},{15,13},{16,18},{21,23},{26,24},{31,29}} | collective-permute-start | bytes 1572872 | tf_op jit(solution)/shard_map/ppermute | solution.py:502
  150.2 16.7 %collective-permute-start.31 = (bf16[256,2048]{1,0:T(8,128)(2,1)S(1)}, bf16[256,2048]{1,0:T(8,128)(2,1)S(1)}, u32[]{:S(2)}, u32[]{:S(2)}) collective-permute-start(bf16[256,2048]{1,0:T(8,128)(2,1)S(1)} %shard_map.93.refs_8_), channel_id=1, source_target_pairs={{0,1},{5,4},{10,11},{15,14},{2,3},{7,6},{8,9},{13,12},{16,17},{21,... | collective-permute-start | bytes 3145736 | tf_op jit(solution)/shard_map/ppermute | solution.py:502
  152.1 19.7 %collective-permute-start.32 = (bf16[128,2048]{1,0:T(8,128)(2,1)S(1)}, bf16[128,2048]{1,0:T(8,128)(2,1)S(1)}, u32[]{:S(2)}, u32[]{:S(2)}) collective-permute-start(bf16[128,2048]{1,0:T(8,128)(2,1)S(1)} %shard_map.94.refs_9_), channel_id=1, source_target_pairs={{0,1},{5,4},{10,11},{15,14},{2,3},{7,6},{8,9},{13,12},{16,17},{21,... | collective-permute-start | bytes 1572872 | tf_op jit(solution)/shard_map/ppermute | solution.py:502
  (10 other events, 10.4 us)

commit v5 on v4

--- a/solution.py
+++ b/solution.py
@@ -115,16 +115,15 @@
     )(value, *deps)
 
 
-def project_kernel(first, blocks, block_rows, tokens, span, *refs):
+def project_kernel(first, blocks, block_rows, tokens, *refs):
     meta_ref, len_refs = refs[0], refs[1 : 1 + blocks]
     x_refs, w_ref = refs[1 + blocks : 1 + 2 * blocks], refs[1 + 2 * blocks]
     out_ref, packed = refs[-2], refs[-1]
-    rows = packed.shape[0]
+    rows, width = packed.shape[0], block_rows
 
     @pl.when(pl.program_id(0) == 0)
     def _():
-        s, _, _, u = where_am_i(meta_ref)
-        width = block_rows
+        s = meta_ref[0]
         lead = (s % 2) == 0
         sums = [total_of(r) for r in len_refs]
         starts = [jnp.where(lead, 0, sums[1]), jnp.where(lead, sums[0], 0)]
@@ -136,7 +135,7 @@
         wanted = lax.broadcasted_iota(jnp.int32, (rows, width), 0)
         picks = []
         for b in range(blocks):
-            start = starts[b] + u * span - first
+            start = starts[b] - first
             spot = jnp.full((1, width), -1, jnp.int32)
             for q in range(width // tokens):
                 length = len_refs[b][q]
@@ -151,25 +150,27 @@
     out_ref[...] = jnp.dot(packed[...], w_ref[...], preferred_element_type=F32).astype(BF16)
 
 
-def project(meta, lens, xs, w, first, rows, span, deps=(), tile=512):
+def project(meta, lens, xs, w, first, rows, total, place, buffer=None, deps=(), tile=512):
     depth, cols = w.shape
     blocks = len(xs)
-    block_rows = lens[0].shape[0] * SLOTS
     tokens = SLOTS
+    width = lens[0].shape[0] * tokens
     smem = pl.BlockSpec(memory_space=pltpu.SMEM)
-    return pl.pallas_call(
-        functools.partial(project_kernel, first, blocks, block_rows, tokens, span),
+    extra = ([] if buffer is None else [buffer]) + list(deps)
+    return pl.pallas_call(
+        functools.partial(project_kernel, first, blocks, width, tokens),
         grid=(cols // tile,),
         in_specs=[smem] * (1 + blocks)
-        + [pl.BlockSpec((block_rows, depth), lambda j: (0, 0))] * blocks
+        + [pl.BlockSpec((width, depth), lambda j: (0, 0))] * blocks
         + [pl.BlockSpec((depth, tile), lambda j: (0, j))]
-        + [pl.BlockSpec(memory_space=pl.ANY)] * len(deps),
-        out_specs=pl.BlockSpec((rows, tile), lambda j: (0, j)),
-        out_shape=jax.ShapeDtypeStruct((rows, cols), BF16),
+        + [pl.BlockSpec(memory_space=pl.ANY)] * len(extra),
+        out_specs=pl.BlockSpec((rows, tile), lambda j: (place, j)),
+        out_shape=jax.ShapeDtypeStruct((total, cols), BF16),
         scratch_shapes=[pltpu.VMEM((rows, depth), BF16)],
+        input_output_aliases={} if buffer is None else {2 + 2 * blocks: 0},
         compiler_params=pltpu.CompilerParams(vmem_limit_bytes=VMEM_LIMIT),
         cost_estimate=LIGHT,
-    )(meta, *lens, *xs, w, *deps)
+    )(meta, *lens, *xs, w, *extra)
 
 
 def visit(meta_ref, req_ref, slot_ref, flip, held, requests, tokens, act):
@@ -541,9 +542,14 @@
     final, carry, parts = {}, [None] * STREAMS, {}
 
     def chunk_of(source, k, j):
-        at = jnp.clip(k - u, 0, steps - 1) * span
+        c = jnp.clip(k - u, 0, steps - 1)
+        at = jnp.where(c < early, c + steps - early, c - early) * span
         lo, hi = bounds[j]
         return lax.dynamic_slice(source, (at, lo), (span, hi - lo))
+
+    def first_chunk(c, j):
+        at = (c + steps - early) * span
+        return parts[0][at : at + span, bounds[j][0] : bounds[j][1]]
 
     def pairs_of(k):
         return [
@@ -555,16 +561,18 @@
 
     last_pairs = pairs_of(steps + 1)
 
-    def chain_step(k, *deps):
+    def chain_step(k, *deps, both=False):
         pairs = pairs_of(k)
         for j in range(STREAMS):
             if k < early:
-                value = parts[0][k * span : (k + 1) * span, bounds[j][0] : bounds[j][1]]
+                value = first_chunk(0, j)
+                for c in range(1, k + 1):
+                    value = jnp.where(k - u >= c, first_chunk(c, j), value)
             else:
                 value = chunk_of(parts[1], k, j)
             if carry[j] is not None:
                 came = carry[j]
-                if deps and not j:
+                if deps and (both or not j):
                     came = after(came, *deps)
                 total = value.astype(F32) + came.astype(F32)
                 value = total.astype(BF16)
@@ -589,7 +597,7 @@
         gots.append(on_mesh(value, beside))
 
     u_vec = u.astype(jnp.int32).reshape(1)
-    parts[0] = project(meta, lens[:2], xs[:2], w, 0, early * span, span)
+    parts[0] = project(meta, lens[:2], xs[:2], w, 0, rows, live, live // rows - 1)
     chain_step(0)
     low = low_rank(
         meta, req, slot, xs[:2], (0, 1), down_t, None, held, rank, tokens, capacity, (parts[0],)
@@ -599,37 +607,39 @@
     x_fsib = on_store(x_far, 1)
     xs = [x_me, x_sib, x_far, x_fsib]
     lens = lens + [lengths_of(x_far), lengths_of(x_fsib)]
-    parts[1] = project(meta, lens, xs, w, 0, live, 0)
+    parts[1] = project(
+        meta, lens, xs, w, rows, live - rows, live, 0, parts[0], (final[1, 0], final[1, 1])
+    )
     chain_step(2)
     low = low_rank(
         meta, req, slot, xs[2:], (2, 3), down_t, low, held, rank, tokens, capacity, (final[2, 0], final[2, 1])
     )
-    lows = [low] + [lax.ppermute(low, "tensor", [(i, i ^ f) for i in range(4)]) for f in (1, 2, 3)]
+    lows = [low] + [lax.ppermute(low, "tensor", [(i, i ^ f) for i in range(4)]) for f in (3, 1, 2)]
     chain_step(3, low)
     delta = up_project(
         meta, req, slot, lows, up_2d, held, rank, tokens, capacity, requests, (final[3, 0], final[3, 1])
     )
     deltas = [delta[0]] + [on_store(delta[i], i) for i in (1, 2, 3)]
     chain_step(4, delta[0])
-    cut = steps - 2
 
     def send_back(low, high, *deps):
-        rows_of = after(parts[1][low * span : (high + 1) * span], *deps)
+        at = (low - early if low >= early else low + steps - early) * span
+        rows_of = after(parts[1][at : at + (high + 1 - low) * span], *deps)
         return on_mesh(rows_of, back_pairs), low, high
 
-    back = [send_back(0, cut - 1, final[4, 0], final[4, 1])]
+    back = [send_back(early, steps - 1, final[4, 0], final[4, 1])]
     chain_step(5, deltas[1])
-    back.append(send_back(cut, steps - 1, final[5, 0], final[5, 1]))
+    back.append(send_back(0, early - 1, final[5, 0], final[5, 1]))
     chain_step(6, deltas[2])
     (two,) = merged(4, 6)
-    chain_step(7, two, deltas[3])
+    (one,) = merged(2, 4, deps=(two,))
+    hand_on(one)
+    chain_step(7, two, deltas[3], one, both=True)
     two = keep(meta, *cross(two))
     three, last = merged(6, 8, True)
     came = on_mesh(last, last_pairs)
-    (one,) = merged(2, 4, deps=(last,))
     three = cross(three)
-    hand_on(one)
-    (four,) = merge(u_vec, [came], [(parts[1], 0, steps - 1)], [steps + 2], deps=(two,))
+    (four,) = merge(u_vec, [came], [(parts[1], early, steps - 1)], [steps + 2], deps=(two,))
     hand_on(two)
     partial = finish(
         meta, req, slot, lens, values[:1], gots[:1], 2 * span, deltas, None, F32, span, held, tokens, capacity,

time: 178 us -> 176 us (0.989)
  waiting for transfers between devices: 32.2 us -> 29.6 us
    ppermute x24, waiting for transfers between devices: 31 us -> 28.2 us  [on_mesh(): lax.ppermute(value, ('tensor', 'store'), [(a * 4 + b, c * 4 + d) for (a,...]
    pallas_call x2, Pallas kernels: 21.4 us -> 19 us  [project(): pl.pallas_call(functools.partial(project_kernel, first, blocks, width, to...]
    slice x4, local copies, waits for them, and re-layouts: 2.59 us -> 4.63 us  [the longest x2 2.69 us: send_back(): rows_of = after(parts[1][at:at + (high + 1 - low) * span], *deps)]
    unnamed x50 -> x44, local copies, waits for them, and re-layouts: 8.52 us -> 7.76 us
  transfers between devices with their start and end apart: 33 -> 33, of which waited for: 9 -> 6; matrix products, arithmetic and copies ran while one was open for 14% -> 16% of each run, Pallas kernels for 29% -> 29%
where the time goes in v5:
time: 176 us; the launch traced here: 174 us
  Pallas kernels  56.5 us (32%)
  starting transfers between devices  52.2 us (30%)
  waiting for transfers between devices  29.6 us (17%)
  other arithmetic  23 us (13%)
  local copies, waits for them, and re-layouts  12.4 us (7%)
    ppermute x24, starting transfers between devices, on_mesh(): lax.ppermute(value, ('tensor', 'store'), [(a * 4 + b, c * 4 + d) for (a,...  43.3 us
    ppermute x24, waiting for transfers between devices, on_mesh(): lax.ppermute(value, ('tensor', 'store'), [(a * 4 + b, c * 4 + d) for (a,...  28.2 us
    convert_element_type x14, other arithmetic, chain_step(): value = total.astype(BF16)  21.5 us
    pallas_call x2, Pallas kernels, project(): pl.pallas_call(functools.partial(project_kernel, first, blocks, width, to...  19 us
    pallas_call x2, Pallas kernels, low_rank(): pl.pallas_call(functools.partial(low_kernel, flips, before is not None, h...  11.7 us
    pallas_call x2, Pallas kernels, finish(): pl.pallas_call(functools.partial(finish_kernel, len(sizes), sizes, first,...  8.21 us
    unnamed x44, local copies, waits for them, and re-layouts  7.76 us
    pallas_call x1, Pallas kernels, up_project(): pl.pallas_call(functools.partial(up_kernel, len(deps), held, rank, reques...  7.28 us
  transfers between devices with their start and end apart: 33, of which 6 were waited for; matrix products, arithmetic and copies ran while one was open for 16% of the time, Pallas kernels for 29%

profile of v5, /device:TPU:21, one launch (start us, length us, event | category | flops | bytes accessed | tf_op | source)
XLA Modules:
  0.0 174.2 jit_solution(13129792977634299817)
XLA Ops:
  1.9 1.6 shard_map.73
  5.5 1.3 collective-permute-done.refs_4_.refs_6_
  9.0 7.5 %shard_map.74.refs_6_.refs_10_ = bf16[768,2048]{1,0:T(8,128)(2,1)} custom-call(s32[2]{0:T(128)S(1)} %pad_add_fusion.refs_0_.meta_ref, s32[16]{0:T(128)S(1)} %copy-done.19, s32[16]{0:T(128)S(1)} %fusion.2.refs_2_.refs_4_, bf16[256,2048]{1,0:T(8,128)(2,1)S(1)} %bitcast.25, bf16[272,2048]{1,0:T(8,128)(2,1)} %copy-done.21, bf16[2048,2048]{1,0:T(8,128)(2,1)} %refs_9_.1), custom_call_target="tpu_custom_call" | custom-call | tf_op jit(solution)/shard_map/pallas_call | solution.py:160
  17.5 1.3 collective-permute-start.3
  19.8 1.3 collective-permute-start.2
  21.1 5.3 %shard_map.75.refs_3_.refs_6_ = bf16[256,128]{1,0:T(8,128)(2,1)S(1)} custom-call(s32[2]{0:T(128)S(1)} %pad_add_fusion.refs_0_.meta_ref, s32[64]{0:T(128)S(1)} %copy-done.17, s32[64]{0:T(128)S(1)} %copy-done.18, bf16[256,2048]{1,0:T(8,128)(2,1)S(1)} %bitcast.26, bf16[272,2048]{1,0:T(8,128)(2,1)} %copy-done.21, bf16[1024,2048]{1,0:T(8,128)(2,1)} %bitcast.28, ...), custom_call_target="tpu_custom_call" | custom-call | tf_op jit(solution)/shard_map/pallas_call | solution.py:239
  27.0 1.8 %add_convert_fusion.13.refs_2_.refs_12_ = bf16[128,896]{1,0:T(8,128)(2,1)} fusion(bf16[128,896]{1,0:T(8,128)(2,1)S(1)} %collective-permute-done.3, bf16[768,2048]{1,0:T(8,128)(2,1)} %shard_map.74.refs_6_.refs_10_, pred[]{:T(512)S(6)} %ge.4), kind=kLoop, calls=%fused_computation.13 | loop fusion | flops 573440 | bytes 917505 | tf_op jit(solution)/shard_map/convert_element_type | solution.py:578
  28.9 3.7 %collective-permute-done.2 = bf16[128,1152]{1,0:T(8,128)(2,1)S(1)} collective-permute-done((bf16[128,1152]{1,0:T(8,128)(2,1)S(1)}, bf16[128,1152]{1,0:T(8,128)(2,1)S(1)}, u32[]{:S(2)}, u32[]{:S(2)}) %collective-permute-start.2) | collective-permute-done | bytes 294944 | tf_op jit(solution)/shard_map/ppermute | solution.py:503
  32.5 1.9 %add_convert_fusion.6.refs_1_.refs_11_ = bf16[128,1152]{1,0:T(8,128)(2,1)} fusion(bf16[128,1152]{1,0:T(8,128)(2,1)S(1)} %collective-permute-done.2, bf16[768,2048]{1,0:T(8,128)(2,1)} %shard_map.74.refs_6_.refs_10_, pred[]{:T(512)S(6)} %ge.4), kind=kLoop, calls=%fused_computation.6 | loop fusion | flops 737280 | bytes 1179649 | tf_op jit(solution)/shard_map/convert_element_type | solution.py:578
  35.6 1.9 %collective-permute-start.7 = (bf16[128,896]{1,0:T(8,128)(2,1)S(1)}, bf16[128,896]{1,0:T(8,128)(2,1)S(1)}, u32[]{:S(2)}, u32[]{:S(2)}) collective-permute-start(bf16[128,896]{1,0:T(8,128)(2,1)S(1)} %copy-done.12), channel_id=1, source_target_pairs={{12,8},{8,4},{13,9},{9,5},{2,6},{6,10},{3,7},{7,11},{28,24},{24,20... | collective-permute-start | bytes 688136 | tf_op jit(solution)/shard_map/ppermute | solution.py:503
  38.2 1.9 %collective-permute-start.5 = (bf16[128,1152]{1,0:T(8,128)(2,1)}, bf16[128,1152]{1,0:T(8,128)(2,1)S(1)}, u32[]{:S(2)}, u32[]{:S(2)}) collective-permute-start(bf16[128,1152]{1,0:T(8,128)(2,1)} %add_convert_fusion.6.refs_1_.refs_11_), channel_id=1, source_target_pairs={{12,8},{8,4},{13,9},{9,5},{2,6},{6,10},{3,7},{7,11},{28,24},{24,20... | collective-permute-start | bytes 884744 | tf_op jit(solution)/shard_map/ppermute | solution.py:503
  41.8 11.5 %shard_map.77.refs_1_ = bf16[768,2048]{1,0:T(8,128)(2,1)} custom-call(s32[2]{0:T(128)S(1)} %pad_add_fusion.refs_0_.meta_ref, s32[16]{0:T(128)S(1)} %copy-done.19, s32[16]{0:T(128)S(1)} %fusion.2.refs_2_.refs_4_, s32[16]{0:T(128)S(1)} %fusion.1.refs_3_.refs_5_, s32[16]{0:T(128)S(1)} %fusion.refs_4_.refs_6_, ...), custom_call_target="tpu_custom_call", output_to_operand_aliasing={{}: (10, {})} | custom-call | tf_op jit(solution)/shard_map/pallas_call | solution.py:160
  53.2 1.7 add_convert_fusion.12.refs_8_.refs_1_
  54.9 1.9 %collective-permute-start.12 = (bf16[128,896]{1,0:T(8,128)(2,1)}, bf16[128,896]{1,0:T(8,128)(2,1)}, u32[]{:S(2)}, u32[]{:S(2)}) collective-permute-start(bf16[128,896]{1,0:T(8,128)(2,1)} %add_convert_fusion.12.refs_8_.refs_1_), channel_id=1, source_target_pairs={{12,8},{8,4},{4,0},{13,9},{9,5},{2,6},{6,10},{3,7},{7,11},{11,15},... | collective-permute-start | bytes 688136 | tf_op jit(solution)/shard_map/ppermute | solution.py:503
  57.9 1.9 %collective-permute-start.6 = (bf16[128,1152]{1,0:T(8,128)(2,1)S(1)}, bf16[128,1152]{1,0:T(8,128)(2,1)}, u32[]{:S(2)}, u32[]{:S(2)}) collective-permute-start(bf16[128,1152]{1,0:T(8,128)(2,1)S(1)} %add_convert_fusion.5.refs_7_.refs_0_), channel_id=1, source_target_pairs={{12,8},{8,4},{4,0},{13,9},{9,5},{2,6},{6,10},{3,7},{7,11},{11,15},... | collective-permute-start | bytes 884744 | tf_op jit(solution)/shard_map/ppermute | solution.py:503
  59.9 6.4 %shard_map.78.refs_1_.refs_0_ = bf16[256,128]{1,0:T(8,128)(2,1)} custom-call(s32[2]{0:T(128)S(1)} %pad_add_fusion.refs_0_.meta_ref, s32[64]{0:T(128)S(1)} %copy-done.17, s32[64]{0:T(128)S(1)} %copy-done.18, bf16[272,2048]{1,0:T(8,128)(2,1)} %shard_map.76.refs_7_.refs_3_, bf16[272,2048]{1,0:T(8,128)(2,1)} %collective-permute-done.4.refs_8_.refs_4_, ...), custom_call_target="tpu_custom_call" | custom-call | tf_op jit(solution)/shard_map/pallas_call | solution.py:239
  66.3 2.2 %collective-permute-start.10 = (bf16[256,128]{1,0:T(8,128)(2,1)}, bf16[256,128]{1,0:T(8,128)(2,1)S(1)}, u32[]{:S(2)}, u32[]{:S(2)}) collective-permute-start(bf16[256,128]{1,0:T(8,128)(2,1)} %shard_map.78.refs_1_.refs_0_), channel_id=1, source_target_pairs={{0,4},{4,0},{8,12},{12,8},{1,5},{5,1},{9,13},{13,9},{2,6},{6,2},{1... | collective-permute-start | bytes 196616 | tf_op jit(solution)/shard_map/ppermute | solution.py:617
  69.7 1.7 add_convert_fusion.11.refs_6_.refs_3_
  71.4 2.1 %collective-permute-start.13 = (bf16[128,896]{1,0:T(8,128)(2,1)}, bf16[128,896]{1,0:T(8,128)(2,1)}, u32[]{:S(2)}, u32[]{:S(2)}) collective-permute-start(bf16[128,896]{1,0:T(8,128)(2,1)} %add_convert_fusion.11.refs_6_.refs_3_), channel_id=1, source_target_pairs={{12,8},{8,4},{4,0},{13,9},{9,5},{2,6},{6,10},{3,7},{7,11},{11,15},... | collective-permute-start | bytes 688136 | tf_op jit(solution)/shard_map/ppermute | solution.py:503
  74.6 2.1 %collective-permute-start.8 = (bf16[128,1152]{1,0:T(8,128)(2,1)S(1)}, bf16[128,1152]{1,0:T(8,128)(2,1)}, u32[]{:S(2)}, u32[]{:S(2)}) collective-permute-start(bf16[128,1152]{1,0:T(8,128)(2,1)S(1)} %add_convert_fusion.4.refs_5_.refs_2_), channel_id=1, source_target_pairs={{12,8},{8,4},{4,0},{13,9},{9,5},{2,6},{6,10},{3,7},{7,11},{11,15},... | collective-permute-start | bytes 884744 | tf_op jit(solution)/shard_map/ppermute | solution.py:503
  76.7 1.6 slice.45.refs_0_
  78.3 7.3 %shard_map.80 = (bf16[128,2048]{1,0:T(8,128)(2,1)S(1)}, bf16[128,2048]{1,0:T(8,128)(2,1)}, bf16[128,2048]{1,0:T(8,128)(2,1)}, bf16[128,2048]{1,0:T(8,128)(2,1)}) custom-call(s32[2]{0:T(128)S(1)} %pad_add_fusion.refs_0_.meta_ref, s32[64]{0:T(128)S(1)} %copy-done.17, s32[64]{0:T(128)S(1)} %copy-done.18, bf16[256,128]{1,0:T(8,128)(2,1)} %shard_map.78.refs_1_.refs_0_, ...), custom_call_target="tpu_custom_call" | custom-call | tf_op jit(solution)/shard_map/pallas_call | solution.py:290
  85.6 2.4 %collective-permute-start.15 = (bf16[128,2048]{1,0:T(8,128)(2,1)}, bf16[128,2048]{1,0:T(8,128)(2,1)}, u32[]{:S(2)}, u32[]{:S(2)}) collective-permute-start(bf16[128,2048]{1,0:T(8,128)(2,1)} %get-tuple-element.12), channel_id=1, source_target_pairs={{0,1},{1,0},{2,3},{3,2},{4,5},{5,4},{6,7},{7,6},{8,9},{9,8},{10,11... | collective-permute-start | bytes 1572872 | tf_op jit(solution)/shard_map/ppermute | solution.py:491
  88.0 1.7 add_convert_fusion.10.refs_2_.refs_1_
  89.7 1.8 %add_convert_fusion.3.refs_1_.refs_0_ = bf16[128,1152]{1,0:T(8,128)(2,1)} fusion(bf16[128,1152]{1,0:T(8,128)(2,1)} %shard_map.81, bf16[768,2048]{1,0:T(8,128)(2,1)S(1)} %copy-done, s32[]{:T(128)S(6)} %select_n.79), kind=kLoop, calls=%fused_computation.3 | loop fusion | flops 589824 | bytes 884740 | tf_op jit(solution)/shard_map/convert_element_type | solution.py:578
  91.5 2.1 %collective-permute-start.17 = (bf16[512,2048]{1,0:T(8,128)(2,1)}, bf16[512,2048]{1,0:T(8,128)(2,1)}, u32[]{:S(2)}, u32[]{:S(2)}) collective-permute-start(bf16[512,2048]{1,0:T(8,128)(2,1)} %shard_map.83), channel_id=1, source_target_pairs={{1,5},{14,10},{17,21},{30,26}} | collective-permute-start | bytes 6291464 | tf_op jit(solution)/shard_map/ppermute | solution.py:503
  93.6 1.9 %collective-permute-start.14 = (bf16[128,1152]{1,0:T(8,128)(2,1)S(1)}, bf16[128,1152]{1,0:T(8,128)(2,1)}, u32[]{:S(2)}, u32[]{:S(2)}) collective-permute-start(bf16[128,1152]{1,0:T(8,128)(2,1)S(1)} %copy-done.4), channel_id=1, source_target_pairs={{12,8},{8,4},{4,0},{13,9},{9,5},{2,6},{6,10},{3,7},{7,11},{11,15},... | collective-permute-start | bytes 884744 | tf_op jit(solution)/shard_map/ppermute | solution.py:503
  96.6 2.1 %collective-permute-start.16 = (bf16[128,896]{1,0:T(8,128)(2,1)}, bf16[128,896]{1,0:T(8,128)(2,1)}, u32[]{:S(2)}, u32[]{:S(2)}) collective-permute-start(bf16[128,896]{1,0:T(8,128)(2,1)} %add_convert_fusion.10.refs_2_.refs_1_), channel_id=1, source_target_pairs={{12,8},{8,4},{4,0},{13,9},{9,5},{2,6},{6,10},{3,7},{7,11},{11,15},... | collective-permute-start | bytes 688136 | tf_op jit(solution)/shard_map/ppermute | solution.py:503
  98.7 5.3 %collective-permute-done.14.refs_0_ = bf16[128,1152]{1,0:T(8,128)(2,1)} collective-permute-done((bf16[128,1152]{1,0:T(8,128)(2,1)S(1)}, bf16[128,1152]{1,0:T(8,128)(2,1)}, u32[]{:S(2)}, u32[]{:S(2)}) %collective-permute-start.14) | collective-permute-done | bytes 294944 | tf_op jit(solution)/shard_map/ppermute | solution.py:503
  104.1 1.8 %add_convert_fusion.2.refs_2_.refs_1_ = bf16[128,1152]{1,0:T(8,128)(2,1)} fusion(bf16[128,1152]{1,0:T(8,128)(2,1)} %shard_map.82, bf16[768,2048]{1,0:T(8,128)(2,1)S(1)} %copy-done, s32[]{:T(128)S(6)} %select_n.85), kind=kLoop, calls=%fused_computation.2 | loop fusion | flops 589824 | bytes 884740 | tf_op jit(solution)/shard_map/convert_element_type | solution.py:578
  105.8 2.2 %collective-permute-start.19 = (bf16[128,1152]{1,0:T(8,128)(2,1)}, bf16[128,1152]{1,0:T(8,128)(2,1)}, u32[]{:S(2)}, u32[]{:S(2)}) collective-permute-start(bf16[128,1152]{1,0:T(8,128)(2,1)} %add_convert_fusion.2.refs_2_.refs_1_), channel_id=1, source_target_pairs={{12,8},{8,4},{4,0},{13,9},{9,5},{2,6},{6,10},{3,7},{7,11},{11,15},... | collective-permute-start | bytes 884744 | tf_op jit(solution)/shard_map/ppermute | solution.py:503
  109.0 1.7 add_convert_fusion.9.refs_3_.refs_2_
  110.7 1.7 collective-permute-start.24
  112.3 3.1 %collective-permute-start.21 = (bf16[128,896]{1,0:T(8,128)(2,1)}, bf16[128,896]{1,0:T(8,128)(2,1)}, u32[]{:S(2)}, u32[]{:S(2)}) collective-permute-start(bf16[128,896]{1,0:T(8,128)(2,1)} %add_convert_fusion.9.refs_3_.refs_2_), channel_id=1, source_target_pairs={{12,8},{8,4},{4,0},{13,9},{9,5},{2,6},{6,10},{3,7},{7,11},{11,15},... | collective-permute-start | bytes 688136 | tf_op jit(solution)/shard_map/ppermute | solution.py:503
  115.5 1.8 %add_convert_fusion.1.refs_0_ = bf16[128,1152]{1,0:T(8,128)(2,1)} fusion(bf16[128,1152]{1,0:T(8,128)(2,1)} %shard_map.86, bf16[768,2048]{1,0:T(8,128)(2,1)S(1)} %copy-done, s32[]{:T(128)S(6)} %select_n.87), kind=kLoop, calls=%fused_computation.1 | loop fusion | flops 589824 | bytes 884740 | tf_op jit(solution)/shard_map/convert_element_type | solution.py:578
  117.2 2.9 %collective-permute-start.22 = (bf16[128,1152]{1,0:T(8,128)(2,1)}, bf16[128,1152]{1,0:T(8,128)(2,1)}, u32[]{:S(2)}, u32[]{:S(2)}) collective-permute-start(bf16[128,1152]{1,0:T(8,128)(2,1)} %add_convert_fusion.1.refs_0_), channel_id=1, source_target_pairs={{8,4},{4,0},{9,5},{6,10},{7,11},{11,15},{24,20},{20,16},{25,21},{2... | collective-permute-start | bytes 884744 | tf_op jit(solution)/shard_map/ppermute | solution.py:503
  120.2 1.6 collective-permute-done.21
  121.7 1.7 add_convert_fusion.8.refs_1_
  123.4 4.0 %collective-permute-start.25 = (bf16[128,896]{1,0:T(8,128)(2,1)}, bf16[128,896]{1,0:T(8,128)(2,1)}, u32[]{:S(2)}, u32[]{:S(2)}) collective-permute-start(bf16[128,896]{1,0:T(8,128)(2,1)} %add_convert_fusion.8.refs_1_), channel_id=1, source_target_pairs={{8,4},{4,0},{9,5},{6,10},{7,11},{11,15},{24,20},{20,16},{25,21},{2... | collective-permute-start | bytes 688136 | tf_op jit(solution)/shard_map/ppermute | solution.py:503
  129.3 2.6 %shard_map.84.own_ref.refs_6_.refs_1_ = bf16[256,2048]{1,0:T(8,128)(2,1)} custom-call(s32[1]{0:T(128)} %bitcast.9.u_ref, bf16[128,1152]{1,0:T(8,128)(2,1)S(1)} %copy-done.4, bf16[128,896]{1,0:T(8,128)(2,1)S(1)} %copy-done.14, bf16[128,1152]{1,0:T(8,128)(2,1)} %add_convert_fusion.2.refs_2_.refs_1_, bf16[128,896]{1,0:T(8,128)(2,1)S(1)} %copy-done.13, ...), custom_call_target="tpu_custom_call" | custom-call | tf_op jit(solution)/shard_map/pallas_call | solution.py:383
  131.9 1.6 collective-permute-start.18
  133.5 2.7 %shard_map.88.refs_3_.refs_7_ = bf16[256,2048]{1,0:T(8,128)(2,1)} custom-call(s32[1]{0:T(128)} %bitcast.9.u_ref, bf16[128,1152]{1,0:T(8,128)(2,1)S(1)} %copy-done.8, bf16[128,896]{1,0:T(8,128)(2,1)} %add_convert_fusion.12.refs_8_.refs_1_, bf16[128,1152]{1,0:T(8,128)(2,1)S(1)} %copy-done.6, bf16[128,896]{1,0:T(8,128)(2,1)} %add_convert_fusion.11.refs_6_.refs_3_, ...), custom_call_target="tpu_custom_call" | custom-call | tf_op jit(solution)/shard_map/pallas_call | solution.py:383
  139.6 1.7 shard_map.91
  144.3 4.0 %shard_map.93.refs_0_.refs_13_ = f32[256,2048]{1,0:T(8,128)S(1)} custom-call(s32[2]{0:T(128)S(1)} %pad_add_fusion.refs_0_.meta_ref, s32[64]{0:T(128)S(1)} %copy-done.17, s32[64]{0:T(128)S(1)} %copy-done.18, s32[16]{0:T(128)S(1)} %copy-done.20, s32[16]{0:T(128)S(1)} %fusion.2.refs_2_.refs_4_, s32[16]{0:T(128)S(1)} %fusion.1.refs_3_.refs_5_, ...), custom_call_target="tpu_custom_call" | custom-call | tf_op jit(solution)/shard_map/pallas_call | solution.py:470
  148.9 1.3 collective-permute-start.31
  150.2 1.3 collective-permute-start.30
  153.3 16.6 %collective-permute-done.32.refs_12_ = bf16[128,2048]{1,0:T(8,128)(2,1)S(1)} collective-permute-done((bf16[128,2048]{1,0:T(8,128)(2,1)S(1)}, bf16[128,2048]{1,0:T(8,128)(2,1)S(1)}, u32[]{:S(2)}, u32[]{:S(2)}) %collective-permute-start.32) | collective-permute-done | bytes 524320 | tf_op jit(solution)/shard_map/ppermute | solution.py:503
  170.0 4.2 %shard_map.96 = bf16[256,2048]{1,0:T(8,128)(2,1)} custom-call(s32[2]{0:T(128)S(1)} %pad_add_fusion.refs_0_.meta_ref, s32[64]{0:T(128)S(1)} %copy-done.17, s32[64]{0:T(128)S(1)} %copy-done.18, s32[16]{0:T(128)S(1)} %copy-done.20, s32[16]{0:T(128)S(1)} %fusion.2.refs_2_.refs_4_, s32[16]{0:T(128)S(1)} %fusion.1.refs_3_.refs_5_, s32[16]{0:T(128)S(1)} %fusion.refs_4_.refs_6_, ...), custom_call_target="tpu_custom_call" | custom-call | tf_op jit(solution)/shard_map/pallas_call | solution.py:470
  (108 shorter events, 28.3 us)
Async XLA Ops:
  0.0 1.2 copy-start.1
  3.5 3.3 %collective-permute-start = (bf16[272,2048]{1,0:T(8,128)(2,1)}, bf16[272,2048]{1,0:T(8,128)(2,1)S(1)}, u32[]{:S(2)}, u32[]{:S(2)}) collective-permute-start(bf16[272,2048]{1,0:T(8,128)(2,1)} %shard_map.73), channel_id=1, source_target_pairs={{0,1},{1,0},{2,3},{3,2},{4,5},{5,4},{6,7},{7,6},{8,9},{9,8},{10,11... | collective-permute-start | bytes 3342344 | tf_op jit(solution)/shard_map/ppermute | solution.py:491
  4.2 30.2 %collective-permute-start.1 = (bf16[272,2048]{1,0:T(8,128)(2,1)}, bf16[272,2048]{1,0:T(8,128)(2,1)}, u32[]{:S(2)}, u32[]{:S(2)}) collective-permute-start(bf16[272,2048]{1,0:T(8,128)(2,1)} %shard_map.73), channel_id=1, source_target_pairs={{0,2},{1,3},{2,0},{3,1},{4,6},{5,7},{6,4},{7,5},{8,10},{9,11},{10,... | collective-permute-start | bytes 3342344 | tf_op jit(solution)/shard_map/ppermute | solution.py:491
  7.8 1.2 copy-start.2
  9.0 12.1 %copy-start.3 = (bf16[16,16,2048]{2,1,0:T(8,128)(2,1)S(1)}, bf16[16,16,2048]{2,1,0:T(8,128)(2,1)}, u32[]{:S(2)}) copy-start(bf16[16,16,2048]{2,1,0:T(8,128)(2,1)} %param.7) | copy-start | bytes 3145732
  9.0 12.1 %copy-start.17 = (s32[64]{0:T(128)S(1)}, s32[64]{0:T(128)}, u32[]{:S(2)}) copy-start(s32[64]{0:T(128)} %refs_1_.11) | copy-start | bytes 772
  9.0 12.1 %copy-start.18 = (s32[64]{0:T(128)S(1)}, s32[64]{0:T(128)}, u32[]{:S(2)}) copy-start(s32[64]{0:T(128)} %refs_2_.7) | copy-start | bytes 772
  17.5 9.5 %collective-permute-start.3 = (bf16[128,896]{1,0:T(8,128)(2,1)S(1)}, bf16[128,896]{1,0:T(8,128)(2,1)S(1)}, u32[]{:S(2)}, u32[]{:S(2)}) collective-permute-start(bf16[128,896]{1,0:T(8,128)(2,1)S(1)} %slice.42), channel_id=1, source_target_pairs={{12,8},{13,9},{2,6},{3,7},{28,24},{29,25},{18,22},{19,23}} | collective-permute-start | bytes 688136 | tf_op jit(solution)/shard_map/ppermute | solution.py:503
  19.8 12.7 %collective-permute-start.2 = (bf16[128,1152]{1,0:T(8,128)(2,1)S(1)}, bf16[128,1152]{1,0:T(8,128)(2,1)S(1)}, u32[]{:S(2)}, u32[]{:S(2)}) collective-permute-start(bf16[128,1152]{1,0:T(8,128)(2,1)S(1)} %slice.40), channel_id=1, source_target_pairs={{12,8},{13,9},{2,6},{3,7},{28,24},{29,25},{18,22},{19,23}} | collective-permute-start | bytes 884744 | tf_op jit(solution)/shard_map/ppermute | solution.py:503
  28.9 6.7 %copy-start.12 = (bf16[128,896]{1,0:T(8,128)(2,1)S(1)}, bf16[128,896]{1,0:T(8,128)(2,1)}, u32[]{:S(2)}) copy-start(bf16[128,896]{1,0:T(8,128)(2,1)} %add_convert_fusion.13.refs_2_.refs_12_) | copy-start | bytes 688132
  34.4 5.7 %collective-permute-start.4 = (bf16[272,2048]{1,0:T(8,128)(2,1)}, bf16[272,2048]{1,0:T(8,128)(2,1)}, u32[]{:S(2)}, u32[]{:S(2)}) collective-permute-start(bf16[272,2048]{1,0:T(8,128)(2,1)} %shard_map.76.refs_7_.refs_3_), channel_id=1, source_target_pairs={{0,1},{1,0},{2,3},{3,2},{4,5},{5,4},{6,7},{7,6},{8,9},{9,8},{10,11... | collective-permute-start | bytes 3342344 | tf_op jit(solution)/shard_map/ppermute | solution.py:491
  35.6 17.6 %collective-permute-start.7 = (bf16[128,896]{1,0:T(8,128)(2,1)S(1)}, bf16[128,896]{1,0:T(8,128)(2,1)S(1)}, u32[]{:S(2)}, u32[]{:S(2)}) collective-permute-start(bf16[128,896]{1,0:T(8,128)(2,1)S(1)} %copy-done.12), channel_id=1, source_target_pairs={{12,8},{8,4},{13,9},{9,5},{2,6},{6,10},{3,7},{7,11},{28,24},{24,20... | collective-permute-start | bytes 688136 | tf_op jit(solution)/shard_map/ppermute | solution.py:503
  38.2 18.6 %collective-permute-start.5 = (bf16[128,1152]{1,0:T(8,128)(2,1)}, bf16[128,1152]{1,0:T(8,128)(2,1)S(1)}, u32[]{:S(2)}, u32[]{:S(2)}) collective-permute-start(bf16[128,1152]{1,0:T(8,128)(2,1)} %add_convert_fusion.6.refs_1_.refs_11_), channel_id=1, source_target_pairs={{12,8},{8,4},{13,9},{9,5},{2,6},{6,10},{3,7},{7,11},{28,24},{24,20... | collective-permute-start | bytes 884744 | tf_op jit(solution)/shard_map/ppermute | solution.py:503
  41.8 18.1 %copy-start.16 = (bf16[256,128]{1,0:T(8,128)(2,1)S(1)}, bf16[256,128]{1,0:T(8,128)(2,1)}, u32[]{:S(2)}) copy-start(bf16[256,128]{1,0:T(8,128)(2,1)} %copy-done.15) | copy-start | bytes 196612
  54.9 14.7 %collective-permute-start.12 = (bf16[128,896]{1,0:T(8,128)(2,1)}, bf16[128,896]{1,0:T(8,128)(2,1)}, u32[]{:S(2)}, u32[]{:S(2)}) collective-permute-start(bf16[128,896]{1,0:T(8,128)(2,1)} %add_convert_fusion.12.refs_8_.refs_1_), channel_id=1, source_target_pairs={{12,8},{8,4},{4,0},{13,9},{9,5},{2,6},{6,10},{3,7},{7,11},{11,15},... | collective-permute-start | bytes 688136 | tf_op jit(solution)/shard_map/ppermute | solution.py:503
  57.9 8.4 %copy-start.7 = (bf16[128,1152]{1,0:T(8,128)(2,1)}, bf16[128,1152]{1,0:T(8,128)(2,1)S(1)}, u32[]{:S(2)}) copy-start(bf16[128,1152]{1,0:T(8,128)(2,1)S(1)} %add_convert_fusion.5.refs_7_.refs_0_) | copy-start | bytes 884740
  57.9 15.6 %collective-permute-start.6 = (bf16[128,1152]{1,0:T(8,128)(2,1)S(1)}, bf16[128,1152]{1,0:T(8,128)(2,1)}, u32[]{:S(2)}, u32[]{:S(2)}) collective-permute-start(bf16[128,1152]{1,0:T(8,128)(2,1)S(1)} %add_convert_fusion.5.refs_7_.refs_0_), channel_id=1, source_target_pairs={{12,8},{8,4},{4,0},{13,9},{9,5},{2,6},{6,10},{3,7},{7,11},{11,15},... | collective-permute-start | bytes 884744 | tf_op jit(solution)/shard_map/ppermute | solution.py:503
  59.9 9.8 %copy-start = (bf16[768,2048]{1,0:T(8,128)(2,1)S(1)}, bf16[768,2048]{1,0:T(8,128)(2,1)}, u32[]{:S(2)}) copy-start(bf16[768,2048]{1,0:T(8,128)(2,1)} %shard_map.77.refs_1_) | copy-start | bytes 9437188
  66.3 12.0 %collective-permute-start.10 = (bf16[256,128]{1,0:T(8,128)(2,1)}, bf16[256,128]{1,0:T(8,128)(2,1)S(1)}, u32[]{:S(2)}, u32[]{:S(2)}) collective-permute-start(bf16[256,128]{1,0:T(8,128)(2,1)} %shard_map.78.refs_1_.refs_0_), channel_id=1, source_target_pairs={{0,4},{4,0},{8,12},{12,8},{1,5},{5,1},{9,13},{13,9},{2,6},{6,2},{1... | collective-permute-start | bytes 196616 | tf_op jit(solution)/shard_map/ppermute | solution.py:617
  68.4 9.9 %collective-permute-start.11 = (bf16[256,128]{1,0:T(8,128)(2,1)}, bf16[256,128]{1,0:T(8,128)(2,1)}, u32[]{:S(2)}, u32[]{:S(2)}) collective-permute-start(bf16[256,128]{1,0:T(8,128)(2,1)} %shard_map.78.refs_1_.refs_0_), channel_id=1, source_target_pairs={{0,8},{4,12},{8,0},{12,4},{1,9},{5,13},{9,1},{13,5},{2,10},{6,14},... | collective-permute-start | bytes 196616 | tf_op jit(solution)/shard_map/ppermute | solution.py:617
  68.4 9.9 %collective-permute-start.9 = (bf16[256,128]{1,0:T(8,128)(2,1)}, bf16[256,128]{1,0:T(8,128)(2,1)}, u32[]{:S(2)}, u32[]{:S(2)}) collective-permute-start(bf16[256,128]{1,0:T(8,128)(2,1)} %shard_map.78.refs_1_.refs_0_), channel_id=1, source_target_pairs={{0,12},{4,8},{8,4},{12,0},{1,13},{5,9},{9,5},{13,1},{2,14},{6,10},... | collective-permute-start | bytes 196616 | tf_op jit(solution)/shard_map/ppermute | solution.py:617
  71.4 16.6 %collective-permute-start.13 = (bf16[128,896]{1,0:T(8,128)(2,1)}, bf16[128,896]{1,0:T(8,128)(2,1)}, u32[]{:S(2)}, u32[]{:S(2)}) collective-permute-start(bf16[128,896]{1,0:T(8,128)(2,1)} %add_convert_fusion.11.refs_6_.refs_3_), channel_id=1, source_target_pairs={{12,8},{8,4},{4,0},{13,9},{9,5},{2,6},{6,10},{3,7},{7,11},{11,15},... | collective-permute-start | bytes 688136 | tf_op jit(solution)/shard_map/ppermute | solution.py:503
  74.5 11.0 %copy-start.5 = (bf16[128,1152]{1,0:T(8,128)(2,1)}, bf16[128,1152]{1,0:T(8,128)(2,1)S(1)}, u32[]{:S(2)}) copy-start(bf16[128,1152]{1,0:T(8,128)(2,1)S(1)} %add_convert_fusion.4.refs_5_.refs_2_) | copy-start | bytes 884740
  74.6 15.1 %collective-permute-start.8 = (bf16[128,1152]{1,0:T(8,128)(2,1)S(1)}, bf16[128,1152]{1,0:T(8,128)(2,1)}, u32[]{:S(2)}, u32[]{:S(2)}) collective-permute-start(bf16[128,1152]{1,0:T(8,128)(2,1)S(1)} %add_convert_fusion.4.refs_5_.refs_2_), channel_id=1, source_target_pairs={{12,8},{8,4},{4,0},{13,9},{9,5},{2,6},{6,10},{3,7},{7,11},{11,15},... | collective-permute-start | bytes 884744 | tf_op jit(solution)/shard_map/ppermute | solution.py:503
  85.6 4.1 %copy-start.10 = (bf16[128,2048]{1,0:T(8,128)(2,1)}, bf16[128,2048]{1,0:T(8,128)(2,1)S(1)}, u32[]{:S(2)}) copy-start(bf16[128,2048]{1,0:T(8,128)(2,1)S(1)} %get-tuple-element.11.refs_1_.refs_9_) | copy-start | bytes 1572868
  85.6 13.1 %collective-permute-start.15 = (bf16[128,2048]{1,0:T(8,128)(2,1)}, bf16[128,2048]{1,0:T(8,128)(2,1)}, u32[]{:S(2)}, u32[]{:S(2)}) collective-permute-start(bf16[128,2048]{1,0:T(8,128)(2,1)} %get-tuple-element.12), channel_id=1, source_target_pairs={{0,1},{1,0},{2,3},{3,2},{4,5},{5,4},{6,7},{7,6},{8,9},{9,8},{10,11... | collective-permute-start | bytes 1572872 | tf_op jit(solution)/shard_map/ppermute | solution.py:491
  91.5 2.1 %copy-start.4 = (bf16[128,1152]{1,0:T(8,128)(2,1)S(1)}, bf16[128,1152]{1,0:T(8,128)(2,1)}, u32[]{:S(2)}) copy-start(bf16[128,1152]{1,0:T(8,128)(2,1)} %add_convert_fusion.3.refs_1_.refs_0_) | copy-start | bytes 884740
  91.5 35.9 %collective-permute-start.17 = (bf16[512,2048]{1,0:T(8,128)(2,1)}, bf16[512,2048]{1,0:T(8,128)(2,1)}, u32[]{:S(2)}, u32[]{:S(2)}) collective-permute-start(bf16[512,2048]{1,0:T(8,128)(2,1)} %shard_map.83), channel_id=1, source_target_pairs={{1,5},{14,10},{17,21},{30,26}} | collective-permute-start | bytes 6291464 | tf_op jit(solution)/shard_map/ppermute | solution.py:503
  93.6 10.5 %collective-permute-start.14 = (bf16[128,1152]{1,0:T(8,128)(2,1)S(1)}, bf16[128,1152]{1,0:T(8,128)(2,1)}, u32[]{:S(2)}, u32[]{:S(2)}) collective-permute-start(bf16[128,1152]{1,0:T(8,128)(2,1)S(1)} %copy-done.4), channel_id=1, source_target_pairs={{12,8},{8,4},{4,0},{13,9},{9,5},{2,6},{6,10},{3,7},{7,11},{11,15},... | collective-permute-start | bytes 884744 | tf_op jit(solution)/shard_map/ppermute | solution.py:503
  96.6 15.7 %collective-permute-start.20 = (bf16[128,2048]{1,0:T(8,128)(2,1)}, bf16[128,2048]{1,0:T(8,128)(2,1)}, u32[]{:S(2)}, u32[]{:S(2)}) collective-permute-start(bf16[128,2048]{1,0:T(8,128)(2,1)} %get-tuple-element.13), channel_id=1, source_target_pairs={{0,2},{1,3},{2,0},{3,1},{4,6},{5,7},{6,4},{7,5},{8,10},{9,11},{10,... | collective-permute-start | bytes 1572872 | tf_op jit(solution)/shard_map/ppermute | solution.py:491
  96.6 12.4 %collective-permute-start.16 = (bf16[128,896]{1,0:T(8,128)(2,1)}, bf16[128,896]{1,0:T(8,128)(2,1)}, u32[]{:S(2)}, u32[]{:S(2)}) collective-permute-start(bf16[128,896]{1,0:T(8,128)(2,1)} %add_convert_fusion.10.refs_2_.refs_1_), channel_id=1, source_target_pairs={{12,8},{8,4},{4,0},{13,9},{9,5},{2,6},{6,10},{3,7},{7,11},{11,15},... | collective-permute-start | bytes 688136 | tf_op jit(solution)/shard_map/ppermute | solution.py:503
  105.8 9.6 %collective-permute-start.19 = (bf16[128,1152]{1,0:T(8,128)(2,1)}, bf16[128,1152]{1,0:T(8,128)(2,1)}, u32[]{:S(2)}, u32[]{:S(2)}) collective-permute-start(bf16[128,1152]{1,0:T(8,128)(2,1)} %add_convert_fusion.2.refs_2_.refs_1_), channel_id=1, source_target_pairs={{12,8},{8,4},{4,0},{13,9},{9,5},{2,6},{6,10},{3,7},{7,11},{11,15},... | collective-permute-start | bytes 884744 | tf_op jit(solution)/shard_map/ppermute | solution.py:503
  110.7 22.8 %collective-permute-start.24 = (bf16[256,2048]{1,0:T(8,128)(2,1)}, bf16[256,2048]{1,0:T(8,128)(2,1)}, u32[]{:S(2)}, u32[]{:S(2)}) collective-permute-start(bf16[256,2048]{1,0:T(8,128)(2,1)} %shard_map.87), channel_id=1, source_target_pairs={{1,5},{14,10},{17,21},{30,26}} | collective-permute-start | bytes 3145736 | tf_op jit(solution)/shard_map/ppermute | solution.py:503
  112.3 25.1 %collective-permute-start.23 = (bf16[128,2048]{1,0:T(8,128)(2,1)}, bf16[128,2048]{1,0:T(8,128)(2,1)}, u32[]{:S(2)}, u32[]{:S(2)}) collective-permute-start(bf16[128,2048]{1,0:T(8,128)(2,1)} %get-tuple-element.14), channel_id=1, source_target_pairs={{0,3},{1,2},{2,1},{3,0},{4,7},{5,6},{6,5},{7,4},{8,11},{9,10},{10,... | collective-permute-start | bytes 1572872 | tf_op jit(solution)/shard_map/ppermute | solution.py:491
  112.3 9.4 %collective-permute-start.21 = (bf16[128,896]{1,0:T(8,128)(2,1)}, bf16[128,896]{1,0:T(8,128)(2,1)}, u32[]{:S(2)}, u32[]{:S(2)}) collective-permute-start(bf16[128,896]{1,0:T(8,128)(2,1)} %add_convert_fusion.9.refs_3_.refs_2_), channel_id=1, source_target_pairs={{12,8},{8,4},{4,0},{13,9},{9,5},{2,6},{6,10},{3,7},{7,11},{11,15},... | collective-permute-start | bytes 688136 | tf_op jit(solution)/shard_map/ppermute | solution.py:503
  117.2 20.2 %collective-permute-start.22 = (bf16[128,1152]{1,0:T(8,128)(2,1)}, bf16[128,1152]{1,0:T(8,128)(2,1)}, u32[]{:S(2)}, u32[]{:S(2)}) collective-permute-start(bf16[128,1152]{1,0:T(8,128)(2,1)} %add_convert_fusion.1.refs_0_), channel_id=1, source_target_pairs={{8,4},{4,0},{9,5},{6,10},{7,11},{11,15},{24,20},{20,16},{25,21},{2... | collective-permute-start | bytes 884744 | tf_op jit(solution)/shard_map/ppermute | solution.py:503
  123.4 15.1 %collective-permute-start.25 = (bf16[128,896]{1,0:T(8,128)(2,1)}, bf16[128,896]{1,0:T(8,128)(2,1)}, u32[]{:S(2)}, u32[]{:S(2)}) collective-permute-start(bf16[128,896]{1,0:T(8,128)(2,1)} %add_convert_fusion.8.refs_1_), channel_id=1, source_target_pairs={{8,4},{4,0},{9,5},{6,10},{7,11},{11,15},{24,20},{20,16},{25,21},{2... | collective-permute-start | bytes 688136 | tf_op jit(solution)/shard_map/ppermute | solution.py:503
  129.3 4.2 %copy-start.6 = (bf16[128,1152]{1,0:T(8,128)(2,1)S(1)}, bf16[128,1152]{1,0:T(8,128)(2,1)}, u32[]{:S(2)}) copy-start(bf16[128,1152]{1,0:T(8,128)(2,1)} %copy-done.5) | copy-start | bytes 884740
  129.3 4.2 %copy-start.8 = (bf16[128,1152]{1,0:T(8,128)(2,1)S(1)}, bf16[128,1152]{1,0:T(8,128)(2,1)}, u32[]{:S(2)}) copy-start(bf16[128,1152]{1,0:T(8,128)(2,1)} %copy-done.7) | copy-start | bytes 884740
  131.9 10.8 %collective-permute-start.18 = (bf16[256,2048]{1,0:T(8,128)(2,1)}, bf16[256,2048]{1,0:T(8,128)(2,1)}, u32[]{:S(2)}, u32[]{:S(2)}) collective-permute-start(bf16[256,2048]{1,0:T(8,128)(2,1)} %shard_map.84.own_ref.refs_6_.refs_1_), channel_id=1, source_target_pairs={{0,2},{5,7},{10,8},{15,13},{16,18},{21,23},{26,24},{31,29}} | collective-permute-start | bytes 3145736 | tf_op jit(solution)/shard_map/ppermute | solution.py:503
  136.2 7.9 %collective-permute-start.27 = (bf16[256,2048]{1,0:T(8,128)(2,1)}, bf16[256,2048]{1,0:T(8,128)(2,1)}, u32[]{:S(2)}, u32[]{:S(2)}) collective-permute-start(bf16[256,2048]{1,0:T(8,128)(2,1)} %shard_map.88.refs_3_.refs_7_), channel_id=1, source_target_pairs={{0,1},{5,4},{10,11},{15,14},{2,3},{7,6},{8,9},{13,12},{16,17},{21,... | collective-permute-start | bytes 3145736 | tf_op jit(solution)/shard_map/ppermute | solution.py:503
  141.2 7.1 %collective-permute-start.26 = (bf16[256,2048]{1,0:T(8,128)(2,1)S(1)}, bf16[256,2048]{1,0:T(8,128)(2,1)S(1)}, u32[]{:S(2)}, u32[]{:S(2)}) collective-permute-start(bf16[256,2048]{1,0:T(8,128)(2,1)S(1)} %get-tuple-element.15.own_ref), channel_id=1, source_target_pairs={{0,2},{5,7},{10,8},{15,13},{16,18},{21,23},{26,24},{31,29}} | collective-permute-start | bytes 3145736 | tf_op jit(solution)/shard_map/ppermute | solution.py:503
  142.0 1.3 collective-permute-start.28
  143.2 1.0 copy-start.11
  143.4 8.0 %collective-permute-start.29 = (bf16[128,2048]{1,0:T(8,128)(2,1)S(1)}, bf16[128,2048]{1,0:T(8,128)(2,1)S(1)}, u32[]{:S(2)}, u32[]{:S(2)}) collective-permute-start(bf16[128,2048]{1,0:T(8,128)(2,1)S(1)} %shard_map.92.refs_13_.own_ref), channel_id=1, source_target_pairs={{0,2},{5,7},{10,8},{15,13},{16,18},{21,23},{26,24},{31,29}} | collective-permute-start | bytes 1572872 | tf_op jit(solution)/shard_map/ppermute | solution.py:503
  148.9 21.1 %collective-permute-start.31 = (bf16[256,2048]{1,0:T(8,128)(2,1)S(1)}, bf16[256,2048]{1,0:T(8,128)(2,1)S(1)}, u32[]{:S(2)}, u32[]{:S(2)}) collective-permute-start(bf16[256,2048]{1,0:T(8,128)(2,1)S(1)} %shard_map.94.refs_8_), channel_id=1, source_target_pairs={{0,1},{5,4},{10,11},{15,14},{2,3},{7,6},{8,9},{13,12},{16,17},{21,... | collective-permute-start | bytes 3145736 | tf_op jit(solution)/shard_map/ppermute | solution.py:503
  150.2 19.8 %collective-permute-start.30 = (bf16[256,2048]{1,0:T(8,128)(2,1)}, bf16[256,2048]{1,0:T(8,128)(2,1)S(1)}, u32[]{:S(2)}, u32[]{:S(2)}) collective-permute-start(bf16[256,2048]{1,0:T(8,128)(2,1)} %shard_map.85.refs_2_.refs_7_), channel_id=1, source_target_pairs={{0,1},{5,4},{10,11},{15,14},{2,3},{7,6},{8,9},{13,12},{16,17},{21,... | collective-permute-start | bytes 3145736 | tf_op jit(solution)/shard_map/ppermute | solution.py:503
  152.0 17.9 %collective-permute-start.32 = (bf16[128,2048]{1,0:T(8,128)(2,1)S(1)}, bf16[128,2048]{1,0:T(8,128)(2,1)S(1)}, u32[]{:S(2)}, u32[]{:S(2)}) collective-permute-start(bf16[128,2048]{1,0:T(8,128)(2,1)S(1)} %shard_map.95.refs_9_), channel_id=1, source_target_pairs={{0,1},{5,4},{10,11},{15,14},{2,3},{7,6},{8,9},{13,12},{16,17},{21,... | collective-permute-start | bytes 1572872 | tf_op jit(solution)/shard_map/ppermute | solution.py:503
  (7 other events, 6.1 us)

commit v6 on v5

--- a/solution.py
+++ b/solution.py
@@ -150,7 +150,7 @@
     out_ref[...] = jnp.dot(packed[...], w_ref[...], preferred_element_type=F32).astype(BF16)
 
 
-def project(meta, lens, xs, w, first, rows, total, place, buffer=None, deps=(), tile=512):
+def project(meta, lens, xs, w, first, rows, total, place, buffer=None, deps=(), tile=1024):
     depth, cols = w.shape
     blocks = len(xs)
     tokens = SLOTS
@@ -283,7 +283,7 @@
         out_refs[i][...] = result[i * size : (i + 1) * size, :]
 
 
-def up_project(meta, req, slot, lows, up_2d, held, rank, tokens, capacity, requests, deps, tile=512):
+def up_project(meta, req, slot, lows, up_2d, held, rank, tokens, capacity, requests, deps, tile=1024):
     cols = up_2d.shape[1]
     size = capacity * tokens
     smem = pl.BlockSpec(memory_space=pltpu.SMEM)
@@ -458,7 +458,7 @@
         run(got_refs)
 
 
-def finish(meta, req, slot, lens, values, gots, first, deltas, acc, out_dtype, span, held, tokens, capacity, deps=(), tile=512):
+def finish(meta, req, slot, lens, values, gots, first, deltas, acc, out_dtype, span, held, tokens, capacity, deps=(), tile=1024):
     requests = lens[0].shape[0]
     rows = requests * tokens
     cols = values[0].shape[1]

time: 176 us -> 173 us (0.983)
  Pallas kernels: 56.5 us -> 52.7 us
    pallas_call x2, Pallas kernels: 8.21 us -> 6.25 us  [finish(): pl.pallas_call(functools.partial(finish_kernel, len(sizes), sizes, first,...]
  transfers between devices with their start and end apart: 33 -> 33, of which waited for: 6 -> 6; matrix products, arithmetic and copies ran while one was open for 16% -> 16% of each run, Pallas kernels for 29% -> 28%
where the time goes in v6:
time: 173 us; the launch traced here: 172 us
  Pallas kernels  52.7 us (30%)
  starting transfers between devices  52.2 us (30%)
  waiting for transfers between devices  30.7 us (18%)
  other arithmetic  23 us (13%)
  local copies, waits for them, and re-layouts  12.4 us (7%)
    ppermute x24, starting transfers between devices, on_mesh(): lax.ppermute(value, ('tensor', 'store'), [(a * 4 + b, c * 4 + d) for (a,...  43.1 us
    ppermute x24, waiting for transfers between devices, on_mesh(): lax.ppermute(value, ('tensor', 'store'), [(a * 4 + b, c * 4 + d) for (a,...  29.4 us
    convert_element_type x14, other arithmetic, chain_step(): value = total.astype(BF16)  21.5 us
    pallas_call x2, Pallas kernels, project(): pl.pallas_call(functools.partial(project_kernel, first, blocks, width, to...  18 us
    pallas_call x2, Pallas kernels, low_rank(): pl.pallas_call(functools.partial(low_kernel, flips, before is not None, h...  11.6 us
    unnamed x44, local copies, waits for them, and re-layouts  7.76 us
    pallas_call x4, Pallas kernels, merge(): pl.pallas_call(functools.partial(merge_kernel, count, streams, bool(backs...  7.03 us
    pallas_call x1, Pallas kernels, up_project(): pl.pallas_call(functools.partial(up_kernel, len(deps), held, rank, reques...  6.62 us
  transfers between devices with their start and end apart: 33, of which 6 were waited for; matrix products, arithmetic and copies ran while one was open for 16% of the time, Pallas kernels for 28%

profile of v6, /device:TPU:21, one launch (start us, length us, event | category | flops | bytes accessed | tf_op | source)
XLA Modules:
  0.0 171.6 jit_solution(12323533051422113852)
XLA Ops:
  1.9 1.6 shard_map.73
  5.5 1.3 collective-permute-done.refs_4_.refs_6_
  9.0 6.7 %shard_map.74.refs_6_.refs_10_ = bf16[768,2048]{1,0:T(8,128)(2,1)} custom-call(s32[2]{0:T(128)S(1)} %pad_add_fusion.refs_0_.meta_ref, s32[16]{0:T(128)S(1)} %copy-done.19, s32[16]{0:T(128)S(1)} %fusion.2.refs_2_.refs_4_, bf16[256,2048]{1,0:T(8,128)(2,1)S(1)} %bitcast.25, bf16[272,2048]{1,0:T(8,128)(2,1)} %copy-done.21, bf16[2048,2048]{1,0:T(8,128)(2,1)} %refs_9_.1), custom_call_target="tpu_custom_call" | custom-call | tf_op jit(solution)/shard_map/pallas_call | solution.py:160
  16.7 1.3 collective-permute-start.3
  19.0 1.3 collective-permute-start.2
  20.3 5.3 %shard_map.75.refs_3_.refs_6_ = bf16[256,128]{1,0:T(8,128)(2,1)S(1)} custom-call(s32[2]{0:T(128)S(1)} %pad_add_fusion.refs_0_.meta_ref, s32[64]{0:T(128)S(1)} %copy-done.17, s32[64]{0:T(128)S(1)} %copy-done.18, bf16[256,2048]{1,0:T(8,128)(2,1)S(1)} %bitcast.26, bf16[272,2048]{1,0:T(8,128)(2,1)} %copy-done.21, bf16[1024,2048]{1,0:T(8,128)(2,1)} %bitcast.28, ...), custom_call_target="tpu_custom_call" | custom-call | tf_op jit(solution)/shard_map/pallas_call | solution.py:239
  26.2 1.8 %add_convert_fusion.13.refs_2_.refs_12_ = bf16[128,896]{1,0:T(8,128)(2,1)} fusion(bf16[128,896]{1,0:T(8,128)(2,1)S(1)} %collective-permute-done.3, bf16[768,2048]{1,0:T(8,128)(2,1)} %shard_map.74.refs_6_.refs_10_, pred[]{:T(512)S(6)} %ge.4), kind=kLoop, calls=%fused_computation.13 | loop fusion | flops 573440 | bytes 917505 | tf_op jit(solution)/shard_map/convert_element_type | solution.py:578
  28.1 3.7 %collective-permute-done.2 = bf16[128,1152]{1,0:T(8,128)(2,1)S(1)} collective-permute-done((bf16[128,1152]{1,0:T(8,128)(2,1)S(1)}, bf16[128,1152]{1,0:T(8,128)(2,1)S(1)}, u32[]{:S(2)}, u32[]{:S(2)}) %collective-permute-start.2) | collective-permute-done | bytes 294944 | tf_op jit(solution)/shard_map/ppermute | solution.py:503
  31.7 1.9 %add_convert_fusion.6.refs_1_.refs_11_ = bf16[128,1152]{1,0:T(8,128)(2,1)} fusion(bf16[128,1152]{1,0:T(8,128)(2,1)S(1)} %collective-permute-done.2, bf16[768,2048]{1,0:T(8,128)(2,1)} %shard_map.74.refs_6_.refs_10_, pred[]{:T(512)S(6)} %ge.4), kind=kLoop, calls=%fused_computation.6 | loop fusion | flops 737280 | bytes 1179649 | tf_op jit(solution)/shard_map/convert_element_type | solution.py:578
  34.8 1.9 %collective-permute-start.7 = (bf16[128,896]{1,0:T(8,128)(2,1)S(1)}, bf16[128,896]{1,0:T(8,128)(2,1)S(1)}, u32[]{:S(2)}, u32[]{:S(2)}) collective-permute-start(bf16[128,896]{1,0:T(8,128)(2,1)S(1)} %copy-done.12), channel_id=1, source_target_pairs={{12,8},{8,4},{13,9},{9,5},{2,6},{6,10},{3,7},{7,11},{28,24},{24,20... | collective-permute-start | bytes 688136 | tf_op jit(solution)/shard_map/ppermute | solution.py:503
  37.4 1.9 %collective-permute-start.5 = (bf16[128,1152]{1,0:T(8,128)(2,1)}, bf16[128,1152]{1,0:T(8,128)(2,1)S(1)}, u32[]{:S(2)}, u32[]{:S(2)}) collective-permute-start(bf16[128,1152]{1,0:T(8,128)(2,1)} %add_convert_fusion.6.refs_1_.refs_11_), channel_id=1, source_target_pairs={{12,8},{8,4},{13,9},{9,5},{2,6},{6,10},{3,7},{7,11},{28,24},{24,20... | collective-permute-start | bytes 884744 | tf_op jit(solution)/shard_map/ppermute | solution.py:503
  41.0 11.2 %shard_map.77.refs_1_ = bf16[768,2048]{1,0:T(8,128)(2,1)} custom-call(s32[2]{0:T(128)S(1)} %pad_add_fusion.refs_0_.meta_ref, s32[16]{0:T(128)S(1)} %copy-done.19, s32[16]{0:T(128)S(1)} %fusion.2.refs_2_.refs_4_, s32[16]{0:T(128)S(1)} %fusion.1.refs_3_.refs_5_, s32[16]{0:T(128)S(1)} %fusion.refs_4_.refs_6_, ...), custom_call_target="tpu_custom_call", output_to_operand_aliasing={{}: (10, {})} | custom-call | tf_op jit(solution)/shard_map/pallas_call | solution.py:160
  52.2 1.7 add_convert_fusion.12.refs_8_.refs_1_
  53.9 1.9 %collective-permute-start.12 = (bf16[128,896]{1,0:T(8,128)(2,1)}, bf16[128,896]{1,0:T(8,128)(2,1)}, u32[]{:S(2)}, u32[]{:S(2)}) collective-permute-start(bf16[128,896]{1,0:T(8,128)(2,1)} %add_convert_fusion.12.refs_8_.refs_1_), channel_id=1, source_target_pairs={{12,8},{8,4},{4,0},{13,9},{9,5},{2,6},{6,10},{3,7},{7,11},{11,15},... | collective-permute-start | bytes 688136 | tf_op jit(solution)/shard_map/ppermute | solution.py:503
  56.9 1.9 %collective-permute-start.6 = (bf16[128,1152]{1,0:T(8,128)(2,1)S(1)}, bf16[128,1152]{1,0:T(8,128)(2,1)}, u32[]{:S(2)}, u32[]{:S(2)}) collective-permute-start(bf16[128,1152]{1,0:T(8,128)(2,1)S(1)} %add_convert_fusion.5.refs_7_.refs_0_), channel_id=1, source_target_pairs={{12,8},{8,4},{4,0},{13,9},{9,5},{2,6},{6,10},{3,7},{7,11},{11,15},... | collective-permute-start | bytes 884744 | tf_op jit(solution)/shard_map/ppermute | solution.py:503
  58.9 6.3 %shard_map.78.refs_1_.refs_0_ = bf16[256,128]{1,0:T(8,128)(2,1)} custom-call(s32[2]{0:T(128)S(1)} %pad_add_fusion.refs_0_.meta_ref, s32[64]{0:T(128)S(1)} %copy-done.17, s32[64]{0:T(128)S(1)} %copy-done.18, bf16[272,2048]{1,0:T(8,128)(2,1)} %shard_map.76.refs_7_.refs_3_, bf16[272,2048]{1,0:T(8,128)(2,1)} %collective-permute-done.4.refs_8_.refs_4_, ...), custom_call_target="tpu_custom_call" | custom-call | tf_op jit(solution)/shard_map/pallas_call | solution.py:239
  65.1 2.2 %collective-permute-start.10 = (bf16[256,128]{1,0:T(8,128)(2,1)}, bf16[256,128]{1,0:T(8,128)(2,1)S(1)}, u32[]{:S(2)}, u32[]{:S(2)}) collective-permute-start(bf16[256,128]{1,0:T(8,128)(2,1)} %shard_map.78.refs_1_.refs_0_), channel_id=1, source_target_pairs={{0,4},{4,0},{8,12},{12,8},{1,5},{5,1},{9,13},{13,9},{2,6},{6,2},{1... | collective-permute-start | bytes 196616 | tf_op jit(solution)/shard_map/ppermute | solution.py:617
  68.6 1.7 add_convert_fusion.11.refs_6_.refs_3_
  70.2 2.1 %collective-permute-start.13 = (bf16[128,896]{1,0:T(8,128)(2,1)}, bf16[128,896]{1,0:T(8,128)(2,1)}, u32[]{:S(2)}, u32[]{:S(2)}) collective-permute-start(bf16[128,896]{1,0:T(8,128)(2,1)} %add_convert_fusion.11.refs_6_.refs_3_), channel_id=1, source_target_pairs={{12,8},{8,4},{4,0},{13,9},{9,5},{2,6},{6,10},{3,7},{7,11},{11,15},... | collective-permute-start | bytes 688136 | tf_op jit(solution)/shard_map/ppermute | solution.py:503
  73.4 2.1 %collective-permute-start.8 = (bf16[128,1152]{1,0:T(8,128)(2,1)S(1)}, bf16[128,1152]{1,0:T(8,128)(2,1)}, u32[]{:S(2)}, u32[]{:S(2)}) collective-permute-start(bf16[128,1152]{1,0:T(8,128)(2,1)S(1)} %add_convert_fusion.4.refs_5_.refs_2_), channel_id=1, source_target_pairs={{12,8},{8,4},{4,0},{13,9},{9,5},{2,6},{6,10},{3,7},{7,11},{11,15},... | collective-permute-start | bytes 884744 | tf_op jit(solution)/shard_map/ppermute | solution.py:503
  75.6 1.6 slice.45.refs_0_
  77.2 6.6 %shard_map.80 = (bf16[128,2048]{1,0:T(8,128)(2,1)S(1)}, bf16[128,2048]{1,0:T(8,128)(2,1)}, bf16[128,2048]{1,0:T(8,128)(2,1)}, bf16[128,2048]{1,0:T(8,128)(2,1)}) custom-call(s32[2]{0:T(128)S(1)} %pad_add_fusion.refs_0_.meta_ref, s32[64]{0:T(128)S(1)} %copy-done.17, s32[64]{0:T(128)S(1)} %copy-done.18, bf16[256,128]{1,0:T(8,128)(2,1)} %shard_map.78.refs_1_.refs_0_, ...), custom_call_target="tpu_custom_call" | custom-call | tf_op jit(solution)/shard_map/pallas_call | solution.py:290
  83.8 2.6 %collective-permute-start.15 = (bf16[128,2048]{1,0:T(8,128)(2,1)}, bf16[128,2048]{1,0:T(8,128)(2,1)}, u32[]{:S(2)}, u32[]{:S(2)}) collective-permute-start(bf16[128,2048]{1,0:T(8,128)(2,1)} %get-tuple-element.12), channel_id=1, source_target_pairs={{0,1},{1,0},{2,3},{3,2},{4,5},{5,4},{6,7},{7,6},{8,9},{9,8},{10,11... | collective-permute-start | bytes 1572872 | tf_op jit(solution)/shard_map/ppermute | solution.py:491
  86.4 1.7 add_convert_fusion.10.refs_2_.refs_1_
  88.1 1.8 %add_convert_fusion.3.refs_1_.refs_0_ = bf16[128,1152]{1,0:T(8,128)(2,1)} fusion(bf16[128,1152]{1,0:T(8,128)(2,1)} %shard_map.81, bf16[768,2048]{1,0:T(8,128)(2,1)S(1)} %copy-done, s32[]{:T(128)S(6)} %select_n.79), kind=kLoop, calls=%fused_computation.3 | loop fusion | flops 589824 | bytes 884740 | tf_op jit(solution)/shard_map/convert_element_type | solution.py:578
  89.9 2.1 %collective-permute-start.17 = (bf16[512,2048]{1,0:T(8,128)(2,1)}, bf16[512,2048]{1,0:T(8,128)(2,1)}, u32[]{:S(2)}, u32[]{:S(2)}) collective-permute-start(bf16[512,2048]{1,0:T(8,128)(2,1)} %shard_map.83), channel_id=1, source_target_pairs={{1,5},{14,10},{17,21},{30,26}} | collective-permute-start | bytes 6291464 | tf_op jit(solution)/shard_map/ppermute | solution.py:503
  92.0 1.9 %collective-permute-start.14 = (bf16[128,1152]{1,0:T(8,128)(2,1)S(1)}, bf16[128,1152]{1,0:T(8,128)(2,1)}, u32[]{:S(2)}, u32[]{:S(2)}) collective-permute-start(bf16[128,1152]{1,0:T(8,128)(2,1)S(1)} %copy-done.4), channel_id=1, source_target_pairs={{12,8},{8,4},{4,0},{13,9},{9,5},{2,6},{6,10},{3,7},{7,11},{11,15},... | collective-permute-start | bytes 884744 | tf_op jit(solution)/shard_map/ppermute | solution.py:503
  95.1 2.2 %collective-permute-start.16 = (bf16[128,896]{1,0:T(8,128)(2,1)}, bf16[128,896]{1,0:T(8,128)(2,1)}, u32[]{:S(2)}, u32[]{:S(2)}) collective-permute-start(bf16[128,896]{1,0:T(8,128)(2,1)} %add_convert_fusion.10.refs_2_.refs_1_), channel_id=1, source_target_pairs={{12,8},{8,4},{4,0},{13,9},{9,5},{2,6},{6,10},{3,7},{7,11},{11,15},... | collective-permute-start | bytes 688136 | tf_op jit(solution)/shard_map/ppermute | solution.py:503
  97.3 5.2 %collective-permute-done.14.refs_0_ = bf16[128,1152]{1,0:T(8,128)(2,1)} collective-permute-done((bf16[128,1152]{1,0:T(8,128)(2,1)S(1)}, bf16[128,1152]{1,0:T(8,128)(2,1)}, u32[]{:S(2)}, u32[]{:S(2)}) %collective-permute-start.14) | collective-permute-done | bytes 294944 | tf_op jit(solution)/shard_map/ppermute | solution.py:503
  102.5 1.8 %add_convert_fusion.2.refs_2_.refs_1_ = bf16[128,1152]{1,0:T(8,128)(2,1)} fusion(bf16[128,1152]{1,0:T(8,128)(2,1)} %shard_map.82, bf16[768,2048]{1,0:T(8,128)(2,1)S(1)} %copy-done, s32[]{:T(128)S(6)} %select_n.85), kind=kLoop, calls=%fused_computation.2 | loop fusion | flops 589824 | bytes 884740 | tf_op jit(solution)/shard_map/convert_element_type | solution.py:578
  104.3 2.2 %collective-permute-start.19 = (bf16[128,1152]{1,0:T(8,128)(2,1)}, bf16[128,1152]{1,0:T(8,128)(2,1)}, u32[]{:S(2)}, u32[]{:S(2)}) collective-permute-start(bf16[128,1152]{1,0:T(8,128)(2,1)} %add_convert_fusion.2.refs_2_.refs_1_), channel_id=1, source_target_pairs={{12,8},{8,4},{4,0},{13,9},{9,5},{2,6},{6,10},{3,7},{7,11},{11,15},... | collective-permute-start | bytes 884744 | tf_op jit(solution)/shard_map/ppermute | solution.py:503
  107.4 1.7 add_convert_fusion.9.refs_3_.refs_2_
  109.1 1.7 collective-permute-start.24
  110.8 3.1 %collective-permute-start.21 = (bf16[128,896]{1,0:T(8,128)(2,1)}, bf16[128,896]{1,0:T(8,128)(2,1)}, u32[]{:S(2)}, u32[]{:S(2)}) collective-permute-start(bf16[128,896]{1,0:T(8,128)(2,1)} %add_convert_fusion.9.refs_3_.refs_2_), channel_id=1, source_target_pairs={{12,8},{8,4},{4,0},{13,9},{9,5},{2,6},{6,10},{3,7},{7,11},{11,15},... | collective-permute-start | bytes 688136 | tf_op jit(solution)/shard_map/ppermute | solution.py:503
  113.8 1.8 %add_convert_fusion.1.refs_0_ = bf16[128,1152]{1,0:T(8,128)(2,1)} fusion(bf16[128,1152]{1,0:T(8,128)(2,1)} %shard_map.86, bf16[768,2048]{1,0:T(8,128)(2,1)S(1)} %copy-done, s32[]{:T(128)S(6)} %select_n.87), kind=kLoop, calls=%fused_computation.1 | loop fusion | flops 589824 | bytes 884740 | tf_op jit(solution)/shard_map/convert_element_type | solution.py:578
  115.6 3.0 %collective-permute-start.22 = (bf16[128,1152]{1,0:T(8,128)(2,1)}, bf16[128,1152]{1,0:T(8,128)(2,1)}, u32[]{:S(2)}, u32[]{:S(2)}) collective-permute-start(bf16[128,1152]{1,0:T(8,128)(2,1)} %add_convert_fusion.1.refs_0_), channel_id=1, source_target_pairs={{8,4},{4,0},{9,5},{6,10},{7,11},{11,15},{24,20},{20,16},{25,21},{2... | collective-permute-start | bytes 884744 | tf_op jit(solution)/shard_map/ppermute | solution.py:503
  118.6 1.9 %collective-permute-done.21 = bf16[128,896]{1,0:T(8,128)(2,1)} collective-permute-done((bf16[128,896]{1,0:T(8,128)(2,1)}, bf16[128,896]{1,0:T(8,128)(2,1)}, u32[]{:S(2)}, u32[]{:S(2)}) %collective-permute-start.21) | collective-permute-done | bytes 229408 | tf_op jit(solution)/shard_map/ppermute | solution.py:503
  120.4 1.7 add_convert_fusion.8.refs_1_
  122.1 3.6 %collective-permute-start.25 = (bf16[128,896]{1,0:T(8,128)(2,1)}, bf16[128,896]{1,0:T(8,128)(2,1)}, u32[]{:S(2)}, u32[]{:S(2)}) collective-permute-start(bf16[128,896]{1,0:T(8,128)(2,1)} %add_convert_fusion.8.refs_1_), channel_id=1, source_target_pairs={{8,4},{4,0},{9,5},{6,10},{7,11},{11,15},{24,20},{20,16},{25,21},{2... | collective-permute-start | bytes 688136 | tf_op jit(solution)/shard_map/ppermute | solution.py:503
  127.6 2.6 %shard_map.84.own_ref.refs_6_.refs_1_ = bf16[256,2048]{1,0:T(8,128)(2,1)} custom-call(s32[1]{0:T(128)} %bitcast.9.u_ref, bf16[128,1152]{1,0:T(8,128)(2,1)S(1)} %copy-done.4, bf16[128,896]{1,0:T(8,128)(2,1)S(1)} %copy-done.14, bf16[128,1152]{1,0:T(8,128)(2,1)} %add_convert_fusion.2.refs_2_.refs_1_, bf16[128,896]{1,0:T(8,128)(2,1)S(1)} %copy-done.13, ...), custom_call_target="tpu_custom_call" | custom-call | tf_op jit(solution)/shard_map/pallas_call | solution.py:383
  130.2 1.6 collective-permute-start.18
  131.8 2.7 %shard_map.88.refs_3_.refs_7_ = bf16[256,2048]{1,0:T(8,128)(2,1)} custom-call(s32[1]{0:T(128)} %bitcast.9.u_ref, bf16[128,1152]{1,0:T(8,128)(2,1)S(1)} %copy-done.8, bf16[128,896]{1,0:T(8,128)(2,1)} %add_convert_fusion.12.refs_8_.refs_1_, bf16[128,1152]{1,0:T(8,128)(2,1)S(1)} %copy-done.6, bf16[128,896]{1,0:T(8,128)(2,1)} %add_convert_fusion.11.refs_6_.refs_3_, ...), custom_call_target="tpu_custom_call" | custom-call | tf_op jit(solution)/shard_map/pallas_call | solution.py:383
  137.9 1.7 shard_map.91
  142.6 3.1 %shard_map.93.refs_0_.refs_13_ = f32[256,2048]{1,0:T(8,128)S(1)} custom-call(s32[2]{0:T(128)S(1)} %pad_add_fusion.refs_0_.meta_ref, s32[64]{0:T(128)S(1)} %copy-done.17, s32[64]{0:T(128)S(1)} %copy-done.18, s32[16]{0:T(128)S(1)} %copy-done.20, s32[16]{0:T(128)S(1)} %fusion.2.refs_2_.refs_4_, s32[16]{0:T(128)S(1)} %fusion.1.refs_3_.refs_5_, ...), custom_call_target="tpu_custom_call" | custom-call | tf_op jit(solution)/shard_map/pallas_call | solution.py:470
  146.3 1.3 collective-permute-start.31
  149.5 1.3 collective-permute-start.32
  150.8 17.6 %collective-permute-done.32.refs_12_ = bf16[128,2048]{1,0:T(8,128)(2,1)S(1)} collective-permute-done((bf16[128,2048]{1,0:T(8,128)(2,1)S(1)}, bf16[128,2048]{1,0:T(8,128)(2,1)S(1)}, u32[]{:S(2)}, u32[]{:S(2)}) %collective-permute-start.32) | collective-permute-done | bytes 524320 | tf_op jit(solution)/shard_map/ppermute | solution.py:503
  168.4 3.2 %shard_map.96 = bf16[256,2048]{1,0:T(8,128)(2,1)} custom-call(s32[2]{0:T(128)S(1)} %pad_add_fusion.refs_0_.meta_ref, s32[64]{0:T(128)S(1)} %copy-done.17, s32[64]{0:T(128)S(1)} %copy-done.18, s32[16]{0:T(128)S(1)} %copy-done.20, s32[16]{0:T(128)S(1)} %fusion.2.refs_2_.refs_4_, s32[16]{0:T(128)S(1)} %fusion.1.refs_3_.refs_5_, s32[16]{0:T(128)S(1)} %fusion.refs_4_.refs_6_, ...), custom_call_target="tpu_custom_call" | custom-call | tf_op jit(solution)/shard_map/pallas_call | solution.py:470
  (108 shorter events, 28.3 us)
Async XLA Ops:
  0.0 1.2 copy-start.1
  3.5 3.3 %collective-permute-start = (bf16[272,2048]{1,0:T(8,128)(2,1)}, bf16[272,2048]{1,0:T(8,128)(2,1)S(1)}, u32[]{:S(2)}, u32[]{:S(2)}) collective-permute-start(bf16[272,2048]{1,0:T(8,128)(2,1)} %shard_map.73), channel_id=1, source_target_pairs={{0,1},{1,0},{2,3},{3,2},{4,5},{5,4},{6,7},{7,6},{8,9},{9,8},{10,11... | collective-permute-start | bytes 3342344 | tf_op jit(solution)/shard_map/ppermute | solution.py:491
  4.2 29.4 %collective-permute-start.1 = (bf16[272,2048]{1,0:T(8,128)(2,1)}, bf16[272,2048]{1,0:T(8,128)(2,1)}, u32[]{:S(2)}, u32[]{:S(2)}) collective-permute-start(bf16[272,2048]{1,0:T(8,128)(2,1)} %shard_map.73), channel_id=1, source_target_pairs={{0,2},{1,3},{2,0},{3,1},{4,6},{5,7},{6,4},{7,5},{8,10},{9,11},{10,... | collective-permute-start | bytes 3342344 | tf_op jit(solution)/shard_map/ppermute | solution.py:491
  7.8 1.2 copy-start.2
  9.0 11.3 %copy-start.3 = (bf16[16,16,2048]{2,1,0:T(8,128)(2,1)S(1)}, bf16[16,16,2048]{2,1,0:T(8,128)(2,1)}, u32[]{:S(2)}) copy-start(bf16[16,16,2048]{2,1,0:T(8,128)(2,1)} %param.7) | copy-start | bytes 3145732
  9.0 11.3 %copy-start.17 = (s32[64]{0:T(128)S(1)}, s32[64]{0:T(128)}, u32[]{:S(2)}) copy-start(s32[64]{0:T(128)} %refs_1_.11) | copy-start | bytes 772
  9.0 11.3 %copy-start.18 = (s32[64]{0:T(128)S(1)}, s32[64]{0:T(128)}, u32[]{:S(2)}) copy-start(s32[64]{0:T(128)} %refs_2_.7) | copy-start | bytes 772
  16.7 9.5 %collective-permute-start.3 = (bf16[128,896]{1,0:T(8,128)(2,1)S(1)}, bf16[128,896]{1,0:T(8,128)(2,1)S(1)}, u32[]{:S(2)}, u32[]{:S(2)}) collective-permute-start(bf16[128,896]{1,0:T(8,128)(2,1)S(1)} %slice.42), channel_id=1, source_target_pairs={{12,8},{13,9},{2,6},{3,7},{28,24},{29,25},{18,22},{19,23}} | collective-permute-start | bytes 688136 | tf_op jit(solution)/shard_map/ppermute | solution.py:503
  19.0 12.7 %collective-permute-start.2 = (bf16[128,1152]{1,0:T(8,128)(2,1)S(1)}, bf16[128,1152]{1,0:T(8,128)(2,1)S(1)}, u32[]{:S(2)}, u32[]{:S(2)}) collective-permute-start(bf16[128,1152]{1,0:T(8,128)(2,1)S(1)} %slice.40), channel_id=1, source_target_pairs={{12,8},{13,9},{2,6},{3,7},{28,24},{29,25},{18,22},{19,23}} | collective-permute-start | bytes 884744 | tf_op jit(solution)/shard_map/ppermute | solution.py:503
  28.1 6.7 %copy-start.12 = (bf16[128,896]{1,0:T(8,128)(2,1)S(1)}, bf16[128,896]{1,0:T(8,128)(2,1)}, u32[]{:S(2)}) copy-start(bf16[128,896]{1,0:T(8,128)(2,1)} %add_convert_fusion.13.refs_2_.refs_12_) | copy-start | bytes 688132
  33.6 5.7 %collective-permute-start.4 = (bf16[272,2048]{1,0:T(8,128)(2,1)}, bf16[272,2048]{1,0:T(8,128)(2,1)}, u32[]{:S(2)}, u32[]{:S(2)}) collective-permute-start(bf16[272,2048]{1,0:T(8,128)(2,1)} %shard_map.76.refs_7_.refs_3_), channel_id=1, source_target_pairs={{0,1},{1,0},{2,3},{3,2},{4,5},{5,4},{6,7},{7,6},{8,9},{9,8},{10,11... | collective-permute-start | bytes 3342344 | tf_op jit(solution)/shard_map/ppermute | solution.py:491
  34.8 17.4 %collective-permute-start.7 = (bf16[128,896]{1,0:T(8,128)(2,1)S(1)}, bf16[128,896]{1,0:T(8,128)(2,1)S(1)}, u32[]{:S(2)}, u32[]{:S(2)}) collective-permute-start(bf16[128,896]{1,0:T(8,128)(2,1)S(1)} %copy-done.12), channel_id=1, source_target_pairs={{12,8},{8,4},{13,9},{9,5},{2,6},{6,10},{3,7},{7,11},{28,24},{24,20... | collective-permute-start | bytes 688136 | tf_op jit(solution)/shard_map/ppermute | solution.py:503
  37.4 18.4 %collective-permute-start.5 = (bf16[128,1152]{1,0:T(8,128)(2,1)}, bf16[128,1152]{1,0:T(8,128)(2,1)S(1)}, u32[]{:S(2)}, u32[]{:S(2)}) collective-permute-start(bf16[128,1152]{1,0:T(8,128)(2,1)} %add_convert_fusion.6.refs_1_.refs_11_), channel_id=1, source_target_pairs={{12,8},{8,4},{13,9},{9,5},{2,6},{6,10},{3,7},{7,11},{28,24},{24,20... | collective-permute-start | bytes 884744 | tf_op jit(solution)/shard_map/ppermute | solution.py:503
  41.0 17.9 %copy-start.16 = (bf16[256,128]{1,0:T(8,128)(2,1)S(1)}, bf16[256,128]{1,0:T(8,128)(2,1)}, u32[]{:S(2)}) copy-start(bf16[256,128]{1,0:T(8,128)(2,1)} %copy-done.15) | copy-start | bytes 196612
  53.9 14.6 %collective-permute-start.12 = (bf16[128,896]{1,0:T(8,128)(2,1)}, bf16[128,896]{1,0:T(8,128)(2,1)}, u32[]{:S(2)}, u32[]{:S(2)}) collective-permute-start(bf16[128,896]{1,0:T(8,128)(2,1)} %add_convert_fusion.12.refs_8_.refs_1_), channel_id=1, source_target_pairs={{12,8},{8,4},{4,0},{13,9},{9,5},{2,6},{6,10},{3,7},{7,11},{11,15},... | collective-permute-start | bytes 688136 | tf_op jit(solution)/shard_map/ppermute | solution.py:503
  56.9 8.3 %copy-start.7 = (bf16[128,1152]{1,0:T(8,128)(2,1)}, bf16[128,1152]{1,0:T(8,128)(2,1)S(1)}, u32[]{:S(2)}) copy-start(bf16[128,1152]{1,0:T(8,128)(2,1)S(1)} %add_convert_fusion.5.refs_7_.refs_0_) | copy-start | bytes 884740
  56.9 15.5 %collective-permute-start.6 = (bf16[128,1152]{1,0:T(8,128)(2,1)S(1)}, bf16[128,1152]{1,0:T(8,128)(2,1)}, u32[]{:S(2)}, u32[]{:S(2)}) collective-permute-start(bf16[128,1152]{1,0:T(8,128)(2,1)S(1)} %add_convert_fusion.5.refs_7_.refs_0_), channel_id=1, source_target_pairs={{12,8},{8,4},{4,0},{13,9},{9,5},{2,6},{6,10},{3,7},{7,11},{11,15},... | collective-permute-start | bytes 884744 | tf_op jit(solution)/shard_map/ppermute | solution.py:503
  58.8 9.7 %copy-start = (bf16[768,2048]{1,0:T(8,128)(2,1)S(1)}, bf16[768,2048]{1,0:T(8,128)(2,1)}, u32[]{:S(2)}) copy-start(bf16[768,2048]{1,0:T(8,128)(2,1)} %shard_map.77.refs_1_) | copy-start | bytes 9437188
  65.1 12.0 %collective-permute-start.10 = (bf16[256,128]{1,0:T(8,128)(2,1)}, bf16[256,128]{1,0:T(8,128)(2,1)S(1)}, u32[]{:S(2)}, u32[]{:S(2)}) collective-permute-start(bf16[256,128]{1,0:T(8,128)(2,1)} %shard_map.78.refs_1_.refs_0_), channel_id=1, source_target_pairs={{0,4},{4,0},{8,12},{12,8},{1,5},{5,1},{9,13},{13,9},{2,6},{6,2},{1... | collective-permute-start | bytes 196616 | tf_op jit(solution)/shard_map/ppermute | solution.py:617
  67.3 9.9 %collective-permute-start.11 = (bf16[256,128]{1,0:T(8,128)(2,1)}, bf16[256,128]{1,0:T(8,128)(2,1)}, u32[]{:S(2)}, u32[]{:S(2)}) collective-permute-start(bf16[256,128]{1,0:T(8,128)(2,1)} %shard_map.78.refs_1_.refs_0_), channel_id=1, source_target_pairs={{0,8},{4,12},{8,0},{12,4},{1,9},{5,13},{9,1},{13,5},{2,10},{6,14},... | collective-permute-start | bytes 196616 | tf_op jit(solution)/shard_map/ppermute | solution.py:617
  67.3 9.9 %collective-permute-start.9 = (bf16[256,128]{1,0:T(8,128)(2,1)}, bf16[256,128]{1,0:T(8,128)(2,1)}, u32[]{:S(2)}, u32[]{:S(2)}) collective-permute-start(bf16[256,128]{1,0:T(8,128)(2,1)} %shard_map.78.refs_1_.refs_0_), channel_id=1, source_target_pairs={{0,12},{4,8},{8,4},{12,0},{1,13},{5,9},{9,5},{13,1},{2,14},{6,10},... | collective-permute-start | bytes 196616 | tf_op jit(solution)/shard_map/ppermute | solution.py:617
  70.2 16.2 %collective-permute-start.13 = (bf16[128,896]{1,0:T(8,128)(2,1)}, bf16[128,896]{1,0:T(8,128)(2,1)}, u32[]{:S(2)}, u32[]{:S(2)}) collective-permute-start(bf16[128,896]{1,0:T(8,128)(2,1)} %add_convert_fusion.11.refs_6_.refs_3_), channel_id=1, source_target_pairs={{12,8},{8,4},{4,0},{13,9},{9,5},{2,6},{6,10},{3,7},{7,11},{11,15},... | collective-permute-start | bytes 688136 | tf_op jit(solution)/shard_map/ppermute | solution.py:503
  73.4 10.4 %copy-start.5 = (bf16[128,1152]{1,0:T(8,128)(2,1)}, bf16[128,1152]{1,0:T(8,128)(2,1)S(1)}, u32[]{:S(2)}) copy-start(bf16[128,1152]{1,0:T(8,128)(2,1)S(1)} %add_convert_fusion.4.refs_5_.refs_2_) | copy-start | bytes 884740
  73.4 14.7 %collective-permute-start.8 = (bf16[128,1152]{1,0:T(8,128)(2,1)S(1)}, bf16[128,1152]{1,0:T(8,128)(2,1)}, u32[]{:S(2)}, u32[]{:S(2)}) collective-permute-start(bf16[128,1152]{1,0:T(8,128)(2,1)S(1)} %add_convert_fusion.4.refs_5_.refs_2_), channel_id=1, source_target_pairs={{12,8},{8,4},{4,0},{13,9},{9,5},{2,6},{6,10},{3,7},{7,11},{11,15},... | collective-permute-start | bytes 884744 | tf_op jit(solution)/shard_map/ppermute | solution.py:503
  83.8 4.3 %copy-start.10 = (bf16[128,2048]{1,0:T(8,128)(2,1)}, bf16[128,2048]{1,0:T(8,128)(2,1)S(1)}, u32[]{:S(2)}) copy-start(bf16[128,2048]{1,0:T(8,128)(2,1)S(1)} %get-tuple-element.11.refs_1_.refs_9_) | copy-start | bytes 1572868
  83.8 13.5 %collective-permute-start.15 = (bf16[128,2048]{1,0:T(8,128)(2,1)}, bf16[128,2048]{1,0:T(8,128)(2,1)}, u32[]{:S(2)}, u32[]{:S(2)}) collective-permute-start(bf16[128,2048]{1,0:T(8,128)(2,1)} %get-tuple-element.12), channel_id=1, source_target_pairs={{0,1},{1,0},{2,3},{3,2},{4,5},{5,4},{6,7},{7,6},{8,9},{9,8},{10,11... | collective-permute-start | bytes 1572872 | tf_op jit(solution)/shard_map/ppermute | solution.py:491
  89.9 2.1 %copy-start.4 = (bf16[128,1152]{1,0:T(8,128)(2,1)S(1)}, bf16[128,1152]{1,0:T(8,128)(2,1)}, u32[]{:S(2)}) copy-start(bf16[128,1152]{1,0:T(8,128)(2,1)} %add_convert_fusion.3.refs_1_.refs_0_) | copy-start | bytes 884740
  89.9 35.9 %collective-permute-start.17 = (bf16[512,2048]{1,0:T(8,128)(2,1)}, bf16[512,2048]{1,0:T(8,128)(2,1)}, u32[]{:S(2)}, u32[]{:S(2)}) collective-permute-start(bf16[512,2048]{1,0:T(8,128)(2,1)} %shard_map.83), channel_id=1, source_target_pairs={{1,5},{14,10},{17,21},{30,26}} | collective-permute-start | bytes 6291464 | tf_op jit(solution)/shard_map/ppermute | solution.py:503
  92.0 10.5 %collective-permute-start.14 = (bf16[128,1152]{1,0:T(8,128)(2,1)S(1)}, bf16[128,1152]{1,0:T(8,128)(2,1)}, u32[]{:S(2)}, u32[]{:S(2)}) collective-permute-start(bf16[128,1152]{1,0:T(8,128)(2,1)S(1)} %copy-done.4), channel_id=1, source_target_pairs={{12,8},{8,4},{4,0},{13,9},{9,5},{2,6},{6,10},{3,7},{7,11},{11,15},... | collective-permute-start | bytes 884744 | tf_op jit(solution)/shard_map/ppermute | solution.py:503
  95.1 15.7 %collective-permute-start.20 = (bf16[128,2048]{1,0:T(8,128)(2,1)}, bf16[128,2048]{1,0:T(8,128)(2,1)}, u32[]{:S(2)}, u32[]{:S(2)}) collective-permute-start(bf16[128,2048]{1,0:T(8,128)(2,1)} %get-tuple-element.13), channel_id=1, source_target_pairs={{0,2},{1,3},{2,0},{3,1},{4,6},{5,7},{6,4},{7,5},{8,10},{9,11},{10,... | collective-permute-start | bytes 1572872 | tf_op jit(solution)/shard_map/ppermute | solution.py:491
  95.1 12.4 %collective-permute-start.16 = (bf16[128,896]{1,0:T(8,128)(2,1)}, bf16[128,896]{1,0:T(8,128)(2,1)}, u32[]{:S(2)}, u32[]{:S(2)}) collective-permute-start(bf16[128,896]{1,0:T(8,128)(2,1)} %add_convert_fusion.10.refs_2_.refs_1_), channel_id=1, source_target_pairs={{12,8},{8,4},{4,0},{13,9},{9,5},{2,6},{6,10},{3,7},{7,11},{11,15},... | collective-permute-start | bytes 688136 | tf_op jit(solution)/shard_map/ppermute | solution.py:503
  104.3 9.6 %collective-permute-start.19 = (bf16[128,1152]{1,0:T(8,128)(2,1)}, bf16[128,1152]{1,0:T(8,128)(2,1)}, u32[]{:S(2)}, u32[]{:S(2)}) collective-permute-start(bf16[128,1152]{1,0:T(8,128)(2,1)} %add_convert_fusion.2.refs_2_.refs_1_), channel_id=1, source_target_pairs={{12,8},{8,4},{4,0},{13,9},{9,5},{2,6},{6,10},{3,7},{7,11},{11,15},... | collective-permute-start | bytes 884744 | tf_op jit(solution)/shard_map/ppermute | solution.py:503
  109.1 22.7 %collective-permute-start.24 = (bf16[256,2048]{1,0:T(8,128)(2,1)}, bf16[256,2048]{1,0:T(8,128)(2,1)}, u32[]{:S(2)}, u32[]{:S(2)}) collective-permute-start(bf16[256,2048]{1,0:T(8,128)(2,1)} %shard_map.87), channel_id=1, source_target_pairs={{1,5},{14,10},{17,21},{30,26}} | collective-permute-start | bytes 3145736 | tf_op jit(solution)/shard_map/ppermute | solution.py:503
  110.8 25.1 %collective-permute-start.23 = (bf16[128,2048]{1,0:T(8,128)(2,1)}, bf16[128,2048]{1,0:T(8,128)(2,1)}, u32[]{:S(2)}, u32[]{:S(2)}) collective-permute-start(bf16[128,2048]{1,0:T(8,128)(2,1)} %get-tuple-element.14), channel_id=1, source_target_pairs={{0,3},{1,2},{2,1},{3,0},{4,7},{5,6},{6,5},{7,4},{8,11},{9,10},{10,... | collective-permute-start | bytes 1572872 | tf_op jit(solution)/shard_map/ppermute | solution.py:491
  110.8 9.7 %collective-permute-start.21 = (bf16[128,896]{1,0:T(8,128)(2,1)}, bf16[128,896]{1,0:T(8,128)(2,1)}, u32[]{:S(2)}, u32[]{:S(2)}) collective-permute-start(bf16[128,896]{1,0:T(8,128)(2,1)} %add_convert_fusion.9.refs_3_.refs_2_), channel_id=1, source_target_pairs={{12,8},{8,4},{4,0},{13,9},{9,5},{2,6},{6,10},{3,7},{7,11},{11,15},... | collective-permute-start | bytes 688136 | tf_op jit(solution)/shard_map/ppermute | solution.py:503
  115.6 20.2 %collective-permute-start.22 = (bf16[128,1152]{1,0:T(8,128)(2,1)}, bf16[128,1152]{1,0:T(8,128)(2,1)}, u32[]{:S(2)}, u32[]{:S(2)}) collective-permute-start(bf16[128,1152]{1,0:T(8,128)(2,1)} %add_convert_fusion.1.refs_0_), channel_id=1, source_target_pairs={{8,4},{4,0},{9,5},{6,10},{7,11},{11,15},{24,20},{20,16},{25,21},{2... | collective-permute-start | bytes 884744 | tf_op jit(solution)/shard_map/ppermute | solution.py:503
  122.1 14.8 %collective-permute-start.25 = (bf16[128,896]{1,0:T(8,128)(2,1)}, bf16[128,896]{1,0:T(8,128)(2,1)}, u32[]{:S(2)}, u32[]{:S(2)}) collective-permute-start(bf16[128,896]{1,0:T(8,128)(2,1)} %add_convert_fusion.8.refs_1_), channel_id=1, source_target_pairs={{8,4},{4,0},{9,5},{6,10},{7,11},{11,15},{24,20},{20,16},{25,21},{2... | collective-permute-start | bytes 688136 | tf_op jit(solution)/shard_map/ppermute | solution.py:503
  127.6 4.2 %copy-start.6 = (bf16[128,1152]{1,0:T(8,128)(2,1)S(1)}, bf16[128,1152]{1,0:T(8,128)(2,1)}, u32[]{:S(2)}) copy-start(bf16[128,1152]{1,0:T(8,128)(2,1)} %copy-done.5) | copy-start | bytes 884740
  127.6 4.2 %copy-start.8 = (bf16[128,1152]{1,0:T(8,128)(2,1)S(1)}, bf16[128,1152]{1,0:T(8,128)(2,1)}, u32[]{:S(2)}) copy-start(bf16[128,1152]{1,0:T(8,128)(2,1)} %copy-done.7) | copy-start | bytes 884740
  130.2 10.8 %collective-permute-start.18 = (bf16[256,2048]{1,0:T(8,128)(2,1)}, bf16[256,2048]{1,0:T(8,128)(2,1)}, u32[]{:S(2)}, u32[]{:S(2)}) collective-permute-start(bf16[256,2048]{1,0:T(8,128)(2,1)} %shard_map.84.own_ref.refs_6_.refs_1_), channel_id=1, source_target_pairs={{0,2},{5,7},{10,8},{15,13},{16,18},{21,23},{26,24},{31,29}} | collective-permute-start | bytes 3145736 | tf_op jit(solution)/shard_map/ppermute | solution.py:503
  134.5 7.9 %collective-permute-start.27 = (bf16[256,2048]{1,0:T(8,128)(2,1)}, bf16[256,2048]{1,0:T(8,128)(2,1)}, u32[]{:S(2)}, u32[]{:S(2)}) collective-permute-start(bf16[256,2048]{1,0:T(8,128)(2,1)} %shard_map.88.refs_3_.refs_7_), channel_id=1, source_target_pairs={{0,1},{5,4},{10,11},{15,14},{2,3},{7,6},{8,9},{13,12},{16,17},{21,... | collective-permute-start | bytes 3145736 | tf_op jit(solution)/shard_map/ppermute | solution.py:503
  139.6 6.1 %collective-permute-start.26 = (bf16[256,2048]{1,0:T(8,128)(2,1)S(1)}, bf16[256,2048]{1,0:T(8,128)(2,1)S(1)}, u32[]{:S(2)}, u32[]{:S(2)}) collective-permute-start(bf16[256,2048]{1,0:T(8,128)(2,1)S(1)} %get-tuple-element.15.own_ref), channel_id=1, source_target_pairs={{0,2},{5,7},{10,8},{15,13},{16,18},{21,23},{26,24},{31,29}} | collective-permute-start | bytes 3145736 | tf_op jit(solution)/shard_map/ppermute | solution.py:503
  140.3 1.3 collective-permute-start.28
  141.6 1.0 copy-start.11
  141.8 7.1 %collective-permute-start.29 = (bf16[128,2048]{1,0:T(8,128)(2,1)S(1)}, bf16[128,2048]{1,0:T(8,128)(2,1)S(1)}, u32[]{:S(2)}, u32[]{:S(2)}) collective-permute-start(bf16[128,2048]{1,0:T(8,128)(2,1)S(1)} %shard_map.92.refs_13_.own_ref), channel_id=1, source_target_pairs={{0,2},{5,7},{10,8},{15,13},{16,18},{21,23},{26,24},{31,29}} | collective-permute-start | bytes 1572872 | tf_op jit(solution)/shard_map/ppermute | solution.py:503
  146.3 22.1 %collective-permute-start.31 = (bf16[256,2048]{1,0:T(8,128)(2,1)S(1)}, bf16[256,2048]{1,0:T(8,128)(2,1)S(1)}, u32[]{:S(2)}, u32[]{:S(2)}) collective-permute-start(bf16[256,2048]{1,0:T(8,128)(2,1)S(1)} %shard_map.94.refs_8_), channel_id=1, source_target_pairs={{0,1},{5,4},{10,11},{15,14},{2,3},{7,6},{8,9},{13,12},{16,17},{21,... | collective-permute-start | bytes 3145736 | tf_op jit(solution)/shard_map/ppermute | solution.py:503
  147.6 20.8 %collective-permute-start.30 = (bf16[256,2048]{1,0:T(8,128)(2,1)}, bf16[256,2048]{1,0:T(8,128)(2,1)S(1)}, u32[]{:S(2)}, u32[]{:S(2)}) collective-permute-start(bf16[256,2048]{1,0:T(8,128)(2,1)} %shard_map.85.refs_2_.refs_7_), channel_id=1, source_target_pairs={{0,1},{5,4},{10,11},{15,14},{2,3},{7,6},{8,9},{13,12},{16,17},{21,... | collective-permute-start | bytes 3145736 | tf_op jit(solution)/shard_map/ppermute | solution.py:503
  149.5 18.9 %collective-permute-start.32 = (bf16[128,2048]{1,0:T(8,128)(2,1)S(1)}, bf16[128,2048]{1,0:T(8,128)(2,1)S(1)}, u32[]{:S(2)}, u32[]{:S(2)}) collective-permute-start(bf16[128,2048]{1,0:T(8,128)(2,1)S(1)} %shard_map.95.refs_9_), channel_id=1, source_target_pairs={{0,1},{5,4},{10,11},{15,14},{2,3},{7,6},{8,9},{13,12},{16,17},{21,... | collective-permute-start | bytes 1572872 | tf_op jit(solution)/shard_map/ppermute | solution.py:503
  (7 other events, 6.1 us)

commit v7 on v6

--- a/solution.py
+++ b/solution.py
@@ -615,7 +615,7 @@
         meta, req, slot, xs[2:], (2, 3), down_t, low, held, rank, tokens, capacity, (final[2, 0], final[2, 1])
     )
     lows = [low] + [lax.ppermute(low, "tensor", [(i, i ^ f) for i in range(4)]) for f in (3, 1, 2)]
-    chain_step(3, low)
+    chain_step(3, low, both=True)
     delta = up_project(
         meta, req, slot, lows, up_2d, held, rank, tokens, capacity, requests, (final[3, 0], final[3, 1])
     )
@@ -634,7 +634,7 @@
     (two,) = merged(4, 6)
     (one,) = merged(2, 4, deps=(two,))
     hand_on(one)
-    chain_step(7, two, deltas[3], one, both=True)
+    chain_step(7, two, deltas[3], both=True)
     two = keep(meta, *cross(two))
     three, last = merged(6, 8, True)
     came = on_mesh(last, last_pairs)

time: 173 us -> 172 us (level)
  transfers between devices with their start and end apart: 33 -> 33, of which waited for: 6 -> 5; matrix products, arithmetic and copies ran while one was open for 16% -> 16% of each run, Pallas kernels for 28% -> 28%
where the time goes in v7:
time: 172 us; the launch traced here: 170 us
  starting transfers between devices  52.7 us (31%)
  Pallas kernels  51.8 us (30%)
  waiting for transfers between devices  29 us (17%)
  other arithmetic  22.4 us (13%)
  local copies, waits for them, and re-layouts  13.4 us (8%)
    ppermute x24, starting transfers between devices, on_mesh(): lax.ppermute(value, ('tensor', 'store'), [(a * 4 + b, c * 4 + d) for (a,...  43.6 us
    ppermute x24, waiting for transfers between devices, on_mesh(): lax.ppermute(value, ('tensor', 'store'), [(a * 4 + b, c * 4 + d) for (a,...  27.7 us
    convert_element_type x14, other arithmetic, chain_step(): value = total.astype(BF16)  21.6 us
    pallas_call x2, Pallas kernels, project(): pl.pallas_call(functools.partial(project_kernel, first, blocks, width, to...  18.1 us
    pallas_call x2, Pallas kernels, low_rank(): pl.pallas_call(functools.partial(low_kernel, flips, before is not None, h...  11.6 us
    unnamed x44, local copies, waits for them, and re-layouts  8.8 us
    pallas_call x1, Pallas kernels, up_project(): pl.pallas_call(functools.partial(up_kernel, len(deps), held, rank, reques...  6.65 us
    pallas_call x4, Pallas kernels, merge(): pl.pallas_call(functools.partial(merge_kernel, count, streams, bool(backs...  6.15 us
  transfers between devices with their start and end apart: 33, of which 5 were waited for; matrix products, arithmetic and copies ran while one was open for 16% of the time, Pallas kernels for 28%

profile of v7, /device:TPU:21, one launch (start us, length us, event | category | flops | bytes accessed | tf_op | source)
XLA Modules:
  0.0 169.9 jit_solution(16610020305867854567)
XLA Ops:
  1.9 1.6 shard_map.73
  5.5 1.3 collective-permute-done.refs_4_.refs_6_
  9.0 6.8 %shard_map.74.refs_6_.refs_10_ = bf16[768,2048]{1,0:T(8,128)(2,1)} custom-call(s32[2]{0:T(128)S(1)} %pad_add_fusion.refs_0_.meta_ref, s32[16]{0:T(128)S(1)} %copy-done.18, s32[16]{0:T(128)S(1)} %fusion.2.refs_2_.refs_4_, bf16[256,2048]{1,0:T(8,128)(2,1)S(1)} %bitcast.25, bf16[272,2048]{1,0:T(8,128)(2,1)} %copy-done.20, bf16[2048,2048]{1,0:T(8,128)(2,1)} %refs_9_.1), custom_call_target="tpu_custom_call" | custom-call | tf_op jit(solution)/shard_map/pallas_call | solution.py:160
  16.8 1.3 collective-permute-start.3
  19.0 1.3 collective-permute-start.2
  20.4 5.2 %shard_map.75.refs_3_.refs_6_ = bf16[256,128]{1,0:T(8,128)(2,1)S(1)} custom-call(s32[2]{0:T(128)S(1)} %pad_add_fusion.refs_0_.meta_ref, s32[64]{0:T(128)S(1)} %copy-done.16, s32[64]{0:T(128)S(1)} %copy-done.17, bf16[256,2048]{1,0:T(8,128)(2,1)S(1)} %bitcast.26, bf16[272,2048]{1,0:T(8,128)(2,1)} %copy-done.20, bf16[1024,2048]{1,0:T(8,128)(2,1)} %bitcast.28, ...), custom_call_target="tpu_custom_call" | custom-call | tf_op jit(solution)/shard_map/pallas_call | solution.py:239
  26.2 1.8 %add_convert_fusion.13.refs_2_.refs_12_ = bf16[128,896]{1,0:T(8,128)(2,1)} fusion(bf16[128,896]{1,0:T(8,128)(2,1)S(1)} %collective-permute-done.3, bf16[768,2048]{1,0:T(8,128)(2,1)} %shard_map.74.refs_6_.refs_10_, pred[]{:T(512)S(6)} %ge.4), kind=kLoop, calls=%fused_computation.13 | loop fusion | flops 573440 | bytes 917505 | tf_op jit(solution)/shard_map/convert_element_type | solution.py:578
  28.1 3.7 %collective-permute-done.2 = bf16[128,1152]{1,0:T(8,128)(2,1)S(1)} collective-permute-done((bf16[128,1152]{1,0:T(8,128)(2,1)S(1)}, bf16[128,1152]{1,0:T(8,128)(2,1)S(1)}, u32[]{:S(2)}, u32[]{:S(2)}) %collective-permute-start.2) | collective-permute-done | bytes 294944 | tf_op jit(solution)/shard_map/ppermute | solution.py:503
  31.8 1.9 %add_convert_fusion.6.refs_1_.refs_11_ = bf16[128,1152]{1,0:T(8,128)(2,1)} fusion(bf16[128,1152]{1,0:T(8,128)(2,1)S(1)} %collective-permute-done.2, bf16[768,2048]{1,0:T(8,128)(2,1)} %shard_map.74.refs_6_.refs_10_, pred[]{:T(512)S(6)} %ge.4), kind=kLoop, calls=%fused_computation.6 | loop fusion | flops 737280 | bytes 1179649 | tf_op jit(solution)/shard_map/convert_element_type | solution.py:578
  34.9 1.9 %collective-permute-start.7 = (bf16[128,896]{1,0:T(8,128)(2,1)S(1)}, bf16[128,896]{1,0:T(8,128)(2,1)S(1)}, u32[]{:S(2)}, u32[]{:S(2)}) collective-permute-start(bf16[128,896]{1,0:T(8,128)(2,1)S(1)} %copy-done.12), channel_id=1, source_target_pairs={{12,8},{8,4},{13,9},{9,5},{2,6},{6,10},{3,7},{7,11},{28,24},{24,20... | collective-permute-start | bytes 688136 | tf_op jit(solution)/shard_map/ppermute | solution.py:503
  37.5 1.9 %collective-permute-start.5 = (bf16[128,1152]{1,0:T(8,128)(2,1)}, bf16[128,1152]{1,0:T(8,128)(2,1)S(1)}, u32[]{:S(2)}, u32[]{:S(2)}) collective-permute-start(bf16[128,1152]{1,0:T(8,128)(2,1)} %add_convert_fusion.6.refs_1_.refs_11_), channel_id=1, source_target_pairs={{12,8},{8,4},{13,9},{9,5},{2,6},{6,10},{3,7},{7,11},{28,24},{24,20... | collective-permute-start | bytes 884744 | tf_op jit(solution)/shard_map/ppermute | solution.py:503
  41.4 11.3 %shard_map.77.refs_1_ = bf16[768,2048]{1,0:T(8,128)(2,1)} custom-call(s32[2]{0:T(128)S(1)} %pad_add_fusion.refs_0_.meta_ref, s32[16]{0:T(128)S(1)} %copy-done.18, s32[16]{0:T(128)S(1)} %fusion.2.refs_2_.refs_4_, s32[16]{0:T(128)S(1)} %fusion.1.refs_3_.refs_5_, s32[16]{0:T(128)S(1)} %fusion.refs_4_.refs_6_, ...), custom_call_target="tpu_custom_call", output_to_operand_aliasing={{}: (10, {})} | custom-call | tf_op jit(solution)/shard_map/pallas_call | solution.py:160
  52.7 1.7 add_convert_fusion.12.refs_8_.refs_1_
  54.4 1.9 %collective-permute-start.12 = (bf16[128,896]{1,0:T(8,128)(2,1)}, bf16[128,896]{1,0:T(8,128)(2,1)}, u32[]{:S(2)}, u32[]{:S(2)}) collective-permute-start(bf16[128,896]{1,0:T(8,128)(2,1)} %add_convert_fusion.12.refs_8_.refs_1_), channel_id=1, source_target_pairs={{12,8},{8,4},{4,0},{13,9},{9,5},{2,6},{6,10},{3,7},{7,11},{11,15},... | collective-permute-start | bytes 688136 | tf_op jit(solution)/shard_map/ppermute | solution.py:503
  57.4 1.9 %collective-permute-start.6 = (bf16[128,1152]{1,0:T(8,128)(2,1)S(1)}, bf16[128,1152]{1,0:T(8,128)(2,1)}, u32[]{:S(2)}, u32[]{:S(2)}) collective-permute-start(bf16[128,1152]{1,0:T(8,128)(2,1)S(1)} %add_convert_fusion.5.refs_7_.refs_0_), channel_id=1, source_target_pairs={{12,8},{8,4},{4,0},{13,9},{9,5},{2,6},{6,10},{3,7},{7,11},{11,15},... | collective-permute-start | bytes 884744 | tf_op jit(solution)/shard_map/ppermute | solution.py:503
  59.3 6.4 %shard_map.78.refs_1_.refs_0_ = bf16[256,128]{1,0:T(8,128)(2,1)} custom-call(s32[2]{0:T(128)S(1)} %pad_add_fusion.refs_0_.meta_ref, s32[64]{0:T(128)S(1)} %copy-done.16, s32[64]{0:T(128)S(1)} %copy-done.17, bf16[272,2048]{1,0:T(8,128)(2,1)} %shard_map.76.refs_7_.refs_3_, bf16[272,2048]{1,0:T(8,128)(2,1)} %copy-done.21, bf16[1024,2048]{1,0:T(8,128)(2,1)} %bitcast.29, ...), custom_call_target="tpu_custom_call" | custom-call | tf_op jit(solution)/shard_map/pallas_call | solution.py:239
  65.7 2.2 %collective-permute-start.10 = (bf16[256,128]{1,0:T(8,128)(2,1)}, bf16[256,128]{1,0:T(8,128)(2,1)S(1)}, u32[]{:S(2)}, u32[]{:S(2)}) collective-permute-start(bf16[256,128]{1,0:T(8,128)(2,1)} %shard_map.78.refs_1_.refs_0_), channel_id=1, source_target_pairs={{0,4},{4,0},{8,12},{12,8},{1,5},{5,1},{9,13},{13,9},{2,6},{6,2},{1... | collective-permute-start | bytes 196616 | tf_op jit(solution)/shard_map/ppermute | solution.py:617
  69.2 1.7 add_convert_fusion.11.refs_6_.refs_3_
  70.8 2.1 %collective-permute-start.13 = (bf16[128,896]{1,0:T(8,128)(2,1)}, bf16[128,896]{1,0:T(8,128)(2,1)}, u32[]{:S(2)}, u32[]{:S(2)}) collective-permute-start(bf16[128,896]{1,0:T(8,128)(2,1)} %add_convert_fusion.11.refs_6_.refs_3_), channel_id=1, source_target_pairs={{12,8},{8,4},{4,0},{13,9},{9,5},{2,6},{6,10},{3,7},{7,11},{11,15},... | collective-permute-start | bytes 688136 | tf_op jit(solution)/shard_map/ppermute | solution.py:503
  74.1 2.1 %collective-permute-start.8 = (bf16[128,1152]{1,0:T(8,128)(2,1)S(1)}, bf16[128,1152]{1,0:T(8,128)(2,1)}, u32[]{:S(2)}, u32[]{:S(2)}) collective-permute-start(bf16[128,1152]{1,0:T(8,128)(2,1)S(1)} %add_convert_fusion.4.refs_5_.refs_2_), channel_id=1, source_target_pairs={{12,8},{8,4},{4,0},{13,9},{9,5},{2,6},{6,10},{3,7},{7,11},{11,15},... | collective-permute-start | bytes 884744 | tf_op jit(solution)/shard_map/ppermute | solution.py:503
  76.2 1.6 slice.45.refs_0_
  77.8 6.7 %shard_map.81 = (bf16[128,2048]{1,0:T(8,128)(2,1)S(1)}, bf16[128,2048]{1,0:T(8,128)(2,1)}, bf16[128,2048]{1,0:T(8,128)(2,1)}, bf16[128,2048]{1,0:T(8,128)(2,1)}) custom-call(s32[2]{0:T(128)S(1)} %pad_add_fusion.refs_0_.meta_ref, s32[64]{0:T(128)S(1)} %copy-done.16, s32[64]{0:T(128)S(1)} %copy-done.17, bf16[256,128]{1,0:T(8,128)(2,1)} %shard_map.78.refs_1_.refs_0_, ...), custom_call_target="tpu_custom_call" | custom-call | tf_op jit(solution)/shard_map/pallas_call | solution.py:290
  84.5 2.5 %collective-permute-start.15 = (bf16[128,2048]{1,0:T(8,128)(2,1)}, bf16[128,2048]{1,0:T(8,128)(2,1)}, u32[]{:S(2)}, u32[]{:S(2)}) collective-permute-start(bf16[128,2048]{1,0:T(8,128)(2,1)} %get-tuple-element.12), channel_id=1, source_target_pairs={{0,1},{1,0},{2,3},{3,2},{4,5},{5,4},{6,7},{7,6},{8,9},{9,8},{10,11... | collective-permute-start | bytes 1572872 | tf_op jit(solution)/shard_map/ppermute | solution.py:491
  86.9 1.7 add_convert_fusion.10.refs_2_.refs_1_
  88.6 1.8 %add_convert_fusion.3.refs_1_.refs_0_ = bf16[128,1152]{1,0:T(8,128)(2,1)} fusion(bf16[128,1152]{1,0:T(8,128)(2,1)} %shard_map.82, bf16[768,2048]{1,0:T(8,128)(2,1)S(1)} %copy-done, s32[]{:T(128)S(6)} %select_n.79), kind=kLoop, calls=%fused_computation.3 | loop fusion | flops 589824 | bytes 884740 | tf_op jit(solution)/shard_map/convert_element_type | solution.py:578
  90.4 2.1 %collective-permute-start.17 = (bf16[512,2048]{1,0:T(8,128)(2,1)}, bf16[512,2048]{1,0:T(8,128)(2,1)}, u32[]{:S(2)}, u32[]{:S(2)}) collective-permute-start(bf16[512,2048]{1,0:T(8,128)(2,1)} %shard_map.84), channel_id=1, source_target_pairs={{1,5},{14,10},{17,21},{30,26}} | collective-permute-start | bytes 6291464 | tf_op jit(solution)/shard_map/ppermute | solution.py:503
  92.5 1.9 %collective-permute-start.14 = (bf16[128,1152]{1,0:T(8,128)(2,1)S(1)}, bf16[128,1152]{1,0:T(8,128)(2,1)}, u32[]{:S(2)}, u32[]{:S(2)}) collective-permute-start(bf16[128,1152]{1,0:T(8,128)(2,1)S(1)} %copy-done.4), channel_id=1, source_target_pairs={{12,8},{8,4},{4,0},{13,9},{9,5},{2,6},{6,10},{3,7},{7,11},{11,15},... | collective-permute-start | bytes 884744 | tf_op jit(solution)/shard_map/ppermute | solution.py:503
  94.5 2.2 %collective-permute-start.16 = (bf16[128,896]{1,0:T(8,128)(2,1)}, bf16[128,896]{1,0:T(8,128)(2,1)}, u32[]{:S(2)}, u32[]{:S(2)}) collective-permute-start(bf16[128,896]{1,0:T(8,128)(2,1)} %add_convert_fusion.10.refs_2_.refs_1_), channel_id=1, source_target_pairs={{12,8},{8,4},{4,0},{13,9},{9,5},{2,6},{6,10},{3,7},{7,11},{11,15},... | collective-permute-start | bytes 688136 | tf_op jit(solution)/shard_map/ppermute | solution.py:503
  96.7 6.3 %collective-permute-done.14.refs_0_ = bf16[128,1152]{1,0:T(8,128)(2,1)} collective-permute-done((bf16[128,1152]{1,0:T(8,128)(2,1)S(1)}, bf16[128,1152]{1,0:T(8,128)(2,1)}, u32[]{:S(2)}, u32[]{:S(2)}) %collective-permute-start.14) | collective-permute-done | bytes 294944 | tf_op jit(solution)/shard_map/ppermute | solution.py:503
  103.0 1.8 %add_convert_fusion.2.refs_2_.refs_1_ = bf16[128,1152]{1,0:T(8,128)(2,1)} fusion(bf16[128,1152]{1,0:T(8,128)(2,1)} %shard_map.83, bf16[768,2048]{1,0:T(8,128)(2,1)S(1)} %copy-done, s32[]{:T(128)S(6)} %select_n.85), kind=kLoop, calls=%fused_computation.2 | loop fusion | flops 589824 | bytes 884740 | tf_op jit(solution)/shard_map/convert_element_type | solution.py:578
  104.8 2.2 %collective-permute-start.19 = (bf16[128,1152]{1,0:T(8,128)(2,1)}, bf16[128,1152]{1,0:T(8,128)(2,1)}, u32[]{:S(2)}, u32[]{:S(2)}) collective-permute-start(bf16[128,1152]{1,0:T(8,128)(2,1)} %add_convert_fusion.2.refs_2_.refs_1_), channel_id=1, source_target_pairs={{12,8},{8,4},{4,0},{13,9},{9,5},{2,6},{6,10},{3,7},{7,11},{11,15},... | collective-permute-start | bytes 884744 | tf_op jit(solution)/shard_map/ppermute | solution.py:503
  108.0 1.7 add_convert_fusion.9.refs_3_.refs_2_
  109.7 3.6 %collective-permute-start.21 = (bf16[128,896]{1,0:T(8,128)(2,1)}, bf16[128,896]{1,0:T(8,128)(2,1)}, u32[]{:S(2)}, u32[]{:S(2)}) collective-permute-start(bf16[128,896]{1,0:T(8,128)(2,1)} %add_convert_fusion.9.refs_3_.refs_2_), channel_id=1, source_target_pairs={{12,8},{8,4},{4,0},{13,9},{9,5},{2,6},{6,10},{3,7},{7,11},{11,15},... | collective-permute-start | bytes 688136 | tf_op jit(solution)/shard_map/ppermute | solution.py:503
  113.3 1.7 collective-permute-start.26
  115.0 1.8 %add_convert_fusion.1.refs_0_ = bf16[128,1152]{1,0:T(8,128)(2,1)} fusion(bf16[128,1152]{1,0:T(8,128)(2,1)} %shard_map.87, bf16[768,2048]{1,0:T(8,128)(2,1)S(1)} %copy-done, s32[]{:T(128)S(6)} %select_n.87), kind=kLoop, calls=%fused_computation.1 | loop fusion | flops 589824 | bytes 884740 | tf_op jit(solution)/shard_map/convert_element_type | solution.py:578
  116.8 2.3 %collective-permute-start.22 = (bf16[128,1152]{1,0:T(8,128)(2,1)}, bf16[128,1152]{1,0:T(8,128)(2,1)}, u32[]{:S(2)}, u32[]{:S(2)}) collective-permute-start(bf16[128,1152]{1,0:T(8,128)(2,1)} %add_convert_fusion.1.refs_0_), channel_id=1, source_target_pairs={{8,4},{4,0},{9,5},{6,10},{7,11},{11,15},{24,20},{20,16},{25,21},{2... | collective-permute-start | bytes 884744 | tf_op jit(solution)/shard_map/ppermute | solution.py:503
  119.6 1.7 add_convert_fusion.8.refs_1_
  121.3 4.2 %collective-permute-start.24 = (bf16[128,896]{1,0:T(8,128)(2,1)}, bf16[128,896]{1,0:T(8,128)(2,1)}, u32[]{:S(2)}, u32[]{:S(2)}) collective-permute-start(bf16[128,896]{1,0:T(8,128)(2,1)} %add_convert_fusion.8.refs_1_), channel_id=1, source_target_pairs={{8,4},{4,0},{9,5},{6,10},{7,11},{11,15},{24,20},{20,16},{25,21},{2... | collective-permute-start | bytes 688136 | tf_op jit(solution)/shard_map/ppermute | solution.py:503
  126.4 2.6 %shard_map.85.own_ref.refs_1_.refs_6_ = bf16[256,2048]{1,0:T(8,128)(2,1)} custom-call(s32[1]{0:T(128)} %bitcast.9.u_ref, bf16[128,1152]{1,0:T(8,128)(2,1)S(1)} %copy-done.4, bf16[128,896]{1,0:T(8,128)(2,1)S(1)} %copy-done.13, bf16[128,1152]{1,0:T(8,128)(2,1)} %add_convert_fusion.2.refs_2_.refs_1_, bf16[128,896]{1,0:T(8,128)(2,1)} %add_convert_fusion.9.refs_3_.refs_2_, ...), custom_call_target="tpu_custom_call" | custom-call | tf_op jit(solution)/shard_map/pallas_call | solution.py:383
  129.0 1.8 %collective-permute-start.18 = (bf16[256,2048]{1,0:T(8,128)(2,1)}, bf16[256,2048]{1,0:T(8,128)(2,1)}, u32[]{:S(2)}, u32[]{:S(2)}) collective-permute-start(bf16[256,2048]{1,0:T(8,128)(2,1)} %shard_map.85.own_ref.refs_1_.refs_6_), channel_id=1, source_target_pairs={{0,2},{5,7},{10,8},{15,13},{16,18},{21,23},{26,24},{31,29}} | collective-permute-start | bytes 3145736 | tf_op jit(solution)/shard_map/ppermute | solution.py:503
  133.9 1.7 shard_map.92.refs_7_
  135.6 1.3 collective-permute-start.27
  136.9 1.7 shard_map.90
  141.6 2.8 %shard_map.94.refs_0_.refs_13_ = f32[256,2048]{1,0:T(8,128)S(1)} custom-call(s32[2]{0:T(128)S(1)} %pad_add_fusion.refs_0_.meta_ref, s32[64]{0:T(128)S(1)} %copy-done.16, s32[64]{0:T(128)S(1)} %copy-done.17, s32[16]{0:T(128)S(1)} %copy-done.19, s32[16]{0:T(128)S(1)} %fusion.2.refs_2_.refs_4_, s32[16]{0:T(128)S(1)} %fusion.1.refs_3_.refs_5_, ...), custom_call_target="tpu_custom_call" | custom-call | tf_op jit(solution)/shard_map/pallas_call | solution.py:470
  145.0 1.3 collective-permute-start.31
  146.3 1.3 collective-permute-start.30
  149.5 17.2 %collective-permute-done.32.refs_12_ = bf16[128,2048]{1,0:T(8,128)(2,1)S(1)} collective-permute-done((bf16[128,2048]{1,0:T(8,128)(2,1)S(1)}, bf16[128,2048]{1,0:T(8,128)(2,1)S(1)}, u32[]{:S(2)}, u32[]{:S(2)}) %collective-permute-start.32) | collective-permute-done | bytes 524320 | tf_op jit(solution)/shard_map/ppermute | solution.py:503
  166.7 3.2 %shard_map.97 = bf16[256,2048]{1,0:T(8,128)(2,1)} custom-call(s32[2]{0:T(128)S(1)} %pad_add_fusion.refs_0_.meta_ref, s32[64]{0:T(128)S(1)} %copy-done.16, s32[64]{0:T(128)S(1)} %copy-done.17, s32[16]{0:T(128)S(1)} %copy-done.19, s32[16]{0:T(128)S(1)} %fusion.2.refs_2_.refs_4_, s32[16]{0:T(128)S(1)} %fusion.1.refs_3_.refs_5_, s32[16]{0:T(128)S(1)} %fusion.refs_4_.refs_6_, ...), custom_call_target="tpu_custom_call" | custom-call | tf_op jit(solution)/shard_map/pallas_call | solution.py:470
  (109 shorter events, 27.0 us)
Async XLA Ops:
  0.0 1.2 copy-start.1
  3.5 3.3 %collective-permute-start = (bf16[272,2048]{1,0:T(8,128)(2,1)}, bf16[272,2048]{1,0:T(8,128)(2,1)S(1)}, u32[]{:S(2)}, u32[]{:S(2)}) collective-permute-start(bf16[272,2048]{1,0:T(8,128)(2,1)} %shard_map.73), channel_id=1, source_target_pairs={{0,1},{1,0},{2,3},{3,2},{4,5},{5,4},{6,7},{7,6},{8,9},{9,8},{10,11... | collective-permute-start | bytes 3342344 | tf_op jit(solution)/shard_map/ppermute | solution.py:491
  4.2 29.5 %collective-permute-start.1 = (bf16[272,2048]{1,0:T(8,128)(2,1)}, bf16[272,2048]{1,0:T(8,128)(2,1)}, u32[]{:S(2)}, u32[]{:S(2)}) collective-permute-start(bf16[272,2048]{1,0:T(8,128)(2,1)} %shard_map.73), channel_id=1, source_target_pairs={{0,2},{1,3},{2,0},{3,1},{4,6},{5,7},{6,4},{7,5},{8,10},{9,11},{10,... | collective-permute-start | bytes 3342344 | tf_op jit(solution)/shard_map/ppermute | solution.py:491
  7.8 1.2 copy-start.2
  9.0 11.3 %copy-start.3 = (bf16[16,16,2048]{2,1,0:T(8,128)(2,1)S(1)}, bf16[16,16,2048]{2,1,0:T(8,128)(2,1)}, u32[]{:S(2)}) copy-start(bf16[16,16,2048]{2,1,0:T(8,128)(2,1)} %param.7) | copy-start | bytes 3145732
  9.0 11.3 %copy-start.16 = (s32[64]{0:T(128)S(1)}, s32[64]{0:T(128)}, u32[]{:S(2)}) copy-start(s32[64]{0:T(128)} %refs_1_.11) | copy-start | bytes 772
  9.0 11.4 %copy-start.17 = (s32[64]{0:T(128)S(1)}, s32[64]{0:T(128)}, u32[]{:S(2)}) copy-start(s32[64]{0:T(128)} %refs_2_.7) | copy-start | bytes 772
  16.8 9.5 %collective-permute-start.3 = (bf16[128,896]{1,0:T(8,128)(2,1)S(1)}, bf16[128,896]{1,0:T(8,128)(2,1)S(1)}, u32[]{:S(2)}, u32[]{:S(2)}) collective-permute-start(bf16[128,896]{1,0:T(8,128)(2,1)S(1)} %slice.42), channel_id=1, source_target_pairs={{12,8},{13,9},{2,6},{3,7},{28,24},{29,25},{18,22},{19,23}} | collective-permute-start | bytes 688136 | tf_op jit(solution)/shard_map/ppermute | solution.py:503
  19.0 12.7 %collective-permute-start.2 = (bf16[128,1152]{1,0:T(8,128)(2,1)S(1)}, bf16[128,1152]{1,0:T(8,128)(2,1)S(1)}, u32[]{:S(2)}, u32[]{:S(2)}) collective-permute-start(bf16[128,1152]{1,0:T(8,128)(2,1)S(1)} %slice.40), channel_id=1, source_target_pairs={{12,8},{13,9},{2,6},{3,7},{28,24},{29,25},{18,22},{19,23}} | collective-permute-start | bytes 884744 | tf_op jit(solution)/shard_map/ppermute | solution.py:503
  28.1 6.8 %copy-start.12 = (bf16[128,896]{1,0:T(8,128)(2,1)S(1)}, bf16[128,896]{1,0:T(8,128)(2,1)}, u32[]{:S(2)}) copy-start(bf16[128,896]{1,0:T(8,128)(2,1)} %add_convert_fusion.13.refs_2_.refs_12_) | copy-start | bytes 688132
  33.7 5.7 %collective-permute-start.4 = (bf16[272,2048]{1,0:T(8,128)(2,1)}, bf16[272,2048]{1,0:T(8,128)(2,1)S(1)}, u32[]{:S(2)}, u32[]{:S(2)}) collective-permute-start(bf16[272,2048]{1,0:T(8,128)(2,1)} %shard_map.76.refs_7_.refs_3_), channel_id=1, source_target_pairs={{0,1},{1,0},{2,3},{3,2},{4,5},{5,4},{6,7},{7,6},{8,9},{9,8},{10,11... | collective-permute-start | bytes 3342344 | tf_op jit(solution)/shard_map/ppermute | solution.py:491
  34.9 17.8 %collective-permute-start.7 = (bf16[128,896]{1,0:T(8,128)(2,1)S(1)}, bf16[128,896]{1,0:T(8,128)(2,1)S(1)}, u32[]{:S(2)}, u32[]{:S(2)}) collective-permute-start(bf16[128,896]{1,0:T(8,128)(2,1)S(1)} %copy-done.12), channel_id=1, source_target_pairs={{12,8},{8,4},{13,9},{9,5},{2,6},{6,10},{3,7},{7,11},{28,24},{24,20... | collective-permute-start | bytes 688136 | tf_op jit(solution)/shard_map/ppermute | solution.py:503
  37.5 18.8 %collective-permute-start.5 = (bf16[128,1152]{1,0:T(8,128)(2,1)}, bf16[128,1152]{1,0:T(8,128)(2,1)S(1)}, u32[]{:S(2)}, u32[]{:S(2)}) collective-permute-start(bf16[128,1152]{1,0:T(8,128)(2,1)} %add_convert_fusion.6.refs_1_.refs_11_), channel_id=1, source_target_pairs={{12,8},{8,4},{13,9},{9,5},{2,6},{6,10},{3,7},{7,11},{28,24},{24,20... | collective-permute-start | bytes 884744 | tf_op jit(solution)/shard_map/ppermute | solution.py:503
  39.4 1.0 copy-start.21
  41.4 17.9 %copy-start.15 = (bf16[256,128]{1,0:T(8,128)(2,1)S(1)}, bf16[256,128]{1,0:T(8,128)(2,1)}, u32[]{:S(2)}) copy-start(bf16[256,128]{1,0:T(8,128)(2,1)} %copy-done.14) | copy-start | bytes 196612
  54.4 14.8 %collective-permute-start.12 = (bf16[128,896]{1,0:T(8,128)(2,1)}, bf16[128,896]{1,0:T(8,128)(2,1)}, u32[]{:S(2)}, u32[]{:S(2)}) collective-permute-start(bf16[128,896]{1,0:T(8,128)(2,1)} %add_convert_fusion.12.refs_8_.refs_1_), channel_id=1, source_target_pairs={{12,8},{8,4},{4,0},{13,9},{9,5},{2,6},{6,10},{3,7},{7,11},{11,15},... | collective-permute-start | bytes 688136 | tf_op jit(solution)/shard_map/ppermute | solution.py:503
  57.4 8.4 %copy-start.7 = (bf16[128,1152]{1,0:T(8,128)(2,1)}, bf16[128,1152]{1,0:T(8,128)(2,1)S(1)}, u32[]{:S(2)}) copy-start(bf16[128,1152]{1,0:T(8,128)(2,1)S(1)} %add_convert_fusion.5.refs_7_.refs_0_) | copy-start | bytes 884740
  57.4 15.6 %collective-permute-start.6 = (bf16[128,1152]{1,0:T(8,128)(2,1)S(1)}, bf16[128,1152]{1,0:T(8,128)(2,1)}, u32[]{:S(2)}, u32[]{:S(2)}) collective-permute-start(bf16[128,1152]{1,0:T(8,128)(2,1)S(1)} %add_convert_fusion.5.refs_7_.refs_0_), channel_id=1, source_target_pairs={{12,8},{8,4},{4,0},{13,9},{9,5},{2,6},{6,10},{3,7},{7,11},{11,15},... | collective-permute-start | bytes 884744 | tf_op jit(solution)/shard_map/ppermute | solution.py:503
  59.3 9.8 %copy-start = (bf16[768,2048]{1,0:T(8,128)(2,1)S(1)}, bf16[768,2048]{1,0:T(8,128)(2,1)}, u32[]{:S(2)}) copy-start(bf16[768,2048]{1,0:T(8,128)(2,1)} %shard_map.77.refs_1_) | copy-start | bytes 9437188
  65.7 12.0 %collective-permute-start.10 = (bf16[256,128]{1,0:T(8,128)(2,1)}, bf16[256,128]{1,0:T(8,128)(2,1)S(1)}, u32[]{:S(2)}, u32[]{:S(2)}) collective-permute-start(bf16[256,128]{1,0:T(8,128)(2,1)} %shard_map.78.refs_1_.refs_0_), channel_id=1, source_target_pairs={{0,4},{4,0},{8,12},{12,8},{1,5},{5,1},{9,13},{13,9},{2,6},{6,2},{1... | collective-permute-start | bytes 196616 | tf_op jit(solution)/shard_map/ppermute | solution.py:617
  67.9 9.9 %collective-permute-start.11 = (bf16[256,128]{1,0:T(8,128)(2,1)}, bf16[256,128]{1,0:T(8,128)(2,1)}, u32[]{:S(2)}, u32[]{:S(2)}) collective-permute-start(bf16[256,128]{1,0:T(8,128)(2,1)} %shard_map.78.refs_1_.refs_0_), channel_id=1, source_target_pairs={{0,8},{4,12},{8,0},{12,4},{1,9},{5,13},{9,1},{13,5},{2,10},{6,14},... | collective-permute-start | bytes 196616 | tf_op jit(solution)/shard_map/ppermute | solution.py:617
  67.9 9.9 %collective-permute-start.9 = (bf16[256,128]{1,0:T(8,128)(2,1)}, bf16[256,128]{1,0:T(8,128)(2,1)}, u32[]{:S(2)}, u32[]{:S(2)}) collective-permute-start(bf16[256,128]{1,0:T(8,128)(2,1)} %shard_map.78.refs_1_.refs_0_), channel_id=1, source_target_pairs={{0,12},{4,8},{8,4},{12,0},{1,13},{5,9},{9,5},{13,1},{2,14},{6,10},... | collective-permute-start | bytes 196616 | tf_op jit(solution)/shard_map/ppermute | solution.py:617
  70.8 16.1 %collective-permute-start.13 = (bf16[128,896]{1,0:T(8,128)(2,1)}, bf16[128,896]{1,0:T(8,128)(2,1)}, u32[]{:S(2)}, u32[]{:S(2)}) collective-permute-start(bf16[128,896]{1,0:T(8,128)(2,1)} %add_convert_fusion.11.refs_6_.refs_3_), channel_id=1, source_target_pairs={{12,8},{8,4},{4,0},{13,9},{9,5},{2,6},{6,10},{3,7},{7,11},{11,15},... | collective-permute-start | bytes 688136 | tf_op jit(solution)/shard_map/ppermute | solution.py:503
  74.0 10.4 %copy-start.5 = (bf16[128,1152]{1,0:T(8,128)(2,1)}, bf16[128,1152]{1,0:T(8,128)(2,1)S(1)}, u32[]{:S(2)}) copy-start(bf16[128,1152]{1,0:T(8,128)(2,1)S(1)} %add_convert_fusion.4.refs_5_.refs_2_) | copy-start | bytes 884740
  74.1 14.6 %collective-permute-start.8 = (bf16[128,1152]{1,0:T(8,128)(2,1)S(1)}, bf16[128,1152]{1,0:T(8,128)(2,1)}, u32[]{:S(2)}, u32[]{:S(2)}) collective-permute-start(bf16[128,1152]{1,0:T(8,128)(2,1)S(1)} %add_convert_fusion.4.refs_5_.refs_2_), channel_id=1, source_target_pairs={{12,8},{8,4},{4,0},{13,9},{9,5},{2,6},{6,10},{3,7},{7,11},{11,15},... | collective-permute-start | bytes 884744 | tf_op jit(solution)/shard_map/ppermute | solution.py:503
  84.5 4.2 %copy-start.10 = (bf16[128,2048]{1,0:T(8,128)(2,1)}, bf16[128,2048]{1,0:T(8,128)(2,1)S(1)}, u32[]{:S(2)}) copy-start(bf16[128,2048]{1,0:T(8,128)(2,1)S(1)} %get-tuple-element.11.refs_1_.refs_9_) | copy-start | bytes 1572868
  84.5 12.3 %collective-permute-start.15 = (bf16[128,2048]{1,0:T(8,128)(2,1)}, bf16[128,2048]{1,0:T(8,128)(2,1)}, u32[]{:S(2)}, u32[]{:S(2)}) collective-permute-start(bf16[128,2048]{1,0:T(8,128)(2,1)} %get-tuple-element.12), channel_id=1, source_target_pairs={{0,1},{1,0},{2,3},{3,2},{4,5},{5,4},{6,7},{7,6},{8,9},{9,8},{10,11... | collective-permute-start | bytes 1572872 | tf_op jit(solution)/shard_map/ppermute | solution.py:491
  90.4 2.1 %copy-start.4 = (bf16[128,1152]{1,0:T(8,128)(2,1)S(1)}, bf16[128,1152]{1,0:T(8,128)(2,1)}, u32[]{:S(2)}) copy-start(bf16[128,1152]{1,0:T(8,128)(2,1)} %add_convert_fusion.3.refs_1_.refs_0_) | copy-start | bytes 884740
  90.4 35.1 %collective-permute-start.17 = (bf16[512,2048]{1,0:T(8,128)(2,1)}, bf16[512,2048]{1,0:T(8,128)(2,1)}, u32[]{:S(2)}, u32[]{:S(2)}) collective-permute-start(bf16[512,2048]{1,0:T(8,128)(2,1)} %shard_map.84), channel_id=1, source_target_pairs={{1,5},{14,10},{17,21},{30,26}} | collective-permute-start | bytes 6291464 | tf_op jit(solution)/shard_map/ppermute | solution.py:503
  92.5 10.5 %collective-permute-start.14 = (bf16[128,1152]{1,0:T(8,128)(2,1)S(1)}, bf16[128,1152]{1,0:T(8,128)(2,1)}, u32[]{:S(2)}, u32[]{:S(2)}) collective-permute-start(bf16[128,1152]{1,0:T(8,128)(2,1)S(1)} %copy-done.4), channel_id=1, source_target_pairs={{12,8},{8,4},{4,0},{13,9},{9,5},{2,6},{6,10},{3,7},{7,11},{11,15},... | collective-permute-start | bytes 884744 | tf_op jit(solution)/shard_map/ppermute | solution.py:503
  94.5 18.9 %collective-permute-start.20 = (bf16[128,2048]{1,0:T(8,128)(2,1)}, bf16[128,2048]{1,0:T(8,128)(2,1)}, u32[]{:S(2)}, u32[]{:S(2)}) collective-permute-start(bf16[128,2048]{1,0:T(8,128)(2,1)} %get-tuple-element.13), channel_id=1, source_target_pairs={{0,2},{1,3},{2,0},{3,1},{4,6},{5,7},{6,4},{7,5},{8,10},{9,11},{10,... | collective-permute-start | bytes 1572872 | tf_op jit(solution)/shard_map/ppermute | solution.py:491
  94.5 13.5 %collective-permute-start.16 = (bf16[128,896]{1,0:T(8,128)(2,1)}, bf16[128,896]{1,0:T(8,128)(2,1)}, u32[]{:S(2)}, u32[]{:S(2)}) collective-permute-start(bf16[128,896]{1,0:T(8,128)(2,1)} %add_convert_fusion.10.refs_2_.refs_1_), channel_id=1, source_target_pairs={{12,8},{8,4},{4,0},{13,9},{9,5},{2,6},{6,10},{3,7},{7,11},{11,15},... | collective-permute-start | bytes 688136 | tf_op jit(solution)/shard_map/ppermute | solution.py:503
  104.8 10.2 %collective-permute-start.19 = (bf16[128,1152]{1,0:T(8,128)(2,1)}, bf16[128,1152]{1,0:T(8,128)(2,1)}, u32[]{:S(2)}, u32[]{:S(2)}) collective-permute-start(bf16[128,1152]{1,0:T(8,128)(2,1)} %add_convert_fusion.2.refs_2_.refs_1_), channel_id=1, source_target_pairs={{12,8},{8,4},{4,0},{13,9},{9,5},{2,6},{6,10},{3,7},{7,11},{11,15},... | collective-permute-start | bytes 884744 | tf_op jit(solution)/shard_map/ppermute | solution.py:503
  108.0 22.8 %collective-permute-start.23 = (bf16[128,2048]{1,0:T(8,128)(2,1)}, bf16[128,2048]{1,0:T(8,128)(2,1)}, u32[]{:S(2)}, u32[]{:S(2)}) collective-permute-start(bf16[128,2048]{1,0:T(8,128)(2,1)} %get-tuple-element.14), channel_id=1, source_target_pairs={{0,3},{1,2},{2,1},{3,0},{4,7},{5,6},{6,5},{7,4},{8,11},{9,10},{10,... | collective-permute-start | bytes 1572872 | tf_op jit(solution)/shard_map/ppermute | solution.py:491
  109.7 9.9 %collective-permute-start.21 = (bf16[128,896]{1,0:T(8,128)(2,1)}, bf16[128,896]{1,0:T(8,128)(2,1)}, u32[]{:S(2)}, u32[]{:S(2)}) collective-permute-start(bf16[128,896]{1,0:T(8,128)(2,1)} %add_convert_fusion.9.refs_3_.refs_2_), channel_id=1, source_target_pairs={{12,8},{8,4},{4,0},{13,9},{9,5},{2,6},{6,10},{3,7},{7,11},{11,15},... | collective-permute-start | bytes 688136 | tf_op jit(solution)/shard_map/ppermute | solution.py:503
  113.3 19.6 %collective-permute-start.26 = (bf16[256,2048]{1,0:T(8,128)(2,1)}, bf16[256,2048]{1,0:T(8,128)(2,1)}, u32[]{:S(2)}, u32[]{:S(2)}) collective-permute-start(bf16[256,2048]{1,0:T(8,128)(2,1)} %shard_map.91), channel_id=1, source_target_pairs={{1,5},{14,10},{17,21},{30,26}} | collective-permute-start | bytes 3145736 | tf_op jit(solution)/shard_map/ppermute | solution.py:503
  116.8 14.0 %collective-permute-start.22 = (bf16[128,1152]{1,0:T(8,128)(2,1)}, bf16[128,1152]{1,0:T(8,128)(2,1)}, u32[]{:S(2)}, u32[]{:S(2)}) collective-permute-start(bf16[128,1152]{1,0:T(8,128)(2,1)} %add_convert_fusion.1.refs_0_), channel_id=1, source_target_pairs={{8,4},{4,0},{9,5},{6,10},{7,11},{11,15},{24,20},{20,16},{25,21},{2... | collective-permute-start | bytes 884744 | tf_op jit(solution)/shard_map/ppermute | solution.py:503
  121.3 9.5 %collective-permute-start.24 = (bf16[128,896]{1,0:T(8,128)(2,1)}, bf16[128,896]{1,0:T(8,128)(2,1)}, u32[]{:S(2)}, u32[]{:S(2)}) collective-permute-start(bf16[128,896]{1,0:T(8,128)(2,1)} %add_convert_fusion.8.refs_1_), channel_id=1, source_target_pairs={{8,4},{4,0},{9,5},{6,10},{7,11},{11,15},{24,20},{20,16},{25,21},{2... | collective-permute-start | bytes 688136 | tf_op jit(solution)/shard_map/ppermute | solution.py:503
  129.0 3.9 %copy-start.6 = (bf16[128,1152]{1,0:T(8,128)(2,1)S(1)}, bf16[128,1152]{1,0:T(8,128)(2,1)}, u32[]{:S(2)}) copy-start(bf16[128,1152]{1,0:T(8,128)(2,1)} %copy-done.5) | copy-start | bytes 884740
  129.0 11.0 %collective-permute-start.18 = (bf16[256,2048]{1,0:T(8,128)(2,1)}, bf16[256,2048]{1,0:T(8,128)(2,1)}, u32[]{:S(2)}, u32[]{:S(2)}) collective-permute-start(bf16[256,2048]{1,0:T(8,128)(2,1)} %shard_map.85.own_ref.refs_1_.refs_6_), channel_id=1, source_target_pairs={{0,2},{5,7},{10,8},{15,13},{16,18},{21,23},{26,24},{31,29}} | collective-permute-start | bytes 3145736 | tf_op jit(solution)/shard_map/ppermute | solution.py:503
  135.6 5.9 %collective-permute-start.27 = (bf16[256,2048]{1,0:T(8,128)(2,1)S(1)}, bf16[256,2048]{1,0:T(8,128)(2,1)S(1)}, u32[]{:S(2)}, u32[]{:S(2)}) collective-permute-start(bf16[256,2048]{1,0:T(8,128)(2,1)S(1)} %shard_map.92.refs_7_), channel_id=1, source_target_pairs={{0,1},{5,4},{10,11},{15,14},{2,3},{7,6},{8,9},{13,12},{16,17},{21,... | collective-permute-start | bytes 3145736 | tf_op jit(solution)/shard_map/ppermute | solution.py:503
  138.6 5.9 %collective-permute-start.25 = (bf16[256,2048]{1,0:T(8,128)(2,1)S(1)}, bf16[256,2048]{1,0:T(8,128)(2,1)S(1)}, u32[]{:S(2)}, u32[]{:S(2)}) collective-permute-start(bf16[256,2048]{1,0:T(8,128)(2,1)S(1)} %get-tuple-element.15.own_ref), channel_id=1, source_target_pairs={{0,2},{5,7},{10,8},{15,13},{16,18},{21,23},{26,24},{31,29}} | collective-permute-start | bytes 3145736 | tf_op jit(solution)/shard_map/ppermute | solution.py:503
  139.3 1.3 collective-permute-start.28
  140.6 1.0 copy-start.11
  140.8 6.9 %collective-permute-start.29 = (bf16[128,2048]{1,0:T(8,128)(2,1)S(1)}, bf16[128,2048]{1,0:T(8,128)(2,1)S(1)}, u32[]{:S(2)}, u32[]{:S(2)}) collective-permute-start(bf16[128,2048]{1,0:T(8,128)(2,1)S(1)} %shard_map.93.refs_13_.own_ref), channel_id=1, source_target_pairs={{0,2},{5,7},{10,8},{15,13},{16,18},{21,23},{26,24},{31,29}} | collective-permute-start | bytes 1572872 | tf_op jit(solution)/shard_map/ppermute | solution.py:503
  145.0 21.7 %collective-permute-start.31 = (bf16[256,2048]{1,0:T(8,128)(2,1)S(1)}, bf16[256,2048]{1,0:T(8,128)(2,1)S(1)}, u32[]{:S(2)}, u32[]{:S(2)}) collective-permute-start(bf16[256,2048]{1,0:T(8,128)(2,1)S(1)} %shard_map.95.refs_8_), channel_id=1, source_target_pairs={{0,1},{5,4},{10,11},{15,14},{2,3},{7,6},{8,9},{13,12},{16,17},{21,... | collective-permute-start | bytes 3145736 | tf_op jit(solution)/shard_map/ppermute | solution.py:503
  146.3 20.4 %collective-permute-start.30 = (bf16[256,2048]{1,0:T(8,128)(2,1)}, bf16[256,2048]{1,0:T(8,128)(2,1)S(1)}, u32[]{:S(2)}, u32[]{:S(2)}) collective-permute-start(bf16[256,2048]{1,0:T(8,128)(2,1)} %shard_map.86.refs_2_.refs_7_), channel_id=1, source_target_pairs={{0,1},{5,4},{10,11},{15,14},{2,3},{7,6},{8,9},{13,12},{16,17},{21,... | collective-permute-start | bytes 3145736 | tf_op jit(solution)/shard_map/ppermute | solution.py:503
  148.2 18.5 %collective-permute-start.32 = (bf16[128,2048]{1,0:T(8,128)(2,1)S(1)}, bf16[128,2048]{1,0:T(8,128)(2,1)S(1)}, u32[]{:S(2)}, u32[]{:S(2)}) collective-permute-start(bf16[128,2048]{1,0:T(8,128)(2,1)S(1)} %shard_map.96.refs_9_), channel_id=1, source_target_pairs={{0,1},{5,4},{10,11},{15,14},{2,3},{7,6},{8,9},{13,12},{16,17},{21,... | collective-permute-start | bytes 1572872 | tf_op jit(solution)/shard_map/ppermute | solution.py:503
  (7 other events, 6.2 us)
